TPU v7x, 32 devices: a whole 2x2x4 slice. The times are simulated.
32 devices in a mesh: dp: 8 (over z, core), tensor: 4 (over y, x).
Axes of the slice: x: 2, y: 2, z: 4, core: 2. Of those that a mesh axis runs over, the one named last changes fastest.
Arguments:
- tokens: bfloat16 [16, 1024, 2048], P(None, ('tensor', 'dp')), may hold values from -6 to 6
- cotangent: bfloat16 [16, 1024, 2048], P('dp', 'tensor'), may hold values from -6 to 6
- lengths: int32 [16], replicated, may hold values from 256 to 1024, as said below
- dealing: int32 [16], replicated, may hold values from 0 to 15, as said below
- query_weight: float32 [2048, 2048], P('dp', 'tensor'), may hold values from -0.125 to 0.125
- key_weight: float32 [2048, 2048], P('dp', 'tensor'), may hold values from -0.125 to 0.125
- value_weight: float32 [2048, 2048], P('dp', 'tensor'), may hold values from -0.125 to 0.125
- output_weight: float32 [2048, 2048], P('tensor', 'dp'), may hold values from -3 to 3
- up_weight: float32 [2048, 8192], P('dp', 'tensor'), may hold values from -0.125 to 0.125
- down_weight: float32 [8192, 2048], P('tensor', 'dp'), may hold values from -0.0625 to 0.0625
- query_bias: float32 [2048], P(('tensor', 'dp')), may hold values from -3 to 3
- value_bias: float32 [2048], P(('tensor', 'dp')), may hold values from -3 to 3
- output_bias: float32 [2048], P(('tensor', 'dp')), may hold values from -3 to 3
- attention_gain: float32 [2048], P(('tensor', 'dp')), may hold values from 0.25 to 1.75
- attention_shift: float32 [2048], P(('tensor', 'dp')), may hold values from -3 to 3
- up_bias: float32 [8192], P(('tensor', 'dp')), may hold values from -3 to 3
- down_bias: float32 [2048], P(('tensor', 'dp')), may hold values from -3 to 3
- feedforward_gain: float32 [2048], P(('tensor', 'dp')), may hold values from 0.25 to 1.75
- feedforward_shift: float32 [2048], P(('tensor', 'dp')), may hold values from -3 to 3
Outputs:
- result: bfloat16 [16, 1024, 2048], P(None, ('tensor', 'dp'))
- token_gradient: bfloat16 [16, 1024, 2048], P(None, ('tensor', 'dp'))
- query_weight_gradient: float32 [2048, 2048], P('dp', 'tensor')
- key_weight_gradient: float32 [2048, 2048], P('dp', 'tensor')
- value_weight_gradient: float32 [2048, 2048], P('dp', 'tensor')
- output_weight_gradient: float32 [2048, 2048], P('tensor', 'dp')
- up_weight_gradient: float32 [2048, 8192], P('dp', 'tensor')
- down_weight_gradient: float32 [8192, 2048], P('tensor', 'dp')
- query_bias_gradient: float32 [2048], P(('tensor', 'dp'))
- value_bias_gradient: float32 [2048], P(('tensor', 'dp'))
- output_bias_gradient: float32 [2048], P(('tensor', 'dp'))
- attention_gain_gradient: float32 [2048], P(('tensor', 'dp'))
- attention_shift_gradient: float32 [2048], P(('tensor', 'dp'))
- up_bias_gradient: float32 [8192], P(('tensor', 'dp'))
- down_bias_gradient: float32 [2048], P(('tensor', 'dp'))
- feedforward_gain_gradient: float32 [2048], P(('tensor', 'dp'))
- feedforward_shift_gradient: float32 [2048], P(('tensor', 'dp'))
Inputs may be any that keep to these rules, and one draw needn't show every extreme that they name: `lengths`: at least 8 sequences are longer than 960 tokens, and at least one has exactly 1024. `dealing`: each sequence stands in exactly one dealt slot.
All inputs are finite; a program needn't handle non-finite values.
Results may differ from a plain program's by a relative error of at most 0.019.
Values may be sent and summed in bfloat16 or wider, within the bound.
No kernel may reach another device: no remote copies, remote signals or barrier semaphores. Data moves between devices by JAX's collectives and lax.ppermute only.
A program may use at most 256 MiB of HBM per device.

v0:
```python
import math

import jax
import jax.numpy as jnp
from jax import lax
from jax.sharding import PartitionSpec as P

HEAD = 128


norm_epsilon = 1e-05
masked_score = -1e30


def layer_norm(inputs, gain, shift):
    centered = inputs - jnp.mean(inputs, axis=-1, keepdims=True)
    variance = jnp.mean(centered * centered, axis=-1, keepdims=True)
    return centered * lax.rsqrt(variance + norm_epsilon) * gain + shift


def gelu_tanh(inputs):
    return jax.nn.gelu(inputs, approximate=True)


def matmul(left, right):
    return jnp.dot(left, right, preferred_element_type=jnp.float32)


def local(
    tokens,
    cotangent,
    lengths,
    dealing,
    query_weight,
    key_weight,
    value_weight,
    output_weight,
    up_weight,
    down_weight,
    query_bias,
    value_bias,
    output_bias,
    attention_gain,
    attention_shift,
    up_bias,
    down_bias,
    feedforward_gain,
    feedforward_shift,
):
    groups = lax.axis_size("dp")
    splits = lax.axis_size("tensor")
    slot_count = cotangent.shape[0]
    local_rows = cotangent.shape[1]
    model_width = cotangent.shape[2]
    arrival_rows = tokens.shape[1]
    sequence_length = local_rows * splits
    all_rows = slot_count * sequence_length
    dealt_tokens = jnp.take(tokens, dealing, axis=0).reshape(
        groups, slot_count, arrival_rows, model_width
    )
    arrived = lax.all_to_all(dealt_tokens, "dp", split_axis=0, concat_axis=2, tiled=True)
    sequence_rows = arrived.reshape(slot_count, local_rows, model_width)
    row_vectors = jnp.stack(
        [
            output_bias,
            attention_gain,
            attention_shift,
            down_bias,
            feedforward_gain,
            feedforward_shift,
        ]
    ).astype(jnp.bfloat16)
    head_vectors = jnp.stack([query_bias, value_bias]).astype(jnp.bfloat16)
    (
        query_block,
        key_block,
        value_block,
        output_block,
        up_block,
        down_block,
        head_bias,
        hidden_bias,
        row_shared,
    ) = (
        lax.all_gather(query_weight.astype(jnp.bfloat16), "dp", axis=0, tiled=True),
        lax.all_gather(key_weight.astype(jnp.bfloat16), "dp", axis=0, tiled=True),
        lax.all_gather(value_weight.astype(jnp.bfloat16), "dp", axis=0, tiled=True),
        lax.all_gather(output_weight.astype(jnp.bfloat16), "dp", axis=1, tiled=True),
        lax.all_gather(up_weight.astype(jnp.bfloat16), "dp", axis=0, tiled=True),
        lax.all_gather(down_weight.astype(jnp.bfloat16), "dp", axis=1, tiled=True),
        lax.all_gather(head_vectors, "dp", axis=1, tiled=True),
        lax.all_gather(up_bias.astype(jnp.bfloat16), "dp", axis=0, tiled=True),
        lax.all_gather(row_vectors, "dp", axis=1, tiled=True),
    )
    full_rows, row_params = (
        lax.all_gather(sequence_rows, "tensor", axis=1, tiled=True),
        lax.all_gather(row_shared, "tensor", axis=1, tiled=True),
    )
    row_params = row_params.astype(jnp.float32)
    flat_rows = full_rows.reshape(all_rows, model_width)
    local_width = query_block.shape[1]
    heads_here = local_width // HEAD
    head_shape = (slot_count, sequence_length, heads_here, HEAD)
    queries = (
        (matmul(flat_rows, query_block) + head_bias[0]).astype(jnp.bfloat16).reshape(head_shape)
    )
    key_rows = matmul(flat_rows, key_block).astype(jnp.bfloat16).reshape(head_shape)
    values = (
        (matmul(flat_rows, value_block) + head_bias[1]).astype(jnp.bfloat16).reshape(head_shape)
    )
    group_index = lax.axis_index("dp")
    dealt_lengths = jnp.take(lengths, dealing, axis=0)
    slot_lengths = lax.dynamic_slice_in_dim(dealt_lengths, group_index * slot_count, slot_count)
    key_valid = jnp.arange(sequence_length)[None, :] < slot_lengths[:, None]
    key_mask = key_valid[:, None, None, :]
    block_rows = min(512, sequence_length)
    block_count = sequence_length // block_rows
    head_root = math.sqrt(HEAD)
    starts = jnp.arange(block_count) * block_rows

    def block_scores(first_row):
        query_part = lax.dynamic_slice_in_dim(queries, first_row, block_rows, 1)
        scores = (
            jnp.einsum("sqhd,skhd->shqk", query_part, key_rows, preferred_element_type=jnp.float32)
            / head_root
        )
        return (query_part, jnp.where(key_mask, scores, masked_score))

    def attend_block(first_row):
        unused_part, scores = block_scores(first_row)
        row_peak = jnp.max(scores, axis=-1, keepdims=True)
        exponent = jnp.exp(scores - row_peak)
        row_total = jnp.sum(exponent, axis=-1, keepdims=True)
        attention = (exponent / row_total).astype(jnp.bfloat16)
        mixture = jnp.einsum(
            "shqk,skhd->sqhd", attention, values, preferred_element_type=jnp.float32
        ).astype(jnp.bfloat16)
        return (mixture, (row_peak + jnp.log(row_total))[..., 0])

    mixtures, log_totals = lax.map(attend_block, starts)
    mixture_rows = jnp.moveaxis(mixtures, 0, 1).reshape(all_rows, local_width)
    head_terms = matmul(mixture_rows, output_block).reshape(
        slot_count, sequence_length, model_width
    )
    attended = lax.psum_scatter(head_terms, "tensor", scatter_dimension=1, tiled=True)
    residual_one = sequence_rows.astype(jnp.float32) + (attended + row_params[0])
    first_norm, norm_one_back = jax.vjp(layer_norm, residual_one, row_params[1], row_params[2])
    first_full = lax.all_gather(
        first_norm.astype(jnp.bfloat16), "tensor", axis=1, tiled=True
    ).reshape(all_rows, model_width)
    hidden = matmul(first_full, up_block) + hidden_bias
    active_out, gelu_back = jax.vjp(gelu_tanh, hidden)
    active = active_out.astype(jnp.bfloat16)
    hidden_terms = matmul(active, down_block).reshape(slot_count, sequence_length, model_width)
    feedforward = lax.psum_scatter(hidden_terms, "tensor", scatter_dimension=1, tiled=True)
    residual_two = first_norm + (feedforward + row_params[3])
    output_rows, norm_two_back = jax.vjp(layer_norm, residual_two, row_params[4], row_params[5])
    grad_two, gain_two_grad, shift_two_grad = norm_two_back(cotangent.astype(jnp.float32))
    down_bias_grad = jnp.sum(grad_two, axis=(0, 1))
    down_full = lax.all_gather(grad_two.astype(jnp.bfloat16), "tensor", axis=1, tiled=True).reshape(
        all_rows, model_width
    )
    down_weight_grad = jnp.einsum(
        "rf,rd->fd", active, down_full, preferred_element_type=jnp.float32
    )
    active_grad = jnp.einsum("rd,fd->rf", down_full, down_block, preferred_element_type=jnp.float32)
    hidden_grad = gelu_back(active_grad)[0].astype(jnp.bfloat16)
    up_bias_grad = jnp.sum(hidden_grad.astype(jnp.float32), axis=0)
    up_weight_grad = jnp.einsum(
        "rd,rf->df", first_full, hidden_grad, preferred_element_type=jnp.float32
    )
    first_terms = jnp.einsum(
        "rf,df->rd", hidden_grad, up_block, preferred_element_type=jnp.float32
    ).reshape(slot_count, sequence_length, model_width)
    norm_two_vectors = jnp.stack([down_bias_grad, gain_two_grad, shift_two_grad])
    first_back, norm_two_sums = (
        lax.psum_scatter(first_terms, "tensor", scatter_dimension=1, tiled=True),
        lax.psum_scatter(norm_two_vectors, "tensor", scatter_dimension=1, tiled=True),
    )
    first_grad = grad_two + first_back
    grad_one, gain_one_grad, shift_one_grad = norm_one_back(first_grad)
    output_bias_grad = jnp.sum(grad_one, axis=(0, 1))
    attended_full = lax.all_gather(
        grad_one.astype(jnp.bfloat16), "tensor", axis=1, tiled=True
    ).reshape(all_rows, model_width)
    output_weight_grad = jnp.einsum(
        "rh,rd->hd", mixture_rows, attended_full, preferred_element_type=jnp.float32
    )
    mixture_grad = (
        jnp.einsum("rd,hd->rh", attended_full, output_block, preferred_element_type=jnp.float32)
        .astype(jnp.bfloat16)
        .reshape(head_shape)
    )

    def back_block(carried, first_row):
        key_total, value_total = carried
        block_index = first_row // block_rows
        query_part, scores = block_scores(first_row)
        grad_part = lax.dynamic_slice_in_dim(mixture_grad, first_row, block_rows, 1)
        attention = jnp.exp(scores - log_totals[block_index][..., None])
        weight_grad = jnp.einsum(
            "sqhd,skhd->shqk", grad_part, values, preferred_element_type=jnp.float32
        )
        score_grad = (
            attention * (weight_grad - jnp.sum(attention * weight_grad, axis=-1, keepdims=True))
        ).astype(jnp.bfloat16)
        query_grad = (
            jnp.einsum("shqk,skhd->sqhd", score_grad, key_rows, preferred_element_type=jnp.float32)
            / head_root
        ).astype(jnp.bfloat16)
        key_total = (
            key_total
            + jnp.einsum(
                "shqk,sqhd->skhd", score_grad, query_part, preferred_element_type=jnp.float32
            )
            / head_root
        )
        value_total = value_total + jnp.einsum(
            "shqk,sqhd->skhd",
            attention.astype(jnp.bfloat16),
            grad_part,
            preferred_element_type=jnp.float32,
        )
        return ((key_total, value_total), query_grad)

    zero_heads = jnp.zeros(head_shape, jnp.float32)
    (key_total, value_total), query_grads = lax.scan(back_block, (zero_heads, zero_heads), starts)
    query_grad_rows = jnp.moveaxis(query_grads, 0, 1).reshape(all_rows, local_width)
    key_grad_rows = key_total.astype(jnp.bfloat16).reshape(all_rows, local_width)
    value_grad_rows = value_total.astype(jnp.bfloat16).reshape(all_rows, local_width)
    query_bias_grad = jnp.sum(query_grad_rows.astype(jnp.float32), axis=0)
    value_bias_grad = jnp.sum(value_grad_rows.astype(jnp.float32), axis=0)
    query_weight_grad = jnp.einsum(
        "rd,rh->dh", flat_rows, query_grad_rows, preferred_element_type=jnp.float32
    )
    key_weight_grad = jnp.einsum(
        "rd,rh->dh", flat_rows, key_grad_rows, preferred_element_type=jnp.float32
    )
    value_weight_grad = jnp.einsum(
        "rd,rh->dh", flat_rows, value_grad_rows, preferred_element_type=jnp.float32
    )
    row_terms = (
        jnp.einsum("rh,dh->rd", query_grad_rows, query_block, preferred_element_type=jnp.float32)
        + jnp.einsum("rh,dh->rd", key_grad_rows, key_block, preferred_element_type=jnp.float32)
        + jnp.einsum("rh,dh->rd", value_grad_rows, value_block, preferred_element_type=jnp.float32)
    )
    row_terms = row_terms.reshape(slot_count, sequence_length, model_width)
    norm_one_vectors = jnp.stack([output_bias_grad, gain_one_grad, shift_one_grad])
    row_back, norm_one_sums = (
        lax.psum_scatter(
            row_terms.astype(jnp.bfloat16), "tensor", scatter_dimension=1, tiled=True
        ).astype(jnp.float32),
        lax.psum_scatter(
            norm_one_vectors.astype(jnp.bfloat16), "tensor", scatter_dimension=1, tiled=True
        ).astype(jnp.float32),
    )
    token_grad = (grad_one + row_back).astype(jnp.bfloat16)
    returned_rows, returned_grads = (
        lax.all_to_all(
            output_rows.astype(jnp.bfloat16).reshape(1, slot_count, local_rows, model_width),
            "dp",
            split_axis=2,
            concat_axis=0,
            tiled=True,
        ),
        lax.all_to_all(
            token_grad.reshape(1, slot_count, local_rows, model_width),
            "dp",
            split_axis=2,
            concat_axis=0,
            tiled=True,
        ),
    )
    inverse = (
        jnp.zeros(dealing.shape, jnp.int32)
        .at[dealing]
        .set(jnp.arange(dealing.shape[0], dtype=jnp.int32))
    )
    result = jnp.take(returned_rows.reshape(tokens.shape), inverse, axis=0)
    token_gradient = jnp.take(returned_grads.reshape(tokens.shape), inverse, axis=0)
    head_vector_grads = jnp.stack([query_bias_grad, value_bias_grad])
    (
        query_sum,
        key_sum,
        value_sum,
        output_sum,
        up_sum,
        down_sum,
        head_share,
        up_bias_sum,
        row_share,
    ) = (
        lax.psum_scatter(
            query_weight_grad.astype(jnp.bfloat16), "dp", scatter_dimension=0, tiled=True
        ).astype(jnp.float32),
        lax.psum_scatter(
            key_weight_grad.astype(jnp.bfloat16), "dp", scatter_dimension=0, tiled=True
        ).astype(jnp.float32),
        lax.psum_scatter(
            value_weight_grad.astype(jnp.bfloat16), "dp", scatter_dimension=0, tiled=True
        ).astype(jnp.float32),
        lax.psum_scatter(
            output_weight_grad.astype(jnp.bfloat16), "dp", scatter_dimension=1, tiled=True
        ).astype(jnp.float32),
        lax.psum_scatter(
            up_weight_grad.astype(jnp.bfloat16), "dp", scatter_dimension=0, tiled=True
        ).astype(jnp.float32),
        lax.psum_scatter(
            down_weight_grad.astype(jnp.bfloat16), "dp", scatter_dimension=1, tiled=True
        ).astype(jnp.float32),
        lax.psum_scatter(
            head_vector_grads.astype(jnp.bfloat16), "dp", scatter_dimension=1, tiled=True
        ).astype(jnp.float32),
        lax.psum_scatter(
            up_bias_grad.astype(jnp.bfloat16), "dp", scatter_dimension=0, tiled=True
        ).astype(jnp.float32),
        lax.psum_scatter(
            jnp.concatenate([norm_one_sums, norm_two_sums], axis=0).astype(jnp.bfloat16),
            "dp",
            scatter_dimension=1,
            tiled=True,
        ).astype(jnp.float32),
    )
    return (
        result,
        token_gradient,
        query_sum,
        key_sum,
        value_sum,
        output_sum,
        up_sum,
        down_sum,
        head_share[0],
        head_share[1],
        row_share[0],
        row_share[1],
        row_share[2],
        up_bias_sum,
        row_share[3],
        row_share[4],
        row_share[5],
    )


def solution(mesh):
    placed = (
        P(None, ("tensor", "dp"), None),
        P("dp", "tensor", None),
        P(),
        P(),
        P("dp", "tensor"),
        P("dp", "tensor"),
        P("dp", "tensor"),
        P("tensor", "dp"),
        P("dp", "tensor"),
        P("tensor", "dp"),
        P(("tensor", "dp")),
        P(("tensor", "dp")),
        P(("tensor", "dp")),
        P(("tensor", "dp")),
        P(("tensor", "dp")),
        P(("tensor", "dp")),
        P(("tensor", "dp")),
        P(("tensor", "dp")),
        P(("tensor", "dp")),
    )
    return jax.shard_map(
        local,
        mesh=mesh,
        in_specs=placed,
        out_specs=(
            P(None, ("tensor", "dp"), None),
            P(None, ("tensor", "dp"), None),
            P("dp", "tensor"),
            P("dp", "tensor"),
            P("dp", "tensor"),
            P("tensor", "dp"),
            P("dp", "tensor"),
            P("tensor", "dp"),
            P(("tensor", "dp")),
            P(("tensor", "dp")),
            P(("tensor", "dp")),
            P(("tensor", "dp")),
            P(("tensor", "dp")),
            P(("tensor", "dp")),
            P(("tensor", "dp")),
            P(("tensor", "dp")),
            P(("tensor", "dp")),
        ),
        check_vma=False,
    )
```

profile of v0, /device:TPU:9, one launch (start us, length us, event | category | flops | bytes accessed | tf_op | source)
XLA Modules:
  0.0 2076.9 jit_solution(10816682756994699043)
XLA Ops:
  22.2 61.5 %all-to-all-done = bf16[8,2,32,2048]{3,2,1,0:T(8,128)(2,1)S(1)} async-done(((bf16[8,2,32,2048]{3,2,1,0:T(8,128)(2,1)}), bf16[8,2,32,2048]{3,2,1,0:T(8,128)(2,1)S(1)}, u32[]{:S(2)}, u32[]{:S(2)}) %all-to-all-start) | async-done | bytes 2097184 | tf_op jit(solution)/shard_map/all_to_all | solution.py:61
  100.2 74.6 %all-gather.14.cloned.1.call-done = bf16[2,1024,2048]{2,1,0:T(8,128)(2,1)} async-done(((bf16[2,256,2048]{2,1,0:T(8,128)(2,1)}), bf16[2,1024,2048]{2,1,0:T(8,128)(2,1)}) %all-gather.14.cloned.1.call-update) | async-done | bytes 8388624 | tf_op jit(solution)/shard_map/all_gather | solution.py:96
  188.9 17.6 all-gather.16.cloned.1.call-done
  220.4 16.7 all-gather.18.cloned.1.call-done
  251.2 34.8 %while.30 = (s32[]{:T(128)}, bf16[2,2,512,4,128]{4,2,3,1,0:T(8,128)(2,1)}, f32[2,2,4,512]{3,2,1,0:T(4,128)S(1)}, s32[2]{0:T(128)S(1)}, bf16[2,1024,4,128]{3,1,2,...) while((s32[]{:T(128)}, ...), condition=%wide.region_3.5_spmd.clone, body=%wide.region_0.4_spmd.clone.sunk | while | flops 2198337536 | bytes 81930512 | solution.py:140
  330.8 130.6 %reduce-scatter.23.cloned.1.call-done = f32[2,256,2048]{2,1,0:T(8,128)} async-done(((f32[2,1024,2048]{2,1,0:T(8,128)}), f32[2,256,2048]{2,1,0:T(8,128)}) %reduce-scatter.23.cloned.1.call-update) | async-done | bytes 4194320 | tf_op jit(solution)/shard_map/reduce_scatter | solution.py:145
  479.2 63.7 %all-gather.26.cloned.1.call-done = bf16[2048,2048]{1,0:T(8,128)(2,1)} async-done(((bf16[256,2048]{1,0:T(8,128)(2,1)}), bf16[2048,2048]{1,0:T(8,128)(2,1)}) %all-gather.26.cloned.1.call-update) | async-done | bytes 8388624 | tf_op jit(solution)/shard_map/all_gather | solution.py:89
  542.9 90.8 %all-gather.24.cloned.1.call-done = bf16[2,1024,2048]{2,1,0:T(8,128)(2,1)} async-done(((bf16[2,256,2048]{2,1,0:T(8,128)(2,1)}), bf16[2,1024,2048]{2,1,0:T(8,128)(2,1)}) %all-gather.24.cloned.1.call-update) | async-done | bytes 8388624 | tf_op jit(solution)/shard_map/all_gather | solution.py:148
  633.7 24.2 %fusion.81 = f32[2048,2048]{1,0:T(8,128)} fusion(bf16[2048,2048]{1,0:T(8,128)(2,1)} %bitcast.288, bf16[2048,2048]{1,0:T(8,128)(2,1)} %all-gather.26.cloned.1.call-done), kind=kOutput, calls=%fused_computation.173 | convolution fusion | flops 17179869184 | bytes 33554432 | tf_op jit(solution)/shard_map/dot_general | solution.py:26
  657.9 58.0 %all-gather.28.cloned.1.call-done = bf16[2048,2048]{1,0:T(8,128)(2,1)} async-done(((bf16[2048,256]{1,0:T(8,128)(2,1)}), bf16[2048,2048]{1,0:T(8,128)(2,1)}) %all-gather.28.cloned.1.call-update) | async-done | bytes 8388624 | tf_op jit(solution)/shard_map/all_gather | solution.py:90
  715.9 26.6 %fusion.73 = f32[2048,2048]{1,0:T(8,128)} fusion(bf16[2048,2048]{1,0:T(8,128)(2,1)} %all-gather.28.cloned.1.call-done, f32[2048,2048]{1,0:T(8,128)} %fusion.81, f32[2048]{0:T(1024)S(1)} %bitcast.275), kind=kOutput, calls=%fused_computation.166 | convolution fusion | flops 17221812224 | bytes 41951232 | tf_op jit(solution)/shard_map/dot_general | solution.py:26
  742.8 154.4 %reduce-scatter.25.cloned.1.call-done = f32[2,256,2048]{2,1,0:T(8,128)} async-done(((f32[2,1024,2048]{2,1,0:T(8,128)}), f32[2,256,2048]{2,1,0:T(8,128)}) %reduce-scatter.25.cloned.1.call-update) | async-done | bytes 4194320 | tf_op jit(solution)/shard_map/reduce_scatter | solution.py:155
  907.1 87.8 %all-gather.30.cloned.1.call-done = bf16[2,1024,2048]{2,1,0:T(8,128)(2,1)} async-done(((bf16[2,256,2048]{2,1,0:T(8,128)(2,1)}), bf16[2,1024,2048]{2,1,0:T(8,128)(2,1)}) %all-gather.30.cloned.1.call-update) | async-done | bytes 8388624 | tf_op jit(solution)/shard_map/all_gather | solution.py:160
  994.9 36.0 %fusion.74 = (bf16[2048]{0:T(1024)(128)(2,1)}, bf16[2048,2048]{1,0:T(8,128)(2,1)}) fusion(f32[2048,2048]{1,0:T(8,128)} %fusion.81, f32[2048]{0:T(1024)S(1)} %bitcast.276, bf16[2048,2048]{1,0:T(8,128)(2,1)} %bitcast.292, bf16[2048,2048]{1,0:T(8,128)(2,1)} %all-gather.28.cloned.1.call-done), kind=kOutput, calls=%fused_computation.167 | convolution fusion | flops 17272141824 | bytes 41955328 | tf_op jit(solution)/shard_map/rd,fd->rf/dot_general | solution.py:166
  1030.9 24.7 %fusion.82 = f32[2048,2048]{1,0:T(8,128)} fusion(bf16[2048,2048]{1,0:T(8,128)(2,1)} %get-tuple-element.387, bf16[2048,2048]{1,0:T(8,128)(2,1)} %all-gather.26.cloned.1.call-done), kind=kOutput, calls=%fused_computation.174 | convolution fusion | flops 17179869184 | bytes 33554432 | tf_op jit(solution)/shard_map/rf,df->rd/dot_general | solution.py:172
  1055.7 153.9 %reduce-scatter.27.cloned.1.call-done = f32[2,256,2048]{2,1,0:T(8,128)} async-done(((f32[2,1024,2048]{2,1,0:T(8,128)}), f32[2,256,2048]{2,1,0:T(8,128)}) %reduce-scatter.27.cloned.1.call-update) | async-done | bytes 4194320 | tf_op jit(solution)/shard_map/reduce_scatter | solution.py:177
  1225.5 85.1 %all-gather.32.cloned.1.call-done = bf16[2,1024,2048]{2,1,0:T(8,128)(2,1)} async-done(((bf16[2,256,2048]{2,1,0:T(8,128)(2,1)}), bf16[2,1024,2048]{2,1,0:T(8,128)(2,1)}) %all-gather.32.cloned.1.call-update) | async-done | bytes 8388624 | tf_op jit(solution)/shard_map/all_gather | solution.py:183
  1326.3 114.2 %while.31 = (s32[]{:T(128)}, f32[2,1024,4,128]{1,3,2,0:T(8,128)}, f32[2,1024,4,128]{1,3,2,0:T(8,128)}, bf16[2,2,512,4,128]{4,2,3,1,0:T(8,128)(2,1)}, s32[2]{0:T(...) while((s32[]{:T(128)}, f32[2,1024,4,128]{1,3,2,0:T(8,128)}, ...), condition=%wide.region_18.20_spmd.clone, body=%wide.region_16.19_spmd.clone.sunk | while | flops 5437913088 | bytes 257024672 | solution.py:227
  1350.4 13.2 multiply_reduce_fusion.6
  1407.5 12.9 multiply_reduce_fusion.6
  1478.4 16.4 add_convert_fusion
  1495.5 27.5 %convolution_convert_fusion = bf16[2048,2048]{1,0:T(8,128)(2,1)} fusion(bf16[2048,2048]{1,0:T(8,128)(2,1)} %bitcast.293, f32[2048,2048]{1,0:T(8,128)} %fusion.81, f32[2048]{0:T(1024)S(1)} %bitcast.277), kind=kOutput, calls=%fused_computation.61 | convolution fusion | flops 17226006528 | bytes 33562624 | tf_op jit(solution)/shard_map/rf,rd->fd/dot_general | solution.py:163
  1523.1 24.0 %convolution_convert_fusion.1 = bf16[2048,2048]{1,0:T(8,128)(2,1)} fusion(bf16[2048,2048]{1,0:T(8,128)(2,1)} %bitcast.289, bf16[2048,2048]{1,0:T(8,128)(2,1)} %get-tuple-element.387), kind=kOutput, calls=%fused_computation.62 | convolution fusion | flops 17184063488 | bytes 25165824 | tf_op jit(solution)/shard_map/rd,rf->df/dot_general | solution.py:169
  1609.0 61.9 %all-to-all-done.1 = bf16[1,2,256,2048]{3,1,0,2:T(2,128)(2,1)} async-done(((bf16[1,2,256,2048]{3,1,0,2:T(2,128)(2,1)}), bf16[1,2,256,2048]{3,1,0,2:T(2,128)(2,1)}, u32[]{:S(2)}, u32[]{:S(2)}) %all-to-all-start.1) | async-done | bytes 2097184 | tf_op jit(solution)/shard_map/all_to_all | solution.py:259
  1682.0 73.4 %all-reduce = bf16[2048]{0:T(1024)(128)(2,1)S(1)} all-reduce(bf16[2048]{0:T(1024)(128)(2,1)S(1)} %copy-done.42), channel_id=16, replica_groups=mesh['dp'=8,'tensor'=4] {'dp'}, use_global_device_ids=true, to_apply=%region_39.41.clone | all-reduce | flops 2048 | bytes 8192
  1765.0 86.4 %reduce-scatter.39.cloned.1.call-done = bf16[256,2048]{1,0:T(8,128)(2,1)} async-done(((bf16[2048,2048]{1,0:T(8,128)(2,1)}), bf16[256,2048]{1,0:T(8,128)(2,1)}) %reduce-scatter.39.cloned.1.call-update) | async-done | bytes 1048592 | tf_op jit(solution)/shard_map/reduce_scatter | solution.py:305
  1854.2 23.5 %reduce-scatter.49.cloned.1.call-done = bf16[64,6]{1,0:T(8,128)(2,1)} async-done(((bf16[512,6]{1,0:T(8,128)(2,1)}), bf16[64,6]{1,0:T(8,128)(2,1)}) %reduce-scatter.49.cloned.1.call-update) | async-done | bytes 784
  1886.5 22.1 %reduce-scatter.43.cloned.1.call-done = bf16[64,2]{1,0:T(8,128)(2,1)} async-done(((bf16[512,2]{1,0:T(8,128)(2,1)}), bf16[64,2]{1,0:T(8,128)(2,1)}) %reduce-scatter.43.cloned.1.call-update) | async-done | bytes 272
  1910.0 36.4 %reduce-scatter.37.cloned.1.call-done = bf16[512,256]{1,0:T(8,128)(2,1)} async-done(((bf16[512,2048]{1,0:T(8,128)(2,1)}), bf16[512,256]{1,0:T(8,128)(2,1)}) %reduce-scatter.37.cloned.1.call-update) | async-done | bytes 262160 | tf_op jit(solution)/shard_map/reduce_scatter | solution.py:302
  1948.2 35.2 %reduce-scatter.33.cloned.1.call-done = bf16[256,512]{1,0:T(8,128)(2,1)} async-done(((bf16[2048,512]{1,0:T(8,128)(2,1)}), bf16[256,512]{1,0:T(8,128)(2,1)}) %reduce-scatter.33.cloned.1.call-update) | async-done | bytes 262160 | tf_op jit(solution)/shard_map/reduce_scatter | solution.py:296
  1985.1 35.1 %reduce-scatter.31.cloned.1.call-done = bf16[256,512]{1,0:T(8,128)(2,1)} async-done(((bf16[2048,512]{1,0:T(8,128)(2,1)}), bf16[256,512]{1,0:T(8,128)(2,1)}) %reduce-scatter.31.cloned.1.call-update) | async-done | bytes 262160 | tf_op jit(solution)/shard_map/reduce_scatter | solution.py:293
  2022.0 35.2 %reduce-scatter.35.cloned.1.call-done = bf16[256,512]{1,0:T(8,128)(2,1)} async-done(((bf16[2048,512]{1,0:T(8,128)(2,1)}), bf16[256,512]{1,0:T(8,128)(2,1)}) %reduce-scatter.35.cloned.1.call-update) | async-done | bytes 262160 | tf_op jit(solution)/shard_map/reduce_scatter | solution.py:299
  (350 shorter events, 439.0 us)
Async XLA Ops:
  15.7 68.0 %all-to-all-start = ((bf16[8,2,32,2048]{3,2,1,0:T(8,128)(2,1)}), bf16[8,2,32,2048]{3,2,1,0:T(8,128)(2,1)S(1)}, u32[]{:S(2)}, u32[]{:S(2)}) async-start(bf16[8,2,32,2048]{3,2,1,0:T(8,128)(2,1)} %bitcast.236), calls=%async_computation | async-start | bytes 4194304 | tf_op jit(solution)/shard_map/all_to_all | solution.py:61
  21.4 78.8 %all-gather.20.cloned.1.call-start = ((), (), s32[]{:S(2)}) async-start(), calls=%async_computation.20 | async-start | bytes 2359296 | tf_op jit(solution)/shard_map/all_gather | solution.py:87
  22.2 152.6 %all-gather.14.cloned.1.call-start = ((), (), s32[]{:S(2)}) async-start(), calls=%async_computation.17 | async-start | bytes 10485760 | tf_op jit(solution)/shard_map/all_gather | solution.py:96
  85.3 121.1 %all-gather.16.cloned.1.call-start = ((), (), s32[]{:S(2)}) async-start(), calls=%async_computation.18 | async-start | bytes 2359296 | tf_op jit(solution)/shard_map/all_gather | solution.py:85
  86.2 150.9 %all-gather.18.cloned.1.call-start = ((), (), s32[]{:S(2)}) async-start(), calls=%async_computation.19 | async-start | bytes 2359296 | tf_op jit(solution)/shard_map/all_gather | solution.py:86
  87.0 208.5 %all-gather.22.cloned.1.call-start = ((), (), s32[]{:S(2)}) async-start(), calls=%async_computation.21 | async-start | bytes 2359296 | tf_op jit(solution)/shard_map/all_gather | solution.py:88
  87.8 373.6 %reduce-scatter.23.cloned.1.call-start = ((), (), s32[]{:S(2)}) async-start(), calls=%async_computation.22 | async-start | bytes 20971520 | tf_op jit(solution)/shard_map/reduce_scatter | solution.py:145
  308.1 153.3 %copy-start.14 = (bf16[1,2,8,32,2048]{4,3,2,1,0:T(8,128)(2,1)S(1)}, bf16[1,2,8,32,2048]{4,3,2,1,0:T(8,128)(2,1)}, u32[]{:S(2)}) copy-start(bf16[1,2,8,32,2048]{4,3,2,1,0:T(8,128)(2,1)} %copy.86) | copy-start | bytes 6291460
  308.1 234.8 %all-gather.26.cloned.1.call-start = ((), (), s32[]{:S(2)}) async-start(), calls=%async_computation.24 | async-start | bytes 9437184 | tf_op jit(solution)/shard_map/all_gather | solution.py:89
  311.1 322.7 %all-gather.24.cloned.1.call-start = ((), (), s32[]{:S(2)}) async-start(), calls=%async_computation.23 | async-start | bytes 10485760 | tf_op jit(solution)/shard_map/all_gather | solution.py:148
  468.4 247.5 %all-gather.28.cloned.1.call-start = ((), (), s32[]{:S(2)}) async-start(), calls=%async_computation.25 | async-start | bytes 9437184 | tf_op jit(solution)/shard_map/all_gather | solution.py:90
  469.5 427.7 %reduce-scatter.25.cloned.1.call-start = ((), (), s32[]{:S(2)}) async-start(), calls=%async_computation.26 | async-start | bytes 20971520 | tf_op jit(solution)/shard_map/reduce_scatter | solution.py:155
  479.2 515.7 %copy-start.40 = (f32[8,1,256]{2,1,0:T(1,128)}, f32[8,1,256]{2,1,0:T(1,128)S(1)}, u32[]{:S(2)}) copy-start(f32[8,1,256]{2,1,0:T(1,128)S(1)} %convert_element_type.220) | copy-start | bytes 24580
  742.5 252.3 %all-gather.30.cloned.1.call-start = ((), (), s32[]{:S(2)}) async-start(), calls=%async_computation.27 | async-start | bytes 10485760 | tf_op jit(solution)/shard_map/all_gather | solution.py:160
  907.1 302.5 %reduce-scatter.27.cloned.1.call-start = ((), (), s32[]{:S(2)}) async-start(), calls=%async_computation.28 | async-start | bytes 20971520 | tf_op jit(solution)/shard_map/reduce_scatter | solution.py:177
  1055.6 154.0 %copy-start.35 = (f32[1,2048]{1,0:T(1,128)S(1)}, f32[1,2048]{1,0:T(1,128)}, u32[]{:S(2)}) copy-start(f32[1,2048]{1,0:T(1,128)} %get-tuple-element.411) | copy-start | bytes 24580
  1055.6 255.0 %all-gather.32.cloned.1.call-start = ((), (), s32[]{:S(2)}) async-start(), calls=%async_computation.29 | async-start | bytes 10485760 | tf_op jit(solution)/shard_map/all_gather | solution.py:183
  1222.8 324.4 %reduce-scatter.45.cloned.1.call-start = ((), (), s32[]{:S(2)}) async-start(), calls=%async_computation.38 | async-start | bytes 655360
  1224.1 324.2 %reduce-scatter.47.cloned.1.call-start = ((), (), s32[]{:S(2)}) async-start(), calls=%async_computation.39 | async-start | bytes 1310720
  1225.5 376.6 %reduce-scatter.29.cloned.1.call-start = ((), (), s32[]{:S(2)}) async-start(), calls=%async_computation.30 | async-start | bytes 10485760 | tf_op jit(solution)/shard_map/reduce_scatter | solution.py:250
  1494.8 267.5 %reduce-scatter.41.cloned.1.call-start = ((), (), s32[]{:S(2)}) async-start(), calls=%async_computation.36 | async-start | bytes 9437184 | tf_op jit(solution)/shard_map/reduce_scatter | solution.py:308
  1523.0 328.4 %reduce-scatter.39.cloned.1.call-start = ((), (), s32[]{:S(2)}) async-start(), calls=%async_computation.35 | async-start | bytes 9437184 | tf_op jit(solution)/shard_map/reduce_scatter | solution.py:305
  1547.1 330.5 %reduce-scatter.49.cloned.1.call-start = ((), (), s32[]{:S(2)}) async-start(), calls=%async_computation.40 | async-start | bytes 147456
  1550.2 358.5 %reduce-scatter.43.cloned.1.call-start = ((), (), s32[]{:S(2)}) async-start(), calls=%async_computation.37 | async-start | bytes 147456
  1551.4 395.0 %reduce-scatter.37.cloned.1.call-start = ((), (), s32[]{:S(2)}) async-start(), calls=%async_computation.34 | async-start | bytes 2359296 | tf_op jit(solution)/shard_map/reduce_scatter | solution.py:302
  1561.6 421.7 %reduce-scatter.33.cloned.1.call-start = ((), (), s32[]{:S(2)}) async-start(), calls=%async_computation.32 | async-start | bytes 2359296 | tf_op jit(solution)/shard_map/reduce_scatter | solution.py:296
  1572.0 448.3 %reduce-scatter.31.cloned.1.call-start = ((), (), s32[]{:S(2)}) async-start(), calls=%async_computation.31 | async-start | bytes 2359296 | tf_op jit(solution)/shard_map/reduce_scatter | solution.py:293
  1587.0 83.9 %all-to-all-start.1 = ((bf16[1,2,256,2048]{3,1,0,2:T(2,128)(2,1)}), bf16[1,2,256,2048]{3,1,0,2:T(2,128)(2,1)}, u32[]{:S(2)}, u32[]{:S(2)}) async-start(bf16[1,2,256,2048]{3,1,0,2:T(2,128)(2,1)} %copy.93), calls=%async_computation.3 | async-start | bytes 4194304 | tf_op jit(solution)/shard_map/all_to_all | solution.py:259
  1592.5 464.7 %reduce-scatter.35.cloned.1.call-start = ((), (), s32[]{:S(2)}) async-start(), calls=%async_computation.33 | async-start | bytes 2359296 | tf_op jit(solution)/shard_map/reduce_scatter | solution.py:299
  1605.5 75.2 %copy-start.54 = (u32[32]{0:T(128)S(1)}, u32[32]{0:T(128)}, u32[]{:S(2)}) copy-start(u32[32]{0:T(128)} %constant.172) | copy-start | bytes 388
  1605.5 76.5 %copy-start.42 = (bf16[2048]{0:T(1024)(128)(2,1)S(1)}, bf16[2048]{0:T(1024)(128)(2,1)}, u32[]{:S(2)}) copy-start(bf16[2048]{0:T(1024)(128)(2,1)} %get-tuple-element.386) | copy-start | bytes 12292
  1670.9 388.1 %all-to-all-start.2 = ((bf16[1,2,256,2048]{3,1,0,2:T(2,128)(2,1)}), bf16[1,2,256,2048]{3,1,0,2:T(2,128)(2,1)S(1)}, u32[]{:S(2)}, u32[]{:S(2)}) async-start(bf16[1,2,256,2048]{3,1,0,2:T(2,128)(2,1)} %copy.103), calls=%async_computation.6 | async-start | bytes 4194304 | tf_op jit(solution)/shard_map/all_to_all | solution.py:266
  (63 other events, 472.1 us)
Sparse Core Ops, SparseCore 0:
  24.4 46.2 all-gather.19
  85.5 89.2 all-gather.13
  176.9 29.4 all-gather.15
  208.5 28.5 all-gather.17
  239.1 32.1 all-gather.21
  308.1 153.2 reduce-scatter.22
  463.0 79.9 all-gather.25
  545.4 88.3 all-gather.23
  635.9 79.9 all-gather.27
  742.7 154.4 reduce-scatter.24
  907.2 87.6 all-gather.29
  1055.7 153.7 reduce-scatter.26
  1222.9 87.6 all-gather.31
  1313.9 24.6 reduce-scatter.44
  1341.6 27.8 reduce-scatter.46
  1495.0 86.4 reduce-scatter.28
  1583.7 178.5 reduce-scatter.40
  1764.6 86.7 reduce-scatter.38
  1854.3 23.3 reduce-scatter.48
  1880.3 28.3 reduce-scatter.42
  1911.1 35.2 reduce-scatter.36
  1948.8 34.4 reduce-scatter.32
  1985.7 34.4 reduce-scatter.30
  2022.5 34.6 reduce-scatter.34
where the time goes:
time: 2090 us; the launch traced here: 2080 us
  waiting for transfers between devices  1340 us (64%)
  matrix products  381 us (18%)
  blocking collectives  114 us (5%)
  other arithmetic  98.6 us (5%)
  local copies, waits for them, and re-layouts  96.2 us (5%)
  starting transfers between devices  21.7 us (1%)
    reduce_scatter x1, waiting for transfers between devices, local(): lax.psum_scatter(hidden_terms, 'tensor', scatter_dimension=1, tiled=True)  154 us
    reduce_scatter x1, waiting for transfers between devices, local(): lax.psum_scatter(first_terms, 'tensor', scatter_dimension=1, tiled=True)  154 us
    reduce_scatter x1, waiting for transfers between devices, local(): lax.psum_scatter(head_terms, 'tensor', scatter_dimension=1, tiled=True)  131 us
    dot_general x6, matrix products, matmul(): return jnp.dot(left, right, preferred_element_type=jnp.float32)  91.5 us
    all_gather x1, waiting for transfers between devices, local(): lax.all_gather(first_norm.astype(jnp.bfloat16), 'tensor', axis=1, tiled=T...  90.8 us
    all_gather x1, waiting for transfers between devices, local(): lax.all_gather(grad_two.astype(jnp.bfloat16), 'tensor', axis=1, tiled=True)  87.8 us
    reduce_scatter x1, waiting for transfers between devices, local(): lax.psum_scatter(up_weight_grad.astype(jnp.bfloat16), 'dp', scatter_dimen...  86.4 us
    all_gather x1, waiting for transfers between devices, local(): lax.all_gather(grad_one.astype(jnp.bfloat16), 'tensor', axis=1, tiled=True)  85.1 us
  transfers between devices with their start and end apart: 27, of which 21 were waited for; matrix products, arithmetic and copies ran while one was open for 20% of the time, Pallas kernels for 0%

commit v1 on v0

v1 whole, which is shorter than its diff:
```python
import functools
import math

import jax
import jax.numpy as jnp
from jax import lax
from jax.experimental import pallas as pl
from jax.experimental.pallas import tpu as pltpu
from jax.sharding import PartitionSpec as P

HEAD = 128
norm_epsilon = 1e-05
masked_score = -1e30
log2_e = math.log2(math.e)
head_scale = 1.0 / math.sqrt(HEAD)
gelu_root = math.sqrt(2.0 / math.pi)
bf16 = jnp.bfloat16
f32 = jnp.float32


def dot(left, right, contract, out=f32):
    return lax.dot_general(left, right, (contract, ((), ())), preferred_element_type=f32).astype(out)


def forward_kernel(bias_ref, qkv_ref, mixed_ref, log_ref, *, heads, query_block):
    rows = qkv_ref.shape[0]
    width = heads * HEAD
    bias = bias_ref[...]
    for head in range(heads):
        low = head * HEAD
        keys = qkv_ref[:, width + low : width + low + HEAD]
        values = qkv_ref[:, 2 * width + low : 2 * width + low + HEAD]
        for first in range(0, rows, query_block):
            part = slice(first, first + query_block)
            queries = qkv_ref[part, low : low + HEAD]
            scores = dot(keys, queries, ((1,), (1,))) * (head_scale * log2_e) + bias
            peak = jnp.max(scores, axis=0, keepdims=True)
            weight = jnp.exp2(scores - peak)
            total = jnp.sum(weight, axis=0, keepdims=True)
            mixed = dot(values, weight.astype(bf16), ((0,), (0,))) * (1.0 / total)
            mixed_ref[part, low : low + HEAD] = mixed.T.astype(bf16)
            log_ref[0, head : head + 1, part] = peak + jnp.log2(total)


def backward_kernel(bias_ref, qkv_ref, mixed_ref, grad_ref, log_ref, out_ref, sum_ref, *, heads, query_block):
    rows = qkv_ref.shape[0]
    width = heads * HEAD
    bias = bias_ref[...]
    for head in range(heads):
        low = head * HEAD
        keys = qkv_ref[:, width + low : width + low + HEAD]
        values = qkv_ref[:, 2 * width + low : 2 * width + low + HEAD]
        key_total = jnp.zeros((rows, HEAD), f32)
        value_total = jnp.zeros((rows, HEAD), f32)
        query_sum = jnp.zeros((1, HEAD), f32)
        for first in range(0, rows, query_block):
            part = slice(first, first + query_block)
            queries = qkv_ref[part, low : low + HEAD]
            grads = grad_ref[part, low : low + HEAD]
            mixed = mixed_ref[part, low : low + HEAD]
            centre = jnp.sum((grads.astype(f32) * mixed.astype(f32)).T, axis=0, keepdims=True)
            scores = dot(keys, queries, ((1,), (1,))) * (head_scale * log2_e) + bias
            weight = jnp.exp2(scores - log_ref[0, head : head + 1, part])
            weight_grad = dot(values, grads, ((1,), (1,)))
            score_grad = (weight * (weight_grad - centre)).astype(bf16)
            value_total = value_total + dot(weight.astype(bf16), grads, ((1,), (0,)))
            key_total = key_total + dot(score_grad, queries, ((1,), (0,)))
            query_grad = dot(keys, score_grad, ((0,), (0,))) * head_scale
            query_grad = query_grad.T.astype(bf16)
            out_ref[part, low : low + HEAD] = query_grad
            query_sum = query_sum + jnp.sum(query_grad.astype(f32), axis=0, keepdims=True)
        out_ref[:, width + low : width + low + HEAD] = (key_total * head_scale).astype(bf16)
        value_total = value_total.astype(bf16)
        out_ref[:, 2 * width + low : 2 * width + low + HEAD] = value_total
        sum_ref[0, :, low : low + HEAD] = query_sum
        sum_ref[0, :, width + low : width + low + HEAD] = jnp.sum(
            value_total.astype(f32), axis=0, keepdims=True
        )


def attend(qkv, bias, halves):
    rows, columns = qkv.shape
    group = columns // halves
    heads = group // (3 * HEAD)
    width = heads * HEAD
    return pl.pallas_call(
        functools.partial(forward_kernel, heads=heads, query_block=min(256, rows)),
        grid=(halves,),
        in_specs=[
            pl.BlockSpec((rows, 1), lambda i: (0, 0)),
            pl.BlockSpec((rows, group), lambda i: (0, i)),
        ],
        out_specs=[
            pl.BlockSpec((rows, width), lambda i: (0, i)),
            pl.BlockSpec((1, heads, rows), lambda i: (i, 0, 0)),
        ],
        out_shape=[
            jax.ShapeDtypeStruct((rows, halves * width), bf16),
            jax.ShapeDtypeStruct((halves, heads, rows), f32),
        ],
        compiler_params=pltpu.CompilerParams(vmem_limit_bytes=40 * 1024 * 1024),
        cost_estimate=pl.CostEstimate(
            flops=4 * halves * heads * rows * rows * HEAD * 4,
            bytes_accessed=rows * columns * 3,
            transcendentals=halves * heads * rows * rows,
        ),
    )(bias, qkv)


def attend_back(qkv, bias, mixed, grads, logs, halves):
    rows, columns = qkv.shape
    group = columns // halves
    heads = group // (3 * HEAD)
    width = heads * HEAD
    return pl.pallas_call(
        functools.partial(backward_kernel, heads=heads, query_block=min(256, rows)),
        grid=(halves,),
        in_specs=[
            pl.BlockSpec((rows, 1), lambda i: (0, 0)),
            pl.BlockSpec((rows, group), lambda i: (0, i)),
            pl.BlockSpec((rows, width), lambda i: (0, i)),
            pl.BlockSpec((rows, width), lambda i: (0, i)),
            pl.BlockSpec((1, heads, rows), lambda i: (i, 0, 0)),
        ],
        out_specs=[
            pl.BlockSpec((rows, group), lambda i: (0, i)),
            pl.BlockSpec((1, 1, 2 * width), lambda i: (i, 0, 0)),
        ],
        out_shape=[
            jax.ShapeDtypeStruct((rows, columns), bf16),
            jax.ShapeDtypeStruct((halves, 1, 2 * width), f32),
        ],
        compiler_params=pltpu.CompilerParams(vmem_limit_bytes=40 * 1024 * 1024),
        cost_estimate=pl.CostEstimate(
            flops=10 * halves * heads * rows * rows * HEAD * 4,
            bytes_accessed=rows * columns * 6,
            transcendentals=halves * heads * rows * rows,
        ),
    )(bias, qkv, mixed, grads, logs)


class TensorAxis:
    def __init__(self):
        self.size = lax.axis_size("tensor")
        self.me = lax.axis_index("tensor")
        self.square = self.size == 4
        if self.square:
            self.origins = self.me ^ jnp.array([0, 1, 3, 2], jnp.int32)
        else:
            self.origins = jnp.arange(self.size, dtype=jnp.int32)

    def swap(self, array, bit):
        return lax.ppermute(array, "tensor", [(i, i ^ bit) for i in range(self.size)])

    def gather(self, block):
        if not self.square:
            return lax.all_gather(block, "tensor", axis=0, tiled=True)
        half = block.shape[0] // 2
        along_x = self.swap(block, 1)
        along_y = self.swap(block, 2)
        top = self.swap(along_y[:half], 1)
        bottom = self.swap(along_x[half:], 2)
        return jnp.concatenate([block, along_x, top, bottom, along_y], axis=0)

    def scatter(self, terms):
        if not self.square:
            return lax.psum_scatter(terms, "tensor", scatter_dimension=0, tiled=True).astype(f32)
        rows, columns = terms.shape[0] // 4, terms.shape[1] // 2
        left, right = terms[:, :columns], terms[:, columns:]
        from_x = self.swap(left[rows : 3 * rows], 1).astype(f32)
        from_y = self.swap(right[2 * rows :], 2).astype(f32)
        onward_y = (left[3 * rows :].astype(f32) + from_x[rows:]).astype(bf16)
        onward_x = (right[rows : 2 * rows].astype(f32) + from_y[:rows]).astype(bf16)
        left = left[:rows].astype(f32) + from_x[:rows] + self.swap(onward_y, 2).astype(f32)
        right = right[:rows].astype(f32) + from_y[rows:] + self.swap(onward_x, 1).astype(f32)
        return jnp.concatenate([left, right], axis=1)


class GroupAxis:
    def __init__(self):
        self.size = lax.axis_size("dp")
        self.me = lax.axis_index("dp")
        self.line = self.size == 8
        self.core = self.me % 2 if self.line else jnp.int32(0)
        self.z = self.me // 2
        n = self.size
        self.next = [(i, (i + 2) % n) for i in range(n)]
        self.last = [(i, (i - 2) % n) for i in range(n)]

    def send(self, array, pairs):
        return lax.ppermute(array, "dp", pairs)

    def other(self, array):
        return self.send(array, [(i, i ^ 1) for i in range(self.size)])

    def order(self, array, axis):
        half = array.shape[axis] // 2
        low = lax.slice_in_dim(array, 0, half, axis=axis)
        high = lax.slice_in_dim(array, half, 2 * half, axis=axis)
        first = self.core == 0
        return jnp.concatenate(
            [jnp.where(first, low, high), jnp.where(first, high, low)], axis=axis
        )

    def gather(self, mine, theirs):
        if not self.line:
            return lax.all_gather(
                jnp.concatenate([mine, theirs], axis=1), "dp", axis=0, tiled=True
            )
        got = self.other(theirs)
        first = self.core == 0
        pair = jnp.concatenate([jnp.where(first, mine, got), jnp.where(first, got, mine)], axis=0)
        behind = self.send(pair, self.next)
        ahead = self.send(pair, self.last)
        far_up = self.send(behind, [(2, 4), (3, 5), (4, 6), (5, 7)])
        far_down = self.send(ahead, [(2, 0), (3, 1), (4, 2), (5, 3)])
        far = jnp.where(self.z >= 2, far_up, far_down)
        full = jnp.zeros((4,) + pair.shape, pair.dtype)
        for step, piece in enumerate((pair, behind, far, ahead)):
            full = lax.dynamic_update_slice(full, piece[None], ((self.z - step) % 4, 0, 0))
        full = full.reshape(-1, pair.shape[1])
        return jnp.concatenate([full, self.other(full)], axis=1)

    def scatter(self, terms):
        if not self.line:
            return lax.psum_scatter(terms, "dp", scatter_dimension=0, tiled=True).astype(f32)
        half = terms.shape[1] // 2
        rows = terms.shape[0] // 4
        chip = (terms[:, :half].astype(f32) + self.other(terms[:, half:]).astype(f32)).astype(bf16)
        chip = chip.reshape(4, rows, half)

        def toward(step):
            return lax.dynamic_index_in_dim(chip, (self.z + step) % 4, 0, False)

        up = self.send(toward(2), [(0, 2), (1, 3), (2, 4), (3, 5)])
        down = self.send(toward(2), [(6, 4), (7, 5), (4, 2), (5, 3)])
        ahead = (toward(1).astype(f32) + up.astype(f32)).astype(bf16)
        behind = (toward(3).astype(f32) + down.astype(f32)).astype(bf16)
        total = (
            toward(0).astype(f32)
            + self.send(ahead, self.next).astype(f32)
            + self.send(behind, self.last).astype(f32)
        ).reshape(2, rows // 2, half)
        mine = lax.dynamic_index_in_dim(total, self.core, 0, False)
        theirs = self.other(lax.dynamic_index_in_dim(total, 1 - self.core, 0, False))
        first = self.core == 0
        return jnp.concatenate([jnp.where(first, mine, theirs), jnp.where(first, theirs, mine)], axis=1)


def split_columns(core, block):
    half = block.shape[1] // 2
    low, high = block[:, :half], block[:, half:]
    return jnp.where(core == 0, low, high), jnp.where(core == 0, high, low)


def after(array, *earlier):
    return lax.optimization_barrier((array,) + earlier)[0]


def norm(rows, gain, shift):
    centred = rows - jnp.mean(rows, axis=-1, keepdims=True)
    inverse = lax.rsqrt(jnp.mean(centred * centred, axis=-1, keepdims=True) + norm_epsilon)
    unit = centred * inverse
    return unit * gain + shift, unit, inverse


def norm_back(grads, unit, inverse, gain):
    scaled = grads * gain
    return inverse * (
        scaled
        - jnp.mean(scaled, axis=-1, keepdims=True)
        - unit * jnp.mean(scaled * unit, axis=-1, keepdims=True)
    )


def gelu(hidden):
    return 0.5 * hidden * (1.0 + jnp.tanh(gelu_root * (hidden + 0.044715 * hidden * hidden * hidden)))


def gelu_slope(hidden):
    square = hidden * hidden
    bend = jnp.tanh(gelu_root * (hidden + 0.044715 * hidden * square))
    return 0.5 * (1.0 + bend) + 0.5 * hidden * (1.0 - bend * bend) * gelu_root * (
        1.0 + 3 * 0.044715 * square
    )


def local(
    tokens,
    cotangent,
    lengths,
    dealing,
    query_weight,
    key_weight,
    value_weight,
    output_weight,
    up_weight,
    down_weight,
    query_bias,
    value_bias,
    output_bias,
    attention_gain,
    attention_shift,
    up_bias,
    down_bias,
    feedforward_gain,
    feedforward_shift,
):
    tensor, group = TensorAxis(), GroupAxis()
    groups, splits = group.size, tensor.size
    core = group.core
    slots, own_rows, model_width = cotangent.shape
    slot_rows = own_rows * splits
    arrival_rows = tokens.shape[1]
    head_width = query_weight.shape[1]
    hidden_width = up_weight.shape[1]
    half = head_width // 2
    piece = query_bias.shape[0]

    head_piece = jnp.concatenate([query_bias, value_bias, up_bias]).astype(bf16)
    row_piece = jnp.concatenate(
        [output_bias, attention_gain, attention_shift, down_bias, feedforward_gain, feedforward_shift]
    ).astype(bf16)
    vectors = lax.all_gather(
        jnp.concatenate([head_piece, row_piece]), ("tensor", "dp"), axis=0, tiled=False
    ).astype(f32)
    head_vectors = lax.dynamic_slice_in_dim(vectors, tensor.me * groups, groups)
    query_bias_here = group.order(head_vectors[:, :piece].reshape(-1), 0)
    value_bias_here = group.order(head_vectors[:, piece : 2 * piece].reshape(-1), 0)
    hidden_bias = group.order(head_vectors[:, 2 * piece : head_piece.shape[0]].reshape(-1), 0)
    row_vectors = vectors[:, head_piece.shape[0] :].reshape(-1, 6, piece)
    row_vectors = jnp.moveaxis(row_vectors, 1, 0).reshape(6, model_width)
    blank = jnp.zeros((half,), f32)
    qkv_bias = jnp.concatenate(
        [query_bias_here[:half], blank, value_bias_here[:half]]
        + [query_bias_here[half:], blank, value_bias_here[half:]]
    )

    slot_dealing = dealing.reshape(groups, slots)

    def arrive(slot):
        sent = jnp.take(tokens, slot_dealing[:, slot], axis=0)
        return lax.all_to_all(sent, "dp", split_axis=0, concat_axis=0, tiled=True).reshape(
            own_rows, model_width
        )

    arrived = [arrive(slot) for slot in range(slots)]

    parts = [split_columns(core, w.astype(bf16)) for w in (query_weight, key_weight, value_weight)]
    qkv_mine = jnp.concatenate([p[0] for p in parts], axis=1)
    qkv_theirs = jnp.concatenate([p[1] for p in parts], axis=1)
    output_mine, output_theirs = split_columns(core, output_weight.astype(bf16).T)
    up_mine, up_theirs = split_columns(core, up_weight.astype(bf16))
    down_mine, down_theirs = split_columns(core, down_weight.astype(bf16).T)
    qkv_block = group.gather(qkv_mine, qkv_theirs)
    output_block = group.gather(after(output_mine, qkv_block), output_theirs)
    up_block = group.gather(after(up_mine, output_block), up_theirs)
    down_block = group.gather(after(down_mine, up_block), down_theirs)

    positions = (tensor.origins[:, None] * own_rows + jnp.arange(own_rows)[None, :]).reshape(-1)
    slot_lengths = lax.dynamic_slice_in_dim(jnp.take(lengths, dealing, axis=0), group.me * slots, slots)
    over_slots = range(slots)
    biases = [
        jnp.where(positions < slot_lengths[slot], 0.0, masked_score).astype(f32)[:, None]
        for slot in over_slots
    ]

    full_rows = [tensor.gather(rows) for rows in arrived]
    qkv = [(dot(rows, qkv_block, ((1,), (0,))) + qkv_bias).astype(bf16) for rows in full_rows]
    attended = [attend(qkv[s], biases[s], 2) for s in over_slots]
    mixed = [a[0] for a in attended]
    logs = [a[1] for a in attended]
    head_sums = [tensor.scatter(dot(m, output_block, ((1,), (1,)), bf16)) for m in mixed]
    first = [
        norm(arrived[s].astype(f32) + (head_sums[s] + row_vectors[0]), row_vectors[1], row_vectors[2])
        for s in over_slots
    ]
    first_full = [tensor.gather(f[0].astype(bf16)) for f in first]
    hidden = [dot(rows, up_block, ((1,), (0,))) + hidden_bias for rows in first_full]
    active = [gelu(h).astype(bf16) for h in hidden]
    hidden_sums = [tensor.scatter(dot(a, down_block, ((1,), (1,)), bf16)) for a in active]
    second = [
        norm(first[s][0] + (hidden_sums[s] + row_vectors[3]), row_vectors[4], row_vectors[5])
        for s in over_slots
    ]

    def give_back(rows):
        return lax.all_to_all(
            rows.astype(bf16).reshape(groups, arrival_rows, model_width),
            "dp",
            split_axis=0,
            concat_axis=0,
            tiled=True,
        )

    returned_rows = [give_back(s[0]) for s in second]

    cotangents = [cotangent[s].astype(f32) for s in over_slots]
    grad_two = [norm_back(cotangents[s], second[s][1], second[s][2], row_vectors[4]) for s in over_slots]
    gain_two_grad = sum(jnp.sum(cotangents[s] * second[s][1], axis=0) for s in over_slots)
    shift_two_grad = sum(jnp.sum(cotangents[s], axis=0) for s in over_slots)
    down_bias_grad = sum(jnp.sum(grad_two[s], axis=0) for s in over_slots)
    down_full = [tensor.gather(g.astype(bf16)) for g in grad_two]
    hidden_grad = [
        (dot(down_full[s], down_block, ((1,), (0,))) * gelu_slope(hidden[s])).astype(bf16)
        for s in over_slots
    ]
    first_back = [tensor.scatter(dot(h, up_block, ((1,), (1,)), bf16)) for h in hidden_grad]
    first_grad = [grad_two[s] + first_back[s] for s in over_slots]
    grad_one = [norm_back(first_grad[s], first[s][1], first[s][2], row_vectors[1]) for s in over_slots]
    grad_one = [lax.optimization_barrier(g) for g in grad_one]
    gain_one_grad = sum(jnp.sum(first_grad[s] * first[s][1], axis=0) for s in over_slots)
    shift_one_grad = sum(jnp.sum(first_grad[s], axis=0) for s in over_slots)
    output_bias_grad = sum(jnp.sum(grad_one[s], axis=0) for s in over_slots)
    attended_full = [tensor.gather(g.astype(bf16)) for g in grad_one]

    def weight_grad(lefts, rights):
        return sum(dot(a, b, ((0,), (0,))) for a, b in zip(lefts, rights)).astype(bf16)

    down_sum = group.scatter(weight_grad(down_full, active))
    up_sum = group.scatter(weight_grad(first_full, hidden_grad))
    up_bias_grad = sum(jnp.sum(h.astype(f32), axis=0) for h in hidden_grad)

    mixed_grad = [dot(rows, output_block, ((1,), (0,)), bf16) for rows in attended_full]
    output_sum = group.scatter(weight_grad(attended_full, mixed))
    attended_back = [
        attend_back(qkv[s], biases[s], mixed[s], mixed_grad[s], logs[s], 2) for s in over_slots
    ]
    qkv_grad = [a[0] for a in attended_back]
    row_back = [tensor.scatter(dot(g, qkv_block, ((1,), (1,)), bf16)) for g in qkv_grad]
    returned_grads = [give_back(grad_one[s] + row_back[s]) for s in over_slots]
    qkv_sum = group.scatter(weight_grad(full_rows, qkv_grad))
    bias_grads = sum(a[1] for a in attended_back).reshape(2, 2, half)

    places = slot_dealing.T.reshape(-1)
    inverse = jnp.zeros(places.shape, jnp.int32).at[places].set(
        jnp.arange(places.shape[0], dtype=jnp.int32)
    )
    result = jnp.take(jnp.concatenate(returned_rows, axis=0), inverse, axis=0)
    token_gradient = jnp.take(jnp.concatenate(returned_grads, axis=0), inverse, axis=0)

    head_grads = jnp.concatenate(
        [
            group.order(bias_grads[:, 0].reshape(-1), 0).reshape(groups, -1),
            group.order(bias_grads[:, 1].reshape(-1), 0).reshape(groups, -1),
            group.order(up_bias_grad, 0).reshape(groups, -1),
        ],
        axis=1,
    )
    head_grads = lax.dynamic_update_slice(
        jnp.zeros((splits * groups, head_grads.shape[1]), f32), head_grads, (tensor.me * groups, 0)
    )
    row_grads = jnp.stack(
        [
            output_bias_grad,
            gain_one_grad,
            shift_one_grad,
            down_bias_grad,
            gain_two_grad,
            shift_two_grad,
        ]
    ).reshape(6, splits * groups, piece)
    row_grads = jnp.moveaxis(row_grads, 0, 1).reshape(splits * groups, -1)
    vector_sums = lax.psum_scatter(
        jnp.concatenate([head_grads, row_grads], axis=1),
        ("tensor", "dp"),
        scatter_dimension=0,
        tiled=True,
    ).reshape(-1)
    ends = [piece, 2 * piece, head_piece.shape[0]]
    ends += [head_piece.shape[0] + piece * (i + 1) for i in range(6)]
    query_share, value_share, up_share, *row_shares = [
        vector_sums[low:high] for low, high in zip([0] + ends, ends)
    ]

    qkv_sum = qkv_sum.reshape(-1, 2, 3, half)
    return (
        result,
        token_gradient,
        qkv_sum[:, :, 0].reshape(-1, head_width),
        qkv_sum[:, :, 1].reshape(-1, head_width),
        qkv_sum[:, :, 2].reshape(-1, head_width),
        output_sum.T,
        up_sum,
        down_sum.T,
        query_share,
        value_share,
        row_shares[0],
        row_shares[1],
        row_shares[2],
        up_share,
        row_shares[3],
        row_shares[4],
        row_shares[5],
    )


def solution(mesh):
    matrix = P("dp", "tensor")
    flipped = P("tensor", "dp")
    vector = P(("tensor", "dp"))
    arrival = P(None, ("tensor", "dp"), None)
    return jax.shard_map(
        local,
        mesh=mesh,
        in_specs=(arrival, P("dp", "tensor", None), P(), P())
        + (matrix, matrix, matrix, flipped, matrix, flipped)
        + (vector,) * 9,
        out_specs=(arrival, arrival) + (matrix, matrix, matrix, flipped, matrix, flipped) + (vector,) * 9,
        check_vma=False,
    )
```

time: 2090 us -> 1470 us (0.70)
  waiting for transfers between devices: 1340 us -> 581 us
  starting transfers between devices: 21.7 us -> 184 us
  matrix products: 381 us -> 264 us
  blocking collectives: 114 us -> 43.9 us
  other arithmetic: 98.6 us -> 165 us
  local copies, waits for them, and re-layouts: 96.2 us -> 158 us
  Pallas kernels: 0 us -> 46.9 us
    reduce_scatter x10 -> x0, waiting for transfers between devices: 673 us -> none  [the longest x1 154 us: local(): lax.psum_scatter(hidden_terms, 'tensor', scatter_dimension=1, tiled=True)]
    ppermute x0 -> x112, waiting for transfers between devices: none -> 497 us  [the longest x64 269 us: swap(): lax.ppermute(array, 'tensor', [(i, i ^ bit) for i in range(self.size)])]
    all_gather x10 -> x0, waiting for transfers between devices: 494 us -> none  [the longest x1 90.8 us: local(): lax.all_gather(first_norm.astype(jnp.bfloat16), 'tensor', axis=1, tiled=T...]
    ppermute x0 -> x112, starting transfers between devices: none -> 138 us  [the longest x48 90.8 us: send(): return lax.ppermute(array, 'dp', pairs)]
    all_to_all x3 -> x6, waiting for transfers between devices: 123 us -> 1.84 us  [the longest x4 1.84 us: give_back(): lax.all_to_all(rows.astype(bf16).reshape(groups, arrival_rows, model_widt...]
    dot_general x32 -> x24, matrix products: 381 us -> 264 us  [dot(): lax.dot_general(left, right, (contract, ((), ())), preferred_element_type...]
    unnamed x1 -> x0, blocking collectives: 73.4 us -> none
    pallas_call x0 -> x4, Pallas kernels: none -> 46.9 us  [the longest x2 24 us: attend(): pl.pallas_call(functools.partial(forward_kernel, heads=heads, query_block...]
  transfers between devices with their start and end apart: 27 -> 119, of which waited for: 21 -> 48; matrix products, arithmetic and copies ran while one was open for 20% -> 36% of each run, Pallas kernels for 0% -> 3%
where the time goes in v1:
time: 1470 us; the launch traced here: 1460 us
  waiting for transfers between devices  581 us (40%)
  matrix products  264 us (18%)
  starting transfers between devices  184 us (13%)
  other arithmetic  165 us (11%)
  local copies, waits for them, and re-layouts  158 us (11%)
  Pallas kernels  46.9 us (3%)
  blocking collectives  43.9 us (3%)
  between operations  17.5 us (1%)
    ppermute x64, waiting for transfers between devices, swap(): lax.ppermute(array, 'tensor', [(i, i ^ bit) for i in range(self.size)])  269 us
    dot_general x24, matrix products, dot(): lax.dot_general(left, right, (contract, ((), ())), preferred_element_type...  264 us
    ppermute x48, waiting for transfers between devices, send(): return lax.ppermute(array, 'dp', pairs)  227 us
    ppermute x48, starting transfers between devices, send(): return lax.ppermute(array, 'dp', pairs)  90.8 us
    unnamed x2, waiting for transfers between devices  82.4 us
    unnamed x336, local copies, waits for them, and re-layouts  64.6 us
    ppermute x64, starting transfers between devices, swap(): lax.ppermute(array, 'tensor', [(i, i ^ bit) for i in range(self.size)])  46.8 us
    all_gather x1, blocking collectives, local(): lax.all_gather(jnp.concatenate([head_piece, row_piece]), ('tensor', 'dp')...  43.9 us
  transfers between devices with their start and end apart: 119, of which 48 were waited for; matrix products, arithmetic and copies ran while one was open for 36% of the time, Pallas kernels for 3%

profile of v1, /device:TPU:9, one launch (start us, length us, event | category | flops | bytes accessed | tf_op | source)
XLA Modules:
  0.0 1460.0 jit_solution(10049068945679219999)
XLA Ops:
  32.8 43.9 %all-gather.1 = bf16[32,1,768]{2,1,0:T(2,128)(2,1)S(1)} all-gather(bf16[1,1,768]{2,1,0:T(2,128)(2,1)S(1)} %reshape.968), channel_id=2, replica_groups=mesh['dp'=8,'tensor'=4] {'tensor','dp'}, dimensions={0}, use_global_device_ids=true | all-gather | bytes 50688 | tf_op jit(solution)/shard_map/all_gather | solution.py:324
  103.6 26.0 %collective-permute-done.11 = bf16[512,256]{1,0:T(8,128)(2,1)} collective-permute-done((bf16[512,256]{1,0:T(8,128)(2,1)}, bf16[512,256]{1,0:T(8,128)(2,1)}, u32[]{:S(2)}, u32[]{:S(2)}) %collective-permute-start.11) | collective-permute-done | bytes 262176 | tf_op jit(solution)/shard_map/ppermute | solution.py:191
  138.1 18.5 %collective-permute-done.13 = bf16[512,256]{1,0:T(8,128)(2,1)} collective-permute-done((bf16[512,256]{1,0:T(8,128)(2,1)}, bf16[512,256]{1,0:T(8,128)(2,1)}, u32[]{:S(2)}, u32[]{:S(2)}) %collective-permute-start.13) | collective-permute-done | bytes 262176 | tf_op jit(solution)/shard_map/ppermute | solution.py:191
  198.0 17.2 %collective-permute-done.40 = bf16[256,2048]{1,0:T(8,128)(2,1)} collective-permute-done((bf16[256,2048]{1,0:T(8,128)(2,1)S(1)}, bf16[256,2048]{1,0:T(8,128)(2,1)}, u32[]{:S(2)}, u32[]{:S(2)}) %collective-permute-start.40) | collective-permute-done | bytes 1048608 | tf_op jit(solution)/shard_map/ppermute | solution.py:153
  218.0 19.7 %collective-permute-done = bf16[256,2048]{1,0:T(8,128)(2,1)S(1)} collective-permute-done((bf16[256,2048]{1,0:T(8,128)(2,1)S(1)}, bf16[256,2048]{1,0:T(8,128)(2,1)S(1)}, u32[]{:S(2)}, u32[]{:S(2)}) %collective-permute-start) | collective-permute-done | bytes 1048608 | tf_op jit(solution)/shard_map/ppermute | solution.py:153
  279.3 12.0 shard_map.324
  308.5 12.0 shard_map.323
  363.3 15.6 %collective-permute-done.28 = bf16[512,1024]{1,0:T(8,128)(2,1)S(1)} collective-permute-done((bf16[512,1024]{1,0:T(8,128)(2,1)}, bf16[512,1024]{1,0:T(8,128)(2,1)S(1)}, u32[]{:S(2)}, u32[]{:S(2)}) %collective-permute-start.28) | collective-permute-done | bytes 1048608 | tf_op jit(solution)/shard_map/ppermute | solution.py:191
  441.5 15.7 %collective-permute-done.49 = bf16[256,2048]{1,0:T(8,128)(2,1)S(1)} collective-permute-done((bf16[256,2048]{1,0:T(8,128)(2,1)S(1)}, bf16[256,2048]{1,0:T(8,128)(2,1)S(1)}, u32[]{:S(2)}, u32[]{:S(2)}) %collective-permute-start.49) | collective-permute-done | bytes 1048608 | tf_op jit(solution)/shard_map/ppermute | solution.py:153
  458.3 21.4 %collective-permute-done.21 = bf16[256,2048]{1,0:T(8,128)(2,1)S(1)} collective-permute-done((bf16[256,2048]{1,0:T(8,128)(2,1)S(1)}, bf16[256,2048]{1,0:T(8,128)(2,1)S(1)}, u32[]{:S(2)}, u32[]{:S(2)}) %collective-permute-start.21) | collective-permute-done | bytes 1048608 | tf_op jit(solution)/shard_map/ppermute | solution.py:153
  500.8 15.1 %fusion.114 = f32[1024,2048]{1,0:T(8,128)} fusion(bf16[1024,2048]{1,0:T(8,128)(2,1)S(1)} %constant_dynamic-update-slice_fusion.16, bf16[2048,1024]{1,0:T(8,128)(2,1)} %collective-permute-done.29, bf16[2048,1024]{1,0:T(8,128)(2,1)} %bitcast.22), kind=kOutput, calls=%fused_computation.408 | convolution fusion | flops 8606711808 | bytes 20971520 | tf_op jit(solution)/shard_map/dot_general | solution.py:22
  515.9 14.2 convolution_convert_fusion.4
  538.8 13.7 fusion.115
  552.5 15.4 %convolution_convert_fusion.6 = bf16[1024,2048]{1,0:T(8,128)(2,1)S(1)} fusion(bf16[2048,1024]{1,0:T(8,128)(2,1)} %collective-permute-done.35, bf16[2048,1024]{1,0:T(8,128)(2,1)} %bitcast.306, f32[1024,2048]{1,0:T(8,128)} %fusion.115, f32[2048]{0:T(1024)S(1)} %pad_maximum_fusion.15), kind=kOutput, calls=%fused_computation.48 | convolution fusion | flops 8629780480 | bytes 20979712 | tf_op jit(solution)/shard_map/dot_general | solution.py:22
  574.2 18.0 %collective-permute-done.36 = bf16[512,1024]{1,0:T(8,128)(2,1)} collective-permute-done((bf16[512,1024]{1,0:T(8,128)(2,1)}, bf16[512,1024]{1,0:T(8,128)(2,1)}, u32[]{:S(2)}, u32[]{:S(2)}) %collective-permute-start.36) | collective-permute-done | bytes 1048608 | tf_op jit(solution)/shard_map/ppermute | solution.py:153
  599.2 15.3 %collective-permute-done.38 = bf16[512,1024]{1,0:T(8,128)(2,1)} collective-permute-done((bf16[512,1024]{1,0:T(8,128)(2,1)}, bf16[512,1024]{1,0:T(8,128)(2,1)}, u32[]{:S(2)}, u32[]{:S(2)}) %collective-permute-start.38) | collective-permute-done | bytes 1048608 | tf_op jit(solution)/shard_map/ppermute | solution.py:153
  677.1 14.6 collective-permute-done.57
  699.9 11.8 all-to-all-start.1
  730.1 18.4 %convert_reduce_fusion.1 = (f32[2048]{0:T(1024)S(1)}, bf16[1024,2048]{1,0:T(8,128)(2,1)}) fusion(f32[1024,2048]{1,0:T(8,128)} %fusion.115, f32[2048]{0:T(1024)S(1)} %pad_maximum_fusion.15, bf16[1024,2048]{1,0:T(8,128)(2,1)} %constant_dynamic-update-slice_fusion.21, bf16[2048,1024]{1,0:T(8,128)(2,1)} %collective-permute-done.35, ...), kind=kOutput, calls=%fused_computation.32 | convolution fusion | flops 8650749952 | bytes 25182208 | tf_op jit(solution)/shard_map/dot_general | solution.py:22
  748.5 12.6 convolution_convert_fusion.3
  768.3 15.5 %fusion.109 = f32[2048,2048]{1,0:T(8,128)} fusion(bf16[1024,2048]{1,0:T(8,128)(2,1)S(1)} %constant_dynamic-update-slice_fusion.31, f32[1024,2048]{1,0:T(8,128)} %fusion.114, f32[2048]{0:T(1024)S(1)} %pad_maximum_fusion.15), kind=kOutput, calls=%fused_computation.407 | convolution fusion | flops 8610906112 | bytes 29368320 | tf_op jit(solution)/shard_map/dot_general | solution.py:22
  783.8 18.4 %convert_reduce_fusion = (f32[2048]{0:T(1024)S(1)}, bf16[1024,2048]{1,0:T(8,128)(2,1)}) fusion(f32[1024,2048]{1,0:T(8,128)} %fusion.114, f32[2048]{0:T(1024)S(1)} %pad_maximum_fusion.15, bf16[1024,2048]{1,0:T(8,128)(2,1)} %copy-done.102, bf16[2048,1024]{1,0:T(8,128)(2,1)} %collective-permute-done.35, bf16[2048,1024]{1,0:T(8,128)(2,1)S(1)} %bitcast.308), kind=kOutput, calls=%fused_computation.31 | convolution fusion | flops 8650749952 | bytes 25182208 | tf_op jit(solution)/shard_map/dot_general | solution.py:22
  802.2 12.7 convolution_convert_fusion.2
  821.3 17.6 %add_convert_fusion = bf16[2048,2048]{1,0:T(8,128)(2,1)} fusion(f32[2048,2048]{1,0:T(8,128)} %fusion.109, bf16[1024,2048]{1,0:T(8,128)(2,1)} %constant_dynamic-update-slice_fusion.21, f32[1024,2048]{1,0:T(8,128)} %fusion.115, f32[2048]{0:T(1024)S(1)} %pad_maximum_fusion.15), kind=kOutput, calls=%fused_computation.6 | convolution fusion | flops 8619294720 | bytes 37756928 | tf_op jit(solution)/shard_map/dot_general | solution.py:22
  841.2 14.4 fusion.142
  911.1 14.6 add_convert_fusion.1
  1031.5 11.6 add_convert_fusion.2
  1091.7 35.6 %collective-permute-done.97 = bf16[512,256]{1,0:T(8,128)(2,1)S(1)} collective-permute-done((bf16[512,256]{1,0:T(8,128)(2,1)S(1)}, bf16[512,256]{1,0:T(8,128)(2,1)S(1)}, u32[]{:S(2)}, u32[]{:S(2)}) %collective-permute-start.97) | collective-permute-done | bytes 262176 | tf_op jit(solution)/shard_map/ppermute | solution.py:191
  1186.8 14.5 collective-permute-done.110
  1222.6 46.0 %collective-permute-done.104 = bf16[512,1024]{1,0:T(8,128)(2,1)} collective-permute-done((bf16[512,1024]{1,0:T(8,128)(2,1)}, bf16[512,1024]{1,0:T(8,128)(2,1)}, u32[]{:S(2)}, u32[]{:S(2)}) %collective-permute-start.104) | collective-permute-done | bytes 1048608 | tf_op jit(solution)/shard_map/ppermute | solution.py:191
  1277.1 82.4 %all-reduce.3.cloned.1.call-done = f32[32,768]{1,0:T(8,128)} async-done(((f32[32,768]{1,0:T(8,128)}), f32[32,768]{1,0:T(8,128)}) %all-reduce.3.cloned.1.call-update) | async-done | bytes 98320
  1383.7 43.1 %collective-permute-done.90 = bf16[512,768]{1,0:T(8,128)(2,1)} collective-permute-done((bf16[512,768]{1,0:T(8,128)(2,1)}, bf16[512,768]{1,0:T(8,128)(2,1)}, u32[]{:S(2)}, u32[]{:S(2)}) %collective-permute-start.90) | collective-permute-done | bytes 786464 | tf_op jit(solution)/shard_map/ppermute | solution.py:191
  (853 shorter events, 764.9 us)
Async XLA Ops:
  9.2 73.9 %collective-permute-start.10 = (bf16[256,256]{1,0:T(8,128)(2,1)}, bf16[256,256]{1,0:T(8,128)(2,1)S(1)}, u32[]{:S(2)}, u32[]{:S(2)}) collective-permute-start(bf16[256,256]{1,0:T(8,128)(2,1)} %get-tuple-element.237), channel_id=1, source_target_pairs={{0,4},{4,0},{8,12},{12,8},{16,20},{20,16},{24,28},{28,24},{1,5},{5... | collective-permute-start | bytes 393224 | tf_op jit(solution)/shard_map/ppermute | solution.py:191
  15.3 67.9 %collective-permute-start.4 = (bf16[256,768]{1,0:T(8,128)(2,1)}, bf16[256,768]{1,0:T(8,128)(2,1)}, u32[]{:S(2)}, u32[]{:S(2)}) collective-permute-start(bf16[256,768]{1,0:T(8,128)(2,1)} %pad_maximum_fusion.12), channel_id=1, source_target_pairs={{0,4},{4,0},{8,12},{12,8},{16,20},{20,16},{24,28},{28,24},{1,5},{5... | collective-permute-start | bytes 1179656 | tf_op jit(solution)/shard_map/ppermute | solution.py:191
  17.4 77.2 %all-to-all-start.2 = ((bf16[8,32,2048]{2,1,0:T(8,128)(2,1)}), bf16[8,32,2048]{2,1,0:T(8,128)(2,1)S(1)}, u32[]{:S(2)}, u32[]{:S(2)}) async-start(bf16[8,32,2048]{2,1,0:T(8,128)(2,1)} %broadcast_select_fusion.2), calls=%async_computation.2 | async-start | bytes 2097152 | tf_op jit(solution)/shard_map/all_to_all | solution.py:343
  25.8 132.1 %collective-permute-start.24 = (bf16[256,1024]{1,0:T(8,128)(2,1)}, bf16[256,1024]{1,0:T(8,128)(2,1)}, u32[]{:S(2)}, u32[]{:S(2)}) collective-permute-start(bf16[256,1024]{1,0:T(8,128)(2,1)} %get-tuple-element.225), channel_id=1, source_target_pairs={{0,4},{4,0},{8,12},{12,8},{16,20},{20,16},{24,28},{28,24},{1,5},{5... | collective-permute-start | bytes 1572872 | tf_op jit(solution)/shard_map/ppermute | solution.py:191
  30.9 136.1 %collective-permute-start.30 = (bf16[256,1024]{1,0:T(8,128)(2,1)}, bf16[256,1024]{1,0:T(8,128)(2,1)}, u32[]{:S(2)}, u32[]{:S(2)}) collective-permute-start(bf16[256,1024]{1,0:T(8,128)(2,1)} %get-tuple-element.229), channel_id=1, source_target_pairs={{0,4},{4,0},{8,12},{12,8},{16,20},{20,16},{24,28},{28,24},{1,5},{5... | collective-permute-start | bytes 1572872 | tf_op jit(solution)/shard_map/ppermute | solution.py:191
  86.7 73.2 %collective-permute-start.5 = (bf16[512,768]{1,0:T(8,128)(2,1)}, bf16[512,768]{1,0:T(8,128)(2,1)}, u32[]{:S(2)}, u32[]{:S(2)}) collective-permute-start(bf16[512,768]{1,0:T(8,128)(2,1)} %pad_maximum_fusion.10), channel_id=1, source_target_pairs={{0,8},{4,12},{8,16},{12,20},{16,24},{20,28},{24,0},{28,4},{1,9},{5... | collective-permute-start | bytes 2359304 | tf_op jit(solution)/shard_map/ppermute | solution.py:191
  86.7 77.3 %collective-permute-start.7 = (bf16[512,768]{1,0:T(8,128)(2,1)}, bf16[512,768]{1,0:T(8,128)(2,1)}, u32[]{:S(2)}, u32[]{:S(2)}) collective-permute-start(bf16[512,768]{1,0:T(8,128)(2,1)} %pad_maximum_fusion.10), channel_id=1, source_target_pairs={{0,24},{4,28},{8,0},{12,4},{16,8},{20,12},{24,16},{28,20},{1,25},{... | collective-permute-start | bytes 2359304 | tf_op jit(solution)/shard_map/ppermute | solution.py:191
  94.6 96.8 %all-to-all-start = ((bf16[8,32,2048]{2,1,0:T(8,128)(2,1)}), bf16[8,32,2048]{2,1,0:T(8,128)(2,1)S(1)}, u32[]{:S(2)}, u32[]{:S(2)}) async-start(bf16[8,32,2048]{2,1,0:T(8,128)(2,1)} %broadcast_select_fusion.3), calls=%async_computation | async-start | bytes 2097152 | tf_op jit(solution)/shard_map/all_to_all | solution.py:343
  186.7 78.3 %collective-permute-start.9 = (bf16[2048,768]{1,0:T(8,128)(2,1)}, bf16[2048,768]{1,0:T(8,128)(2,1)}, u32[]{:S(2)}, u32[]{:S(2)}) collective-permute-start(bf16[2048,768]{1,0:T(8,128)(2,1)} %bitcast.8), channel_id=1, source_target_pairs={{0,4},{4,0},{8,12},{12,8},{16,20},{20,16},{24,28},{28,24},{1,5},{5... | collective-permute-start | bytes 9437192 | tf_op jit(solution)/shard_map/ppermute | solution.py:191
  249.1 78.2 %collective-permute-start.33 = (bf16[512,1024]{1,0:T(8,128)(2,1)S(1)}, bf16[512,1024]{1,0:T(8,128)(2,1)S(1)}, u32[]{:S(2)}, u32[]{:S(2)}) collective-permute-start(bf16[512,1024]{1,0:T(8,128)(2,1)S(1)} %copy-done.90), channel_id=1, source_target_pairs={{0,24},{4,28},{8,0},{12,4},{16,8},{20,12},{24,16},{28,20},{1,25},{... | collective-permute-start | bytes 3145736 | tf_op jit(solution)/shard_map/ppermute | solution.py:191
  260.1 70.5 %collective-permute-start.25 = (bf16[512,1024]{1,0:T(8,128)(2,1)}, bf16[512,1024]{1,0:T(8,128)(2,1)}, u32[]{:S(2)}, u32[]{:S(2)}) collective-permute-start(bf16[512,1024]{1,0:T(8,128)(2,1)} %pad_maximum_fusion.8), channel_id=1, source_target_pairs={{0,8},{4,12},{8,16},{12,20},{16,24},{20,28},{24,0},{28,4},{1,9},{5... | collective-permute-start | bytes 3145736 | tf_op jit(solution)/shard_map/ppermute | solution.py:191
  261.1 77.0 %collective-permute-start.27 = (bf16[512,1024]{1,0:T(8,128)(2,1)}, bf16[512,1024]{1,0:T(8,128)(2,1)}, u32[]{:S(2)}, u32[]{:S(2)}) collective-permute-start(bf16[512,1024]{1,0:T(8,128)(2,1)} %pad_maximum_fusion.8), channel_id=1, source_target_pairs={{0,24},{4,28},{8,0},{12,4},{16,8},{20,12},{24,16},{28,20},{1,25},{... | collective-permute-start | bytes 3145736 | tf_op jit(solution)/shard_map/ppermute | solution.py:191
  265.0 76.6 %collective-permute-start.32 = (bf16[512,1024]{1,0:T(8,128)(2,1)}, bf16[512,1024]{1,0:T(8,128)(2,1)}, u32[]{:S(2)}, u32[]{:S(2)}) collective-permute-start(bf16[512,1024]{1,0:T(8,128)(2,1)} %collective-permute-done.31), channel_id=1, source_target_pairs={{8,16},{12,20},{16,24},{20,28},{9,17},{13,21},{17,25},{21,29},{10,... | collective-permute-start | bytes 3145736 | tf_op jit(solution)/shard_map/ppermute | solution.py:191
  416.7 84.1 %collective-permute-start.29 = (bf16[2048,1024]{1,0:T(8,128)(2,1)}, bf16[2048,1024]{1,0:T(8,128)(2,1)}, u32[]{:S(2)}, u32[]{:S(2)}) collective-permute-start(bf16[2048,1024]{1,0:T(8,128)(2,1)} %bitcast.22), channel_id=1, source_target_pairs={{0,4},{4,0},{8,12},{12,8},{16,20},{20,16},{24,28},{28,24},{1,5},{5... | collective-permute-start | bytes 12582920 | tf_op jit(solution)/shard_map/ppermute | solution.py:191
  437.7 78.1 %collective-permute-start.35 = (bf16[2048,1024]{1,0:T(8,128)(2,1)S(1)}, bf16[2048,1024]{1,0:T(8,128)(2,1)}, u32[]{:S(2)}, u32[]{:S(2)}) collective-permute-start(bf16[2048,1024]{1,0:T(8,128)(2,1)S(1)} %bitcast.304), channel_id=1, source_target_pairs={{0,4},{4,0},{8,12},{12,8},{16,20},{20,16},{24,28},{28,24},{1,5},{5... | collective-permute-start | bytes 12582920 | tf_op jit(solution)/shard_map/ppermute | solution.py:191
  699.9 204.6 %all-to-all-start.1 = ((bf16[8,32,2048]{2,1,0:T(8,128)(2,1)}), bf16[8,32,2048]{2,1,0:T(8,128)(2,1)}, u32[]{:S(2)}, u32[]{:S(2)}) async-start(bf16[8,32,2048]{2,1,0:T(8,128)(2,1)} %get-tuple-element.260), calls=%async_computation.1 | async-start | bytes 2097152 | tf_op jit(solution)/shard_map/all_to_all | solution.py:388
  761.3 77.5 %collective-permute-start.60 = (bf16[512,1024]{1,0:T(8,128)(2,1)S(1)}, bf16[512,1024]{1,0:T(8,128)(2,1)S(1)}, u32[]{:S(2)}, u32[]{:S(2)}) collective-permute-start(bf16[512,1024]{1,0:T(8,128)(2,1)S(1)} %get-tuple-element.177), channel_id=1, source_target_pairs={{0,1},{1,0},{2,3},{3,2},{4,5},{5,4},{6,7},{7,6},{8,9},{9,8},{10,11... | collective-permute-start | bytes 3145736 | tf_op jit(solution)/shard_map/ppermute | solution.py:153
  761.7 97.3 %collective-permute-start.62 = (bf16[512,1024]{1,0:T(8,128)(2,1)S(1)}, bf16[512,1024]{1,0:T(8,128)(2,1)S(1)}, u32[]{:S(2)}, u32[]{:S(2)}) collective-permute-start(bf16[512,1024]{1,0:T(8,128)(2,1)S(1)} %get-tuple-element.178), channel_id=1, source_target_pairs={{0,2},{1,3},{2,0},{3,1},{4,6},{5,7},{6,4},{7,5},{8,10},{9,11},{10,... | collective-permute-start | bytes 3145736 | tf_op jit(solution)/shard_map/ppermute | solution.py:153
  868.2 191.5 %collective-permute-start.106 = (bf16[2048,1024]{1,0:T(8,128)(2,1)}, bf16[2048,1024]{1,0:T(8,128)(2,1)}, u32[]{:S(2)}, u32[]{:S(2)}) collective-permute-start(bf16[2048,1024]{1,0:T(8,128)(2,1)} %slice.906), channel_id=1, source_target_pairs={{0,4},{4,0},{8,12},{12,8},{16,20},{20,16},{24,28},{28,24},{1,5},{5... | collective-permute-start | bytes 12582920 | tf_op jit(solution)/shard_map/ppermute | solution.py:191
  946.7 118.6 %collective-permute-start.100 = (bf16[2048,1024]{1,0:T(8,128)(2,1)}, bf16[2048,1024]{1,0:T(8,128)(2,1)}, u32[]{:S(2)}, u32[]{:S(2)}) collective-permute-start(bf16[2048,1024]{1,0:T(8,128)(2,1)} %slice.904), channel_id=1, source_target_pairs={{0,4},{4,0},{8,12},{12,8},{16,20},{20,16},{24,28},{28,24},{1,5},{5... | collective-permute-start | bytes 12582920 | tf_op jit(solution)/shard_map/ppermute | solution.py:191
  999.2 73.1 %collective-permute-start.84 = (bf16[512,1024]{1,0:T(8,128)(2,1)}, bf16[512,1024]{1,0:T(8,128)(2,1)}, u32[]{:S(2)}, u32[]{:S(2)}) collective-permute-start(bf16[512,1024]{1,0:T(8,128)(2,1)} %get-tuple-element.181), channel_id=1, source_target_pairs={{0,1},{1,0},{2,3},{3,2},{4,5},{5,4},{6,7},{7,6},{8,9},{9,8},{10,11... | collective-permute-start | bytes 3145736 | tf_op jit(solution)/shard_map/ppermute | solution.py:153
  1000.5 79.4 %collective-permute-start.86 = (bf16[512,1024]{1,0:T(8,128)(2,1)}, bf16[512,1024]{1,0:T(8,128)(2,1)}, u32[]{:S(2)}, u32[]{:S(2)}) collective-permute-start(bf16[512,1024]{1,0:T(8,128)(2,1)} %get-tuple-element.182), channel_id=1, source_target_pairs={{0,2},{1,3},{2,0},{3,1},{4,6},{5,7},{6,4},{7,5},{8,10},{9,11},{10,... | collective-permute-start | bytes 3145736 | tf_op jit(solution)/shard_map/ppermute | solution.py:153
  1072.4 65.6 %collective-permute-start.109 = (bf16[512,1024]{1,0:T(8,128)(2,1)S(1)}, bf16[512,1024]{1,0:T(8,128)(2,1)S(1)}, u32[]{:S(2)}, u32[]{:S(2)}) collective-permute-start(bf16[512,1024]{1,0:T(8,128)(2,1)S(1)} %dynamic-slice_bitcast_fusion.1), channel_id=1, source_target_pairs={{24,16},{28,20},{16,8},{20,12},{25,17},{29,21},{17,9},{21,13},{26,... | collective-permute-start | bytes 3145736 | tf_op jit(solution)/shard_map/ppermute | solution.py:191
  1135.9 74.4 %collective-permute-start.88 = (bf16[2048,768]{1,0:T(8,128)(2,1)}, bf16[2048,768]{1,0:T(8,128)(2,1)}, u32[]{:S(2)}, u32[]{:S(2)}) collective-permute-start(bf16[2048,768]{1,0:T(8,128)(2,1)} %slice.897), channel_id=1, source_target_pairs={{0,4},{4,0},{8,12},{12,8},{16,20},{20,16},{24,28},{28,24},{1,5},{5... | collective-permute-start | bytes 9437192 | tf_op jit(solution)/shard_map/ppermute | solution.py:191
  1171.4 192.3 %all-to-all-start.5 = ((bf16[8,32,2048]{2,1,0:T(8,128)(2,1)}), bf16[8,32,2048]{2,1,0:T(8,128)(2,1)}, u32[]{:S(2)}, u32[]{:S(2)}) async-start(bf16[8,32,2048]{2,1,0:T(8,128)(2,1)} %bitcast.300), calls=%async_computation.5 | async-start | bytes 2097152 | tf_op jit(solution)/shard_map/all_to_all | solution.py:388
  1178.7 180.8 %all-reduce.3.cloned.1.call-start = ((), (), s32[]{:S(2)}) async-start(), calls=%async_computation.6 | async-start | bytes 196608
  1181.5 87.1 %collective-permute-start.104 = (bf16[512,1024]{1,0:T(8,128)(2,1)}, bf16[512,1024]{1,0:T(8,128)(2,1)}, u32[]{:S(2)}, u32[]{:S(2)}) collective-permute-start(bf16[512,1024]{1,0:T(8,128)(2,1)} %get-tuple-element.170), channel_id=1, source_target_pairs={{0,24},{4,28},{8,0},{12,4},{16,8},{20,12},{24,16},{28,20},{1,25},{... | collective-permute-start | bytes 3145736 | tf_op jit(solution)/shard_map/ppermute | solution.py:191
  1205.0 165.1 %collective-permute-start.111 = (f32[256,1024]{1,0:T(8,128)}, f32[256,1024]{1,0:T(8,128)}, u32[]{:S(2)}, u32[]{:S(2)}) collective-permute-start(f32[256,1024]{1,0:T(8,128)} %dynamic-slice_bitcast_fusion), channel_id=1, source_target_pairs={{0,4},{4,0},{8,12},{12,8},{16,20},{20,16},{24,28},{28,24},{1,5},{5... | collective-permute-start | bytes 3145736 | tf_op jit(solution)/shard_map/ppermute | solution.py:191
  1214.8 156.9 %collective-permute-start.91 = (bf16[512,768]{1,0:T(8,128)(2,1)}, bf16[512,768]{1,0:T(8,128)(2,1)}, u32[]{:S(2)}, u32[]{:S(2)}) collective-permute-start(bf16[512,768]{1,0:T(8,128)(2,1)} %dynamic-slice_bitcast_fusion.5), channel_id=1, source_target_pairs={{24,16},{28,20},{16,8},{20,12},{25,17},{29,21},{17,9},{21,13},{26,... | collective-permute-start | bytes 2359304 | tf_op jit(solution)/shard_map/ppermute | solution.py:191
  1216.1 155.6 %collective-permute-start.89 = (bf16[512,768]{1,0:T(8,128)(2,1)}, bf16[512,768]{1,0:T(8,128)(2,1)}, u32[]{:S(2)}, u32[]{:S(2)}) collective-permute-start(bf16[512,768]{1,0:T(8,128)(2,1)} %dynamic-slice_bitcast_fusion.5), channel_id=1, source_target_pairs={{0,8},{4,12},{8,16},{12,20},{1,9},{5,13},{9,17},{13,21},{2,10},{6,... | collective-permute-start | bytes 2359304 | tf_op jit(solution)/shard_map/ppermute | solution.py:191
  1273.4 107.1 %collective-permute-start.105 = (f32[256,1024]{1,0:T(8,128)}, f32[256,1024]{1,0:T(8,128)}, u32[]{:S(2)}, u32[]{:S(2)}) collective-permute-start(f32[256,1024]{1,0:T(8,128)} %dynamic-slice_bitcast_fusion.2), channel_id=1, source_target_pairs={{0,4},{4,0},{8,12},{12,8},{16,20},{20,16},{24,28},{28,24},{1,5},{5... | collective-permute-start | bytes 3145736 | tf_op jit(solution)/shard_map/ppermute | solution.py:191
  1363.7 68.6 %all-to-all-start.4 = ((bf16[8,32,2048]{2,1,0:T(8,128)(2,1)}), bf16[8,32,2048]{2,1,0:T(8,128)(2,1)}, u32[]{:S(2)}, u32[]{:S(2)}) async-start(bf16[8,32,2048]{2,1,0:T(8,128)(2,1)} %bitcast.299), calls=%async_computation.4 | async-start | bytes 2097152 | tf_op jit(solution)/shard_map/all_to_all | solution.py:388
  (231 other events, 5621.4 us)
Sparse Core Ops, SparseCore 0:
  1187.0 172.5 all-reduce.2

commit v2 on v1

v2 whole, which is shorter than its diff:
```python
import functools
import math

import jax
import jax.numpy as jnp
from jax import lax
from jax.experimental import pallas as pl
from jax.experimental.pallas import tpu as pltpu
from jax.sharding import PartitionSpec as P

HEAD = 128
norm_epsilon = 1e-05
masked_score = -1e30
log2_e = math.log2(math.e)
head_scale = 1.0 / math.sqrt(HEAD)
gelu_root = math.sqrt(2.0 / math.pi)
bf16 = jnp.bfloat16
f32 = jnp.float32
MIB = 1024 * 1024
TALL = ((1,), (0,))
FLAT = ((1,), (1,))
DEEP = ((0,), (0,))


def dot(left, right, contract):
    return lax.dot_general(left, right, (contract, ((), ())), preferred_element_type=f32)


def shape(dims, dtype):
    return jax.ShapeDtypeStruct(tuple(dims), dtype)


def whole(array):
    return pl.BlockSpec(array.shape, lambda *i: (0,) * array.ndim)


def launch(body, grid, ins, in_specs, outs, out_specs, later=(), scratch=(), flops=0, nbytes=0, exps=0):
    later = tuple(later)
    count, skip = len(ins), len(later)

    def run(*refs):
        body(refs[:count], refs[count + skip :])

    return pl.pallas_call(
        run,
        grid=grid,
        in_specs=list(in_specs) + [pl.BlockSpec(memory_space=pl.ANY)] * skip,
        out_specs=list(out_specs),
        out_shape=list(outs),
        scratch_shapes=list(scratch),
        compiler_params=pltpu.CompilerParams(vmem_limit_bytes=56 * MIB),
        cost_estimate=pl.CostEstimate(flops=int(flops), bytes_accessed=int(nbytes), transcendentals=int(exps)),
    )(*ins, *later)


def attend(qkv, bias, halves, later=()):
    rows, columns = qkv.shape
    group = columns // halves
    heads = group // (3 * HEAD)
    width = heads * HEAD
    block = min(256, rows)

    def body(ins, outs):
        bias_ref, qkv_ref = ins
        mixed_ref, log_ref = outs
        shift = bias_ref[...]
        for head in range(heads):
            low = head * HEAD
            keys = qkv_ref[:, width + low : width + low + HEAD]
            values = qkv_ref[:, 2 * width + low : 2 * width + low + HEAD]
            for first in range(0, rows, block):
                part = slice(first, first + block)
                queries = qkv_ref[part, low : low + HEAD]
                scores = dot(keys, queries, FLAT) * (head_scale * log2_e) + shift
                peak = jnp.max(scores, axis=0, keepdims=True)
                weight = jnp.exp2(scores - peak)
                total = jnp.sum(weight, axis=0, keepdims=True)
                mixed = dot(values, weight.astype(bf16), DEEP) * (1.0 / total)
                mixed_ref[part, low : low + HEAD] = mixed.T.astype(bf16)
                log_ref[0, head : head + 1, part] = peak + jnp.log2(total)

    return launch(
        body,
        (halves,),
        [bias, qkv],
        [pl.BlockSpec((rows, 1), lambda i: (0, 0)), pl.BlockSpec((rows, group), lambda i: (0, i))],
        [shape((rows, halves * width), bf16), shape((halves, heads, rows), f32)],
        [pl.BlockSpec((rows, width), lambda i: (0, i)), pl.BlockSpec((1, heads, rows), lambda i: (i, 0, 0))],
        later,
        flops=4 * halves * heads * rows * rows * HEAD * 4,
        nbytes=rows * columns * 3,
        exps=halves * heads * rows * rows,
    )


def attend_back(qkv, bias, mixed, grads, logs, halves, later=()):
    rows, columns = qkv.shape
    group = columns // halves
    heads = group // (3 * HEAD)
    width = heads * HEAD
    block = min(256, rows)

    def body(ins, outs):
        bias_ref, qkv_ref, mixed_ref, grad_ref, log_ref = ins
        out_ref, sum_ref = outs
        shift = bias_ref[...]
        for head in range(heads):
            low = head * HEAD
            keys = qkv_ref[:, width + low : width + low + HEAD]
            values = qkv_ref[:, 2 * width + low : 2 * width + low + HEAD]
            key_total = jnp.zeros((rows, HEAD), f32)
            value_total = jnp.zeros((rows, HEAD), f32)
            query_sum = jnp.zeros((1, HEAD), f32)
            for first in range(0, rows, block):
                part = slice(first, first + block)
                queries = qkv_ref[part, low : low + HEAD]
                grad = grad_ref[part, low : low + HEAD]
                mix = mixed_ref[part, low : low + HEAD]
                centre = jnp.sum((grad.astype(f32) * mix.astype(f32)).T, axis=0, keepdims=True)
                scores = dot(keys, queries, FLAT) * (head_scale * log2_e) + shift
                weight = jnp.exp2(scores - log_ref[0, head : head + 1, part])
                weight_grad = dot(values, grad, FLAT)
                score_grad = (weight * (weight_grad - centre)).astype(bf16)
                value_total = value_total + dot(weight.astype(bf16), grad, TALL)
                key_total = key_total + dot(score_grad, queries, TALL)
                query_grad = (dot(keys, score_grad, DEEP) * head_scale).T.astype(bf16)
                out_ref[part, low : low + HEAD] = query_grad
                query_sum = query_sum + jnp.sum(query_grad.astype(f32), axis=0, keepdims=True)
            value_total = value_total.astype(bf16)
            out_ref[:, width + low : width + low + HEAD] = (key_total * head_scale).astype(bf16)
            out_ref[:, 2 * width + low : 2 * width + low + HEAD] = value_total
            sum_ref[0, :, low : low + HEAD] = query_sum
            sum_ref[0, :, width + low : width + low + HEAD] = jnp.sum(
                value_total.astype(f32), axis=0, keepdims=True
            )

    columns_of = lambda n: pl.BlockSpec((rows, n), lambda i: (0, i))
    return launch(
        body,
        (halves,),
        [bias, qkv, mixed, grads, logs],
        [
            pl.BlockSpec((rows, 1), lambda i: (0, 0)),
            columns_of(group),
            columns_of(width),
            columns_of(width),
            pl.BlockSpec((1, heads, rows), lambda i: (i, 0, 0)),
        ],
        [shape((rows, columns), bf16), shape((halves, 1, 2 * width), f32)],
        [columns_of(group), pl.BlockSpec((1, 1, 2 * width), lambda i: (i, 0, 0))],
        later,
        flops=10 * halves * heads * rows * rows * HEAD * 4,
        nbytes=rows * columns * 6,
        exps=halves * heads * rows * rows,
    )


def tile_of(width, most):
    tile = min(width, most)
    while width % tile:
        tile //= 2
    return tile


def rows_matmul(pieces, weights, finish, extras, kinds, later=(), most=512):
    rows = sum(p.shape[0] for p in pieces)
    inner, half = weights[0].shape
    tile = tile_of(half, most)
    steps = half // tile

    def body(ins, refs):
        piece_refs = ins[: len(pieces)]
        low_ref, high_ref = ins[len(pieces) : len(pieces) + 2]
        extra_refs = ins[len(pieces) + 2 :]
        out_refs, gathered = refs[: len(kinds)], refs[len(kinds)]
        step = pl.program_id(0)

        @pl.when(step == 0)
        def _():
            first = 0
            for ref in piece_refs:
                gathered[first : first + ref.shape[0], :] = ref[...]
                first += ref.shape[0]

        def part(weight_ref):
            product = dot(gathered[...], weight_ref[...], TALL)
            for ref, value in zip(out_refs, finish(product, *[r[...] for r in extra_refs])):
                ref[...] = value

        @pl.when(step < steps)
        def _():
            part(low_ref)

        @pl.when(step >= steps)
        def _():
            part(high_ref)

    def along(n):
        return pl.BlockSpec((n, tile), lambda j: (0, j))

    return launch(
        body,
        (2 * steps,),
        [*pieces, *weights, *extras],
        [whole(p) for p in pieces]
        + [
            pl.BlockSpec((inner, tile), lambda j: (0, jnp.minimum(j, steps - 1))),
            pl.BlockSpec((inner, tile), lambda j: (0, jnp.maximum(j - steps, 0))),
        ]
        + [along(e.shape[0]) for e in extras],
        [shape((n, 2 * half), dtype) for n, dtype in kinds],
        [along(n) for n, _ in kinds],
        later,
        scratch=[pltpu.VMEM((rows, inner), bf16)],
        flops=2 * rows * inner * half * 2,
        nbytes=2 * (rows * inner + 2 * inner * half) + sum(8 * n * half for n, _ in kinds),
    )


def terms_matmul(left, weights, count, later=(), most=512):
    rows, inner = left.shape
    outer, half = weights[0].shape
    tile = tile_of(outer // 2, most)
    steps = outer // 2 // tile
    piece = rows // count

    def body(ins, outs):
        left_ref, low_ref, high_ref = ins
        step = pl.program_id(0)
        product = dot(left_ref[:, :half], low_ref[...], FLAT) + dot(left_ref[:, half:], high_ref[...], FLAT)
        product = product.astype(bf16)
        for side in range(2):

            @pl.when((step < steps) if side == 0 else (step >= steps))
            def _():
                for i in range(count):
                    outs[2 * i + side][...] = product[i * piece : (i + 1) * piece]

    places = [
        lambda j: (0, jnp.minimum(j, steps - 1)),
        lambda j: (0, jnp.maximum(j - steps, 0)),
    ]
    outs = launch(
        body,
        (2 * steps,),
        [left, *weights],
        [whole(left)] + [pl.BlockSpec((tile, half), lambda j: (j, 0))] * 2,
        [shape((piece, outer // 2), bf16)] * (2 * count),
        [pl.BlockSpec((piece, tile), places[i % 2]) for i in range(2 * count)],
        later,
        flops=2 * rows * inner * outer,
        nbytes=2 * (rows * inner + outer * inner + rows * outer),
    )
    return [outs[2 * i : 2 * i + 2] for i in range(count)]


def weight_grad(lefts, rights, later=(), most=256):
    flat = [p for pieces in lefts for p in pieces]
    outer = flat[0].shape[1]
    rows, columns = rights[0].shape
    half = columns // 2
    tile = tile_of(outer, most)
    slots = len(rights)

    def body(ins, refs):
        piece_refs, right_refs = ins[: len(flat)], ins[len(flat) :]
        mine_ref, theirs_ref, gathered = refs
        first = 0
        for ref in piece_refs:
            gathered[first : first + ref.shape[0], :] = ref[...]
            first += ref.shape[0]
        total = None
        for slot in range(slots):
            term = dot(gathered[slot * rows : (slot + 1) * rows, :], right_refs[slot][...], DEEP)
            total = term if total is None else total + term
        mine_ref[...] = total[:, :half].astype(bf16)
        theirs_ref[...] = total[:, half:].astype(bf16)

    return launch(
        body,
        (outer // tile,),
        [*flat, *rights],
        [pl.BlockSpec((p.shape[0], tile), lambda j: (0, j)) for p in flat] + [whole(r) for r in rights],
        [shape((outer, half), bf16)] * 2,
        [pl.BlockSpec((tile, half), lambda j: (j, 0))] * 2,
        later,
        scratch=[pltpu.VMEM((slots * rows, tile), bf16)],
        flops=2 * slots * rows * outer * columns,
        nbytes=2 * (slots * rows * (outer + columns) + outer * columns),
    )


def norm_tiles(body, rows, width, left, right, tiled, vectors, outs, halves, sums, later):
    steps = 4
    tile = rows // steps
    n_left, n_right, n_tiled = len(left), len(right), len(tiled)

    def run(ins, refs):
        step = pl.program_id(0)
        left_refs = ins[:n_left]
        right_refs = ins[n_left : n_left + n_right]
        tiled_refs = ins[n_left + n_right : n_left + n_right + n_tiled]
        vector_ref = ins[-1] if vectors is not None else None

        def added(group):
            total = group[0][...].astype(f32)
            for ref in group[1:]:
                total = total + ref[...].astype(f32)
            return total

        both = jnp.concatenate([added(left_refs), added(right_refs)], axis=1)
        values, split, totals = body(both, [r[...] for r in tiled_refs], vector_ref)
        for ref, value in zip(refs, values):
            ref[...] = value.astype(ref.dtype)
        split_refs = refs[len(outs) : len(outs) + 2 * halves]
        for i, value in enumerate(split):
            top, bottom = split_refs[2 * i], split_refs[2 * i + 1]

            @pl.when(step < steps // 2)
            def _():
                top[...] = value.astype(bf16)

            @pl.when(step >= steps // 2)
            def _():
                bottom[...] = value.astype(bf16)

        if sums:
            sum_ref = refs[-1]

            @pl.when(step == 0)
            def _():
                sum_ref[...] = jnp.zeros_like(sum_ref)

            for i, value in enumerate(totals):
                sum_ref[i : i + 1, :] += jnp.sum(value, axis=0, keepdims=True)

    def of(columns):
        return pl.BlockSpec((tile, columns), lambda i: (i, 0))

    top = pl.BlockSpec((tile, width), lambda i: (jnp.minimum(i, steps // 2 - 1), 0))
    bottom = pl.BlockSpec((tile, width), lambda i: (jnp.maximum(i - steps // 2, 0), 0))
    ins = [*left, *right, *tiled] + ([vectors] if vectors is not None else [])
    return launch(
        run,
        (steps,),
        ins,
        [of(a.shape[1]) for a in (*left, *right, *tiled)] + ([whole(vectors)] if vectors is not None else []),
        [shape((rows, c), dtype) for c, dtype in outs]
        + [shape((rows // 2, width), bf16)] * (2 * halves)
        + ([shape((8, width), f32)] if sums else []),
        [of(c) for c, _ in outs]
        + [top, bottom] * halves
        + ([pl.BlockSpec((8, width), lambda i: (0, 0))] if sums else []),
        later,
        flops=rows * width * 20,
        nbytes=rows * width * 16,
    )


def normed(values):
    centred = values - jnp.mean(values, axis=-1, keepdims=True)
    inverse = lax.rsqrt(jnp.mean(centred * centred, axis=-1, keepdims=True) + norm_epsilon)
    return centred * inverse, inverse


def norm_back(grads, unit, inverse, gain):
    scaled = grads * gain
    return inverse * (
        scaled
        - jnp.mean(scaled, axis=-1, keepdims=True)
        - unit * jnp.mean(scaled * unit, axis=-1, keepdims=True)
    )


def first_norm(terms, rows, vectors, later=()):
    def body(both, tiled, v):
        unit, inverse = normed(tiled[0].astype(f32) + (both + v[0:1, :]))
        return [unit, inverse], [unit * v[1:2, :] + v[2:3, :]], []

    n, width = rows.shape
    unit, inverse, top, bottom = norm_tiles(
        body, n, width, *terms, [rows], vectors, [(width, f32), (1, f32)], 1, False, later
    )
    return (top, bottom), unit, inverse


def second_norm(terms, unit, cotangent, vectors, later=()):
    def body(both, tiled, v):
        first, grads = tiled[0] * v[1:2, :] + v[2:3, :], tiled[1].astype(f32)
        unit_two, inverse = normed(first + (both + v[3:4, :]))
        back = norm_back(grads, unit_two, inverse, v[4:5, :])
        return [unit_two * v[4:5, :] + v[5:6, :], back], [back], [back, grads * unit_two, grads]

    n, width = unit.shape
    rows, back, top, bottom, sums = norm_tiles(
        body, n, width, *terms, [unit, cotangent], vectors, [(width, bf16), (width, f32)], 1, True, later
    )
    return rows, back, (top, bottom), sums


def first_norm_back(terms, back_two, unit, inverse, vectors, later=()):
    def body(both, tiled, v):
        grads = tiled[0] + both
        back = norm_back(grads, tiled[1], tiled[2], v[1:2, :])
        return [back], [back], [back, grads * tiled[1], grads]

    n, width = unit.shape
    back, top, bottom, sums = norm_tiles(
        body, n, width, *terms, [back_two, unit, inverse], vectors, [(width, f32)], 1, True, later
    )
    return back, (top, bottom), sums


def input_grad(terms, back, later=()):
    def body(both, tiled, v):
        return [tiled[0] + both], [], []

    n, width = back.shape
    return norm_tiles(body, n, width, *terms, [back], None, [(width, bf16)], 0, False, later)[0]


class TensorAxis:
    def __init__(self):
        self.size = lax.axis_size("tensor")
        self.me = lax.axis_index("tensor")
        self.square = self.size == 4
        if self.square:
            self.origins = self.me ^ jnp.array([0, 1, 3, 2], jnp.int32)
        else:
            self.origins = jnp.arange(self.size, dtype=jnp.int32)

    def swap(self, array, bit):
        return lax.ppermute(array, "tensor", [(i, i ^ bit) for i in range(self.size)])

    def gather(self, halves):
        if not self.square:
            return [lax.all_gather(jnp.concatenate(halves, axis=0), "tensor", axis=0, tiled=True)]
        top, bottom = halves
        y_top, x_bottom = self.swap(top, 2), self.swap(bottom, 1)
        y_bottom, x_top = self.swap(bottom, 2), self.swap(top, 1)
        far_top, far_bottom = self.swap(y_top, 1), self.swap(x_bottom, 2)
        return [top, bottom, x_top, x_bottom, far_top, far_bottom, y_top, y_bottom]

    def scatter(self, terms):
        if not self.square:
            full = jnp.concatenate([jnp.concatenate(t, axis=1) for t in terms], axis=0)
            mine = lax.psum_scatter(full, "tensor", scatter_dimension=0, tiled=True)
            half = mine.shape[1] // 2
            return [mine[:, :half]], [mine[:, half:]]
        (left_0, right_0), (left_1, right_1), (left_3, right_3), (left_2, right_2) = terms
        left_onward, right_onward = self.swap(left_3, 1), self.swap(right_3, 2)
        left_near, right_near = self.swap(left_1, 1), self.swap(right_2, 2)
        left_far = self.swap((left_2.astype(f32) + left_onward.astype(f32)).astype(bf16), 2)
        right_far = self.swap((right_1.astype(f32) + right_onward.astype(f32)).astype(bf16), 1)
        return [left_0, left_near, left_far], [right_0, right_near, right_far]


class GroupAxis:
    def __init__(self):
        self.size = lax.axis_size("dp")
        self.me = lax.axis_index("dp")
        self.line = self.size == 8
        self.core = self.me % 2 if self.line else jnp.int32(0)
        self.z = self.me // 2
        n = self.size
        self.next = [(i, (i + 2) % n) for i in range(n)]
        self.last = [(i, (i - 2) % n) for i in range(n)]

    def send(self, array, pairs):
        return lax.ppermute(array, "dp", pairs)

    def other(self, array):
        return self.send(array, [(i, i ^ 1) for i in range(self.size)])

    def order(self, array, axis):
        half = array.shape[axis] // 2
        low = lax.slice_in_dim(array, 0, half, axis=axis)
        high = lax.slice_in_dim(array, half, 2 * half, axis=axis)
        first = self.core == 0
        return jnp.concatenate([jnp.where(first, low, high), jnp.where(first, high, low)], axis=axis)

    def pair(self, mine, got, later):
        rows, width = mine.shape

        def body(ins, outs):
            place, mine_ref, got_ref = ins
            outs[0][pl.ds(pl.multiple_of(place[0] * rows, rows), rows), :] = mine_ref[...]
            outs[0][pl.ds(pl.multiple_of((1 - place[0]) * rows, rows), rows), :] = got_ref[...]

        return launch(
            body,
            (1,),
            [self.core.reshape(1), mine, got],
            [pl.BlockSpec(memory_space=pltpu.SMEM), whole(mine), whole(got)],
            [shape((2 * rows, width), bf16)],
            [pl.BlockSpec((2 * rows, width), lambda i: (0, 0))],
            later,
            nbytes=8 * rows * width,
        )[0]

    def assemble(self, pair, behind, far_up, far_down, ahead):
        rows, width = pair.shape

        def body(place, *refs):
            out = refs[-1]
            step = pl.program_id(0)

            def put(ref, when):
                @pl.when(when)
                def _():
                    out[0] = ref[...]

            put(refs[0], step == 0)
            put(refs[1], step == 1)
            put(refs[2], (step == 2) & (place[0] >= 2))
            put(refs[3], (step == 2) & (place[0] < 2))
            put(refs[4], step == 3)

        return pl.pallas_call(
            body,
            grid_spec=pltpu.PrefetchScalarGridSpec(
                num_scalar_prefetch=1,
                grid=(4,),
                in_specs=[pl.BlockSpec((rows, width), lambda k, place: (0, 0))] * 5,
                out_specs=pl.BlockSpec((1, rows, width), lambda k, place: ((place[0] - k + 4) % 4, 0, 0)),
            ),
            out_shape=shape((4, rows, width), bf16),
            compiler_params=pltpu.CompilerParams(vmem_limit_bytes=56 * MIB),
            cost_estimate=pl.CostEstimate(flops=0, bytes_accessed=18 * rows * width, transcendentals=0),
        )(self.z.reshape(1), pair, behind, far_up, far_down, ahead)

    def gather(self, mine, theirs, later=()):
        if not self.line:
            full = lax.all_gather(jnp.concatenate([mine, theirs], axis=1), "dp", axis=0, tiled=True)
            half = mine.shape[1]
            return (full[:, :half], full[:, half:]), (), ()
        pair = self.pair(mine, self.other(theirs), later)
        behind = self.send(pair, self.next)
        ahead = self.send(pair, self.last)
        far_up = self.send(behind, [(2, 4), (3, 5), (4, 6), (5, 7)])
        far_down = self.send(ahead, [(2, 0), (3, 1), (4, 2), (5, 3)])
        full = self.assemble(pair, behind, far_up, far_down, ahead).reshape(-1, pair.shape[1])
        return (full, self.other(full)), (pair,), (behind, ahead)

    def scatter(self, mine, theirs):
        if not self.line:
            full = jnp.concatenate([mine, theirs], axis=1)
            return lax.psum_scatter(full, "dp", scatter_dimension=0, tiled=True).astype(f32), (), ()
        got = self.other(theirs)
        rows = mine.shape[0] // 4

        def toward(step):
            first = ((self.z + step) % 4) * rows
            parts = [lax.dynamic_slice_in_dim(a, first, rows).astype(f32) for a in (mine, got)]
            return parts[0] + parts[1]

        far = toward(2).astype(bf16)
        up = self.send(far, [(0, 2), (1, 3), (2, 4), (3, 5)])
        down = self.send(far, [(6, 4), (7, 5), (4, 2), (5, 3)])
        ahead = (toward(1) + up.astype(f32)).astype(bf16)
        behind = (toward(3) + down.astype(f32)).astype(bf16)
        total = (
            toward(0)
            + self.send(ahead, self.next).astype(f32)
            + self.send(behind, self.last).astype(f32)
        ).reshape(2, rows // 2, -1)
        own = lax.dynamic_index_in_dim(total, self.core, 0, False)
        others = self.other(lax.dynamic_index_in_dim(total, 1 - self.core, 0, False))
        first = self.core == 0
        out = jnp.concatenate([jnp.where(first, own, others), jnp.where(first, others, own)], axis=1)
        return out, (far,), (ahead, behind)


def add_up(array, axis):
    size = lax.axis_size(axis)
    bit = 1
    while bit < size:
        array = array + lax.ppermute(array, axis, [(i, i ^ bit) for i in range(size)])
        bit *= 2
    return array


def split_columns(core, block):
    half = block.shape[1] // 2
    low, high = block[:, :half], block[:, half:]
    return jnp.where(core == 0, low, high), jnp.where(core == 0, high, low)


def gelu(hidden):
    return 0.5 * hidden * (1.0 + jnp.tanh(gelu_root * (hidden + 0.044715 * hidden * hidden * hidden)))


def gelu_slope(hidden):
    square = hidden * hidden
    bend = jnp.tanh(gelu_root * (hidden + 0.044715 * hidden * square))
    return 0.5 * (1.0 + bend) + 0.5 * hidden * (1.0 - bend * bend) * gelu_root * (
        1.0 + 3 * 0.044715 * square
    )


def local(
    tokens,
    cotangent,
    lengths,
    dealing,
    query_weight,
    key_weight,
    value_weight,
    output_weight,
    up_weight,
    down_weight,
    query_bias,
    value_bias,
    output_bias,
    attention_gain,
    attention_shift,
    up_bias,
    down_bias,
    feedforward_gain,
    feedforward_shift,
):
    tensor, group = TensorAxis(), GroupAxis()
    groups, splits = group.size, tensor.size
    core = group.core
    slots, own_rows, model_width = cotangent.shape
    over = range(slots)
    slot_rows = own_rows * splits
    arrival_rows = tokens.shape[1]
    head_width = query_weight.shape[1]
    half = head_width // 2
    piece = query_bias.shape[0]
    count = splits

    parts = [split_columns(core, w.astype(bf16)) for w in (query_weight, key_weight, value_weight)]
    qkv_mine = jnp.concatenate([p[0] for p in parts], axis=1)
    qkv_theirs = jnp.concatenate([p[1] for p in parts], axis=1)
    qkv_weight, _, near = group.gather(qkv_mine, qkv_theirs)
    mid_weight, _, mid_near = group.gather(*split_columns(core, output_weight.astype(bf16).T), near)
    up_full, up_sent, up_near = group.gather(*split_columns(core, up_weight.astype(bf16)), mid_near)
    down_full, down_sent, _ = group.gather(*split_columns(core, down_weight.astype(bf16).T), up_near)

    slot_dealing = dealing.reshape(groups, slots)

    def arrive(slot):
        places = slot_dealing[:, slot]
        if slot > 0 and near:
            places = places + (near[0][0, 0].astype(f32) * 0.0).astype(jnp.int32)
        sent = jnp.take(tokens, places, axis=0, mode="clip")
        return lax.all_to_all(sent, "dp", split_axis=0, concat_axis=0, tiled=True).reshape(
            own_rows, model_width
        )

    arrived = [arrive(slot) for slot in over]

    head_piece = jnp.concatenate([query_bias, value_bias, up_bias]).astype(bf16)
    row_piece = jnp.concatenate(
        [output_bias, attention_gain, attention_shift, down_bias, feedforward_gain, feedforward_shift]
    ).astype(bf16)
    own_vectors = jnp.concatenate([head_piece, row_piece]).astype(f32)[None]
    table = lax.dynamic_update_slice(
        jnp.zeros((splits * groups, own_vectors.shape[1]), f32),
        own_vectors,
        (tensor.me * groups + group.me, 0),
    )
    vectors = add_up(add_up(table, "dp"), "tensor")
    head_vectors = lax.dynamic_slice_in_dim(vectors, tensor.me * groups, groups)
    query_bias_here = group.order(head_vectors[:, :piece].reshape(-1), 0)
    value_bias_here = group.order(head_vectors[:, piece : 2 * piece].reshape(-1), 0)
    hidden_bias = group.order(head_vectors[:, 2 * piece : head_piece.shape[0]].reshape(-1), 0)[None]
    row_vectors = vectors[:, head_piece.shape[0] :].reshape(-1, 6, piece)
    row_vectors = jnp.moveaxis(row_vectors, 1, 0).reshape(6, model_width)
    row_vectors = jnp.concatenate([row_vectors, jnp.zeros((2, model_width), f32)], axis=0)
    blank = jnp.zeros((half,), f32)
    qkv_bias = jnp.concatenate(
        [query_bias_here[:half], blank, value_bias_here[:half]]
        + [query_bias_here[half:], blank, value_bias_here[half:]]
    )[None]

    positions = (tensor.origins[:, None] * own_rows + jnp.arange(own_rows)[None, :]).reshape(-1)
    slot_lengths = lax.dynamic_slice_in_dim(jnp.take(lengths, dealing, axis=0), group.me * slots, slots)
    biases = [
        jnp.where(positions < slot_lengths[s], 0.0, masked_score).astype(f32)[:, None] for s in over
    ]

    rows_bf16 = [(slot_rows, bf16)]
    token_pieces = [tensor.gather((a[: own_rows // 2], a[own_rows // 2 :])) for a in arrived]
    qkv, mixed, logs, terms = [], [], [], []
    before = ()
    for s in over:
        qkv += rows_matmul(
            token_pieces[s],
            qkv_weight,
            lambda product, bias: ((product + bias).astype(bf16),),
            [qkv_bias],
            rows_bf16,
            before,
            most=256,
        )
        mix, log = attend(qkv[s], biases[s], 2)
        mixed.append(mix)
        logs.append(log)
        term = terms_matmul(mix, mid_weight, count, up_sent)
        terms.append(term)
        before = (term[0][0],)
    first = [
        first_norm(tensor.scatter(terms[s]), arrived[s], row_vectors, (terms[-1][0][0],) + tuple(down_sent))
        for s in over
    ]
    first_pieces = [tensor.gather(f[0]) for f in first]
    hidden, active, terms = [], [], []
    before = ()
    for s in over:
        wide, narrow = rows_matmul(
            first_pieces[s],
            up_full,
            lambda product, bias: (product + bias, gelu(product + bias).astype(bf16)),
            [hidden_bias],
            [(slot_rows, f32), (slot_rows, bf16)],
            before,
        )
        hidden.append(wide)
        active.append(narrow)
        term = terms_matmul(narrow, down_full, count)
        terms.append(term)
        before = (term[0][0],)
    second = [
        second_norm(tensor.scatter(terms[s]), first[s][1], cotangent[s], row_vectors, (terms[-1][0][0],))
        for s in over
    ]

    def give_back(rows):
        return lax.all_to_all(
            rows.reshape(groups, arrival_rows, model_width), "dp", split_axis=0, concat_axis=0, tiled=True
        )

    returned_rows = [give_back(s[0]) for s in second]

    down_pieces = [tensor.gather(s[2]) for s in second]
    hidden_grad, up_sums, terms = [], [], []
    before = ()

    def through_gelu(product, wide):
        grad = (product * gelu_slope(wide)).astype(bf16)
        return grad, jnp.sum(grad.astype(f32), axis=0, keepdims=True)

    for s in over:
        grad, total = rows_matmul(
            down_pieces[s],
            down_full,
            through_gelu,
            [hidden[s]],
            [(slot_rows, bf16), (1, f32)],
            before,
        )
        hidden_grad.append(grad)
        up_sums.append(total)
        term = terms_matmul(grad, up_full, count)
        terms.append(term)
        before = (term[0][0],)
    down_mine, down_theirs = weight_grad(down_pieces, active, before)
    down_sum, down_far, down_near = group.scatter(down_mine, down_theirs)
    up_mine, up_theirs = weight_grad(first_pieces, hidden_grad, (down_mine,))
    up_sum, up_far, up_near_grads = group.scatter(up_mine, up_theirs)
    first_back = [
        first_norm_back(
            tensor.scatter(terms[s]),
            second[s][1],
            first[s][1],
            first[s][2],
            row_vectors,
            (terms[-1][0][0],) if s == 0 else (up_mine,),
        )
        for s in over
    ]
    grad_pieces = [tensor.gather(f[1]) for f in first_back]

    qkv_grad, bias_sums, terms = [], [], []
    before = (up_mine,) + tuple(down_far)
    pending = [tuple(up_far), tuple(down_near)]
    for s in over:
        (mixed_grad,) = rows_matmul(
            grad_pieces[s], mid_weight, lambda product: (product.astype(bf16),), [], rows_bf16, before
        )
        held = pending[min(s, 1)]
        if s == slots - 1:
            mid_mine, mid_theirs = weight_grad(grad_pieces, mixed, (mixed_grad,))
            held = held + (mid_mine,)
        grad, sums = attend_back(qkv[s], biases[s], mixed[s], mixed_grad, logs[s], 2, held)
        qkv_grad.append(grad)
        bias_sums.append(sums)
        term = terms_matmul(grad, qkv_weight, count, tuple(up_near_grads) if s == slots - 1 else ())
        terms.append(term)
        before = (term[0][0],)
    mid_sum, _, _ = group.scatter(mid_mine, mid_theirs)
    returned_grads = [give_back(input_grad(tensor.scatter(terms[s]), first_back[s][0])) for s in over]
    qkv_sum, _, _ = group.scatter(*weight_grad(token_pieces, qkv_grad, before))

    places = slot_dealing.T.reshape(-1)
    inverse = jnp.zeros(places.shape, jnp.int32).at[places].set(
        jnp.arange(places.shape[0], dtype=jnp.int32)
    )
    result = jnp.take(jnp.concatenate(returned_rows, axis=0), inverse, axis=0, mode="clip")
    token_gradient = jnp.take(jnp.concatenate(returned_grads, axis=0), inverse, axis=0, mode="clip")

    bias_total = sum(bias_sums).reshape(2, 2, half)
    head_grads = jnp.concatenate(
        [
            group.order(bias_total[:, 0].reshape(-1), 0),
            group.order(bias_total[:, 1].reshape(-1), 0),
            group.order(sum(up_sums)[0], 0),
        ]
    )
    row_grads = jnp.concatenate(
        [sum(f[2] for f in first_back)[:3], sum(s[3] for s in second)[:3]], axis=0
    ).reshape(-1)
    row_grads = add_up(row_grads.reshape(-1, 128), "tensor")
    grads = add_up(jnp.concatenate([row_grads, head_grads.reshape(-1, 128)], axis=0), "dp").reshape(-1)
    row_shares = lax.dynamic_slice_in_dim(
        grads[: 6 * model_width].reshape(6, splits * groups, piece), tensor.me * groups + group.me, 1, axis=1
    )[:, 0]

    def share(low, width):
        return lax.dynamic_index_in_dim(grads[low : low + groups * width].reshape(groups, width), group.me, 0, False)

    base = 6 * model_width
    query_share = share(base, piece)
    value_share = share(base + head_width, piece)
    up_share = share(base + 2 * head_width, up_bias.shape[0])

    qkv_sum = qkv_sum.reshape(-1, 2, 3, half)
    return (
        result,
        token_gradient,
        qkv_sum[:, :, 0].reshape(-1, head_width),
        qkv_sum[:, :, 1].reshape(-1, head_width),
        qkv_sum[:, :, 2].reshape(-1, head_width),
        mid_sum.T,
        up_sum,
        down_sum.T,
        query_share,
        value_share,
        row_shares[0],
        row_shares[1],
        row_shares[2],
        up_share,
        row_shares[3],
        row_shares[4],
        row_shares[5],
    )


def solution(mesh):
    matrix = P("dp", "tensor")
    flipped = P("tensor", "dp")
    vector = P(("tensor", "dp"))
    arrival = P(None, ("tensor", "dp"), None)
    return jax.shard_map(
        local,
        mesh=mesh,
        in_specs=(arrival, P("dp", "tensor", None), P(), P())
        + (matrix, matrix, matrix, flipped, matrix, flipped)
        + (vector,) * 9,
        out_specs=(arrival, arrival) + (matrix, matrix, matrix, flipped, matrix, flipped) + (vector,) * 9,
        check_vma=False,
    )
```

time: 1470 us -> 1380 us (0.939)
  Pallas kernels: 46.9 us -> 412 us
  matrix products: 264 us -> 0 us
  starting transfers between devices: 184 us -> 296 us
  local copies, waits for them, and re-layouts: 158 us -> 51.2 us
  other arithmetic: 165 us -> 69 us
  blocking collectives: 43.9 us -> 0 us
  waiting for transfers between devices: 581 us -> 539 us
    pallas_call x4 -> x40, Pallas kernels: 46.9 us -> 412 us  [the longest x36 395 us: launch(): pl.pallas_call(run, grid=grid, in_specs=list(in_specs) + [pl.BlockSpec(me...]
    dot_general x24 -> x0, matrix products: 264 us -> none  [dot(): lax.dot_general(left, right, (contract, ((), ())), preferred_element_type...]
    unnamed x2 -> x0, waiting for transfers between devices: 82.4 us -> none
    ppermute x0 -> x10, waiting for transfers between devices: none -> 61.7 us  [add_up(): lax.ppermute(array, axis, [(i, i ^ bit) for i in range(size)])]
    ppermute x64 -> x96, waiting for transfers between devices: 269 us -> 212 us  [swap(): lax.ppermute(array, 'tensor', [(i, i ^ bit) for i in range(self.size)])]
    ppermute x48, starting transfers between devices: 90.8 us -> 135 us  [send(): return lax.ppermute(array, 'dp', pairs)]
    all_gather x1 -> x0, blocking collectives: 43.9 us -> none  [local(): lax.all_gather(jnp.concatenate([head_piece, row_piece]), ('tensor', 'dp')...]
    unnamed x336 -> x331, local copies, waits for them, and re-layouts: 64.6 us -> 26.4 us
  transfers between devices with their start and end apart: 119 -> 160, of which waited for: 48 -> 61; matrix products, arithmetic and copies ran while one was open for 36% -> 7% of each run, Pallas kernels for 3% -> 24%
where the time goes in v2:
time: 1380 us; the launch traced here: 1370 us
  waiting for transfers between devices  539 us (39%)
  Pallas kernels  412 us (30%)
  starting transfers between devices  296 us (21%)
  other arithmetic  69 us (5%)
  local copies, waits for them, and re-layouts  51.2 us (4%)
    pallas_call x36, Pallas kernels, launch(): pl.pallas_call(run, grid=grid, in_specs=list(in_specs) + [pl.BlockSpec(me...  395 us
    ppermute x48, waiting for transfers between devices, send(): return lax.ppermute(array, 'dp', pairs)  252 us
    ppermute x96, waiting for transfers between devices, swap(): lax.ppermute(array, 'tensor', [(i, i ^ bit) for i in range(self.size)])  212 us
    ppermute x48, starting transfers between devices, send(): return lax.ppermute(array, 'dp', pairs)  135 us
    ppermute x96, starting transfers between devices, swap(): lax.ppermute(array, 'tensor', [(i, i ^ bit) for i in range(self.size)])  70 us
    ppermute x10, waiting for transfers between devices, add_up(): lax.ppermute(array, axis, [(i, i ^ bit) for i in range(size)])  61.7 us
    all_to_all x4, starting transfers between devices, give_back(): lax.all_to_all(rows.reshape(groups, arrival_rows, model_width), 'dp', spl...  35.8 us
    all_to_all x2, starting transfers between devices, arrive(): lax.all_to_all(sent, 'dp', split_axis=0, concat_axis=0, tiled=True)  31.9 us
  transfers between devices with their start and end apart: 160, of which 61 were waited for; matrix products, arithmetic and copies ran while one was open for 7% of the time, Pallas kernels for 24%

profile of v2, /device:TPU:9, one launch (start us, length us, event | category | flops | bytes accessed | tf_op | source)
XLA Modules:
  0.0 1370.8 jit_solution(11972980920559860412)
XLA Ops:
  14.0 14.0 %collective-permute-done.7.refs_1_.refs_3_ = bf16[512,768]{1,0:T(8,128)(2,1)S(1)} collective-permute-done((bf16[512,768]{1,0:T(8,128)(2,1)}, bf16[512,768]{1,0:T(8,128)(2,1)S(1)}, u32[]{:S(2)}, u32[]{:S(2)}) %collective-permute-start.7) | collective-permute-done | bytes 786464 | tf_op jit(solution)/shard_map/ppermute | solution.py:470
  31.1 23.2 %all-to-all-start = ((bf16[8,32,2048]{2,1,0:T(8,128)(2,1)}), bf16[8,32,2048]{2,1,0:T(8,128)(2,1)S(1)}, u32[]{:S(2)}, u32[]{:S(2)}) async-start(bf16[8,32,2048]{2,1,0:T(8,128)(2,1)} %gather_fusion.1), calls=%async_computation | async-start | bytes 2097152 | tf_op jit(solution)/shard_map/all_to_all | solution.py:649
  60.4 28.2 %collective-permute-done.18.refs_1_.refs_3_ = bf16[512,256]{1,0:T(8,128)(2,1)S(1)} collective-permute-done((bf16[512,256]{1,0:T(8,128)(2,1)}, bf16[512,256]{1,0:T(8,128)(2,1)S(1)}, u32[]{:S(2)}, u32[]{:S(2)}) %collective-permute-start.18) | collective-permute-done | bytes 262176 | tf_op jit(solution)/shard_map/ppermute | solution.py:470
  88.6 24.1 %collective-permute-done.20.refs_4_ = bf16[512,256]{1,0:T(8,128)(2,1)} collective-permute-done((bf16[512,256]{1,0:T(8,128)(2,1)}, bf16[512,256]{1,0:T(8,128)(2,1)}, u32[]{:S(2)}, u32[]{:S(2)}) %collective-permute-start.20) | collective-permute-done | bytes 262176 | tf_op jit(solution)/shard_map/ppermute | solution.py:470
  141.7 21.5 %collective-permute-start.50 = (bf16[512,1024]{1,0:T(8,128)(2,1)}, bf16[512,1024]{1,0:T(8,128)(2,1)}, u32[]{:S(2)}, u32[]{:S(2)}) collective-permute-start(bf16[512,1024]{1,0:T(8,128)(2,1)} %shard_map.334.refs_9_.refs_0_), channel_id=1, source_target_pairs={{0,24},{4,28},{8,0},{12,4},{16,8},{20,12},{24,16},{28,20},{1,25},{... | collective-permute-start | bytes 3145736 | tf_op jit(solution)/shard_map/ppermute | solution.py:470
  163.3 16.3 %collective-permute-start.14 = (f32[32,768]{1,0:T(8,128)S(1)}, f32[32,768]{1,0:T(8,128)S(1)}, u32[]{:S(2)}, u32[]{:S(2)}) collective-permute-start(f32[32,768]{1,0:T(8,128)S(1)} %add.369), channel_id=1, source_target_pairs={{0,16},{4,20},{8,24},{12,28},{16,0},{20,4},{24,8},{28,12},{1,17},{... | collective-permute-start | bytes 294920 | tf_op jit(solution)/shard_map/ppermute | solution.py:578
  186.9 38.6 %collective-permute-done.14 = f32[32,768]{1,0:T(8,128)S(1)} collective-permute-done((f32[32,768]{1,0:T(8,128)S(1)}, f32[32,768]{1,0:T(8,128)S(1)}, u32[]{:S(2)}, u32[]{:S(2)}) %collective-permute-start.14) | collective-permute-done | bytes 98336 | tf_op jit(solution)/shard_map/ppermute | solution.py:578
  246.9 22.5 %collective-permute-done.19.refs_2_ = bf16[512,256]{1,0:T(8,128)(2,1)S(1)} collective-permute-done((bf16[512,256]{1,0:T(8,128)(2,1)S(1)}, bf16[512,256]{1,0:T(8,128)(2,1)S(1)}, u32[]{:S(2)}, u32[]{:S(2)}) %collective-permute-start.19) | collective-permute-done | bytes 262176 | tf_op jit(solution)/shard_map/ppermute | solution.py:470
  375.2 13.9 %shard_map.326 = (bf16[1024,512]{1,0:T(8,128)(2,1)}, f32[2,2,1024]{2,1,0:T(2,128)}) custom-call(f32[1024,1]{1,0:T(8,128)} %bitcast.136, bf16[1024,1536]{1,0:T(8,128)(2,1)} %shard_map.325.refs_1_), custom_call_target="tpu_custom_call" | custom-call | flops 8589934592 | bytes 4718592 | tf_op jit(solution)/shard_map/pallas_call | solution.py:44
  412.5 14.0 %shard_map.332 = (bf16[1024,512]{1,0:T(8,128)(2,1)}, f32[2,2,1024]{2,1,0:T(2,128)}) custom-call(f32[1024,1]{1,0:T(8,128)} %bitcast.134, bf16[1024,1536]{1,0:T(8,128)(2,1)} %shard_map.331.refs_1_), custom_call_target="tpu_custom_call" | custom-call | flops 8589934592 | bytes 4718592 | tf_op jit(solution)/shard_map/pallas_call | solution.py:44
  533.6 16.9 %shard_map.337 = (f32[1024,2048]{1,0:T(8,128)}, bf16[1024,2048]{1,0:T(8,128)(2,1)}) custom-call(bf16[128,2048]{1,0:T(8,128)(2,1)} %get-tuple-element.142.refs_0_, bf16[128,2048]{1,0:T(8,128)(2,1)} %get-tuple-element.143.refs_1_, bf16[128,2048]{1,0:T(8,128)(2,1)} %collective-permute-done.39.refs_2_, bf16[128,2048]{1,0:T(8,128)(2,1)} %copy-done.107, ...), custom_call_target="tpu_custom_call" | custom-call | flops 8589934592 | bytes 29360128 | tf_op jit(solution)/shard_map/pallas_call | solution.py:44
  550.5 14.2 %shard_map.339 = (bf16[256,1024]{1,0:T(8,128)(2,1)}, bf16[256,1024]{1,0:T(8,128)(2,1)}, bf16[256,1024]{1,0:T(8,128)(2,1)}, bf16[256,1024]{1,0:T(8,128)(2,1)}, bf...) custom-call(bf16[1024,2048]{1,0:T(8,128)(2,1)} %get-tuple-element.14, ...), custom_call_target="tpu_custom_call" | custom-call | flops 8589934592 | bytes 16777216 | tf_op jit(solution)/shard_map/pallas_call | solution.py:44
  568.5 16.7 %shard_map.341 = (f32[1024,2048]{1,0:T(8,128)}, bf16[1024,2048]{1,0:T(8,128)(2,1)}) custom-call(bf16[128,2048]{1,0:T(8,128)(2,1)} %get-tuple-element.161.refs_0_.refs_8_, bf16[128,2048]{1,0:T(8,128)(2,1)} %get-tuple-element.162.refs_1_.refs_9_, bf16[128,2048]{1,0:T(8,128)(2,1)} %copy-done.115, bf16[128,2048]{1,0:T(8,128)(2,1)} %copy-done.110, ...), custom_call_target="tpu_custom_call" | custom-call | flops 8589934592 | bytes 29360128 | tf_op jit(solution)/shard_map/pallas_call | solution.py:44
  585.2 14.6 %shard_map.342 = (bf16[256,1024]{1,0:T(8,128)(2,1)}, bf16[256,1024]{1,0:T(8,128)(2,1)}, bf16[256,1024]{1,0:T(8,128)(2,1)}, bf16[256,1024]{1,0:T(8,128)(2,1)}, bf...) custom-call(bf16[1024,2048]{1,0:T(8,128)(2,1)} %get-tuple-element.16, ...), custom_call_target="tpu_custom_call" | custom-call | flops 8589934592 | bytes 16777216 | tf_op jit(solution)/shard_map/pallas_call | solution.py:44
  611.3 16.8 %collective-permute-done.58.refs_5_ = bf16[256,1024]{1,0:T(8,128)(2,1)S(1)} collective-permute-done((bf16[256,1024]{1,0:T(8,128)(2,1)S(1)}, bf16[256,1024]{1,0:T(8,128)(2,1)S(1)}, u32[]{:S(2)}, u32[]{:S(2)}) %collective-permute-start.58) | collective-permute-done | bytes 524320 | tf_op jit(solution)/shard_map/ppermute | solution.py:433
  684.1 19.3 %shard_map.345 = (bf16[1024,2048]{1,0:T(8,128)(2,1)}, f32[1,2048]{1,0:T(1,128)}) custom-call(bf16[128,2048]{1,0:T(8,128)(2,1)} %get-tuple-element.175.refs_0_, bf16[128,2048]{1,0:T(8,128)(2,1)} %get-tuple-element.176.refs_1_, bf16[128,2048]{1,0:T(8,128)(2,1)} %copy-done.122, bf16[128,2048]{1,0:T(8,128)(2,1)} %copy-done.121, bf16[128,2048]{1,0:T(8,128)(2,1)} %copy-done.134, ...), custom_call_target="tpu_custom_call" | custom-call | flops 8589934592 | bytes 20979712 | tf_op jit(solution)/shard_map/pallas_call | solution.py:44
  703.4 14.6 %shard_map.346 = (bf16[256,1024]{1,0:T(8,128)(2,1)}, bf16[256,1024]{1,0:T(8,128)(2,1)}, bf16[256,1024]{1,0:T(8,128)(2,1)}, bf16[256,1024]{1,0:T(8,128)(2,1)}, bf...) custom-call(bf16[1024,2048]{1,0:T(8,128)(2,1)} %get-tuple-element.17, ...), custom_call_target="tpu_custom_call" | custom-call | flops 8589934592 | bytes 16777216 | tf_op jit(solution)/shard_map/pallas_call | solution.py:44
  719.3 19.3 %shard_map.347 = (bf16[1024,2048]{1,0:T(8,128)(2,1)}, f32[1,2048]{1,0:T(1,128)}) custom-call(bf16[128,2048]{1,0:T(8,128)(2,1)} %get-tuple-element.189.refs_0_.refs_8_, bf16[128,2048]{1,0:T(8,128)(2,1)} %get-tuple-element.190.refs_1_.refs_9_, bf16[128,2048]{1,0:T(8,128)(2,1)} %copy-done.138, bf16[128,2048]{1,0:T(8,128)(2,1)} %copy-done.132, ...), custom_call_target="tpu_custom_call" | custom-call | flops 8589934592 | bytes 20979712 | tf_op jit(solution)/shard_map/pallas_call | solution.py:44
  738.6 14.3 %shard_map.348 = (bf16[256,1024]{1,0:T(8,128)(2,1)}, bf16[256,1024]{1,0:T(8,128)(2,1)}, bf16[256,1024]{1,0:T(8,128)(2,1)}, bf16[256,1024]{1,0:T(8,128)(2,1)}, bf...) custom-call(bf16[1024,2048]{1,0:T(8,128)(2,1)} %get-tuple-element.19, ...), custom_call_target="tpu_custom_call" | custom-call | flops 8589934592 | bytes 16777216 | tf_op jit(solution)/shard_map/pallas_call | solution.py:44
  752.9 24.1 %shard_map.350 = (bf16[2048,1024]{1,0:T(8,128)(2,1)}, bf16[2048,1024]{1,0:T(8,128)(2,1)}) custom-call(bf16[128,2048]{1,0:T(8,128)(2,1)} %get-tuple-element.175.refs_0_, bf16[128,2048]{1,0:T(8,128)(2,1)} %get-tuple-element.176.refs_1_, bf16[128,2048]{1,0:T(8,128)(2,1)} %copy-done.122, bf16[128,2048]{1,0:T(8,128)(2,1)} %copy-done.121, ...), custom_call_target="tpu_custom_call" | custom-call | flops 17179869184 | bytes 25165824 | tf_op jit(solution)/shard_map/pallas_call | solution.py:44
  777.1 24.7 %shard_map.351 = (bf16[2048,1024]{1,0:T(8,128)(2,1)}, bf16[2048,1024]{1,0:T(8,128)(2,1)}) custom-call(bf16[128,2048]{1,0:T(8,128)(2,1)} %get-tuple-element.142.refs_0_, bf16[128,2048]{1,0:T(8,128)(2,1)} %get-tuple-element.143.refs_1_, bf16[128,2048]{1,0:T(8,128)(2,1)} %collective-permute-done.39.refs_2_, bf16[128,2048]{1,0:T(8,128)(2,1)} %copy-done.107, ...), custom_call_target="tpu_custom_call" | custom-call | flops 17179869184 | bytes 25165824 | tf_op jit(solution)/shard_map/pallas_call | solution.py:44
  801.9 22.7 %collective-permute-start.102 = (bf16[2048,1024]{1,0:T(8,128)(2,1)}, bf16[2048,1024]{1,0:T(8,128)(2,1)}, u32[]{:S(2)}, u32[]{:S(2)}) collective-permute-start(bf16[2048,1024]{1,0:T(8,128)(2,1)} %get-tuple-element.200), channel_id=1, source_target_pairs={{0,4},{4,0},{8,12},{12,8},{16,20},{20,16},{24,28},{28,24},{1,5},{5... | collective-permute-start | bytes 12582920 | tf_op jit(solution)/shard_map/ppermute | solution.py:470
  930.5 15.2 %all-to-all-start.2 = ((bf16[8,32,2048]{2,1,0:T(8,128)(2,1)}), bf16[8,32,2048]{2,1,0:T(8,128)(2,1)S(1)}, u32[]{:S(2)}, u32[]{:S(2)}) async-start(bf16[8,32,2048]{2,1,0:T(8,128)(2,1)} %bitcast.20), calls=%async_computation.2 | async-start | bytes 2097152 | tf_op jit(solution)/shard_map/all_to_all | solution.py:732
  964.4 14.4 %shard_map.353 = (bf16[1024,1536]{1,0:T(8,128)(2,1)}, f32[2,1,512]{2,1,0:T(1,128)}) custom-call(f32[1024,1]{1,0:T(8,128)} %bitcast.137, bf16[1024,1536]{1,0:T(8,128)(2,1)} %shard_map.325.refs_1_, bf16[1024,512]{1,0:T(8,128)(2,1)} %get-tuple-element.131.refs_0_.refs_2_.refs_16_, bf16[1024,512]{1,0:T(8,128)(2,1)} %shard_map.352.refs_3_, ...), custom_call_target="tpu_custom_call" | custom-call | flops 21474836480 | bytes 9437184 | tf_op jit(solution)/shard_map/pallas_call | solution.py:44
  1034.0 14.5 %shard_map.359 = (bf16[1024,1536]{1,0:T(8,128)(2,1)}, f32[2,1,512]{2,1,0:T(1,128)}) custom-call(f32[1024,1]{1,0:T(8,128)} %bitcast.135, bf16[1024,1536]{1,0:T(8,128)(2,1)} %shard_map.331.refs_1_, bf16[1024,512]{1,0:T(8,128)(2,1)} %get-tuple-element.140.refs_0_.refs_17_.refs_2_, bf16[1024,512]{1,0:T(8,128)(2,1)} %shard_map.357.refs_18_.refs_3_, ...), custom_call_target="tpu_custom_call" | custom-call | flops 21474836480 | bytes 9437184 | tf_op jit(solution)/shard_map/pallas_call | solution.py:44
  1065.8 19.1 %shard_map.362 = (bf16[2048,768]{1,0:T(8,128)(2,1)}, bf16[2048,768]{1,0:T(8,128)(2,1)}) custom-call(bf16[128,2048]{1,0:T(8,128)(2,1)} %bitcast.1.refs_0_, bf16[128,2048]{1,0:T(8,128)(2,1)} %bitcast.2.refs_1_, bf16[128,2048]{1,0:T(8,128)(2,1)} %collective-permute-done.refs_2_, bf16[128,2048]{1,0:T(8,128)(2,1)} %collective-permute-done.1.refs_3_, ...), custom_call_target="tpu_custom_call" | custom-call | flops 12884901888 | bytes 20971520 | tf_op jit(solution)/shard_map/pallas_call | solution.py:44
  1098.8 17.6 %collective-permute-done.152 = f32[120,128]{1,0:T(8,128)S(1)} collective-permute-done((f32[120,128]{1,0:T(8,128)S(1)}, f32[120,128]{1,0:T(8,128)S(1)}, u32[]{:S(2)}, u32[]{:S(2)}) %collective-permute-start.152) | collective-permute-done | bytes 61472 | tf_op jit(solution)/shard_map/ppermute | solution.py:578
  1175.6 46.6 %collective-permute-done.146 = bf16[512,1024]{1,0:T(8,128)(2,1)} collective-permute-done((bf16[512,1024]{1,0:T(8,128)(2,1)}, bf16[512,1024]{1,0:T(8,128)(2,1)}, u32[]{:S(2)}, u32[]{:S(2)}) %collective-permute-start.146) | collective-permute-done | bytes 1048608 | tf_op jit(solution)/shard_map/ppermute | solution.py:470
  1225.7 20.7 %collective-permute-done.147 = bf16[512,1024]{1,0:T(8,128)(2,1)} collective-permute-done((bf16[512,1024]{1,0:T(8,128)(2,1)S(1)}, bf16[512,1024]{1,0:T(8,128)(2,1)}, u32[]{:S(2)}, u32[]{:S(2)}) %collective-permute-start.147) | collective-permute-done | bytes 1048608 | tf_op jit(solution)/shard_map/ppermute | solution.py:470
  1271.1 12.8 collective-permute-done.132
  1283.9 17.9 %collective-permute-done.134 = bf16[512,768]{1,0:T(8,128)(2,1)S(1)} collective-permute-done((bf16[512,768]{1,0:T(8,128)(2,1)S(1)}, bf16[512,768]{1,0:T(8,128)(2,1)S(1)}, u32[]{:S(2)}, u32[]{:S(2)}) %collective-permute-start.134) | collective-permute-done | bytes 786464 | tf_op jit(solution)/shard_map/ppermute | solution.py:470
  1347.0 13.4 all-to-all-done.5
  (806 shorter events, 740.4 us)
Async XLA Ops:
  31.1 200.9 %all-to-all-start = ((bf16[8,32,2048]{2,1,0:T(8,128)(2,1)}), bf16[8,32,2048]{2,1,0:T(8,128)(2,1)S(1)}, u32[]{:S(2)}, u32[]{:S(2)}) async-start(bf16[8,32,2048]{2,1,0:T(8,128)(2,1)} %gather_fusion.1), calls=%async_computation | async-start | bytes 2097152 | tf_op jit(solution)/shard_map/all_to_all | solution.py:649
  59.8 52.9 %collective-permute-start.20 = (bf16[512,256]{1,0:T(8,128)(2,1)}, bf16[512,256]{1,0:T(8,128)(2,1)}, u32[]{:S(2)}, u32[]{:S(2)}) collective-permute-start(bf16[512,256]{1,0:T(8,128)(2,1)} %shard_map.327.refs_0_), channel_id=1, source_target_pairs={{0,24},{4,28},{8,0},{12,4},{16,8},{20,12},{24,16},{28,20},{1,25},{... | collective-permute-start | bytes 786440 | tf_op jit(solution)/shard_map/ppermute | solution.py:470
  120.7 58.9 %collective-permute-start.10 = (bf16[512,768]{1,0:T(8,128)(2,1)}, bf16[512,768]{1,0:T(8,128)(2,1)}, u32[]{:S(2)}, u32[]{:S(2)}) collective-permute-start(bf16[512,768]{1,0:T(8,128)(2,1)} %collective-permute-done.9.refs_4_), channel_id=1, source_target_pairs={{8,0},{12,4},{16,8},{20,12},{9,1},{13,5},{17,9},{21,13},{10,2},{14... | collective-permute-start | bytes 2359304 | tf_op jit(solution)/shard_map/ppermute | solution.py:470
  122.6 57.0 %collective-permute-start.8 = (bf16[512,768]{1,0:T(8,128)(2,1)}, bf16[512,768]{1,0:T(8,128)(2,1)}, u32[]{:S(2)}, u32[]{:S(2)}) collective-permute-start(bf16[512,768]{1,0:T(8,128)(2,1)} %copy-done.9), channel_id=1, source_target_pairs={{8,16},{12,20},{16,24},{20,28},{9,17},{13,21},{17,25},{21,29},{10,... | collective-permute-start | bytes 2359304 | tf_op jit(solution)/shard_map/ppermute | solution.py:470
  141.3 130.9 %collective-permute-start.48 = (bf16[512,1024]{1,0:T(8,128)(2,1)}, bf16[512,1024]{1,0:T(8,128)(2,1)}, u32[]{:S(2)}, u32[]{:S(2)}) collective-permute-start(bf16[512,1024]{1,0:T(8,128)(2,1)} %shard_map.334.refs_9_.refs_0_), channel_id=1, source_target_pairs={{0,8},{4,12},{8,16},{12,20},{16,24},{20,28},{24,0},{28,4},{1,9},{5... | collective-permute-start | bytes 3145736 | tf_op jit(solution)/shard_map/ppermute | solution.py:470
  141.7 130.9 %collective-permute-start.50 = (bf16[512,1024]{1,0:T(8,128)(2,1)}, bf16[512,1024]{1,0:T(8,128)(2,1)}, u32[]{:S(2)}, u32[]{:S(2)}) collective-permute-start(bf16[512,1024]{1,0:T(8,128)(2,1)} %shard_map.334.refs_9_.refs_0_), channel_id=1, source_target_pairs={{0,24},{4,28},{8,0},{12,4},{16,8},{20,12},{24,16},{28,20},{1,25},{... | collective-permute-start | bytes 3145736 | tf_op jit(solution)/shard_map/ppermute | solution.py:470
  163.3 62.3 %collective-permute-start.14 = (f32[32,768]{1,0:T(8,128)S(1)}, f32[32,768]{1,0:T(8,128)S(1)}, u32[]{:S(2)}, u32[]{:S(2)}) collective-permute-start(f32[32,768]{1,0:T(8,128)S(1)} %add.369), channel_id=1, source_target_pairs={{0,16},{4,20},{8,24},{12,28},{16,0},{20,4},{24,8},{28,12},{1,17},{... | collective-permute-start | bytes 294920 | tf_op jit(solution)/shard_map/ppermute | solution.py:578
  183.9 178.7 %collective-permute-start.11 = (bf16[2048,768]{1,0:T(8,128)(2,1)}, bf16[2048,768]{1,0:T(8,128)(2,1)}, u32[]{:S(2)}, u32[]{:S(2)}) collective-permute-start(bf16[2048,768]{1,0:T(8,128)(2,1)} %bitcast.121), channel_id=1, source_target_pairs={{0,4},{4,0},{8,12},{12,8},{16,20},{20,16},{24,28},{28,24},{1,5},{5... | collective-permute-start | bytes 9437192 | tf_op jit(solution)/shard_map/ppermute | solution.py:470
  232.0 76.9 %all-to-all-start.1 = ((bf16[8,32,2048]{2,1,0:T(8,128)(2,1)}), bf16[8,32,2048]{2,1,0:T(8,128)(2,1)S(1)}, u32[]{:S(2)}, u32[]{:S(2)}) async-start(bf16[8,32,2048]{2,1,0:T(8,128)(2,1)} %gather_fusion.2), calls=%async_computation.1 | async-start | bytes 2097152 | tf_op jit(solution)/shard_map/all_to_all | solution.py:649
  389.1 143.9 %collective-permute-start.47 = (bf16[2048,1024]{1,0:T(8,128)(2,1)}, bf16[2048,1024]{1,0:T(8,128)(2,1)}, u32[]{:S(2)}, u32[]{:S(2)}) collective-permute-start(bf16[2048,1024]{1,0:T(8,128)(2,1)} %bitcast.15.refs_8_.refs_1_), channel_id=1, source_target_pairs={{0,4},{4,0},{8,12},{12,8},{16,20},{20,16},{24,28},{28,24},{1,5},{5... | collective-permute-start | bytes 12582920 | tf_op jit(solution)/shard_map/ppermute | solution.py:470
  426.5 123.9 %collective-permute-start.52 = (bf16[2048,1024]{1,0:T(8,128)(2,1)}, bf16[2048,1024]{1,0:T(8,128)(2,1)}, u32[]{:S(2)}, u32[]{:S(2)}) collective-permute-start(bf16[2048,1024]{1,0:T(8,128)(2,1)} %bitcast.17.refs_1_.refs_8_), channel_id=1, source_target_pairs={{0,4},{4,0},{8,12},{12,8},{16,20},{20,16},{24,28},{28,24},{1,5},{5... | collective-permute-start | bytes 12582920 | tf_op jit(solution)/shard_map/ppermute | solution.py:470
  660.8 57.2 %collective-permute-start.89 = (bf16[128,2048]{1,0:T(8,128)(2,1)}, bf16[128,2048]{1,0:T(8,128)(2,1)S(1)}, u32[]{:S(2)}, u32[]{:S(2)}) collective-permute-start(bf16[128,2048]{1,0:T(8,128)(2,1)} %get-tuple-element.189.refs_0_.refs_8_), channel_id=1, source_target_pairs={{0,1},{1,0},{2,3},{3,2},{4,5},{5,4},{6,7},{7,6},{8,9},{9,8},{10,11... | collective-permute-start | bytes 1572872 | tf_op jit(solution)/shard_map/ppermute | solution.py:433
  801.9 127.0 %collective-permute-start.102 = (bf16[2048,1024]{1,0:T(8,128)(2,1)}, bf16[2048,1024]{1,0:T(8,128)(2,1)}, u32[]{:S(2)}, u32[]{:S(2)}) collective-permute-start(bf16[2048,1024]{1,0:T(8,128)(2,1)} %get-tuple-element.200), channel_id=1, source_target_pairs={{0,4},{4,0},{8,12},{12,8},{16,20},{20,16},{24,28},{28,24},{1,5},{5... | collective-permute-start | bytes 12582920 | tf_op jit(solution)/shard_map/ppermute | solution.py:470
  824.5 105.1 %collective-permute-start.101 = (bf16[2048,1024]{1,0:T(8,128)(2,1)}, bf16[2048,1024]{1,0:T(8,128)(2,1)}, u32[]{:S(2)}, u32[]{:S(2)}) collective-permute-start(bf16[2048,1024]{1,0:T(8,128)(2,1)} %get-tuple-element.198), channel_id=1, source_target_pairs={{0,4},{4,0},{8,12},{12,8},{16,20},{20,16},{24,28},{28,24},{1,5},{5... | collective-permute-start | bytes 12582920 | tf_op jit(solution)/shard_map/ppermute | solution.py:470
  930.5 155.4 %all-to-all-start.2 = ((bf16[8,32,2048]{2,1,0:T(8,128)(2,1)}), bf16[8,32,2048]{2,1,0:T(8,128)(2,1)S(1)}, u32[]{:S(2)}, u32[]{:S(2)}) async-start(bf16[8,32,2048]{2,1,0:T(8,128)(2,1)} %bitcast.20), calls=%async_computation.2 | async-start | bytes 2097152 | tf_op jit(solution)/shard_map/all_to_all | solution.py:732
  954.7 73.2 %collective-permute-start.121 = (bf16[512,1024]{1,0:T(8,128)(2,1)}, bf16[512,1024]{1,0:T(8,128)(2,1)S(1)}, u32[]{:S(2)}, u32[]{:S(2)}) collective-permute-start(bf16[512,1024]{1,0:T(8,128)(2,1)} %add_convert_fusion.5.refs_11_), channel_id=1, source_target_pairs={{0,8},{4,12},{8,16},{12,20},{1,9},{5,13},{9,17},{13,21},{2,10},{6,... | collective-permute-start | bytes 3145736 | tf_op jit(solution)/shard_map/ppermute | solution.py:470
  992.0 56.5 %collective-permute-start.123 = (bf16[512,1024]{1,0:T(8,128)(2,1)}, bf16[512,1024]{1,0:T(8,128)(2,1)S(1)}, u32[]{:S(2)}, u32[]{:S(2)}) collective-permute-start(bf16[512,1024]{1,0:T(8,128)(2,1)} %add_convert_fusion.4.refs_5_), channel_id=1, source_target_pairs={{0,8},{4,12},{8,16},{12,20},{1,9},{5,13},{9,17},{13,21},{2,10},{6,... | collective-permute-start | bytes 3145736 | tf_op jit(solution)/shard_map/ppermute | solution.py:470
  996.0 53.2 %collective-permute-start.124 = (bf16[512,1024]{1,0:T(8,128)(2,1)}, bf16[512,1024]{1,0:T(8,128)(2,1)}, u32[]{:S(2)}, u32[]{:S(2)}) collective-permute-start(bf16[512,1024]{1,0:T(8,128)(2,1)} %add_convert_fusion.4.refs_5_), channel_id=1, source_target_pairs={{24,16},{28,20},{16,8},{20,12},{25,17},{29,21},{17,9},{21,13},{26,... | collective-permute-start | bytes 3145736 | tf_op jit(solution)/shard_map/ppermute | solution.py:470
  1015.5 75.8 %collective-permute-start.137 = (bf16[2048,256]{1,0:T(8,128)(2,1)}, bf16[2048,256]{1,0:T(8,128)(2,1)}, u32[]{:S(2)}, u32[]{:S(2)}) collective-permute-start(bf16[2048,256]{1,0:T(8,128)(2,1)} %get-tuple-element.236), channel_id=1, source_target_pairs={{0,4},{4,0},{8,12},{12,8},{16,20},{20,16},{24,28},{28,24},{1,5},{5... | collective-permute-start | bytes 3145736 | tf_op jit(solution)/shard_map/ppermute | solution.py:470
  1027.9 68.2 %collective-permute-start.104 = (bf16[256,1024]{1,0:T(8,128)(2,1)}, bf16[256,1024]{1,0:T(8,128)(2,1)}, u32[]{:S(2)}, u32[]{:S(2)}) collective-permute-start(bf16[256,1024]{1,0:T(8,128)(2,1)} %get-tuple-element.205), channel_id=1, source_target_pairs={{0,1},{1,0},{2,3},{3,2},{4,5},{5,4},{6,7},{7,6},{8,9},{9,8},{10,11... | collective-permute-start | bytes 1572872 | tf_op jit(solution)/shard_map/ppermute | solution.py:433
  1028.4 69.9 %collective-permute-start.103 = (bf16[256,1024]{1,0:T(8,128)(2,1)}, bf16[256,1024]{1,0:T(8,128)(2,1)}, u32[]{:S(2)}, u32[]{:S(2)}) collective-permute-start(bf16[256,1024]{1,0:T(8,128)(2,1)} %get-tuple-element.203), channel_id=1, source_target_pairs={{0,1},{1,0},{2,3},{3,2},{4,5},{5,4},{6,7},{7,6},{8,9},{9,8},{10,11... | collective-permute-start | bytes 1572872 | tf_op jit(solution)/shard_map/ppermute | solution.py:433
  1048.5 84.2 %collective-permute-start.106 = (bf16[256,1024]{1,0:T(8,128)(2,1)}, bf16[256,1024]{1,0:T(8,128)(2,1)}, u32[]{:S(2)}, u32[]{:S(2)}) collective-permute-start(bf16[256,1024]{1,0:T(8,128)(2,1)} %get-tuple-element.207), channel_id=1, source_target_pairs={{0,2},{1,3},{2,0},{3,1},{4,6},{5,7},{6,4},{7,5},{8,10},{9,11},{10,... | collective-permute-start | bytes 1572872 | tf_op jit(solution)/shard_map/ppermute | solution.py:433
  1085.0 138.5 %collective-permute-start.131 = (bf16[2048,768]{1,0:T(8,128)(2,1)}, bf16[2048,768]{1,0:T(8,128)(2,1)}, u32[]{:S(2)}, u32[]{:S(2)}) collective-permute-start(bf16[2048,768]{1,0:T(8,128)(2,1)} %get-tuple-element.235), channel_id=1, source_target_pairs={{0,4},{4,0},{8,12},{12,8},{16,20},{20,16},{24,28},{28,24},{1,5},{5... | collective-permute-start | bytes 9437192 | tf_op jit(solution)/shard_map/ppermute | solution.py:470
  1085.9 51.1 %all-to-all-start.3 = ((bf16[8,32,2048]{2,1,0:T(8,128)(2,1)}), bf16[8,32,2048]{2,1,0:T(8,128)(2,1)}, u32[]{:S(2)}, u32[]{:S(2)}) async-start(bf16[8,32,2048]{2,1,0:T(8,128)(2,1)} %bitcast.22), calls=%async_computation.3 | async-start | bytes 2097152 | tf_op jit(solution)/shard_map/all_to_all | solution.py:732
  1144.8 161.5 %all-to-all-start.4 = ((bf16[8,32,2048]{2,1,0:T(8,128)(2,1)}), bf16[8,32,2048]{2,1,0:T(8,128)(2,1)S(1)}, u32[]{:S(2)}, u32[]{:S(2)}) async-start(bf16[8,32,2048]{2,1,0:T(8,128)(2,1)} %bitcast.119), calls=%async_computation.4 | async-start | bytes 2097152 | tf_op jit(solution)/shard_map/all_to_all | solution.py:732
  1154.2 68.0 %collective-permute-start.146 = (bf16[512,1024]{1,0:T(8,128)(2,1)}, bf16[512,1024]{1,0:T(8,128)(2,1)}, u32[]{:S(2)}, u32[]{:S(2)}) collective-permute-start(bf16[512,1024]{1,0:T(8,128)(2,1)} %get-tuple-element.284.refs_5_), channel_id=1, source_target_pairs={{0,8},{4,12},{8,16},{12,20},{16,24},{20,28},{24,0},{28,4},{1,9},{5... | collective-permute-start | bytes 3145736 | tf_op jit(solution)/shard_map/ppermute | solution.py:470
  1157.7 88.6 %collective-permute-start.147 = (bf16[512,1024]{1,0:T(8,128)(2,1)S(1)}, bf16[512,1024]{1,0:T(8,128)(2,1)}, u32[]{:S(2)}, u32[]{:S(2)}) collective-permute-start(bf16[512,1024]{1,0:T(8,128)(2,1)S(1)} %copy-done.17), channel_id=1, source_target_pairs={{0,24},{4,28},{8,0},{12,4},{16,8},{20,12},{24,16},{28,20},{1,25},{... | collective-permute-start | bytes 3145736 | tf_op jit(solution)/shard_map/ppermute | solution.py:470
  1172.3 76.0 %collective-permute-start.130 = (bf16[256,1024]{1,0:T(8,128)(2,1)}, bf16[256,1024]{1,0:T(8,128)(2,1)}, u32[]{:S(2)}, u32[]{:S(2)}) collective-permute-start(bf16[256,1024]{1,0:T(8,128)(2,1)} %add_convert_fusion.9), channel_id=1, source_target_pairs={{0,1},{1,0},{2,3},{3,2},{4,5},{5,4},{6,7},{7,6},{8,9},{9,8},{10,11... | collective-permute-start | bytes 1572872 | tf_op jit(solution)/shard_map/ppermute | solution.py:433
  1174.4 92.7 %collective-permute-start.143 = (bf16[512,1024]{1,0:T(8,128)(2,1)}, bf16[512,1024]{1,0:T(8,128)(2,1)S(1)}, u32[]{:S(2)}, u32[]{:S(2)}) collective-permute-start(bf16[512,1024]{1,0:T(8,128)(2,1)} %get-tuple-element.282.refs_3_), channel_id=1, source_target_pairs={{0,8},{4,12},{8,16},{12,20},{16,24},{20,28},{24,0},{28,4},{1,9},{5... | collective-permute-start | bytes 3145736 | tf_op jit(solution)/shard_map/ppermute | solution.py:470
  1248.3 53.4 %collective-permute-start.134 = (bf16[512,768]{1,0:T(8,128)(2,1)S(1)}, bf16[512,768]{1,0:T(8,128)(2,1)S(1)}, u32[]{:S(2)}, u32[]{:S(2)}) collective-permute-start(bf16[512,768]{1,0:T(8,128)(2,1)S(1)} %add_convert_fusion.8), channel_id=1, source_target_pairs={{24,16},{28,20},{16,8},{20,12},{25,17},{29,21},{17,9},{21,13},{26,... | collective-permute-start | bytes 2359304 | tf_op jit(solution)/shard_map/ppermute | solution.py:470
  1253.8 63.0 %collective-permute-start.148 = (f32[256,1024]{1,0:T(8,128)}, f32[256,1024]{1,0:T(8,128)}, u32[]{:S(2)}, u32[]{:S(2)}) collective-permute-start(f32[256,1024]{1,0:T(8,128)} %dynamic-slice_bitcast_fusion), channel_id=1, source_target_pairs={{0,4},{4,0},{8,12},{12,8},{16,20},{20,16},{24,28},{28,24},{1,5},{5... | collective-permute-start | bytes 3145736 | tf_op jit(solution)/shard_map/ppermute | solution.py:470
  1306.4 53.9 %all-to-all-start.5 = ((bf16[8,32,2048]{2,1,0:T(8,128)(2,1)}), bf16[8,32,2048]{2,1,0:T(8,128)(2,1)}, u32[]{:S(2)}, u32[]{:S(2)}) async-start(bf16[8,32,2048]{2,1,0:T(8,128)(2,1)} %bitcast.120), calls=%async_computation.5 | async-start | bytes 2097152 | tf_op jit(solution)/shard_map/all_to_all | solution.py:732
  (282 other events, 5944.2 us)

commit v3 on v2

v3 whole, which is shorter than its diff:
```python
import functools
import math

import jax
import jax.numpy as jnp
from jax import lax
from jax.experimental import pallas as pl
from jax.experimental.pallas import tpu as pltpu
from jax.sharding import PartitionSpec as P

HEAD = 128
norm_epsilon = 1e-05
masked_score = -1e30
log2_e = math.log2(math.e)
head_scale = 1.0 / math.sqrt(HEAD)
gelu_root = math.sqrt(2.0 / math.pi)
bf16 = jnp.bfloat16
f32 = jnp.float32
MIB = 1024 * 1024
TALL = ((1,), (0,))
FLAT = ((1,), (1,))
DEEP = ((0,), (0,))


def dot(left, right, contract):
    return lax.dot_general(left, right, (contract, ((), ())), preferred_element_type=f32)


def shape(dims, dtype):
    return jax.ShapeDtypeStruct(tuple(dims), dtype)


def whole(array):
    return pl.BlockSpec(array.shape, lambda *i: (0,) * array.ndim)


def launch(body, grid, ins, in_specs, outs, out_specs, later=(), scratch=(), flops=0, nbytes=0, exps=0):
    later = tuple(later)
    count, skip = len(ins), len(later)

    def run(*refs):
        body(refs[:count], refs[count + skip :])

    return pl.pallas_call(
        run,
        grid=grid,
        in_specs=list(in_specs) + [pl.BlockSpec(memory_space=pl.ANY)] * skip,
        out_specs=list(out_specs),
        out_shape=list(outs),
        scratch_shapes=list(scratch),
        compiler_params=pltpu.CompilerParams(vmem_limit_bytes=60 * MIB),
        cost_estimate=pl.CostEstimate(flops=int(flops), bytes_accessed=int(nbytes), transcendentals=int(exps)),
    )(*ins, *later)


def attend(qkv, bias, halves, later=()):
    rows, columns = qkv.shape
    group = columns // halves
    heads = group // (3 * HEAD)
    width = heads * HEAD
    block = min(256, rows)

    def body(ins, outs):
        bias_ref, qkv_ref = ins
        mixed_ref, log_ref = outs
        shift = bias_ref[...]
        for head in range(heads):
            low = head * HEAD
            keys = qkv_ref[:, width + low : width + low + HEAD]
            values = qkv_ref[:, 2 * width + low : 2 * width + low + HEAD]
            for first in range(0, rows, block):
                part = slice(first, first + block)
                queries = qkv_ref[part, low : low + HEAD]
                scores = dot(keys, queries, FLAT) * (head_scale * log2_e) + shift
                peak = jnp.max(scores, axis=0, keepdims=True)
                weight = jnp.exp2(scores - peak)
                total = jnp.sum(weight, axis=0, keepdims=True)
                mixed = dot(values, weight.astype(bf16), DEEP) * (1.0 / total)
                mixed_ref[part, low : low + HEAD] = mixed.T.astype(bf16)
                log_ref[0, head : head + 1, part] = peak + jnp.log2(total)

    return launch(
        body,
        (halves,),
        [bias, qkv],
        [pl.BlockSpec((rows, 1), lambda i: (0, 0)), pl.BlockSpec((rows, group), lambda i: (0, i))],
        [shape((rows, halves * width), bf16), shape((halves, heads, rows), f32)],
        [pl.BlockSpec((rows, width), lambda i: (0, i)), pl.BlockSpec((1, heads, rows), lambda i: (i, 0, 0))],
        later,
        flops=4 * halves * heads * rows * rows * HEAD * 4,
        nbytes=rows * columns * 3,
        exps=halves * heads * rows * rows,
    )


def attend_back(qkv, bias, mixed, grads, logs, halves, later=()):
    rows, columns = qkv.shape
    group = columns // halves
    heads = group // (3 * HEAD)
    width = heads * HEAD
    block = min(256, rows)

    def body(ins, outs):
        bias_ref, qkv_ref, mixed_ref, grad_ref, log_ref = ins
        out_ref, sum_ref = outs
        shift = bias_ref[...]
        for head in range(heads):
            low = head * HEAD
            keys = qkv_ref[:, width + low : width + low + HEAD]
            values = qkv_ref[:, 2 * width + low : 2 * width + low + HEAD]
            key_total = jnp.zeros((rows, HEAD), f32)
            value_total = jnp.zeros((rows, HEAD), f32)
            query_sum = jnp.zeros((1, HEAD), f32)
            for first in range(0, rows, block):
                part = slice(first, first + block)
                queries = qkv_ref[part, low : low + HEAD]
                grad = grad_ref[part, low : low + HEAD]
                mix = mixed_ref[part, low : low + HEAD]
                centre = jnp.sum((grad.astype(f32) * mix.astype(f32)).T, axis=0, keepdims=True)
                scores = dot(keys, queries, FLAT) * (head_scale * log2_e) + shift
                weight = jnp.exp2(scores - log_ref[0, head : head + 1, part])
                weight_grad = dot(values, grad, FLAT)
                score_grad = (weight * (weight_grad - centre)).astype(bf16)
                value_total = value_total + dot(weight.astype(bf16), grad, TALL)
                key_total = key_total + dot(score_grad, queries, TALL)
                query_grad = (dot(keys, score_grad, DEEP) * head_scale).T.astype(bf16)
                out_ref[part, low : low + HEAD] = query_grad
                query_sum = query_sum + jnp.sum(query_grad.astype(f32), axis=0, keepdims=True)
            value_total = value_total.astype(bf16)
            out_ref[:, width + low : width + low + HEAD] = (key_total * head_scale).astype(bf16)
            out_ref[:, 2 * width + low : 2 * width + low + HEAD] = value_total
            sum_ref[0, :, low : low + HEAD] = query_sum
            sum_ref[0, :, width + low : width + low + HEAD] = jnp.sum(
                value_total.astype(f32), axis=0, keepdims=True
            )

    columns_of = lambda n: pl.BlockSpec((rows, n), lambda i: (0, i))
    return launch(
        body,
        (halves,),
        [bias, qkv, mixed, grads, logs],
        [
            pl.BlockSpec((rows, 1), lambda i: (0, 0)),
            columns_of(group),
            columns_of(width),
            columns_of(width),
            pl.BlockSpec((1, heads, rows), lambda i: (i, 0, 0)),
        ],
        [shape((rows, columns), bf16), shape((halves, 1, 2 * width), f32)],
        [columns_of(group), pl.BlockSpec((1, 1, 2 * width), lambda i: (i, 0, 0))],
        later,
        flops=10 * halves * heads * rows * rows * HEAD * 4,
        nbytes=rows * columns * 6,
        exps=halves * heads * rows * rows,
    )


def tile_of(width, most):
    tile = min(width, most)
    while width % tile:
        tile //= 2
    return tile


def rows_matmul(pieces, weight, width, finish, extras, kinds, later=(), most=512):
    rows = sum(p.shape[0] for p in pieces)
    inner = weight.shape[0]
    tile = tile_of(width, most)

    def body(ins, refs):
        piece_refs, weight_ref = ins[: len(pieces)], ins[len(pieces)]
        extra_refs = ins[len(pieces) + 1 :]
        out_refs, gathered = refs[: len(kinds)], refs[len(kinds)]

        @pl.when(pl.program_id(0) == 0)
        def _():
            first = 0
            for ref in piece_refs:
                gathered[first : first + ref.shape[0], :] = ref[...]
                first += ref.shape[0]

        product = dot(gathered[...], weight_ref[...], TALL)
        for ref, value in zip(out_refs, finish(product, *[r[...] for r in extra_refs])):
            ref[...] = value

    def along(n):
        return pl.BlockSpec((n, tile), lambda j: (0, j))

    return launch(
        body,
        (width // tile,),
        [*pieces, weight, *extras],
        [whole(p) for p in pieces] + [along(inner)] + [along(e.shape[0]) for e in extras],
        [shape((n, width), dtype) for n, dtype in kinds],
        [along(n) for n, _ in kinds],
        later,
        scratch=[pltpu.VMEM((rows, inner), bf16)],
        flops=2 * rows * inner * width,
        nbytes=2 * (rows * inner + inner * width) + sum(4 * n * width for n, _ in kinds),
    )


def terms_matmul(left, weight, spans, later=(), most=512):
    rows, inner = left.shape
    outer = weight.shape[0]
    tile = tile_of(outer // 2, most)
    steps = outer // 2 // tile

    def body(ins, outs):
        left_ref, weight_ref = ins
        step = pl.program_id(0)
        product = dot(left_ref[...], weight_ref[...], FLAT).astype(bf16)
        groups = outs[: len(spans[0])], outs[len(spans[0]) :]
        for side in range(2):

            @pl.when((step < steps) if side == 0 else (step >= steps))
            def _():
                for ref, (low, high) in zip(groups[side], spans[side]):
                    ref[...] = product[low:high]

    places = [
        lambda j: (0, jnp.minimum(j, steps - 1)),
        lambda j: (0, jnp.maximum(j - steps, 0)),
    ]
    sizes = [(side, high - low) for side in range(2) for low, high in spans[side]]
    outs = launch(
        body,
        (2 * steps,),
        [left, weight],
        [whole(left), pl.BlockSpec((tile, inner), lambda j: (j, 0))],
        [shape((n, outer // 2), bf16) for _, n in sizes],
        [pl.BlockSpec((n, tile), places[side]) for side, n in sizes],
        later,
        flops=2 * rows * inner * outer,
        nbytes=2 * (rows * inner + outer * inner + rows * outer),
    )
    return outs[: len(spans[0])], outs[len(spans[0]) :]


def weight_grad(lefts, rights, later=(), core=None, most=256):
    flat = [p for pieces in lefts for p in pieces]
    outer = flat[0].shape[1]
    rows, columns = rights[0].shape
    tile = tile_of(outer, most)
    slots = len(rights)
    scalars = [] if core is None else [core.reshape(1)]

    def body(ins, refs):
        ins = ins[len(scalars) :] if core is None else ins[1:]
        piece_refs, right_refs = ins[: len(flat)], ins[len(flat) :]
        gathered = refs[-1]
        first = 0
        for ref in piece_refs:
            gathered[first : first + ref.shape[0], :] = ref[...]
            first += ref.shape[0]
        total = None
        for slot in range(slots):
            term = dot(gathered[slot * rows : (slot + 1) * rows, :], right_refs[slot][...], DEEP)
            total = term if total is None else total + term
        refs[0][...] = total.astype(bf16)

    def body_apart(ins, refs):
        parity = lax.rem(pl.program_id(0), 2)
        total_ref = refs[2]
        body(ins, (total_ref, refs[3]))

        @pl.when(parity == ins[0][0])
        def _():
            refs[0][...] = total_ref[...]

        @pl.when(parity != ins[0][0])
        def _():
            refs[1][...] = total_ref[...]

    outs = [shape((outer, columns), bf16)] if core is None else [shape((outer // 2, columns), bf16)] * 2
    where = (lambda j: (j, 0)) if core is None else (lambda j: (j // 2, 0))
    result = launch(
        body if core is None else body_apart,
        (outer // tile,),
        [*scalars, *flat, *rights],
        [pl.BlockSpec(memory_space=pltpu.SMEM)] * len(scalars)
        + [pl.BlockSpec((p.shape[0], tile), lambda j: (0, j)) for p in flat]
        + [whole(r) for r in rights],
        outs,
        [pl.BlockSpec((tile, columns), where)] * len(outs),
        later,
        scratch=([] if core is None else [pltpu.VMEM((tile, columns), bf16)])
        + [pltpu.VMEM((slots * rows, tile), bf16)],
        flops=2 * slots * rows * outer * columns,
        nbytes=2 * (slots * rows * (outer + columns) + outer * columns),
    )
    return result[0] if core is None else result


def norm_tiles(body, rows, width, left, right, tiled, vectors, outs, sums, later):
    steps = 4
    tile = rows // steps
    n_left, n_right, n_tiled = len(left), len(right), len(tiled)

    def run(ins, refs):
        step = pl.program_id(0)
        left_refs = ins[:n_left]
        right_refs = ins[n_left : n_left + n_right]
        tiled_refs = ins[n_left + n_right : n_left + n_right + n_tiled]
        vector_ref = ins[-1] if vectors is not None else None

        def added(group):
            total = group[0][...].astype(f32)
            for ref in group[1:]:
                total = total + ref[...].astype(f32)
            return total

        both = jnp.concatenate([added(left_refs), added(right_refs)], axis=1)
        values, totals = body(both, [r[...] for r in tiled_refs], vector_ref)
        for ref, value in zip(refs, values):
            ref[...] = value.astype(ref.dtype)
        if sums:
            sum_ref = refs[-1]

            @pl.when(step == 0)
            def _():
                sum_ref[...] = jnp.zeros_like(sum_ref)

            for i, value in enumerate(totals):
                sum_ref[i : i + 1, :] += jnp.sum(value, axis=0, keepdims=True)

    def of(columns):
        return pl.BlockSpec((tile, columns), lambda i: (i, 0))

    ins = [*left, *right, *tiled] + ([vectors] if vectors is not None else [])
    return launch(
        run,
        (steps,),
        ins,
        [of(a.shape[1]) for a in (*left, *right, *tiled)] + ([whole(vectors)] if vectors is not None else []),
        [shape((rows, c), dtype) for c, dtype in outs]
        + ([shape((8, width), f32)] if sums else []),
        [of(c) for c, _ in outs]
        + ([pl.BlockSpec((8, width), lambda i: (0, 0))] if sums else []),
        later,
        flops=rows * width * 20,
        nbytes=rows * width * 16,
    )


def normed(values):
    centred = values - jnp.mean(values, axis=-1, keepdims=True)
    inverse = lax.rsqrt(jnp.mean(centred * centred, axis=-1, keepdims=True) + norm_epsilon)
    return centred * inverse, inverse


def norm_back(grads, unit, inverse, gain):
    scaled = grads * gain
    return inverse * (
        scaled
        - jnp.mean(scaled, axis=-1, keepdims=True)
        - unit * jnp.mean(scaled * unit, axis=-1, keepdims=True)
    )


def first_norm(terms, rows, vectors, later=()):
    def body(both, tiled, v):
        unit, inverse = normed(tiled[0].astype(f32) + (both + v[0:1, :]))
        return [unit * v[1:2, :] + v[2:3, :], unit, inverse], []

    n, width = rows.shape
    kinds = [(width, bf16), (width, f32), (1, f32)]
    return norm_tiles(body, n, width, *terms, [rows], vectors, kinds, False, later)


def second_norm(terms, unit, cotangent, vectors, later=()):
    def body(both, tiled, v):
        first, grads = tiled[0] * v[1:2, :] + v[2:3, :], tiled[1].astype(f32)
        unit_two, inverse = normed(first + (both + v[3:4, :]))
        back = norm_back(grads, unit_two, inverse, v[4:5, :])
        return [unit_two * v[4:5, :] + v[5:6, :], back, back], [back, grads * unit_two, grads]

    n, width = unit.shape
    kinds = [(width, bf16), (width, f32), (width, bf16)]
    return norm_tiles(body, n, width, *terms, [unit, cotangent], vectors, kinds, True, later)


def first_norm_back(terms, back_two, unit, inverse, vectors, later=()):
    def body(both, tiled, v):
        grads = tiled[0] + both
        back = norm_back(grads, tiled[1], tiled[2], v[1:2, :])
        return [back, back], [back, grads * tiled[1], grads]

    n, width = unit.shape
    kinds = [(width, f32), (width, bf16)]
    return norm_tiles(body, n, width, *terms, [back_two, unit, inverse], vectors, kinds, True, later)


def input_grad(terms, back, later=()):
    def body(both, tiled, v):
        return [tiled[0] + both], []

    n, width = back.shape
    return norm_tiles(body, n, width, *terms, [back], None, [(width, bf16)], False, later)[0]


class TensorAxis:
    def __init__(self):
        self.size = lax.axis_size("tensor")
        self.me = lax.axis_index("tensor")
        self.square = self.size == 4
        if self.square:
            self.origins = self.me ^ jnp.array([0, 1, 3, 2], jnp.int32)
        else:
            self.origins = jnp.arange(self.size, dtype=jnp.int32)

    def swap(self, array, bit):
        return lax.ppermute(array, "tensor", [(i, i ^ bit) for i in range(self.size)])

    def gather(self, block):
        if not self.square:
            return [lax.all_gather(block, "tensor", axis=0, tiled=True)]
        half = block.shape[0] // 2
        along_x, along_y = self.swap(block, 1), self.swap(block, 2)
        far_top, far_bottom = self.swap(along_y[:half], 1), self.swap(along_x[half:], 2)
        return [block, along_x, far_top, far_bottom, along_y]

    def spans(self, rows):
        if not self.square:
            return [(0, rows)], [(0, rows)]
        r = rows // 4
        return [(r, 3 * r), (3 * r, 4 * r), (0, r)], [(2 * r, 4 * r), (r, 2 * r), (0, r)]

    def line_up(self, block):
        if not self.square:
            return lax.all_gather(block, "tensor", axis=1, tiled=True)
        width = block.shape[1]
        full = jnp.zeros((block.shape[0], 4 * width), block.dtype)
        for bits in range(4):
            piece = self.swap(block, bits) if bits else block
            full = lax.dynamic_update_slice(full, piece, (0, (self.me ^ bits) * width))
        return full

    def scatter(self, terms):
        left, right = terms
        if not self.square:
            full = jnp.concatenate([left[0], right[0]], axis=1)
            mine = lax.psum_scatter(full, "tensor", scatter_dimension=0, tiled=True)
            half = mine.shape[1] // 2
            return ([mine[:, :half]], [mine[:, half:]]), ()
        rows = left[1].shape[0]
        from_x, from_y = self.swap(left[0], 1), self.swap(right[0], 2)
        left_far = self.swap((left[1].astype(f32) + from_x[rows:].astype(f32)).astype(bf16), 2)
        right_far = self.swap((right[1].astype(f32) + from_y[:rows].astype(f32)).astype(bf16), 1)
        return ([left[2], from_x, left_far], [right[2], from_y[rows:], right_far]), (from_x, from_y)


class GroupAxis:
    def __init__(self):
        self.size = lax.axis_size("dp")
        self.me = lax.axis_index("dp")
        self.line = self.size == 8
        self.z = self.me // 2
        n = self.size
        self.next = [(i, (i + 2) % n) for i in range(n)]
        self.last = [(i, (i - 2) % n) for i in range(n)]

    def send(self, array, pairs):
        return lax.ppermute(array, "dp", pairs)

    def gather(self, shard):
        return lax.all_gather(shard, "dp", axis=0, tiled=True)

    def scatter(self, terms):
        return lax.psum_scatter(terms, "dp", scatter_dimension=0, tiled=True).astype(f32)

    def weight_scatter(self, lefts, rights, later):
        if not self.line:
            terms = weight_grad(lefts, rights, later)
            return self.scatter(terms), terms, (), (), ()
        mine, theirs = weight_grad(lefts, rights, later, self.me % 2, lefts[0][0].shape[1] // self.size)
        got = self.send(theirs, [(i, i ^ 1) for i in range(self.size)])
        rows = mine.shape[0] // 4

        def toward(step):
            first = ((self.z + step) % 4) * rows
            parts = [lax.dynamic_slice_in_dim(a, first, rows).astype(f32) for a in (mine, got)]
            return parts[0] + parts[1]

        far = toward(2).astype(bf16)
        up = self.send(far, [(0, 2), (1, 3), (2, 4), (3, 5)])
        down = self.send(far, [(6, 4), (7, 5), (4, 2), (5, 3)])
        ahead = (toward(1) + up.astype(f32)).astype(bf16)
        behind = (toward(3) + down.astype(f32)).astype(bf16)
        ahead, behind = self.send(ahead, self.next), self.send(behind, self.last)
        total = toward(0) + ahead.astype(f32) + behind.astype(f32)
        return total, mine, (got,), (up, down), (ahead, behind)


def add_up(array, axis):
    size = lax.axis_size(axis)
    bit = 1
    while bit < size:
        array = array + lax.ppermute(array, axis, [(i, i ^ bit) for i in range(size)])
        bit *= 2
    return array


def gelu(hidden):
    return 0.5 * hidden * (1.0 + jnp.tanh(gelu_root * (hidden + 0.044715 * hidden * hidden * hidden)))


def gelu_slope(hidden):
    square = hidden * hidden
    bend = jnp.tanh(gelu_root * (hidden + 0.044715 * hidden * square))
    return 0.5 * (1.0 + bend) + 0.5 * hidden * (1.0 - bend * bend) * gelu_root * (
        1.0 + 3 * 0.044715 * square
    )


def local(
    tokens,
    cotangent,
    lengths,
    dealing,
    query_weight,
    key_weight,
    value_weight,
    output_weight,
    up_weight,
    down_weight,
    query_bias,
    value_bias,
    output_bias,
    attention_gain,
    attention_shift,
    up_bias,
    down_bias,
    feedforward_gain,
    feedforward_shift,
):
    tensor, group = TensorAxis(), GroupAxis()
    groups, splits = group.size, tensor.size
    slots, own_rows, model_width = cotangent.shape
    over = range(slots)
    slot_rows = own_rows * splits
    arrival_rows = tokens.shape[1]
    head_width = query_weight.shape[1]
    half = head_width // 2
    piece = query_bias.shape[0]
    hidden_width = up_weight.shape[1]
    spans = tensor.spans(slot_rows)

    slot_dealing = dealing.reshape(groups, slots)
    sent = jnp.take(tokens, dealing, axis=0, mode="clip").reshape(groups, slots, arrival_rows, model_width)
    came = lax.all_to_all(sent, "dp", split_axis=0, concat_axis=0, tiled=True)
    arrived = [came[:, s].reshape(own_rows, model_width) for s in over]

    head_piece = jnp.concatenate([query_bias, value_bias, up_bias]).astype(bf16)
    row_piece = jnp.concatenate(
        [output_bias, attention_gain, attention_shift, down_bias, feedforward_gain, feedforward_shift]
    ).astype(bf16)
    vector = jnp.concatenate([head_piece, row_piece])
    shard_rows, spare = query_weight.shape[0], 128
    padded = jnp.zeros((shard_rows * spare,), bf16).at[: vector.shape[0]].set(vector)
    three = [w.astype(bf16) for w in (query_weight, key_weight, value_weight)]
    qkv_weight = group.gather(
        jnp.concatenate(
            [w[:, :half] for w in three] + [w[:, half:] for w in three] + [padded.reshape(shard_rows, spare)],
            axis=1,
        )
    )
    mid_weight = group.gather(output_weight.astype(bf16).T)
    up_full = group.gather(up_weight.astype(bf16))
    down_full = group.gather(down_weight.astype(bf16).T)
    used = -(-vector.shape[0] // spare)
    table = qkv_weight[:, 3 * head_width :].reshape(groups, shard_rows, spare)[:, :used]
    table = table.reshape(groups, -1)[:, : vector.shape[0]]
    head_vectors = table.astype(f32)
    row_table = table[:, head_piece.shape[0] :].reshape(groups, 6, piece)
    row_table = jnp.moveaxis(row_table, 1, 0).reshape(6, groups * piece)
    row_vectors = tensor.line_up(row_table).astype(f32)
    query_bias_here = head_vectors[:, :piece].reshape(-1)
    value_bias_here = head_vectors[:, piece : 2 * piece].reshape(-1)
    hidden_bias = head_vectors[:, 2 * piece : head_piece.shape[0]].reshape(1, -1)
    row_vectors = jnp.concatenate([row_vectors, jnp.zeros((2, model_width), f32)], axis=0)
    blank = jnp.zeros((half,), f32)
    qkv_bias = jnp.concatenate(
        [query_bias_here[:half], blank, value_bias_here[:half]]
        + [query_bias_here[half:], blank, value_bias_here[half:]]
    )[None]

    positions = (tensor.origins[:, None] * own_rows + jnp.arange(own_rows)[None, :]).reshape(-1)
    slot_lengths = lax.dynamic_slice_in_dim(jnp.take(lengths, dealing, axis=0), group.me * slots, slots)
    biases = [
        jnp.where(positions < slot_lengths[s], 0.0, masked_score).astype(f32)[:, None] for s in over
    ]

    rows_bf16 = [(slot_rows, bf16)]
    token_pieces = [tensor.gather(a) for a in arrived]
    qkv, mixed, logs, terms = [], [], [], []
    before = ()
    for s in over:
        qkv += rows_matmul(
            token_pieces[s],
            qkv_weight,
            3 * head_width,
            lambda product, bias: ((product + bias).astype(bf16),),
            [qkv_bias],
            rows_bf16,
            before,
            most=256,
        )
        mix, log = attend(qkv[s], biases[s], 2)
        mixed.append(mix)
        logs.append(log)
        terms.append(terms_matmul(mix, mid_weight, spans))
        before = (terms[s][0][0],)
    first = [first_norm(tensor.scatter(terms[s])[0], arrived[s], row_vectors, before) for s in over]
    first_pieces = [tensor.gather(f[0]) for f in first]
    hidden, active, terms = [], [], []
    before = ()
    for s in over:
        wide, narrow = rows_matmul(
            first_pieces[s],
            up_full,
            hidden_width,
            lambda product, bias: (product + bias, gelu(product + bias).astype(bf16)),
            [hidden_bias],
            [(slot_rows, f32), (slot_rows, bf16)],
            before,
        )
        hidden.append(wide)
        active.append(narrow)
        terms.append(terms_matmul(narrow, down_full, spans))
        before = (terms[s][0][0],)
    second = [
        second_norm(tensor.scatter(terms[s])[0], first[s][1], cotangent[s], row_vectors, before) for s in over
    ]

    def give_back(rows):
        return lax.all_to_all(
            rows.reshape(groups, arrival_rows, model_width), "dp", split_axis=0, concat_axis=0, tiled=True
        )

    returned_rows = [give_back(s[0]) for s in second]

    down_pieces = [tensor.gather(s[2]) for s in second]
    hidden_grad, up_sums, terms = [], [], []
    before = ()

    def through_gelu(product, wide):
        grad = (product * gelu_slope(wide)).astype(bf16)
        return grad, jnp.sum(grad.astype(f32), axis=0, keepdims=True)

    for s in over:
        grad, total = rows_matmul(
            down_pieces[s],
            down_full,
            hidden_width,
            through_gelu,
            [hidden[s]],
            [(slot_rows, bf16), (1, f32)],
            before if s == 0 else before + (returned_rows[0],),
        )
        hidden_grad.append(grad)
        up_sums.append(total)
        terms.append(terms_matmul(grad, up_full, spans))
        before = (terms[s][0][0],)
    first_back = []

    first_sums = [tensor.scatter(t) for t in terms]

    def back_to_first(s, later):
        first_back.append(
            first_norm_back(
                first_sums[s][0], second[s][1], first[s][1], first[s][2], row_vectors, later
            )
        )
        return tensor.gather(first_back[s][1])

    grad_pieces = [back_to_first(0, before)]
    down_terms = weight_grad(down_pieces, active, (first_back[0][0], *returned_rows))
    down_sum = group.scatter(down_terms)
    up_terms = weight_grad(
        first_pieces, hidden_grad, (down_terms, *first_sums[-1][1], *grad_pieces[0][1:2], *grad_pieces[0][4:])
    )
    up_sum = group.scatter(up_terms)
    grad_pieces += [back_to_first(s, (up_terms,)) for s in over[1:]]

    def attention_in(s, later):
        return rows_matmul(
            grad_pieces[s],
            mid_weight,
            head_width,
            lambda product: (product.astype(bf16),),
            [],
            rows_bf16,
            later,
        )[0]

    def attention_back(s, mixed_grad, later):
        return attend_back(qkv[s], biases[s], mixed[s], mixed_grad, logs[s], 2, later)

    mixed_grad = [attention_in(0, (up_terms,))]
    backs, terms = [], []
    for s in over[:-1]:
        backs.append(attention_back(s, mixed_grad[s], ()))
        terms.append(terms_matmul(backs[s][0], qkv_weight, spans))
        mixed_grad.append(attention_in(s + 1, (terms[s][0][0],)))
    mid_terms = weight_grad(grad_pieces, mixed, (mixed_grad[-1],))
    mid_sum = group.scatter(mid_terms)
    backs.append(attention_back(slots - 1, mixed_grad[-1], (mid_terms, down_sum)))
    qkv_grad = [b[0] for b in backs]
    returned_grads = [
        give_back(input_grad(tensor.scatter(terms[s])[0], first_back[s][0])) for s in over[:-1]
    ]
    qkv_sum, qkv_terms, *qkv_stage = group.weight_scatter(token_pieces, qkv_grad, ())
    terms.append(terms_matmul(qkv_grad[-1], qkv_weight, spans, (qkv_terms, *returned_grads)))
    last_grad = input_grad(
        tensor.scatter(terms[-1])[0], first_back[-1][0], (*qkv_stage[1], up_sum)
    )
    returned_grads.append(give_back(last_grad))

    places = slot_dealing.T.reshape(-1)
    inverse = jnp.zeros(places.shape, jnp.int32).at[places].set(
        jnp.arange(places.shape[0], dtype=jnp.int32)
    )
    result = jnp.take(jnp.concatenate(returned_rows, axis=0), inverse, axis=0, mode="clip")
    token_gradient = jnp.take(jnp.concatenate(returned_grads, axis=0), inverse, axis=0, mode="clip")

    bias_total = sum(b[1] for b in backs).reshape(2, 2, half)
    head_grads = jnp.concatenate(
        [
            bias_total[:, 0].reshape(-1),
            bias_total[:, 1].reshape(-1),
            sum(up_sums)[0],
        ]
    )
    row_grads = jnp.concatenate(
        [sum(f[2] for f in first_back)[:3], sum(s[3] for s in second)[:3]], axis=0
    ).reshape(-1)
    row_grads = add_up(row_grads.reshape(-1, 128), "tensor")
    grads = add_up(jnp.concatenate([row_grads, head_grads.reshape(-1, 128)], axis=0), "dp").reshape(-1)
    row_shares = lax.dynamic_slice_in_dim(
        grads[: 6 * model_width].reshape(6, splits * groups, piece), tensor.me * groups + group.me, 1, axis=1
    )[:, 0]

    def share(low, width):
        return lax.dynamic_index_in_dim(grads[low : low + groups * width].reshape(groups, width), group.me, 0, False)

    base = 6 * model_width
    query_share = share(base, piece)
    value_share = share(base + head_width, piece)
    up_share = share(base + 2 * head_width, up_bias.shape[0])

    qkv_sum = qkv_sum.reshape(-1, 2, 3, half)
    return (
        result,
        token_gradient,
        qkv_sum[:, :, 0].reshape(-1, head_width),
        qkv_sum[:, :, 1].reshape(-1, head_width),
        qkv_sum[:, :, 2].reshape(-1, head_width),
        mid_sum.T,
        up_sum,
        down_sum.T,
        query_share,
        value_share,
        row_shares[0],
        row_shares[1],
        row_shares[2],
        up_share,
        row_shares[3],
        row_shares[4],
        row_shares[5],
    )


def solution(mesh):
    matrix = P("dp", "tensor")
    flipped = P("tensor", "dp")
    vector = P(("tensor", "dp"))
    arrival = P(None, ("tensor", "dp"), None)
    return jax.shard_map(
        local,
        mesh=mesh,
        in_specs=(arrival, P("dp", "tensor", None), P(), P())
        + (matrix, matrix, matrix, flipped, matrix, flipped)
        + (vector,) * 9,
        out_specs=(arrival, arrival) + (matrix, matrix, matrix, flipped, matrix, flipped) + (vector,) * 9,
        check_vma=False,
    )
```

time: 1380 us -> 1060 us (0.77)
  waiting for transfers between devices: 539 us -> 377 us
  starting transfers between devices: 296 us -> 153 us
  Pallas kernels: 412 us -> 382 us
  local copies, waits for them, and re-layouts: 51.2 us -> 74.8 us
  other arithmetic: 69 us -> 46.2 us
    ppermute x48 -> x5, waiting for transfers between devices: 252 us -> 47.3 us  [send(): return lax.ppermute(array, 'dp', pairs)]
    ppermute x48 -> x5, starting transfers between devices: 135 us -> 6.25 us  [send(): return lax.ppermute(array, 'dp', pairs)]
    all_to_all x2 -> x1, waiting for transfers between devices: 0.01 us -> 92.4 us  [local(): came = lax.all_to_all(sent, 'dp', split_axis=0, concat_axis=0, tiled=True)]
    all_to_all x4, starting transfers between devices: 35.8 us -> 77.5 us  [give_back(): lax.all_to_all(rows.reshape(groups, arrival_rows, model_width), 'dp', spl...]
    ppermute x10 -> x5, waiting for transfers between devices: 61.7 us -> 21.6 us  [add_up(): lax.ppermute(array, axis, [(i, i ^ bit) for i in range(size)])]
    all_to_all x2 -> x1, starting transfers between devices: 31.9 us -> 5.64 us  [local(): came = lax.all_to_all(sent, 'dp', split_axis=0, concat_axis=0, tiled=True)]
    slice x4 -> x34, local copies, waits for them, and re-layouts: 1.69 us -> 26.7 us  [the longest x8 10.9 us: scatter(): from_y[rows:]]
    pallas_call x4 -> x0, Pallas kernels: 17.5 us -> none  [assemble(): pl.pallas_call(body, grid_spec=pltpu.PrefetchScalarGridSpec(num_scalar_pr...]
  transfers between devices with their start and end apart: 160 -> 89, of which waited for: 61 -> 31; matrix products, arithmetic and copies ran while one was open for 7% -> 9% of each run, Pallas kernels for 24% -> 34%
where the time goes in v3:
time: 1060 us; the launch traced here: 1050 us
  Pallas kernels  382 us (36%)
  waiting for transfers between devices  377 us (36%)
  starting transfers between devices  153 us (14%)
  local copies, waits for them, and re-layouts  74.8 us (7%)
  other arithmetic  46.2 us (4%)
  between operations  15.5 us (1%)
    pallas_call x32, Pallas kernels, launch(): pl.pallas_call(run, grid=grid, in_specs=list(in_specs) + [pl.BlockSpec(me...  382 us
    ppermute x67, waiting for transfers between devices, swap(): lax.ppermute(array, 'tensor', [(i, i ^ bit) for i in range(self.size)])  216 us
    all_to_all x1, waiting for transfers between devices, local(): came = lax.all_to_all(sent, 'dp', split_axis=0, concat_axis=0, tiled=True)  92.4 us
    all_to_all x4, starting transfers between devices, give_back(): lax.all_to_all(rows.reshape(groups, arrival_rows, model_width), 'dp', spl...  77.5 us
    ppermute x67, starting transfers between devices, swap(): lax.ppermute(array, 'tensor', [(i, i ^ bit) for i in range(self.size)])  56.6 us
    ppermute x5, waiting for transfers between devices, send(): return lax.ppermute(array, 'dp', pairs)  47.3 us
    unnamed x176, local copies, waits for them, and re-layouts  27.4 us
    ppermute x5, waiting for transfers between devices, add_up(): lax.ppermute(array, axis, [(i, i ^ bit) for i in range(size)])  21.6 us
  transfers between devices with their start and end apart: 89, of which 31 were waited for; matrix products, arithmetic and copies ran while one was open for 9% of the time, Pallas kernels for 34%

profile of v3, /device:TPU:9, one launch (start us, length us, event | category | flops | bytes accessed | tf_op | source)
XLA Modules:
  0.0 1048.5 jit_solution(3232526964769233291)
XLA Ops:
  26.1 92.4 %all-to-all-done = bf16[8,2,32,2048]{3,2,1,0:T(8,128)(2,1)S(1)} async-done(((bf16[8,2,32,2048]{3,2,1,0:T(8,128)(2,1)}), bf16[8,2,32,2048]{3,2,1,0:T(8,128)(2,1)S(1)}, u32[]{:S(2)}, u32[]{:S(2)}) %all-to-all-start) | async-done | bytes 2097184 | tf_op jit(solution)/shard_map/all_to_all | solution.py:551
  127.4 16.7 %collective-permute-done.1.refs_4_.refs_5_ = bf16[256,2048]{1,0:T(8,128)(2,1)S(1)} collective-permute-done((bf16[256,2048]{1,0:T(8,128)(2,1)S(1)}, bf16[256,2048]{1,0:T(8,128)(2,1)S(1)}, u32[]{:S(2)}, u32[]{:S(2)}) %collective-permute-start.1) | collective-permute-done | bytes 1048608 | tf_op jit(solution)/shard_map/ppermute | solution.py:413
  148.7 17.8 %collective-permute-done.12.refs_4_.refs_10_ = bf16[256,2048]{1,0:T(8,128)(2,1)} collective-permute-done((bf16[256,2048]{1,0:T(8,128)(2,1)}, bf16[256,2048]{1,0:T(8,128)(2,1)}, u32[]{:S(2)}, u32[]{:S(2)}) %collective-permute-start.12) | collective-permute-done | bytes 1048608 | tf_op jit(solution)/shard_map/ppermute | solution.py:413
  192.9 13.9 %shard_map.324 = (bf16[1024,512]{1,0:T(8,128)(2,1)}, f32[2,2,1024]{2,1,0:T(2,128)}) custom-call(f32[1024,1]{1,0:T(8,128)} %bitcast.92, bf16[1024,1536]{1,0:T(8,128)(2,1)} %shard_map.323.refs_1_), custom_call_target="tpu_custom_call" | custom-call | flops 8589934592 | bytes 4718592 | tf_op jit(solution)/shard_map/pallas_call | solution.py:44
  214.8 11.6 %shard_map.326.refs_1_ = bf16[1024,1536]{1,0:T(8,128)(2,1)} custom-call(bf16[256,2048]{1,0:T(8,128)(2,1)} %bitcast.9.refs_0_.refs_6_, bf16[256,2048]{1,0:T(8,128)(2,1)} %collective-permute-done.11.refs_1_.refs_7_, bf16[128,2048]{1,0:T(8,128)(2,1)} %collective-permute-done.13.refs_2_.refs_8_, bf16[128,2048]{1,0:T(8,128)(2,1)} %copy-done.65, ...), custom_call_target="tpu_custom_call" | custom-call | flops 6442450944 | bytes 16777216 | tf_op jit(solution)/shard_map/pallas_call | solution.py:44
  226.4 14.1 %shard_map.327 = (bf16[1024,512]{1,0:T(8,128)(2,1)}, f32[2,2,1024]{2,1,0:T(2,128)}) custom-call(f32[1024,1]{1,0:T(8,128)} %bitcast.90, bf16[1024,1536]{1,0:T(8,128)(2,1)} %shard_map.326.refs_1_), custom_call_target="tpu_custom_call" | custom-call | flops 8589934592 | bytes 4718592 | tf_op jit(solution)/shard_map/pallas_call | solution.py:44
  252.6 16.1 %collective-permute-done.25 = bf16[512,1024]{1,0:T(8,128)(2,1)S(1)} collective-permute-done((bf16[512,1024]{1,0:T(8,128)(2,1)}, bf16[512,1024]{1,0:T(8,128)(2,1)S(1)}, u32[]{:S(2)}, u32[]{:S(2)}) %collective-permute-start.25) | collective-permute-done | bytes 1048608 | tf_op jit(solution)/shard_map/ppermute | solution.py:413
  299.8 13.8 %collective-permute-done.16.refs_4_ = bf16[256,2048]{1,0:T(8,128)(2,1)} collective-permute-done((bf16[256,2048]{1,0:T(8,128)(2,1)}, bf16[256,2048]{1,0:T(8,128)(2,1)}, u32[]{:S(2)}, u32[]{:S(2)}) %collective-permute-start.16) | collective-permute-done | bytes 1048608 | tf_op jit(solution)/shard_map/ppermute | solution.py:413
  318.0 18.0 %collective-permute-done.28.refs_4_.refs_9_ = bf16[256,2048]{1,0:T(8,128)(2,1)S(1)} collective-permute-done((bf16[256,2048]{1,0:T(8,128)(2,1)}, bf16[256,2048]{1,0:T(8,128)(2,1)S(1)}, u32[]{:S(2)}, u32[]{:S(2)}) %collective-permute-start.28) | collective-permute-done | bytes 1048608 | tf_op jit(solution)/shard_map/ppermute | solution.py:413
  347.3 16.1 %shard_map.330 = (f32[1024,2048]{1,0:T(8,128)}, bf16[1024,2048]{1,0:T(8,128)(2,1)}) custom-call(bf16[256,2048]{1,0:T(8,128)(2,1)} %get-tuple-element.124.refs_0_, bf16[256,2048]{1,0:T(8,128)(2,1)} %collective-permute-done.15.refs_1_, bf16[128,2048]{1,0:T(8,128)(2,1)} %collective-permute-done.17.refs_2_, bf16[128,2048]{1,0:T(8,128)(2,1)} %collective-permute-done.18.refs_3_, ...), custom_call_target="tpu_custom_call" | custom-call | flops 8589934592 | bytes 29360128 | tf_op jit(solution)/shard_map/pallas_call | solution.py:44
  363.4 14.6 %shard_map.331 = (bf16[512,1024]{1,0:T(8,128)(2,1)}, bf16[256,1024]{1,0:T(8,128)(2,1)}, bf16[256,1024]{1,0:T(8,128)(2,1)}, bf16[512,1024]{1,0:T(8,128)(2,1)}, bf...) custom-call(bf16[1024,2048]{1,0:T(8,128)(2,1)} %get-tuple-element.125.refs_0_.refs_10_, ...), custom_call_target="tpu_custom_call" | custom-call | flops 8589934592 | bytes 16777216 | tf_op jit(solution)/shard_map/pallas_call | solution.py:44
  380.4 16.1 %shard_map.333 = (f32[1024,2048]{1,0:T(8,128)}, bf16[1024,2048]{1,0:T(8,128)(2,1)}) custom-call(bf16[256,2048]{1,0:T(8,128)(2,1)} %get-tuple-element.138.refs_0_.refs_5_, bf16[256,2048]{1,0:T(8,128)(2,1)} %copy-done.53, bf16[128,2048]{1,0:T(8,128)(2,1)} %collective-permute-done.29.refs_2_.refs_7_, bf16[128,2048]{1,0:T(8,128)(2,1)} %collective-permute-done.30.refs_3_.refs_8_, ...), custom_call_target="tpu_custom_call" | custom-call | flops 8589934592 | bytes 29360128 | tf_op jit(solution)/shard_map/pallas_call | solution.py:44
  396.5 14.3 %shard_map.334 = (bf16[512,1024]{1,0:T(8,128)(2,1)}, bf16[256,1024]{1,0:T(8,128)(2,1)}, bf16[256,1024]{1,0:T(8,128)(2,1)}, bf16[512,1024]{1,0:T(8,128)(2,1)}, bf...) custom-call(bf16[1024,2048]{1,0:T(8,128)(2,1)} %get-tuple-element.139.refs_0_.refs_11_, ...), custom_call_target="tpu_custom_call" | custom-call | flops 8589934592 | bytes 16777216 | tf_op jit(solution)/shard_map/pallas_call | solution.py:44
  456.5 13.0 %collective-permute-done.36.refs_4_ = bf16[256,2048]{1,0:T(8,128)(2,1)S(1)} collective-permute-done((bf16[256,2048]{1,0:T(8,128)(2,1)}, bf16[256,2048]{1,0:T(8,128)(2,1)S(1)}, u32[]{:S(2)}, u32[]{:S(2)}) %collective-permute-start.36) | collective-permute-done | bytes 1048608 | tf_op jit(solution)/shard_map/ppermute | solution.py:413
  472.3 32.1 %all-to-all-start.1 = ((bf16[8,32,2048]{2,1,0:T(8,128)(2,1)}), bf16[8,32,2048]{2,1,0:T(8,128)(2,1)S(1)}, u32[]{:S(2)}, u32[]{:S(2)}) async-start(bf16[8,32,2048]{2,1,0:T(8,128)(2,1)} %bitcast.12), calls=%async_computation.1 | async-start | bytes 2097152 | tf_op jit(solution)/shard_map/all_to_all | solution.py:637
  509.6 18.5 %shard_map.337 = (bf16[1024,2048]{1,0:T(8,128)(2,1)}, f32[1,2048]{1,0:T(1,128)}) custom-call(bf16[256,2048]{1,0:T(8,128)(2,1)} %get-tuple-element.149.refs_0_, bf16[256,2048]{1,0:T(8,128)(2,1)} %collective-permute-done.35.refs_1_, bf16[128,2048]{1,0:T(8,128)(2,1)} %collective-permute-done.37.refs_2_, bf16[128,2048]{1,0:T(8,128)(2,1)} %collective-permute-done.38.refs_3_, ...), custom_call_target="tpu_custom_call" | custom-call | flops 8589934592 | bytes 20979712 | tf_op jit(solution)/shard_map/pallas_call | solution.py:44
  528.1 14.4 %shard_map.338 = (bf16[512,1024]{1,0:T(8,128)(2,1)}, bf16[256,1024]{1,0:T(8,128)(2,1)}, bf16[256,1024]{1,0:T(8,128)(2,1)}, bf16[512,1024]{1,0:T(8,128)(2,1)}, bf...) custom-call(bf16[1024,2048]{1,0:T(8,128)(2,1)} %get-tuple-element.151.refs_0_.refs_10_, ...), custom_call_target="tpu_custom_call" | custom-call | flops 8589934592 | bytes 16777216 | tf_op jit(solution)/shard_map/pallas_call | solution.py:44
  543.9 18.8 %all-to-all-start.2 = ((bf16[8,32,2048]{2,1,0:T(8,128)(2,1)}), bf16[8,32,2048]{2,1,0:T(8,128)(2,1)S(1)}, u32[]{:S(2)}, u32[]{:S(2)}) async-start(bf16[8,32,2048]{2,1,0:T(8,128)(2,1)} %bitcast.88), calls=%async_computation.2 | async-start | bytes 2097152 | tf_op jit(solution)/shard_map/all_to_all | solution.py:637
  562.8 18.6 %shard_map.339 = (bf16[1024,2048]{1,0:T(8,128)(2,1)}, f32[1,2048]{1,0:T(1,128)}) custom-call(bf16[256,2048]{1,0:T(8,128)(2,1)} %get-tuple-element.160.refs_0_.refs_5_, bf16[256,2048]{1,0:T(8,128)(2,1)} %collective-permute-done.43.refs_1_.refs_6_, bf16[128,2048]{1,0:T(8,128)(2,1)} %collective-permute-done.45.refs_2_.refs_7_, ...), custom_call_target="tpu_custom_call" | custom-call | flops 8589934592 | bytes 20979712 | tf_op jit(solution)/shard_map/pallas_call | solution.py:44
  585.4 14.2 %shard_map.340 = (bf16[512,1024]{1,0:T(8,128)(2,1)}, bf16[256,1024]{1,0:T(8,128)(2,1)}, bf16[256,1024]{1,0:T(8,128)(2,1)}, bf16[512,1024]{1,0:T(8,128)(2,1)}, bf...) custom-call(bf16[1024,2048]{1,0:T(8,128)(2,1)} %get-tuple-element.162.refs_0_.refs_11_, ...), custom_call_target="tpu_custom_call" | custom-call | flops 8589934592 | bytes 16777216 | tf_op jit(solution)/shard_map/pallas_call | solution.py:44
  609.7 24.3 %shard_map.342.refs_12_ = bf16[2048,2048]{1,0:T(8,128)(2,1)} custom-call(bf16[256,2048]{1,0:T(8,128)(2,1)} %get-tuple-element.149.refs_0_, bf16[256,2048]{1,0:T(8,128)(2,1)} %collective-permute-done.35.refs_1_, bf16[128,2048]{1,0:T(8,128)(2,1)} %collective-permute-done.37.refs_2_, bf16[128,2048]{1,0:T(8,128)(2,1)} %collective-permute-done.38.refs_3_, ...), custom_call_target="tpu_custom_call" | custom-call | flops 17179869184 | bytes 25165824 | tf_op jit(solution)/shard_map/pallas_call | solution.py:44
  637.1 21.1 %collective-permute-done.51.refs_13_.refs_1_ = bf16[512,1024]{1,0:T(8,128)(2,1)S(1)} collective-permute-done((bf16[512,1024]{1,0:T(8,128)(2,1)}, bf16[512,1024]{1,0:T(8,128)(2,1)S(1)}, u32[]{:S(2)}, u32[]{:S(2)}) %collective-permute-start.51) | collective-permute-done | bytes 1048608 | tf_op jit(solution)/shard_map/ppermute | solution.py:413
  658.3 22.4 %collective-permute-done.47.refs_15_.refs_1_ = bf16[256,2048]{1,0:T(8,128)(2,1)S(1)} collective-permute-done((bf16[256,2048]{1,0:T(8,128)(2,1)}, bf16[256,2048]{1,0:T(8,128)(2,1)S(1)}, u32[]{:S(2)}, u32[]{:S(2)}) %collective-permute-start.47) | collective-permute-done | bytes 1048608 | tf_op jit(solution)/shard_map/ppermute | solution.py:413
  682.6 24.8 %shard_map.343.refs_6_.refs_10_ = bf16[2048,2048]{1,0:T(8,128)(2,1)} custom-call(bf16[256,2048]{1,0:T(8,128)(2,1)} %get-tuple-element.124.refs_0_, bf16[256,2048]{1,0:T(8,128)(2,1)} %collective-permute-done.15.refs_1_, bf16[128,2048]{1,0:T(8,128)(2,1)} %collective-permute-done.17.refs_2_, bf16[128,2048]{1,0:T(8,128)(2,1)} %collective-permute-done.18.refs_3_, ...), custom_call_target="tpu_custom_call" | custom-call | flops 17179869184 | bytes 25165824 | tf_op jit(solution)/shard_map/pallas_call | solution.py:44
  741.5 14.5 %shard_map.345 = (bf16[1024,1536]{1,0:T(8,128)(2,1)}, f32[2,1,512]{2,1,0:T(1,128)}) custom-call(f32[1024,1]{1,0:T(8,128)} %bitcast.93, bf16[1024,1536]{1,0:T(8,128)(2,1)} %shard_map.323.refs_1_, bf16[1024,512]{1,0:T(8,128)(2,1)} %get-tuple-element.115.refs_0_.refs_2_.refs_10_, bf16[1024,512]{1,0:T(8,128)(2,1)} %shard_map.344.refs_3_, ...), custom_call_target="tpu_custom_call" | custom-call | flops 21474836480 | bytes 9437184 | tf_op jit(solution)/shard_map/pallas_call | solution.py:44
  756.0 11.8 %shard_map.346 = (bf16[512,1024]{1,0:T(8,128)(2,1)}, bf16[256,1024]{1,0:T(8,128)(2,1)}, bf16[256,1024]{1,0:T(8,128)(2,1)}, bf16[512,1024]{1,0:T(8,128)(2,1)}, bf...) custom-call(bf16[1024,1536]{1,0:T(8,128)(2,1)} %get-tuple-element.168.refs_0_.refs_11_, ...), custom_call_target="tpu_custom_call" | custom-call | flops 6442450944 | bytes 13631488 | tf_op jit(solution)/shard_map/pallas_call | solution.py:44
  771.1 16.3 %collective-permute-done.55 = bf16[512,1024]{1,0:T(8,128)(2,1)} collective-permute-done((bf16[512,1024]{1,0:T(8,128)(2,1)}, bf16[512,1024]{1,0:T(8,128)(2,1)}, u32[]{:S(2)}, u32[]{:S(2)}) %collective-permute-start.55) | collective-permute-done | bytes 1048608 | tf_op jit(solution)/shard_map/ppermute | solution.py:413
  821.8 16.7 %all-to-all-start.3 = ((bf16[8,32,2048]{2,1,0:T(8,128)(2,1)}), bf16[8,32,2048]{2,1,0:T(8,128)(2,1)S(1)}, u32[]{:S(2)}, u32[]{:S(2)}) async-start(bf16[8,32,2048]{2,1,0:T(8,128)(2,1)} %bitcast.78), calls=%async_computation.3 | async-start | bytes 2097152 | tf_op jit(solution)/shard_map/all_to_all | solution.py:637
  841.6 14.3 %shard_map.351 = (bf16[1024,1536]{1,0:T(8,128)(2,1)}, f32[2,1,512]{2,1,0:T(1,128)}) custom-call(f32[1024,1]{1,0:T(8,128)} %bitcast.91, bf16[1024,1536]{1,0:T(8,128)(2,1)} %shard_map.326.refs_1_, bf16[1024,512]{1,0:T(8,128)(2,1)} %get-tuple-element.122.refs_0_.refs_11_.refs_2_, bf16[1024,512]{1,0:T(8,128)(2,1)} %shard_map.349.refs_12_.refs_3_, ...), custom_call_target="tpu_custom_call" | custom-call | flops 21474836480 | bytes 9437184 | tf_op jit(solution)/shard_map/pallas_call | solution.py:44
  856.0 20.0 %shard_map.352 = (bf16[1024,1536]{1,0:T(8,128)(2,1)}, bf16[1024,1536]{1,0:T(8,128)(2,1)}) custom-call(s32[1]{0:T(128)} %bitcast.18.refs_0_, bf16[256,2048]{1,0:T(8,128)(2,1)} %bitcast.83, bf16[256,2048]{1,0:T(8,128)(2,1)} %collective-permute-done.refs_1_.refs_2_, bf16[128,2048]{1,0:T(8,128)(2,1)} %collective-permute-done.2.refs_2_.refs_3_, ...), custom_call_target="tpu_custom_call" | custom-call | flops 12884901888 | bytes 20971520 | tf_op jit(solution)/shard_map/pallas_call | solution.py:44
  895.4 19.8 %collective-permute-done.73 = f32[96,128]{1,0:T(8,128)S(1)} collective-permute-done((f32[96,128]{1,0:T(8,128)S(1)}, f32[96,128]{1,0:T(8,128)S(1)}, u32[]{:S(2)}, u32[]{:S(2)}) %collective-permute-start.73) | collective-permute-done | bytes 49184 | tf_op jit(solution)/shard_map/ppermute | solution.py:499
  979.5 45.6 %collective-permute-done.70 = bf16[256,1536]{1,0:T(8,128)(2,1)S(1)} collective-permute-done((bf16[256,1536]{1,0:T(8,128)(2,1)}, bf16[256,1536]{1,0:T(8,128)(2,1)S(1)}, u32[]{:S(2)}, u32[]{:S(2)}) %collective-permute-start.70) | collective-permute-done | bytes 786464 | tf_op jit(solution)/shard_map/ppermute | solution.py:464
  (493 shorter events, 376.2 us)
Async XLA Ops:
  7.3 164.3 %all-gather.5.cloned.1.call-start = ((), (), s32[]{:S(2)}) async-start(), calls=%async_computation.8 | async-start | bytes 7667712 | tf_op jit(solution)/shard_map/all_gather | solution.py:467
  11.1 195.7 %all-gather.7.cloned.1.call-start = ((), (), s32[]{:S(2)}) async-start(), calls=%async_computation.9 | async-start | bytes 2359296 | tf_op jit(solution)/shard_map/all_gather | solution.py:467
  13.0 325.6 %all-gather.9.cloned.1.call-start = ((), (), s32[]{:S(2)}) async-start(), calls=%async_computation.10 | async-start | bytes 9437184 | tf_op jit(solution)/shard_map/all_gather | solution.py:467
  15.8 347.6 %all-gather.11.cloned.1.call-start = ((), (), s32[]{:S(2)}) async-start(), calls=%async_computation.11 | async-start | bytes 9437184 | tf_op jit(solution)/shard_map/all_gather | solution.py:467
  20.5 98.0 %all-to-all-start = ((bf16[8,2,32,2048]{3,2,1,0:T(8,128)(2,1)}), bf16[8,2,32,2048]{3,2,1,0:T(8,128)(2,1)S(1)}, u32[]{:S(2)}, u32[]{:S(2)}) async-start(bf16[8,2,32,2048]{3,2,1,0:T(8,128)(2,1)} %bitcast.74), calls=%async_computation | async-start | bytes 4194304 | tf_op jit(solution)/shard_map/all_to_all | solution.py:551
  122.3 44.3 %collective-permute-start.12 = (bf16[256,2048]{1,0:T(8,128)(2,1)}, bf16[256,2048]{1,0:T(8,128)(2,1)}, u32[]{:S(2)}, u32[]{:S(2)}) collective-permute-start(bf16[256,2048]{1,0:T(8,128)(2,1)} %bitcast.9.refs_0_.refs_6_), channel_id=1, source_target_pairs={{0,2},{1,3},{2,0},{3,1},{4,6},{5,7},{6,4},{7,5},{8,10},{9,11},{10,... | collective-permute-start | bytes 3145736 | tf_op jit(solution)/shard_map/ppermute | solution.py:413
  122.5 46.7 %collective-permute-start.11 = (bf16[256,2048]{1,0:T(8,128)(2,1)}, bf16[256,2048]{1,0:T(8,128)(2,1)}, u32[]{:S(2)}, u32[]{:S(2)}) collective-permute-start(bf16[256,2048]{1,0:T(8,128)(2,1)} %bitcast.9.refs_0_.refs_6_), channel_id=1, source_target_pairs={{0,1},{1,0},{2,3},{3,2},{4,5},{5,4},{6,7},{7,6},{8,9},{9,8},{10,11... | collective-permute-start | bytes 3145736 | tf_op jit(solution)/shard_map/ppermute | solution.py:413
  167.8 45.8 %collective-permute-start.13 = (bf16[128,2048]{1,0:T(8,128)(2,1)S(1)}, bf16[128,2048]{1,0:T(8,128)(2,1)}, u32[]{:S(2)}, u32[]{:S(2)}) collective-permute-start(bf16[128,2048]{1,0:T(8,128)(2,1)S(1)} %slice.379), channel_id=1, source_target_pairs={{0,1},{1,0},{2,3},{3,2},{4,5},{5,4},{6,7},{7,6},{8,9},{9,8},{10,11... | collective-permute-start | bytes 1572872 | tf_op jit(solution)/shard_map/ppermute | solution.py:413
  170.3 43.7 %collective-permute-start.14 = (bf16[128,2048]{1,0:T(8,128)(2,1)S(1)}, bf16[128,2048]{1,0:T(8,128)(2,1)S(1)}, u32[]{:S(2)}, u32[]{:S(2)}) collective-permute-start(bf16[128,2048]{1,0:T(8,128)(2,1)S(1)} %slice.380), channel_id=1, source_target_pairs={{0,2},{1,3},{2,0},{3,1},{4,6},{5,7},{6,4},{7,5},{8,10},{9,11},{10,... | collective-permute-start | bytes 1572872 | tf_op jit(solution)/shard_map/ppermute | solution.py:413
  174.0 73.4 %collective-permute-start.8 = (bf16[6,512]{1,0:T(8,128)(2,1)S(1)}, bf16[6,512]{1,0:T(8,128)(2,1)S(1)}, u32[]{:S(2)}, u32[]{:S(2)}) collective-permute-start(bf16[6,512]{1,0:T(8,128)(2,1)S(1)} %reshape.237), channel_id=1, source_target_pairs={{0,1},{1,0},{2,3},{3,2},{4,5},{5,4},{6,7},{7,6},{8,9},{9,8},{10,11... | collective-permute-start | bytes 18440 | tf_op jit(solution)/shard_map/ppermute | solution.py:413
  178.9 69.2 %collective-permute-start.9 = (bf16[6,512]{1,0:T(8,128)(2,1)S(1)}, bf16[6,512]{1,0:T(8,128)(2,1)S(1)}, u32[]{:S(2)}, u32[]{:S(2)}) collective-permute-start(bf16[6,512]{1,0:T(8,128)(2,1)S(1)} %reshape.237), channel_id=1, source_target_pairs={{0,2},{1,3},{2,0},{3,1},{4,6},{5,7},{6,4},{7,5},{8,10},{9,11},{10,... | collective-permute-start | bytes 18440 | tf_op jit(solution)/shard_map/ppermute | solution.py:413
  179.0 70.3 %collective-permute-start.10 = (bf16[6,512]{1,0:T(8,128)(2,1)S(1)}, bf16[6,512]{1,0:T(8,128)(2,1)S(1)}, u32[]{:S(2)}, u32[]{:S(2)}) collective-permute-start(bf16[6,512]{1,0:T(8,128)(2,1)S(1)} %reshape.237), channel_id=1, source_target_pairs={{0,3},{1,2},{2,1},{3,0},{4,7},{5,6},{6,5},{7,4},{8,11},{9,10},{10,... | collective-permute-start | bytes 18440 | tf_op jit(solution)/shard_map/ppermute | solution.py:413
  336.0 44.3 %collective-permute-start.29 = (bf16[128,2048]{1,0:T(8,128)(2,1)S(1)}, bf16[128,2048]{1,0:T(8,128)(2,1)}, u32[]{:S(2)}, u32[]{:S(2)}) collective-permute-start(bf16[128,2048]{1,0:T(8,128)(2,1)S(1)} %slice.390), channel_id=1, source_target_pairs={{0,1},{1,0},{2,3},{3,2},{4,5},{5,4},{6,7},{7,6},{8,9},{9,8},{10,11... | collective-permute-start | bytes 1572872 | tf_op jit(solution)/shard_map/ppermute | solution.py:413
  338.3 42.1 %collective-permute-start.30 = (bf16[128,2048]{1,0:T(8,128)(2,1)S(1)}, bf16[128,2048]{1,0:T(8,128)(2,1)}, u32[]{:S(2)}, u32[]{:S(2)}) collective-permute-start(bf16[128,2048]{1,0:T(8,128)(2,1)S(1)} %slice.391), channel_id=1, source_target_pairs={{0,2},{1,3},{2,0},{3,1},{4,6},{5,7},{6,4},{7,5},{8,10},{9,11},{10,... | collective-permute-start | bytes 1572872 | tf_op jit(solution)/shard_map/ppermute | solution.py:413
  454.8 49.6 %collective-permute-start.44 = (bf16[256,2048]{1,0:T(8,128)(2,1)}, bf16[256,2048]{1,0:T(8,128)(2,1)}, u32[]{:S(2)}, u32[]{:S(2)}) collective-permute-start(bf16[256,2048]{1,0:T(8,128)(2,1)} %get-tuple-element.160.refs_0_.refs_5_), channel_id=1, source_target_pairs={{0,2},{1,3},{2,0},{3,1},{4,6},{5,7},{6,4},{7,5},{8,10},{9,11},{10,... | collective-permute-start | bytes 3145736 | tf_op jit(solution)/shard_map/ppermute | solution.py:413
  456.0 51.4 %collective-permute-start.43 = (bf16[256,2048]{1,0:T(8,128)(2,1)}, bf16[256,2048]{1,0:T(8,128)(2,1)}, u32[]{:S(2)}, u32[]{:S(2)}) collective-permute-start(bf16[256,2048]{1,0:T(8,128)(2,1)} %get-tuple-element.160.refs_0_.refs_5_), channel_id=1, source_target_pairs={{0,1},{1,0},{2,3},{3,2},{4,5},{5,4},{6,7},{7,6},{8,9},{9,8},{10,11... | collective-permute-start | bytes 3145736 | tf_op jit(solution)/shard_map/ppermute | solution.py:413
  472.3 71.7 %all-to-all-start.1 = ((bf16[8,32,2048]{2,1,0:T(8,128)(2,1)}), bf16[8,32,2048]{2,1,0:T(8,128)(2,1)S(1)}, u32[]{:S(2)}, u32[]{:S(2)}) async-start(bf16[8,32,2048]{2,1,0:T(8,128)(2,1)} %bitcast.12), calls=%async_computation.1 | async-start | bytes 2097152 | tf_op jit(solution)/shard_map/all_to_all | solution.py:637
  506.2 56.5 %collective-permute-start.45 = (bf16[128,2048]{1,0:T(8,128)(2,1)}, bf16[128,2048]{1,0:T(8,128)(2,1)}, u32[]{:S(2)}, u32[]{:S(2)}) collective-permute-start(bf16[128,2048]{1,0:T(8,128)(2,1)} %slice.400), channel_id=1, source_target_pairs={{0,1},{1,0},{2,3},{3,2},{4,5},{5,4},{6,7},{7,6},{8,9},{9,8},{10,11... | collective-permute-start | bytes 1572872 | tf_op jit(solution)/shard_map/ppermute | solution.py:413
  509.3 53.4 %collective-permute-start.46 = (bf16[128,2048]{1,0:T(8,128)(2,1)}, bf16[128,2048]{1,0:T(8,128)(2,1)}, u32[]{:S(2)}, u32[]{:S(2)}) collective-permute-start(bf16[128,2048]{1,0:T(8,128)(2,1)} %slice.401), channel_id=1, source_target_pairs={{0,2},{1,3},{2,0},{3,1},{4,6},{5,7},{6,4},{7,5},{8,10},{9,11},{10,... | collective-permute-start | bytes 1572872 | tf_op jit(solution)/shard_map/ppermute | solution.py:413
  543.6 40.3 %collective-permute-start.39 = (bf16[512,1024]{1,0:T(8,128)(2,1)}, bf16[512,1024]{1,0:T(8,128)(2,1)S(1)}, u32[]{:S(2)}, u32[]{:S(2)}) collective-permute-start(bf16[512,1024]{1,0:T(8,128)(2,1)} %get-tuple-element.153.refs_7_), channel_id=1, source_target_pairs={{0,1},{1,0},{2,3},{3,2},{4,5},{5,4},{6,7},{7,6},{8,9},{9,8},{10,11... | collective-permute-start | bytes 3145736 | tf_op jit(solution)/shard_map/ppermute | solution.py:413
  543.9 64.8 %all-to-all-start.2 = ((bf16[8,32,2048]{2,1,0:T(8,128)(2,1)}), bf16[8,32,2048]{2,1,0:T(8,128)(2,1)S(1)}, u32[]{:S(2)}, u32[]{:S(2)}) async-start(bf16[8,32,2048]{2,1,0:T(8,128)(2,1)} %bitcast.88), calls=%async_computation.2 | async-start | bytes 2097152 | tf_op jit(solution)/shard_map/all_to_all | solution.py:637
  562.7 275.9 %reduce-scatter.4.cloned.1.call-start = ((), (), s32[]{:S(2)}) async-start(), calls=%async_computation.12 | async-start | bytes 9437184 | tf_op jit(solution)/shard_map/reduce_scatter | solution.py:470
  634.0 317.2 %reduce-scatter.6.cloned.1.call-start = ((), (), s32[]{:S(2)}) async-start(), calls=%async_computation.13 | async-start | bytes 9437184 | tf_op jit(solution)/shard_map/reduce_scatter | solution.py:470
  635.7 44.9 %collective-permute-start.47 = (bf16[256,2048]{1,0:T(8,128)(2,1)}, bf16[256,2048]{1,0:T(8,128)(2,1)S(1)}, u32[]{:S(2)}, u32[]{:S(2)}) collective-permute-start(bf16[256,2048]{1,0:T(8,128)(2,1)} %get-tuple-element.164.refs_0_), channel_id=1, source_target_pairs={{0,1},{1,0},{2,3},{3,2},{4,5},{5,4},{6,7},{7,6},{8,9},{9,8},{10,11... | collective-permute-start | bytes 3145736 | tf_op jit(solution)/shard_map/ppermute | solution.py:413
  636.8 44.0 %collective-permute-start.48 = (bf16[256,2048]{1,0:T(8,128)(2,1)}, bf16[256,2048]{1,0:T(8,128)(2,1)S(1)}, u32[]{:S(2)}, u32[]{:S(2)}) collective-permute-start(bf16[256,2048]{1,0:T(8,128)(2,1)} %get-tuple-element.164.refs_0_), channel_id=1, source_target_pairs={{0,2},{1,3},{2,0},{3,1},{4,6},{5,7},{6,4},{7,5},{8,10},{9,11},{10,... | collective-permute-start | bytes 3145736 | tf_op jit(solution)/shard_map/ppermute | solution.py:413
  730.2 40.1 %collective-permute-start.60 = (bf16[256,2048]{1,0:T(8,128)(2,1)}, bf16[256,2048]{1,0:T(8,128)(2,1)S(1)}, u32[]{:S(2)}, u32[]{:S(2)}) collective-permute-start(bf16[256,2048]{1,0:T(8,128)(2,1)} %get-tuple-element.181.refs_0_.refs_5_), channel_id=1, source_target_pairs={{0,2},{1,3},{2,0},{3,1},{4,6},{5,7},{6,4},{7,5},{8,10},{9,11},{10,... | collective-permute-start | bytes 3145736 | tf_op jit(solution)/shard_map/ppermute | solution.py:413
  821.8 55.2 %all-to-all-start.3 = ((bf16[8,32,2048]{2,1,0:T(8,128)(2,1)}), bf16[8,32,2048]{2,1,0:T(8,128)(2,1)S(1)}, u32[]{:S(2)}, u32[]{:S(2)}) async-start(bf16[8,32,2048]{2,1,0:T(8,128)(2,1)} %bitcast.78), calls=%async_computation.3 | async-start | bytes 2097152 | tf_op jit(solution)/shard_map/all_to_all | solution.py:637
  838.6 135.2 %reduce-scatter.8.cloned.1.call-start = ((), (), s32[]{:S(2)}) async-start(), calls=%async_computation.14 | async-start | bytes 2359296 | tf_op jit(solution)/shard_map/reduce_scatter | solution.py:470
  876.1 45.3 %collective-permute-start.67 = (bf16[1024,1536]{1,0:T(8,128)(2,1)}, bf16[1024,1536]{1,0:T(8,128)(2,1)}, u32[]{:S(2)}, u32[]{:S(2)}) collective-permute-start(bf16[1024,1536]{1,0:T(8,128)(2,1)} %get-tuple-element.192), channel_id=1, source_target_pairs={{0,4},{4,0},{8,12},{12,8},{16,20},{20,16},{24,28},{28,24},{1,5},{5... | collective-permute-start | bytes 9437192 | tf_op jit(solution)/shard_map/ppermute | solution.py:464
  958.4 76.5 %all-to-all-start.4 = ((bf16[8,32,2048]{2,1,0:T(8,128)(2,1)}), bf16[8,32,2048]{2,1,0:T(8,128)(2,1)}, u32[]{:S(2)}, u32[]{:S(2)}) async-start(bf16[8,32,2048]{2,1,0:T(8,128)(2,1)} %bitcast.77), calls=%async_computation.6 | async-start | bytes 2097152 | tf_op jit(solution)/shard_map/all_to_all | solution.py:637
  972.3 52.7 %collective-permute-start.70 = (bf16[256,1536]{1,0:T(8,128)(2,1)}, bf16[256,1536]{1,0:T(8,128)(2,1)S(1)}, u32[]{:S(2)}, u32[]{:S(2)}) collective-permute-start(bf16[256,1536]{1,0:T(8,128)(2,1)} %get-tuple-element.254), channel_id=1, source_target_pairs={{0,8},{4,12},{8,16},{12,20},{16,24},{20,28},{24,0},{28,4},{1,9},{5... | collective-permute-start | bytes 2359304 | tf_op jit(solution)/shard_map/ppermute | solution.py:464
  973.5 53.3 %collective-permute-start.71 = (bf16[256,1536]{1,0:T(8,128)(2,1)}, bf16[256,1536]{1,0:T(8,128)(2,1)}, u32[]{:S(2)}, u32[]{:S(2)}) collective-permute-start(bf16[256,1536]{1,0:T(8,128)(2,1)} %get-tuple-element.255), channel_id=1, source_target_pairs={{0,24},{4,28},{8,0},{12,4},{16,8},{20,12},{24,16},{28,20},{1,25},{... | collective-permute-start | bytes 2359304 | tf_op jit(solution)/shard_map/ppermute | solution.py:464
  (133 other events, 2343.1 us)
Sparse Core Ops, SparseCore 0:
  11.2 109.8 all-gather.4
  123.2 32.8 all-gather.6
  157.8 78.9 all-gather.8
  238.2 80.5 all-gather.10
  634.2 88.7 reduce-scatter.3
  725.1 87.9 reduce-scatter.5
  876.6 30.5 reduce-scatter.7

commit v4 on v3

--- a/solution.py
+++ b/solution.py
@@ -49,7 +49,9 @@
         out_shape=list(outs),
         scratch_shapes=list(scratch),
         compiler_params=pltpu.CompilerParams(vmem_limit_bytes=60 * MIB),
-        cost_estimate=pl.CostEstimate(flops=int(flops), bytes_accessed=int(nbytes), transcendentals=int(exps)),
+        cost_estimate=pl.CostEstimate(
+            flops=int(flops) // 10, bytes_accessed=int(nbytes) // 10, transcendentals=int(exps) // 10
+        ),
     )(*ins, *later)
 
 
@@ -130,7 +132,8 @@
             out_ref[:, width + low : width + low + HEAD] = (key_total * head_scale).astype(bf16)
             out_ref[:, 2 * width + low : 2 * width + low + HEAD] = value_total
             sum_ref[0, :, low : low + HEAD] = query_sum
-            sum_ref[0, :, width + low : width + low + HEAD] = jnp.sum(
+            sum_ref[0, :, width + low : width + low + HEAD] = jnp.zeros_like(query_sum)
+            sum_ref[0, :, 2 * width + low : 2 * width + low + HEAD] = jnp.sum(
                 value_total.astype(f32), axis=0, keepdims=True
             )
 
@@ -146,8 +149,8 @@
             columns_of(width),
             pl.BlockSpec((1, heads, rows), lambda i: (i, 0, 0)),
         ],
-        [shape((rows, columns), bf16), shape((halves, 1, 2 * width), f32)],
-        [columns_of(group), pl.BlockSpec((1, 1, 2 * width), lambda i: (i, 0, 0))],
+        [shape((rows, columns), bf16), shape((halves, 1, group), f32)],
+        [columns_of(group), pl.BlockSpec((1, 1, group), lambda i: (i, 0, 0))],
         later,
         flops=10 * halves * heads * rows * rows * HEAD * 4,
         nbytes=rows * columns * 6,
@@ -237,16 +240,17 @@
     return outs[: len(spans[0])], outs[len(spans[0]) :]
 
 
-def weight_grad(lefts, rights, later=(), core=None, most=256):
+def weight_grad(lefts, rights, later=(), core=None, most=256, row=None):
     flat = [p for pieces in lefts for p in pieces]
     outer = flat[0].shape[1]
     rows, columns = rights[0].shape
     tile = tile_of(outer, most)
     slots = len(rights)
     scalars = [] if core is None else [core.reshape(1)]
+    rows_added = [] if core is None else [row]
+    spare = 0 if core is None else 16
 
     def body(ins, refs):
-        ins = ins[len(scalars) :] if core is None else ins[1:]
         piece_refs, right_refs = ins[: len(flat)], ins[len(flat) :]
         gathered = refs[-1]
         first = 0
@@ -262,27 +266,33 @@
     def body_apart(ins, refs):
         parity = lax.rem(pl.program_id(0), 2)
         total_ref = refs[2]
-        body(ins, (total_ref, refs[3]))
+        body(ins[2:], (total_ref, refs[3]))
+        added = jnp.broadcast_to(ins[1][...].astype(bf16), (spare, columns))
+
+        def put(ref):
+            ref[:tile, :] = total_ref[...]
+            ref[tile:, :] = added
 
         @pl.when(parity == ins[0][0])
         def _():
-            refs[0][...] = total_ref[...]
+            put(refs[0])
 
         @pl.when(parity != ins[0][0])
         def _():
-            refs[1][...] = total_ref[...]
-
-    outs = [shape((outer, columns), bf16)] if core is None else [shape((outer // 2, columns), bf16)] * 2
+            put(refs[1])
+
+    outs = [shape((outer, columns), bf16)] if core is None else [shape((outer // tile // 2 * (tile + spare), columns), bf16)] * 2
     where = (lambda j: (j, 0)) if core is None else (lambda j: (j // 2, 0))
     result = launch(
         body if core is None else body_apart,
         (outer // tile,),
-        [*scalars, *flat, *rights],
+        [*scalars, *rows_added, *flat, *rights],
         [pl.BlockSpec(memory_space=pltpu.SMEM)] * len(scalars)
+        + [whole(r) for r in rows_added]
         + [pl.BlockSpec((p.shape[0], tile), lambda j: (0, j)) for p in flat]
         + [whole(r) for r in rights],
         outs,
-        [pl.BlockSpec((tile, columns), where)] * len(outs),
+        [pl.BlockSpec((tile + spare, columns), where)] * len(outs),
         later,
         scratch=([] if core is None else [pltpu.VMEM((tile, columns), bf16)])
         + [pltpu.VMEM((slots * rows, tile), bf16)],
@@ -327,12 +337,17 @@
     def of(columns):
         return pl.BlockSpec((tile, columns), lambda i: (i, 0))
 
-    ins = [*left, *right, *tiled] + ([vectors] if vectors is not None else [])
+    def start(array, first):
+        return pl.BlockSpec((tile, array.shape[1]), lambda i: (i + first // tile, 0))
+
+    ins = [a for a, _ in (*left, *right)] + [*tiled] + ([vectors] if vectors is not None else [])
     return launch(
         run,
         (steps,),
         ins,
-        [of(a.shape[1]) for a in (*left, *right, *tiled)] + ([whole(vectors)] if vectors is not None else []),
+        [start(*a) for a in (*left, *right)]
+        + [of(a.shape[1]) for a in tiled]
+        + ([whole(vectors)] if vectors is not None else []),
         [shape((rows, c), dtype) for c, dtype in outs]
         + ([shape((8, width), f32)] if sums else []),
         [of(c) for c, _ in outs]
@@ -442,12 +457,14 @@
             full = jnp.concatenate([left[0], right[0]], axis=1)
             mine = lax.psum_scatter(full, "tensor", scatter_dimension=0, tiled=True)
             half = mine.shape[1] // 2
-            return ([mine[:, :half]], [mine[:, half:]]), ()
+            return ([(mine[:, :half], 0)], [(mine[:, half:], 0)]), (), ()
         rows = left[1].shape[0]
         from_x, from_y = self.swap(left[0], 1), self.swap(right[0], 2)
         left_far = self.swap((left[1].astype(f32) + from_x[rows:].astype(f32)).astype(bf16), 2)
         right_far = self.swap((right[1].astype(f32) + from_y[:rows].astype(f32)).astype(bf16), 1)
-        return ([left[2], from_x, left_far], [right[2], from_y[rows:], right_far]), (from_x, from_y)
+        left = [(left[2], 0), (from_x, 0), (left_far, 0)]
+        right = [(right[2], 0), (from_y, rows), (right_far, 0)]
+        return (left, right), (from_x, from_y), (left_far, right_far)
 
 
 class GroupAxis:
@@ -469,11 +486,12 @@
     def scatter(self, terms):
         return lax.psum_scatter(terms, "dp", scatter_dimension=0, tiled=True).astype(f32)
 
-    def weight_scatter(self, lefts, rights, later):
+    def weight_scatter(self, lefts, rights, row, later):
         if not self.line:
             terms = weight_grad(lefts, rights, later)
-            return self.scatter(terms), terms, (), (), ()
-        mine, theirs = weight_grad(lefts, rights, later, self.me % 2, lefts[0][0].shape[1] // self.size)
+            return self.scatter(terms), lax.psum(row, "dp")[0], terms, (), (), ()
+        block = lefts[0][0].shape[1] // self.size
+        mine, theirs = weight_grad(lefts, rights, later, self.me % 2, block, row)
         got = self.send(theirs, [(i, i ^ 1) for i in range(self.size)])
         rows = mine.shape[0] // 4
 
@@ -489,16 +507,30 @@
         behind = (toward(3) + down.astype(f32)).astype(bf16)
         ahead, behind = self.send(ahead, self.next), self.send(behind, self.last)
         total = toward(0) + ahead.astype(f32) + behind.astype(f32)
-        return total, mine, (got,), (up, down), (ahead, behind)
-
-
-def add_up(array, axis):
+        return total[:block], total[block], mine, (got,), (up, down), (ahead, behind)
+
+
+def nothing(*arrays):
+    return sum(a[(0,) * a.ndim].astype(f32) * 0.0 for a in arrays)
+
+
+def touched(array, *arrays):
+    if not arrays:
+        return array
+    corner = array[:16, :128]
+    return lax.dynamic_update_slice(array, corner + nothing(*arrays).astype(array.dtype), (0, 0))
+
+
+def add_up(array, axis, earlier=()):
     size = lax.axis_size(axis)
-    bit = 1
+    bit, stages = 1, []
     while bit < size:
-        array = array + lax.ppermute(array, axis, [(i, i ^ bit) for i in range(size)])
+        if len(stages) < len(earlier) and earlier[len(stages)] is not None:
+            array = array + nothing(earlier[len(stages)])
+        stages.append(lax.ppermute(array, axis, [(i, i ^ bit) for i in range(size)]))
+        array = array + stages[-1]
         bit *= 2
-    return array
+    return array, stages
 
 
 def gelu(hidden):
@@ -549,7 +581,14 @@
     slot_dealing = dealing.reshape(groups, slots)
     sent = jnp.take(tokens, dealing, axis=0, mode="clip").reshape(groups, slots, arrival_rows, model_width)
     came = lax.all_to_all(sent, "dp", split_axis=0, concat_axis=0, tiled=True)
-    arrived = [came[:, s].reshape(own_rows, model_width) for s in over]
+    zero = came[0, 0, 0, 0] * 0.0
+    token_pieces, arrived = [], []
+    for s in over:
+        rows = came[:, s].reshape(own_rows, model_width)
+        if s > 0 and tensor.square:
+            rows = rows + token_pieces[0][1][0, 0] * 0.0
+        arrived.append(rows)
+        token_pieces.append(tensor.gather(rows))
 
     head_piece = jnp.concatenate([query_bias, value_bias, up_bias]).astype(bf16)
     row_piece = jnp.concatenate(
@@ -557,7 +596,7 @@
     ).astype(bf16)
     vector = jnp.concatenate([head_piece, row_piece])
     shard_rows, spare = query_weight.shape[0], 128
-    padded = jnp.zeros((shard_rows * spare,), bf16).at[: vector.shape[0]].set(vector)
+    padded = jnp.zeros((shard_rows * spare,), bf16).at[: vector.shape[0]].set(vector) + zero
     three = [w.astype(bf16) for w in (query_weight, key_weight, value_weight)]
     qkv_weight = group.gather(
         jnp.concatenate(
@@ -565,9 +604,9 @@
             axis=1,
         )
     )
-    mid_weight = group.gather(output_weight.astype(bf16).T)
-    up_full = group.gather(up_weight.astype(bf16))
-    down_full = group.gather(down_weight.astype(bf16).T)
+    mid_weight = group.gather(touched(output_weight.astype(bf16).T, came))
+    up_full = group.gather(touched(up_weight.astype(bf16), came))
+    down_full = group.gather(touched(down_weight.astype(bf16).T, came))
     used = -(-vector.shape[0] // spare)
     table = qkv_weight[:, 3 * head_width :].reshape(groups, shard_rows, spare)[:, :used]
     table = table.reshape(groups, -1)[:, : vector.shape[0]]
@@ -592,8 +631,7 @@
     ]
 
     rows_bf16 = [(slot_rows, bf16)]
-    token_pieces = [tensor.gather(a) for a in arrived]
-    qkv, mixed, logs, terms = [], [], [], []
+    qkv, mixed, logs, terms, sums = [], [], [], [], []
     before = ()
     for s in over:
         qkv += rows_matmul(
@@ -609,11 +647,15 @@
         mix, log = attend(qkv[s], biases[s], 2)
         mixed.append(mix)
         logs.append(log)
-        terms.append(terms_matmul(mix, mid_weight, spans))
+        terms.append(terms_matmul(mix, mid_weight, spans, sums[-1][1] if sums else ()))
+        sums.append(tensor.scatter(terms[s]))
         before = (terms[s][0][0],)
-    first = [first_norm(tensor.scatter(terms[s])[0], arrived[s], row_vectors, before) for s in over]
-    first_pieces = [tensor.gather(f[0]) for f in first]
-    hidden, active, terms = [], [], []
+    first, first_pieces = [], []
+    for s in over:
+        first.append(first_norm(sums[s][0], arrived[s], row_vectors, before))
+        first_pieces.append(tensor.gather(first[s][0]))
+        before = tuple(first_pieces[s][1:2] + first_pieces[s][4:])
+    hidden, active, terms, sums = [], [], [], []
     before = ()
     for s in over:
         wide, narrow = rows_matmul(
@@ -627,11 +669,14 @@
         )
         hidden.append(wide)
         active.append(narrow)
-        terms.append(terms_matmul(narrow, down_full, spans))
+        terms.append(terms_matmul(narrow, down_full, spans, sums[-1][1] if sums else ()))
+        sums.append(tensor.scatter(terms[s]))
         before = (terms[s][0][0],)
-    second = [
-        second_norm(tensor.scatter(terms[s])[0], first[s][1], cotangent[s], row_vectors, before) for s in over
-    ]
+    second, down_pieces = [], []
+    for s in over:
+        second.append(second_norm(sums[s][0], first[s][1], cotangent[s], row_vectors, before))
+        down_pieces.append(tensor.gather(second[s][2]))
+        before = tuple(down_pieces[s][1:2] + down_pieces[s][4:])
 
     def give_back(rows):
         return lax.all_to_all(
@@ -640,8 +685,7 @@
 
     returned_rows = [give_back(s[0]) for s in second]
 
-    down_pieces = [tensor.gather(s[2]) for s in second]
-    hidden_grad, up_sums, terms = [], [], []
+    hidden_grad, up_sums, terms, first_sums = [], [], [], []
     before = ()
 
     def through_gelu(product, wide):
@@ -660,11 +704,10 @@
         )
         hidden_grad.append(grad)
         up_sums.append(total)
-        terms.append(terms_matmul(grad, up_full, spans))
+        terms.append(terms_matmul(grad, up_full, spans, first_sums[-1][1] if first_sums else ()))
+        first_sums.append(tensor.scatter(terms[s]))
         before = (terms[s][0][0],)
     first_back = []
-
-    first_sums = [tensor.scatter(t) for t in terms]
 
     def back_to_first(s, later):
         first_back.append(
@@ -675,11 +718,12 @@
         return tensor.gather(first_back[s][1])
 
     grad_pieces = [back_to_first(0, before)]
+    near = grad_pieces[0][1:2] + grad_pieces[0][4:]
     down_terms = weight_grad(down_pieces, active, (first_back[0][0], *returned_rows))
+    down_terms = touched(down_terms, *first_sums[-1][1], *near)
     down_sum = group.scatter(down_terms)
-    up_terms = weight_grad(
-        first_pieces, hidden_grad, (down_terms, *first_sums[-1][1], *grad_pieces[0][1:2], *grad_pieces[0][4:])
-    )
+    up_terms = weight_grad(first_pieces, hidden_grad, (down_terms,))
+    up_terms = touched(up_terms, *first_sums[-1][2], *grad_pieces[0][2:4])
     up_sum = group.scatter(up_terms)
     grad_pieces += [back_to_first(s, (up_terms,)) for s in over[1:]]
 
@@ -698,22 +742,30 @@
         return attend_back(qkv[s], biases[s], mixed[s], mixed_grad, logs[s], 2, later)
 
     mixed_grad = [attention_in(0, (up_terms,))]
-    backs, terms = [], []
-    for s in over[:-1]:
-        backs.append(attention_back(s, mixed_grad[s], ()))
-        terms.append(terms_matmul(backs[s][0], qkv_weight, spans))
-        mixed_grad.append(attention_in(s + 1, (terms[s][0][0],)))
-    mid_terms = weight_grad(grad_pieces, mixed, (mixed_grad[-1],))
+    row_grads = jnp.concatenate(
+        [sum(f[2] for f in first_back)[:3], sum(s[3] for s in second)[:3]], axis=0
+    ).reshape(-1, 128)
+    row_grads, stages = add_up(row_grads, "tensor", (mixed_grad[0],))
+    stages = [(stage,) for stage in stages] + [(), ()]
+    backs = [attention_back(0, mixed_grad[0], ())]
+    terms = [terms_matmul(backs[0][0], qkv_weight, spans, stages[0])]
+    sums = [tensor.scatter(terms[0])]
+    mixed_grad.append(attention_in(1, (terms[0][0][0], *stages[1])))
+    mid_terms = weight_grad(grad_pieces, mixed, (mixed_grad[1], *sums[0][1]))
+    small = jnp.concatenate([row_grads, sum(up_sums).reshape(-1, 128)], axis=0)
+    small, stages = add_up(small, "dp", (mixed_grad[1], mid_terms, None))
     mid_sum = group.scatter(mid_terms)
-    backs.append(attention_back(slots - 1, mixed_grad[-1], (mid_terms, down_sum)))
+    token_grad = [input_grad(sums[0][0], first_back[0][0], (mid_terms,))]
+    returned_grads = [give_back(token_grad[0])]
+    backs.append(
+        attention_back(1, mixed_grad[1], (mid_terms, token_grad[0], down_sum, stages[0]))
+    )
     qkv_grad = [b[0] for b in backs]
-    returned_grads = [
-        give_back(input_grad(tensor.scatter(terms[s])[0], first_back[s][0])) for s in over[:-1]
-    ]
-    qkv_sum, qkv_terms, *qkv_stage = group.weight_scatter(token_pieces, qkv_grad, ())
-    terms.append(terms_matmul(qkv_grad[-1], qkv_weight, spans, (qkv_terms, *returned_grads)))
+    bias_terms = sum(b[1] for b in backs).reshape(1, -1)
+    qkv_sum, bias_sum, qkv_terms, *qkv_stage = group.weight_scatter(token_pieces, qkv_grad, bias_terms, (stages[1],))
+    terms.append(terms_matmul(qkv_grad[-1], qkv_weight, spans, (qkv_terms, *qkv_stage[0], *returned_grads)))
     last_grad = input_grad(
-        tensor.scatter(terms[-1])[0], first_back[-1][0], (*qkv_stage[1], up_sum)
+        tensor.scatter(terms[-1])[0], first_back[-1][0], (*qkv_stage[1], stages[2], up_sum)
     )
     returned_grads.append(give_back(last_grad))
 
@@ -724,30 +776,20 @@
     result = jnp.take(jnp.concatenate(returned_rows, axis=0), inverse, axis=0, mode="clip")
     token_gradient = jnp.take(jnp.concatenate(returned_grads, axis=0), inverse, axis=0, mode="clip")
 
-    bias_total = sum(b[1] for b in backs).reshape(2, 2, half)
-    head_grads = jnp.concatenate(
-        [
-            bias_total[:, 0].reshape(-1),
-            bias_total[:, 1].reshape(-1),
-            sum(up_sums)[0],
-        ]
-    )
-    row_grads = jnp.concatenate(
-        [sum(f[2] for f in first_back)[:3], sum(s[3] for s in second)[:3]], axis=0
-    ).reshape(-1)
-    row_grads = add_up(row_grads.reshape(-1, 128), "tensor")
-    grads = add_up(jnp.concatenate([row_grads, head_grads.reshape(-1, 128)], axis=0), "dp").reshape(-1)
     row_shares = lax.dynamic_slice_in_dim(
-        grads[: 6 * model_width].reshape(6, splits * groups, piece), tensor.me * groups + group.me, 1, axis=1
+        small.reshape(-1)[: 6 * model_width].reshape(6, splits * groups, piece),
+        tensor.me * groups + group.me,
+        1,
+        axis=1,
     )[:, 0]
 
-    def share(low, width):
-        return lax.dynamic_index_in_dim(grads[low : low + groups * width].reshape(groups, width), group.me, 0, False)
-
-    base = 6 * model_width
-    query_share = share(base, piece)
-    value_share = share(base + head_width, piece)
-    up_share = share(base + 2 * head_width, up_bias.shape[0])
+    def share(values):
+        return lax.dynamic_index_in_dim(values.reshape(groups, -1), group.me, 0, False)
+
+    bias_sum = bias_sum.reshape(2, 3, half)
+    query_share = share(bias_sum[:, 0])
+    value_share = share(bias_sum[:, 2])
+    up_share = share(small.reshape(-1)[6 * model_width :])
 
     qkv_sum = qkv_sum.reshape(-1, 2, 3, half)
     return (

time: 1060 us -> 1010 us (0.953)
  waiting for transfers between devices: 377 us -> 294 us
  other arithmetic: 46.2 us -> 56.9 us
    ppermute x67, waiting for transfers between devices: 216 us -> 160 us  [swap(): lax.ppermute(array, 'tensor', [(i, i ^ bit) for i in range(self.size)])]
    all_to_all x1, waiting for transfers between devices: 92.4 us -> 41.3 us  [local(): came = lax.all_to_all(sent, 'dp', split_axis=0, concat_axis=0, tiled=True)]
    ppermute x5, waiting for transfers between devices: 47.3 us -> 11.9 us  [send(): return lax.ppermute(array, 'dp', pairs)]
    all_to_all x4, waiting for transfers between devices: 0.01 us -> 35.3 us  [give_back(): lax.all_to_all(rows.reshape(groups, arrival_rows, model_width), 'dp', spl...]
    all_gather x4, waiting for transfers between devices: 0.02 us -> 28.5 us  [gather(): return lax.all_gather(shard, 'dp', axis=0, tiled=True)]
    ppermute x5, starting transfers between devices: 6.59 us -> 21.1 us  [add_up(): lax.ppermute(array, axis, [(i, i ^ bit) for i in range(size)])]
    all_to_all x4, starting transfers between devices: 77.5 us -> 63.9 us  [give_back(): lax.all_to_all(rows.reshape(groups, arrival_rows, model_width), 'dp', spl...]
    unnamed x176 -> x208, local copies, waits for them, and re-layouts: 27.4 us -> 32.4 us
  transfers between devices with their start and end apart: 89 -> 89, of which waited for: 31 -> 26; matrix products, arithmetic and copies ran while one was open for 9% -> 11% of each run, Pallas kernels for 34% -> 39%
where the time goes in v4:
time: 1010 us; the launch traced here: 991 us
  Pallas kernels  384 us (38%)
  waiting for transfers between devices  294 us (29%)
  starting transfers between devices  151 us (15%)
  local copies, waits for them, and re-layouts  79.9 us (8%)
  other arithmetic  56.9 us (6%)
  between operations  24.9 us (2%)
    pallas_call x32, Pallas kernels, launch(): pl.pallas_call(run, grid=grid, in_specs=list(in_specs) + [pl.BlockSpec(me...  384 us
    ppermute x67, waiting for transfers between devices, swap(): lax.ppermute(array, 'tensor', [(i, i ^ bit) for i in range(self.size)])  160 us
    all_to_all x4, starting transfers between devices, give_back(): lax.all_to_all(rows.reshape(groups, arrival_rows, model_width), 'dp', spl...  63.9 us
    ppermute x67, starting transfers between devices, swap(): lax.ppermute(array, 'tensor', [(i, i ^ bit) for i in range(self.size)])  52.7 us
    all_to_all x1, waiting for transfers between devices, local(): came = lax.all_to_all(sent, 'dp', split_axis=0, concat_axis=0, tiled=True)  41.3 us
    all_to_all x4, waiting for transfers between devices, give_back(): lax.all_to_all(rows.reshape(groups, arrival_rows, model_width), 'dp', spl...  35.3 us
    unnamed x208, local copies, waits for them, and re-layouts  32.4 us
    all_gather x4, waiting for transfers between devices, gather(): return lax.all_gather(shard, 'dp', axis=0, tiled=True)  28.5 us
  transfers between devices with their start and end apart: 89, of which 26 were waited for; matrix products, arithmetic and copies ran while one was open for 11% of the time, Pallas kernels for 39%

profile of v4, /device:TPU:9, one launch (start us, length us, event | category | flops | bytes accessed | tf_op | source)
XLA Modules:
  0.0 991.1 jit_solution(565801993590367019)
XLA Ops:
  20.8 41.3 %all-to-all-done = bf16[8,2,32,2048]{3,2,1,0:T(8,128)(2,1)S(1)} async-done(((bf16[8,2,32,2048]{3,2,1,0:T(8,128)(2,1)}), bf16[8,2,32,2048]{3,2,1,0:T(8,128)(2,1)S(1)}, u32[]{:S(2)}, u32[]{:S(2)}) %all-to-all-start) | async-done | bytes 2097184 | tf_op jit(solution)/shard_map/all_to_all | solution.py:583
  80.4 18.2 %collective-permute-done.refs_1_.refs_3_ = bf16[256,2048]{1,0:T(8,128)(2,1)S(1)} collective-permute-done((bf16[256,2048]{1,0:T(8,128)(2,1)S(1)}, bf16[256,2048]{1,0:T(8,128)(2,1)S(1)}, u32[]{:S(2)}, u32[]{:S(2)}) %collective-permute-start) | collective-permute-done | bytes 1048608 | tf_op jit(solution)/shard_map/ppermute | solution.py:428
  106.8 26.4 %all-gather.5.cloned.1.call-done.refs_5_.refs_1_ = bf16[2048,1664]{1,0:T(8,128)(2,1)} async-done(((bf16[256,1664]{1,0:T(8,128)(2,1)}), bf16[2048,1664]{1,0:T(8,128)(2,1)}) %all-gather.5.cloned.1.call-update) | async-done | bytes 6815760 | tf_op jit(solution)/shard_map/all_gather | solution.py:484
  149.3 13.9 %shard_map.324 = (bf16[1024,512]{1,0:T(8,128)(2,1)}, f32[2,2,1024]{2,1,0:T(2,128)}) custom-call(f32[1024,1]{1,0:T(8,128)} %bitcast.95, bf16[1024,1536]{1,0:T(8,128)(2,1)} %shard_map.323.refs_1_), custom_call_target="tpu_custom_call" | custom-call | flops 858993472 | bytes 471859 | tf_op jit(solution)/shard_map/pallas_call | solution.py:44
  180.8 27.5 %collective-permute-done.13.refs_2_.refs_9_ = bf16[128,2048]{1,0:T(8,128)(2,1)} collective-permute-done((bf16[128,2048]{1,0:T(8,128)(2,1)}, bf16[128,2048]{1,0:T(8,128)(2,1)}, u32[]{:S(2)}, u32[]{:S(2)}) %collective-permute-start.13) | collective-permute-done | bytes 524320 | tf_op jit(solution)/shard_map/ppermute | solution.py:428
  210.6 11.7 %shard_map.326.refs_1_ = bf16[1024,1536]{1,0:T(8,128)(2,1)} custom-call(bf16[256,2048]{1,0:T(8,128)(2,1)} %bitcast.81, bf16[256,2048]{1,0:T(8,128)(2,1)} %collective-permute-done.11.refs_1_.refs_8_, bf16[128,2048]{1,0:T(8,128)(2,1)} %collective-permute-done.13.refs_2_.refs_9_, bf16[128,2048]{1,0:T(8,128)(2,1)} %copy-done.41, ...), custom_call_target="tpu_custom_call" | custom-call | flops 644245120 | bytes 1677721 | tf_op jit(solution)/shard_map/pallas_call | solution.py:44
  222.3 14.2 %shard_map.327 = (bf16[1024,512]{1,0:T(8,128)(2,1)}, f32[2,2,1024]{2,1,0:T(2,128)}) custom-call(f32[1024,1]{1,0:T(8,128)} %bitcast.91, bf16[1024,1536]{1,0:T(8,128)(2,1)} %shard_map.326.refs_1_), custom_call_target="tpu_custom_call" | custom-call | flops 858993472 | bytes 471859 | tf_op jit(solution)/shard_map/pallas_call | solution.py:44
  259.5 13.4 %collective-permute-done.25.refs_4_ = bf16[512,1024]{1,0:T(8,128)(2,1)S(1)} collective-permute-done((bf16[512,1024]{1,0:T(8,128)(2,1)}, bf16[512,1024]{1,0:T(8,128)(2,1)S(1)}, u32[]{:S(2)}, u32[]{:S(2)}) %collective-permute-start.25) | collective-permute-done | bytes 1048608 | tf_op jit(solution)/shard_map/ppermute | solution.py:428
  277.2 18.2 %collective-permute-done.16.refs_4_.refs_9_ = bf16[256,2048]{1,0:T(8,128)(2,1)S(1)} collective-permute-done((bf16[256,2048]{1,0:T(8,128)(2,1)}, bf16[256,2048]{1,0:T(8,128)(2,1)S(1)}, u32[]{:S(2)}, u32[]{:S(2)}) %collective-permute-start.16) | collective-permute-done | bytes 1048608 | tf_op jit(solution)/shard_map/ppermute | solution.py:428
  320.2 16.1 %shard_map.330 = (f32[1024,2048]{1,0:T(8,128)}, bf16[1024,2048]{1,0:T(8,128)(2,1)}) custom-call(bf16[256,2048]{1,0:T(8,128)(2,1)} %get-tuple-element.124.refs_0_, bf16[256,2048]{1,0:T(8,128)(2,1)} %copy-done.10, bf16[128,2048]{1,0:T(8,128)(2,1)} %copy-done.39, bf16[128,2048]{1,0:T(8,128)(2,1)} %collective-permute-done.18.refs_3_, ...), custom_call_target="tpu_custom_call" | custom-call | flops 858993472 | bytes 2936012 | tf_op jit(solution)/shard_map/pallas_call | solution.py:44
  336.3 14.6 %shard_map.331 = (bf16[512,1024]{1,0:T(8,128)(2,1)}, bf16[256,1024]{1,0:T(8,128)(2,1)}, bf16[256,1024]{1,0:T(8,128)(2,1)}, bf16[512,1024]{1,0:T(8,128)(2,1)}, bf...) custom-call(bf16[1024,2048]{1,0:T(8,128)(2,1)} %get-tuple-element.125.refs_0_.refs_10_, ...), custom_call_target="tpu_custom_call" | custom-call | flops 858993472 | bytes 1677721 | tf_op jit(solution)/shard_map/pallas_call | solution.py:44
  354.2 16.6 %collective-permute-done.21.refs_3_.refs_4_ = bf16[512,1024]{1,0:T(8,128)(2,1)S(1)} collective-permute-done((bf16[512,1024]{1,0:T(8,128)(2,1)}, bf16[512,1024]{1,0:T(8,128)(2,1)S(1)}, u32[]{:S(2)}, u32[]{:S(2)}) %collective-permute-start.21) | collective-permute-done | bytes 1048608 | tf_op jit(solution)/shard_map/ppermute | solution.py:428
  383.0 16.1 %shard_map.333 = (f32[1024,2048]{1,0:T(8,128)}, bf16[1024,2048]{1,0:T(8,128)(2,1)}) custom-call(bf16[256,2048]{1,0:T(8,128)(2,1)} %get-tuple-element.138.refs_0_.refs_5_, bf16[256,2048]{1,0:T(8,128)(2,1)} %copy-done.19, bf16[128,2048]{1,0:T(8,128)(2,1)} %copy-done.37, bf16[128,2048]{1,0:T(8,128)(2,1)} %collective-permute-done.30.refs_3_.refs_8_, ...), custom_call_target="tpu_custom_call" | custom-call | flops 858993472 | bytes 2936012 | tf_op jit(solution)/shard_map/pallas_call | solution.py:44
  399.0 14.4 %shard_map.334 = (bf16[512,1024]{1,0:T(8,128)(2,1)}, bf16[256,1024]{1,0:T(8,128)(2,1)}, bf16[256,1024]{1,0:T(8,128)(2,1)}, bf16[512,1024]{1,0:T(8,128)(2,1)}, bf...) custom-call(bf16[1024,2048]{1,0:T(8,128)(2,1)} %get-tuple-element.139.refs_0_.refs_11_, ...), custom_call_target="tpu_custom_call" | custom-call | flops 858993472 | bytes 1677721 | tf_op jit(solution)/shard_map/pallas_call | solution.py:44
  424.8 16.0 %all-to-all-start.1 = ((bf16[8,32,2048]{2,1,0:T(8,128)(2,1)}), bf16[8,32,2048]{2,1,0:T(8,128)(2,1)S(1)}, u32[]{:S(2)}, u32[]{:S(2)}) async-start(bf16[8,32,2048]{2,1,0:T(8,128)(2,1)} %bitcast.102), calls=%async_computation.1 | async-start | bytes 2097152 | tf_op jit(solution)/shard_map/all_to_all | solution.py:682
  473.2 18.5 %shard_map.337 = (bf16[1024,2048]{1,0:T(8,128)(2,1)}, f32[1,2048]{1,0:T(1,128)}) custom-call(bf16[256,2048]{1,0:T(8,128)(2,1)} %get-tuple-element.148.refs_0_, bf16[256,2048]{1,0:T(8,128)(2,1)} %copy-done.8, bf16[128,2048]{1,0:T(8,128)(2,1)} %copy-done.38, bf16[128,2048]{1,0:T(8,128)(2,1)} %collective-permute-done.38.refs_3_, bf16[256,2048]{1,0:T(8,128)(2,1)} %copy-done.7, ...), custom_call_target="tpu_custom_call" | custom-call | flops 858993472 | bytes 2097971 | tf_op jit(solution)/shard_map/pallas_call | solution.py:44
  491.7 14.4 %shard_map.338 = (bf16[512,1024]{1,0:T(8,128)(2,1)}, bf16[256,1024]{1,0:T(8,128)(2,1)}, bf16[256,1024]{1,0:T(8,128)(2,1)}, bf16[512,1024]{1,0:T(8,128)(2,1)}, bf...) custom-call(bf16[1024,2048]{1,0:T(8,128)(2,1)} %get-tuple-element.151.refs_0_.refs_10_, ...), custom_call_target="tpu_custom_call" | custom-call | flops 858993472 | bytes 1677721 | tf_op jit(solution)/shard_map/pallas_call | solution.py:44
  511.8 28.3 %all-to-all-start.2 = ((bf16[8,32,2048]{2,1,0:T(8,128)(2,1)}), bf16[8,32,2048]{2,1,0:T(8,128)(2,1)S(1)}, u32[]{:S(2)}, u32[]{:S(2)}) async-start(bf16[8,32,2048]{2,1,0:T(8,128)(2,1)} %bitcast.101), calls=%async_computation.2 | async-start | bytes 2097152 | tf_op jit(solution)/shard_map/all_to_all | solution.py:682
  546.4 18.7 %shard_map.339 = (bf16[1024,2048]{1,0:T(8,128)(2,1)}, f32[1,2048]{1,0:T(1,128)}) custom-call(bf16[256,2048]{1,0:T(8,128)(2,1)} %get-tuple-element.160.refs_0_.refs_5_, bf16[256,2048]{1,0:T(8,128)(2,1)} %collective-permute-done.43.refs_1_.refs_6_, bf16[128,2048]{1,0:T(8,128)(2,1)} %collective-permute-done.45.refs_2_.refs_7_, ...), custom_call_target="tpu_custom_call" | custom-call | flops 858993472 | bytes 2097971 | tf_op jit(solution)/shard_map/pallas_call | solution.py:44
  565.1 14.3 %shard_map.340 = (bf16[512,1024]{1,0:T(8,128)(2,1)}, bf16[256,1024]{1,0:T(8,128)(2,1)}, bf16[256,1024]{1,0:T(8,128)(2,1)}, bf16[512,1024]{1,0:T(8,128)(2,1)}, bf...) custom-call(bf16[1024,2048]{1,0:T(8,128)(2,1)} %get-tuple-element.162.refs_0_.refs_11_, ...), custom_call_target="tpu_custom_call" | custom-call | flops 858993472 | bytes 1677721 | tf_op jit(solution)/shard_map/pallas_call | solution.py:44
  590.5 24.3 %shard_map.342 = bf16[2048,2048]{1,0:T(8,128)(2,1)} custom-call(bf16[256,2048]{1,0:T(8,128)(2,1)} %get-tuple-element.148.refs_0_, bf16[256,2048]{1,0:T(8,128)(2,1)} %copy-done.8, bf16[128,2048]{1,0:T(8,128)(2,1)} %copy-done.38, bf16[128,2048]{1,0:T(8,128)(2,1)} %collective-permute-done.38.refs_3_, bf16[256,2048]{1,0:T(8,128)(2,1)} %copy-done.7, ...), custom_call_target="tpu_custom_call" | custom-call | flops 1717986944 | bytes 2516582 | tf_op jit(solution)/shard_map/pallas_call | solution.py:44
  636.7 25.5 %shard_map.343 = bf16[2048,2048]{1,0:T(8,128)(2,1)} custom-call(bf16[256,2048]{1,0:T(8,128)(2,1)} %get-tuple-element.124.refs_0_, bf16[256,2048]{1,0:T(8,128)(2,1)} %copy-done.10, bf16[128,2048]{1,0:T(8,128)(2,1)} %copy-done.39, bf16[128,2048]{1,0:T(8,128)(2,1)} %collective-permute-done.18.refs_3_, bf16[256,2048]{1,0:T(8,128)(2,1)} %copy-done.9, ...), custom_call_target="tpu_custom_call" | custom-call | flops 1717986944 | bytes 2516582 | tf_op jit(solution)/shard_map/pallas_call | solution.py:44
  684.2 14.4 %shard_map.345 = (bf16[1024,1536]{1,0:T(8,128)(2,1)}, f32[2,1,768]{2,1,0:T(1,128)}) custom-call(f32[1024,1]{1,0:T(8,128)} %bitcast.96, bf16[1024,1536]{1,0:T(8,128)(2,1)} %shard_map.323.refs_1_, bf16[1024,512]{1,0:T(8,128)(2,1)} %get-tuple-element.115.refs_0_.refs_2_.refs_10_, bf16[1024,512]{1,0:T(8,128)(2,1)} %shard_map.344.refs_3_, ...), custom_call_target="tpu_custom_call" | custom-call | flops 2147483648 | bytes 943718 | tf_op jit(solution)/shard_map/pallas_call | solution.py:44
  699.2 11.7 %shard_map.347 = (bf16[512,1024]{1,0:T(8,128)(2,1)}, bf16[256,1024]{1,0:T(8,128)(2,1)}, bf16[256,1024]{1,0:T(8,128)(2,1)}, bf16[512,1024]{1,0:T(8,128)(2,1)}, bf...) custom-call(bf16[1024,1536]{1,0:T(8,128)(2,1)} %get-tuple-element.170.refs_0_.refs_12_, ...), custom_call_target="tpu_custom_call" | custom-call | flops 644245120 | bytes 1363148 | tf_op jit(solution)/shard_map/pallas_call | solution.py:44
  729.2 16.8 %collective-permute-done.64.refs_7_ = f32[96,128]{1,0:T(8,128)S(1)} collective-permute-done((f32[96,128]{1,0:T(8,128)S(1)}, f32[96,128]{1,0:T(8,128)S(1)}, u32[]{:S(2)}, u32[]{:S(2)}) %collective-permute-start.64) | collective-permute-done | bytes 49184 | tf_op jit(solution)/shard_map/ppermute | solution.py:530
  754.9 15.5 %collective-permute-start.65 = (f32[112,128]{1,0:T(8,128)S(1)}, f32[112,128]{1,0:T(8,128)S(1)}, u32[]{:S(2)}, u32[]{:S(2)}) collective-permute-start(f32[112,128]{1,0:T(8,128)S(1)} %maximum_add_fusion.1), channel_id=1, source_target_pairs={{0,4},{4,0},{8,12},{12,8},{16,20},{20,16},{24,28},{28,24},{1,5},{5... | collective-permute-start | bytes 172040 | tf_op jit(solution)/shard_map/ppermute | solution.py:530
  793.6 14.4 %shard_map.351 = (bf16[1024,1536]{1,0:T(8,128)(2,1)}, f32[2,1,768]{2,1,0:T(1,128)}) custom-call(f32[1024,1]{1,0:T(8,128)} %bitcast.92, bf16[1024,1536]{1,0:T(8,128)(2,1)} %shard_map.326.refs_1_, bf16[1024,512]{1,0:T(8,128)(2,1)} %get-tuple-element.122.refs_0_.refs_11_.refs_2_, bf16[1024,512]{1,0:T(8,128)(2,1)} %shard_map.348.refs_12_.refs_3_, ...), custom_call_target="tpu_custom_call" | custom-call | flops 2147483648 | bytes 943718 | tf_op jit(solution)/shard_map/pallas_call | solution.py:44
  809.9 20.3 %shard_map.352 = (bf16[1088,1536]{1,0:T(8,128)(2,1)}, bf16[1088,1536]{1,0:T(8,128)(2,1)}) custom-call(s32[1]{0:T(128)} %bitcast.26.refs_0_, f32[1,1536]{1,0:T(1,128)} %bitcast.108, bf16[256,2048]{1,0:T(8,128)(2,1)} %bitcast.88, bf16[256,2048]{1,0:T(8,128)(2,1)} %copy-done.25, bf16[128,2048]{1,0:T(8,128)(2,1)} %copy-done.40, ...), custom_call_target="tpu_custom_call" | custom-call | flops 1288490240 | bytes 2097152 | tf_op jit(solution)/shard_map/pallas_call | solution.py:44
  840.2 30.7 %all-to-all-done.3.refs_4_ = bf16[8,32,2048]{2,1,0:T(8,128)(2,1)S(1)} async-done(((bf16[8,32,2048]{2,1,0:T(8,128)(2,1)}), bf16[8,32,2048]{2,1,0:T(8,128)(2,1)S(1)}, u32[]{:S(2)}, u32[]{:S(2)}) %all-to-all-start.3) | async-done | bytes 1048608 | tf_op jit(solution)/shard_map/all_to_all | solution.py:682
  871.9 11.8 %shard_map.353 = (bf16[512,1024]{1,0:T(8,128)(2,1)}, bf16[256,1024]{1,0:T(8,128)(2,1)}, bf16[256,1024]{1,0:T(8,128)(2,1)}, bf16[512,1024]{1,0:T(8,128)(2,1)}, bf...) custom-call(bf16[1024,1536]{1,0:T(8,128)(2,1)} %get-tuple-element.189.refs_13_.refs_0_, ...), custom_call_target="tpu_custom_call" | custom-call | flops 644245120 | bytes 1363148 | tf_op jit(solution)/shard_map/pallas_call | solution.py:44
  894.2 13.0 %collective-permute-done.70.refs_4_ = bf16[512,1024]{1,0:T(8,128)(2,1)S(1)} collective-permute-done((bf16[512,1024]{1,0:T(8,128)(2,1)}, bf16[512,1024]{1,0:T(8,128)(2,1)S(1)}, u32[]{:S(2)}, u32[]{:S(2)}) %collective-permute-start.70) | collective-permute-done | bytes 1048608 | tf_op jit(solution)/shard_map/ppermute | solution.py:428
  948.9 11.9 %collective-permute-done.76 = bf16[272,1536]{1,0:T(8,128)(2,1)} collective-permute-done((bf16[272,1536]{1,0:T(8,128)(2,1)}, bf16[272,1536]{1,0:T(8,128)(2,1)}, u32[]{:S(2)}, u32[]{:S(2)}) %collective-permute-start.76) | collective-permute-done | bytes 835616 | tf_op jit(solution)/shard_map/ppermute | solution.py:481
  (537 shorter events, 383.2 us)
Async XLA Ops:
  10.8 51.3 %all-to-all-start = ((bf16[8,2,32,2048]{3,2,1,0:T(8,128)(2,1)}), bf16[8,2,32,2048]{3,2,1,0:T(8,128)(2,1)S(1)}, u32[]{:S(2)}, u32[]{:S(2)}) async-start(bf16[8,2,32,2048]{3,2,1,0:T(8,128)(2,1)} %bitcast.89), calls=%async_computation | async-start | bytes 4194304 | tf_op jit(solution)/shard_map/all_to_all | solution.py:583
  16.7 116.5 %all-gather.5.cloned.1.call-start = ((), (), s32[]{:S(2)}) async-start(), calls=%async_computation.8 | async-start | bytes 7667712 | tf_op jit(solution)/shard_map/all_gather | solution.py:484
  64.3 101.2 %all-gather.7.cloned.1.call-start = ((), (), s32[]{:S(2)}) async-start(), calls=%async_computation.9 | async-start | bytes 2359296 | tf_op jit(solution)/shard_map/all_gather | solution.py:484
  66.9 248.0 %all-gather.9.cloned.1.call-start = ((), (), s32[]{:S(2)}) async-start(), calls=%async_computation.10 | async-start | bytes 9437184 | tf_op jit(solution)/shard_map/all_gather | solution.py:484
  69.7 266.6 %all-gather.11.cloned.1.call-start = ((), (), s32[]{:S(2)}) async-start(), calls=%async_computation.11 | async-start | bytes 9437184 | tf_op jit(solution)/shard_map/all_gather | solution.py:484
  101.1 73.5 %collective-permute-start.12 = (bf16[256,2048]{1,0:T(8,128)(2,1)S(1)}, bf16[256,2048]{1,0:T(8,128)(2,1)}, u32[]{:S(2)}, u32[]{:S(2)}) collective-permute-start(bf16[256,2048]{1,0:T(8,128)(2,1)S(1)} %bitcast.79), channel_id=1, source_target_pairs={{0,2},{1,3},{2,0},{3,1},{4,6},{5,7},{6,4},{7,5},{8,10},{9,11},{10,... | collective-permute-start | bytes 3145736 | tf_op jit(solution)/shard_map/ppermute | solution.py:428
  102.4 74.4 %collective-permute-start.11 = (bf16[256,2048]{1,0:T(8,128)(2,1)S(1)}, bf16[256,2048]{1,0:T(8,128)(2,1)}, u32[]{:S(2)}, u32[]{:S(2)}) collective-permute-start(bf16[256,2048]{1,0:T(8,128)(2,1)S(1)} %bitcast.80), channel_id=1, source_target_pairs={{0,1},{1,0},{2,3},{3,2},{4,5},{5,4},{6,7},{7,6},{8,9},{9,8},{10,11... | collective-permute-start | bytes 3145736 | tf_op jit(solution)/shard_map/ppermute | solution.py:428
  172.2 64.4 %collective-permute-start.4 = (bf16[512,1024]{1,0:T(8,128)(2,1)}, bf16[512,1024]{1,0:T(8,128)(2,1)S(1)}, u32[]{:S(2)}, u32[]{:S(2)}) collective-permute-start(bf16[512,1024]{1,0:T(8,128)(2,1)} %get-tuple-element.117.refs_7_), channel_id=1, source_target_pairs={{0,1},{1,0},{2,3},{3,2},{4,5},{5,4},{6,7},{7,6},{8,9},{9,8},{10,11... | collective-permute-start | bytes 3145736 | tf_op jit(solution)/shard_map/ppermute | solution.py:428
  173.4 65.6 %collective-permute-start.6 = (bf16[512,1024]{1,0:T(8,128)(2,1)}, bf16[512,1024]{1,0:T(8,128)(2,1)S(1)}, u32[]{:S(2)}, u32[]{:S(2)}) collective-permute-start(bf16[512,1024]{1,0:T(8,128)(2,1)} %get-tuple-element.120), channel_id=1, source_target_pairs={{0,2},{1,3},{2,0},{3,1},{4,6},{5,7},{6,4},{7,5},{8,10},{9,11},{10,... | collective-permute-start | bytes 3145736 | tf_op jit(solution)/shard_map/ppermute | solution.py:428
  179.6 67.7 %collective-permute-start.8 = (bf16[6,512]{1,0:T(8,128)(2,1)S(1)}, bf16[6,512]{1,0:T(8,128)(2,1)S(1)}, u32[]{:S(2)}, u32[]{:S(2)}) collective-permute-start(bf16[6,512]{1,0:T(8,128)(2,1)S(1)} %reshape.278), channel_id=1, source_target_pairs={{0,1},{1,0},{2,3},{3,2},{4,5},{5,4},{6,7},{7,6},{8,9},{9,8},{10,11... | collective-permute-start | bytes 18440 | tf_op jit(solution)/shard_map/ppermute | solution.py:428
  208.3 39.9 %collective-permute-start.9 = (bf16[6,512]{1,0:T(8,128)(2,1)S(1)}, bf16[6,512]{1,0:T(8,128)(2,1)S(1)}, u32[]{:S(2)}, u32[]{:S(2)}) collective-permute-start(bf16[6,512]{1,0:T(8,128)(2,1)S(1)} %reshape.278), channel_id=1, source_target_pairs={{0,2},{1,3},{2,0},{3,1},{4,6},{5,7},{6,4},{7,5},{8,10},{9,11},{10,... | collective-permute-start | bytes 18440 | tf_op jit(solution)/shard_map/ppermute | solution.py:428
  209.5 39.2 %collective-permute-start.10 = (bf16[6,512]{1,0:T(8,128)(2,1)S(1)}, bf16[6,512]{1,0:T(8,128)(2,1)S(1)}, u32[]{:S(2)}, u32[]{:S(2)}) collective-permute-start(bf16[6,512]{1,0:T(8,128)(2,1)S(1)} %reshape.278), channel_id=1, source_target_pairs={{0,3},{1,2},{2,1},{3,0},{4,7},{5,6},{6,5},{7,4},{8,11},{9,10},{10,... | collective-permute-start | bytes 18440 | tf_op jit(solution)/shard_map/ppermute | solution.py:428
  258.5 39.0 %collective-permute-start.15 = (bf16[256,2048]{1,0:T(8,128)(2,1)}, bf16[256,2048]{1,0:T(8,128)(2,1)S(1)}, u32[]{:S(2)}, u32[]{:S(2)}) collective-permute-start(bf16[256,2048]{1,0:T(8,128)(2,1)} %get-tuple-element.124.refs_0_), channel_id=1, source_target_pairs={{0,1},{1,0},{2,3},{3,2},{4,5},{5,4},{6,7},{7,6},{8,9},{9,8},{10,11... | collective-permute-start | bytes 3145736 | tf_op jit(solution)/shard_map/ppermute | solution.py:428
  313.5 38.8 %collective-permute-start.28 = (bf16[256,2048]{1,0:T(8,128)(2,1)}, bf16[256,2048]{1,0:T(8,128)(2,1)S(1)}, u32[]{:S(2)}, u32[]{:S(2)}) collective-permute-start(bf16[256,2048]{1,0:T(8,128)(2,1)} %get-tuple-element.138.refs_0_.refs_5_), channel_id=1, source_target_pairs={{0,2},{1,3},{2,0},{3,1},{4,6},{5,7},{6,4},{7,5},{8,10},{9,11},{10,... | collective-permute-start | bytes 3145736 | tf_op jit(solution)/shard_map/ppermute | solution.py:428
  313.8 39.0 %collective-permute-start.27 = (bf16[256,2048]{1,0:T(8,128)(2,1)}, bf16[256,2048]{1,0:T(8,128)(2,1)S(1)}, u32[]{:S(2)}, u32[]{:S(2)}) collective-permute-start(bf16[256,2048]{1,0:T(8,128)(2,1)} %get-tuple-element.138.refs_0_.refs_5_), channel_id=1, source_target_pairs={{0,1},{1,0},{2,3},{3,2},{4,5},{5,4},{6,7},{7,6},{8,9},{9,8},{10,11... | collective-permute-start | bytes 3145736 | tf_op jit(solution)/shard_map/ppermute | solution.py:428
  372.0 44.6 %collective-permute-start.22 = (bf16[256,1024]{1,0:T(8,128)(2,1)}, bf16[256,1024]{1,0:T(8,128)(2,1)}, u32[]{:S(2)}, u32[]{:S(2)}) collective-permute-start(bf16[256,1024]{1,0:T(8,128)(2,1)} %add_convert_fusion.15), channel_id=1, source_target_pairs={{0,1},{1,0},{2,3},{3,2},{4,5},{5,4},{6,7},{7,6},{8,9},{9,8},{10,11... | collective-permute-start | bytes 1572872 | tf_op jit(solution)/shard_map/ppermute | solution.py:428
  373.5 43.0 %collective-permute-start.20 = (bf16[256,1024]{1,0:T(8,128)(2,1)}, bf16[256,1024]{1,0:T(8,128)(2,1)}, u32[]{:S(2)}, u32[]{:S(2)}) collective-permute-start(bf16[256,1024]{1,0:T(8,128)(2,1)} %add_convert_fusion.16), channel_id=1, source_target_pairs={{0,2},{1,3},{2,0},{3,1},{4,6},{5,7},{6,4},{7,5},{8,10},{9,11},{10,... | collective-permute-start | bytes 1572872 | tf_op jit(solution)/shard_map/ppermute | solution.py:428
  424.8 87.0 %all-to-all-start.1 = ((bf16[8,32,2048]{2,1,0:T(8,128)(2,1)}), bf16[8,32,2048]{2,1,0:T(8,128)(2,1)S(1)}, u32[]{:S(2)}, u32[]{:S(2)}) async-start(bf16[8,32,2048]{2,1,0:T(8,128)(2,1)} %bitcast.102), calls=%async_computation.1 | async-start | bytes 2097152 | tf_op jit(solution)/shard_map/all_to_all | solution.py:682
  468.0 40.1 %collective-permute-start.44 = (bf16[256,2048]{1,0:T(8,128)(2,1)}, bf16[256,2048]{1,0:T(8,128)(2,1)S(1)}, u32[]{:S(2)}, u32[]{:S(2)}) collective-permute-start(bf16[256,2048]{1,0:T(8,128)(2,1)} %get-tuple-element.160.refs_0_.refs_5_), channel_id=1, source_target_pairs={{0,2},{1,3},{2,0},{3,1},{4,6},{5,7},{6,4},{7,5},{8,10},{9,11},{10,... | collective-permute-start | bytes 3145736 | tf_op jit(solution)/shard_map/ppermute | solution.py:428
  468.3 40.7 %collective-permute-start.43 = (bf16[256,2048]{1,0:T(8,128)(2,1)}, bf16[256,2048]{1,0:T(8,128)(2,1)}, u32[]{:S(2)}, u32[]{:S(2)}) collective-permute-start(bf16[256,2048]{1,0:T(8,128)(2,1)} %get-tuple-element.160.refs_0_.refs_5_), channel_id=1, source_target_pairs={{0,1},{1,0},{2,3},{3,2},{4,5},{5,4},{6,7},{7,6},{8,9},{9,8},{10,11... | collective-permute-start | bytes 3145736 | tf_op jit(solution)/shard_map/ppermute | solution.py:428
  511.8 77.7 %all-to-all-start.2 = ((bf16[8,32,2048]{2,1,0:T(8,128)(2,1)}), bf16[8,32,2048]{2,1,0:T(8,128)(2,1)S(1)}, u32[]{:S(2)}, u32[]{:S(2)}) async-start(bf16[8,32,2048]{2,1,0:T(8,128)(2,1)} %bitcast.101), calls=%async_computation.2 | async-start | bytes 2097152 | tf_op jit(solution)/shard_map/all_to_all | solution.py:682
  540.1 249.7 %reduce-scatter.4.cloned.1.call-start = ((), (), s32[]{:S(2)}) async-start(), calls=%async_computation.12 | async-start | bytes 9437184 | tf_op jit(solution)/shard_map/reduce_scatter | solution.py:487
  622.2 297.8 %reduce-scatter.6.cloned.1.call-start = ((), (), s32[]{:S(2)}) async-start(), calls=%async_computation.13 | async-start | bytes 9437184 | tf_op jit(solution)/shard_map/reduce_scatter | solution.py:487
  673.2 39.3 %collective-permute-start.61 = (bf16[256,2048]{1,0:T(8,128)(2,1)}, bf16[256,2048]{1,0:T(8,128)(2,1)S(1)}, u32[]{:S(2)}, u32[]{:S(2)}) collective-permute-start(bf16[256,2048]{1,0:T(8,128)(2,1)} %get-tuple-element.185.refs_0_.refs_5_), channel_id=1, source_target_pairs={{0,2},{1,3},{2,0},{3,1},{4,6},{5,7},{6,4},{7,5},{8,10},{9,11},{10,... | collective-permute-start | bytes 3145736 | tf_op jit(solution)/shard_map/ppermute | solution.py:428
  674.5 38.5 %collective-permute-start.60 = (bf16[256,2048]{1,0:T(8,128)(2,1)}, bf16[256,2048]{1,0:T(8,128)(2,1)}, u32[]{:S(2)}, u32[]{:S(2)}) collective-permute-start(bf16[256,2048]{1,0:T(8,128)(2,1)} %get-tuple-element.185.refs_0_.refs_5_), channel_id=1, source_target_pairs={{0,1},{1,0},{2,3},{3,2},{4,5},{5,4},{6,7},{7,6},{8,9},{9,8},{10,11... | collective-permute-start | bytes 3145736 | tf_op jit(solution)/shard_map/ppermute | solution.py:428
  726.1 57.1 %collective-permute-start.59 = (bf16[256,1024]{1,0:T(8,128)(2,1)}, bf16[256,1024]{1,0:T(8,128)(2,1)}, u32[]{:S(2)}, u32[]{:S(2)}) collective-permute-start(bf16[256,1024]{1,0:T(8,128)(2,1)} %add_convert_fusion.5), channel_id=1, source_target_pairs={{0,1},{1,0},{2,3},{3,2},{4,5},{5,4},{6,7},{7,6},{8,9},{9,8},{10,11... | collective-permute-start | bytes 1572872 | tf_op jit(solution)/shard_map/ppermute | solution.py:428
  727.6 55.6 %collective-permute-start.57 = (bf16[256,1024]{1,0:T(8,128)(2,1)}, bf16[256,1024]{1,0:T(8,128)(2,1)}, u32[]{:S(2)}, u32[]{:S(2)}) collective-permute-start(bf16[256,1024]{1,0:T(8,128)(2,1)} %add_convert_fusion.6), channel_id=1, source_target_pairs={{0,2},{1,3},{2,0},{3,1},{4,6},{5,7},{6,4},{7,5},{8,10},{9,11},{10,... | collective-permute-start | bytes 1572872 | tf_op jit(solution)/shard_map/ppermute | solution.py:428
  830.2 40.7 %collective-permute-start.67 = (bf16[1088,1536]{1,0:T(8,128)(2,1)}, bf16[1088,1536]{1,0:T(8,128)(2,1)}, u32[]{:S(2)}, u32[]{:S(2)}) collective-permute-start(bf16[1088,1536]{1,0:T(8,128)(2,1)} %get-tuple-element.193), channel_id=1, source_target_pairs={{0,4},{4,0},{8,12},{12,8},{16,20},{20,16},{24,28},{28,24},{1,5},{5... | collective-permute-start | bytes 10027016 | tf_op jit(solution)/shard_map/ppermute | solution.py:481
  830.7 40.2 %all-to-all-start.3 = ((bf16[8,32,2048]{2,1,0:T(8,128)(2,1)}), bf16[8,32,2048]{2,1,0:T(8,128)(2,1)S(1)}, u32[]{:S(2)}, u32[]{:S(2)}) async-start(bf16[8,32,2048]{2,1,0:T(8,128)(2,1)} %bitcast.23), calls=%async_computation.3 | async-start | bytes 2097152 | tf_op jit(solution)/shard_map/all_to_all | solution.py:682
  839.5 105.6 %reduce-scatter.8.cloned.1.call-start = ((), (), s32[]{:S(2)}) async-start(), calls=%async_computation.14 | async-start | bytes 2359296 | tf_op jit(solution)/shard_map/reduce_scatter | solution.py:487
  917.6 43.1 %collective-permute-start.76 = (bf16[272,1536]{1,0:T(8,128)(2,1)}, bf16[272,1536]{1,0:T(8,128)(2,1)}, u32[]{:S(2)}, u32[]{:S(2)}) collective-permute-start(bf16[272,1536]{1,0:T(8,128)(2,1)} %get-tuple-element.257), channel_id=1, source_target_pairs={{0,24},{4,28},{8,0},{12,4},{16,8},{20,12},{24,16},{28,20},{1,25},{... | collective-permute-start | bytes 2506760 | tf_op jit(solution)/shard_map/ppermute | solution.py:481
  927.8 49.7 %all-to-all-start.4 = ((bf16[8,32,2048]{2,1,0:T(8,128)(2,1)}), bf16[8,32,2048]{2,1,0:T(8,128)(2,1)}, u32[]{:S(2)}, u32[]{:S(2)}) async-start(bf16[8,32,2048]{2,1,0:T(8,128)(2,1)} %bitcast.94), calls=%async_computation.6 | async-start | bytes 2097152 | tf_op jit(solution)/shard_map/all_to_all | solution.py:682
  (149 other events, 2286.9 us)
Sparse Core Ops, SparseCore 0:
  64.4 68.6 all-gather.4
  135.3 30.1 all-gather.6
  167.1 78.9 all-gather.8
  247.5 80.5 all-gather.10
  622.3 97.6 reduce-scatter.3
  722.1 87.0 reduce-scatter.5
  843.2 44.5 reduce-scatter.7

commit v5 on v4

--- a/solution.py
+++ b/solution.py
@@ -17,6 +17,7 @@
 bf16 = jnp.bfloat16
 f32 = jnp.float32
 MIB = 1024 * 1024
+cost = 2.0
 TALL = ((1,), (0,))
 FLAT = ((1,), (1,))
 DEEP = ((0,), (0,))
@@ -50,7 +51,7 @@
         scratch_shapes=list(scratch),
         compiler_params=pltpu.CompilerParams(vmem_limit_bytes=60 * MIB),
         cost_estimate=pl.CostEstimate(
-            flops=int(flops) // 10, bytes_accessed=int(nbytes) // 10, transcendentals=int(exps) // 10
+            flops=int(cost * flops), bytes_accessed=int(cost * nbytes), transcendentals=int(cost * exps)
         ),
     )(*ins, *later)
 
@@ -630,9 +631,12 @@
         jnp.where(positions < slot_lengths[s], 0.0, masked_score).astype(f32)[:, None] for s in over
     ]
 
+    def near(pieces):
+        return tuple(pieces[1:2] + pieces[4:])
+
     rows_bf16 = [(slot_rows, bf16)]
     qkv, mixed, logs, terms, sums = [], [], [], [], []
-    before = ()
+    before = near(token_pieces[1])
     for s in over:
         qkv += rows_matmul(
             token_pieces[s],
@@ -654,7 +658,7 @@
     for s in over:
         first.append(first_norm(sums[s][0], arrived[s], row_vectors, before))
         first_pieces.append(tensor.gather(first[s][0]))
-        before = tuple(first_pieces[s][1:2] + first_pieces[s][4:])
+        before = near(first_pieces[s])
     hidden, active, terms, sums = [], [], [], []
     before = ()
     for s in over:
@@ -669,14 +673,14 @@
         )
         hidden.append(wide)
         active.append(narrow)
-        terms.append(terms_matmul(narrow, down_full, spans, sums[-1][1] if sums else ()))
+        terms.append(terms_matmul(narrow, down_full, spans, sums[-1][1] if sums else near(first_pieces[1])))
         sums.append(tensor.scatter(terms[s]))
         before = (terms[s][0][0],)
     second, down_pieces = [], []
     for s in over:
         second.append(second_norm(sums[s][0], first[s][1], cotangent[s], row_vectors, before))
         down_pieces.append(tensor.gather(second[s][2]))
-        before = tuple(down_pieces[s][1:2] + down_pieces[s][4:])
+        before = near(down_pieces[s])
 
     def give_back(rows):
         return lax.all_to_all(
@@ -700,11 +704,12 @@
             through_gelu,
             [hidden[s]],
             [(slot_rows, bf16), (1, f32)],
-            before if s == 0 else before + (returned_rows[0],),
+            before,
         )
         hidden_grad.append(grad)
         up_sums.append(total)
-        terms.append(terms_matmul(grad, up_full, spans, first_sums[-1][1] if first_sums else ()))
+        held = first_sums[-1][1] if first_sums else (*near(down_pieces[1]), returned_rows[0])
+        terms.append(terms_matmul(grad, up_full, spans, held))
         first_sums.append(tensor.scatter(terms[s]))
         before = (terms[s][0][0],)
     first_back = []
@@ -718,14 +723,12 @@
         return tensor.gather(first_back[s][1])
 
     grad_pieces = [back_to_first(0, before)]
-    near = grad_pieces[0][1:2] + grad_pieces[0][4:]
+    flying = (*first_sums[1][1], *near(grad_pieces[0]))
     down_terms = weight_grad(down_pieces, active, (first_back[0][0], *returned_rows))
-    down_terms = touched(down_terms, *first_sums[-1][1], *near)
-    down_sum = group.scatter(down_terms)
     up_terms = weight_grad(first_pieces, hidden_grad, (down_terms,))
-    up_terms = touched(up_terms, *first_sums[-1][2], *grad_pieces[0][2:4])
-    up_sum = group.scatter(up_terms)
-    grad_pieces += [back_to_first(s, (up_terms,)) for s in over[1:]]
+    down_sum = group.scatter(touched(down_terms, up_terms, *flying))
+    up_sum = group.scatter(touched(up_terms, *flying))
+    grad_pieces.append(back_to_first(1, (up_terms,)))
 
     def attention_in(s, later):
         return rows_matmul(
@@ -748,24 +751,24 @@
     row_grads, stages = add_up(row_grads, "tensor", (mixed_grad[0],))
     stages = [(stage,) for stage in stages] + [(), ()]
     backs = [attention_back(0, mixed_grad[0], ())]
-    terms = [terms_matmul(backs[0][0], qkv_weight, spans, stages[0])]
+    terms = [terms_matmul(backs[0][0], qkv_weight, spans, (*stages[0], *near(grad_pieces[1])))]
     sums = [tensor.scatter(terms[0])]
     mixed_grad.append(attention_in(1, (terms[0][0][0], *stages[1])))
-    mid_terms = weight_grad(grad_pieces, mixed, (mixed_grad[1], *sums[0][1]))
+    mid_terms = weight_grad(grad_pieces, mixed, (mixed_grad[1],))
     small = jnp.concatenate([row_grads, sum(up_sums).reshape(-1, 128)], axis=0)
     small, stages = add_up(small, "dp", (mixed_grad[1], mid_terms, None))
-    mid_sum = group.scatter(mid_terms)
-    token_grad = [input_grad(sums[0][0], first_back[0][0], (mid_terms,))]
+    mid_sum = group.scatter(touched(mid_terms, *sums[0][1]))
+    backs.append(attention_back(1, mixed_grad[1], (mid_terms, *sums[0][1], stages[0])))
+    token_grad = [input_grad(sums[0][0], first_back[0][0], (backs[1][0],))]
     returned_grads = [give_back(token_grad[0])]
-    backs.append(
-        attention_back(1, mixed_grad[1], (mid_terms, token_grad[0], down_sum, stages[0]))
-    )
     qkv_grad = [b[0] for b in backs]
     bias_terms = sum(b[1] for b in backs).reshape(1, -1)
-    qkv_sum, bias_sum, qkv_terms, *qkv_stage = group.weight_scatter(token_pieces, qkv_grad, bias_terms, (stages[1],))
-    terms.append(terms_matmul(qkv_grad[-1], qkv_weight, spans, (qkv_terms, *qkv_stage[0], *returned_grads)))
+    qkv_sum, bias_sum, qkv_terms, *qkv_stage = group.weight_scatter(
+        token_pieces, qkv_grad, bias_terms, (token_grad[0], down_sum, stages[1])
+    )
+    terms.append(terms_matmul(qkv_grad[-1], qkv_weight, spans, (qkv_terms,)))
     last_grad = input_grad(
-        tensor.scatter(terms[-1])[0], first_back[-1][0], (*qkv_stage[1], stages[2], up_sum)
+        tensor.scatter(terms[-1])[0], first_back[-1][0], (*qkv_stage[1], *returned_grads, stages[2])
     )
     returned_grads.append(give_back(last_grad))
 
@@ -774,6 +777,7 @@
         jnp.arange(places.shape[0], dtype=jnp.int32)
     )
     result = jnp.take(jnp.concatenate(returned_rows, axis=0), inverse, axis=0, mode="clip")
+    inverse = inverse + nothing(up_sum, mid_sum).astype(jnp.int32)
     token_gradient = jnp.take(jnp.concatenate(returned_grads, axis=0), inverse, axis=0, mode="clip")
 
     row_shares = lax.dynamic_slice_in_dim(

time: 1010 us -> 985 us (0.975)
  starting transfers between devices: 151 us -> 110 us
  waiting for transfers between devices: 294 us -> 306 us
    ppermute x5, waiting for transfers between devices: 11.9 us -> 56.1 us  [send(): return lax.ppermute(array, 'dp', pairs)]
    reduce_scatter x3, waiting for transfers between devices: 0.01 us -> 36.2 us  [scatter(): lax.psum_scatter(terms, 'dp', scatter_dimension=0, tiled=True).astype(f32)]
    all_to_all x4, waiting for transfers between devices: 35.3 us -> 0.01 us  [give_back(): lax.all_to_all(rows.reshape(groups, arrival_rows, model_width), 'dp', spl...]
    all_to_all x4, starting transfers between devices: 63.9 us -> 32.7 us  [give_back(): lax.all_to_all(rows.reshape(groups, arrival_rows, model_width), 'dp', spl...]
    ppermute x5, waiting for transfers between devices: 16.8 us -> 0.01 us  [add_up(): lax.ppermute(array, axis, [(i, i ^ bit) for i in range(size)])]
    ppermute x67, waiting for transfers between devices: 160 us -> 145 us  [swap(): lax.ppermute(array, 'tensor', [(i, i ^ bit) for i in range(self.size)])]
    unnamed x208 -> x202, local copies, waits for them, and re-layouts: 32.4 us -> 34.3 us
  transfers between devices with their start and end apart: 89 -> 89, of which waited for: 26 -> 28; matrix products, arithmetic and copies ran while one was open for 11% -> 11% of each run, Pallas kernels for 39% -> 40%
where the time goes in v5:
time: 985 us; the launch traced here: 973 us
  Pallas kernels  393 us (40%)
  waiting for transfers between devices  306 us (31%)
  starting transfers between devices  110 us (11%)
  local copies, waits for them, and re-layouts  86 us (9%)
  other arithmetic  52.2 us (5%)
  between operations  25.8 us (3%)
    pallas_call x32, Pallas kernels, launch(): pl.pallas_call(run, grid=grid, in_specs=list(in_specs) + [pl.BlockSpec(me...  393 us
    ppermute x67, waiting for transfers between devices, swap(): lax.ppermute(array, 'tensor', [(i, i ^ bit) for i in range(self.size)])  145 us
    ppermute x5, waiting for transfers between devices, send(): return lax.ppermute(array, 'dp', pairs)  56.1 us
    ppermute x67, starting transfers between devices, swap(): lax.ppermute(array, 'tensor', [(i, i ^ bit) for i in range(self.size)])  50.5 us
    all_to_all x1, waiting for transfers between devices, local(): came = lax.all_to_all(sent, 'dp', split_axis=0, concat_axis=0, tiled=True)  41.3 us
    reduce_scatter x3, waiting for transfers between devices, scatter(): lax.psum_scatter(terms, 'dp', scatter_dimension=0, tiled=True).astype(f32)  36.2 us
    unnamed x202, local copies, waits for them, and re-layouts  34.3 us
    all_to_all x4, starting transfers between devices, give_back(): lax.all_to_all(rows.reshape(groups, arrival_rows, model_width), 'dp', spl...  32.7 us
  transfers between devices with their start and end apart: 89, of which 28 were waited for; matrix products, arithmetic and copies ran while one was open for 11% of the time, Pallas kernels for 40%

profile of v5, /device:TPU:9, one launch (start us, length us, event | category | flops | bytes accessed | tf_op | source)
XLA Modules:
  0.0 972.6 jit_solution(11286290836998548096)
XLA Ops:
  20.8 41.3 %all-to-all-done = bf16[8,2,32,2048]{3,2,1,0:T(8,128)(2,1)S(1)} async-done(((bf16[8,2,32,2048]{3,2,1,0:T(8,128)(2,1)}), bf16[8,2,32,2048]{3,2,1,0:T(8,128)(2,1)S(1)}, u32[]{:S(2)}, u32[]{:S(2)}) %all-to-all-start) | async-done | bytes 2097184 | tf_op jit(solution)/shard_map/all_to_all | solution.py:584
  76.6 21.9 %collective-permute-done.refs_1_.refs_3_ = bf16[256,2048]{1,0:T(8,128)(2,1)S(1)} collective-permute-done((bf16[256,2048]{1,0:T(8,128)(2,1)S(1)}, bf16[256,2048]{1,0:T(8,128)(2,1)S(1)}, u32[]{:S(2)}, u32[]{:S(2)}) %collective-permute-start) | collective-permute-done | bytes 1048608 | tf_op jit(solution)/shard_map/ppermute | solution.py:429
  111.9 13.7 %collective-permute-done.5.refs_8_.refs_4_.refs_11_ = bf16[256,2048]{1,0:T(8,128)(2,1)} collective-permute-done((bf16[256,2048]{1,0:T(8,128)(2,1)S(1)}, bf16[256,2048]{1,0:T(8,128)(2,1)}, u32[]{:S(2)}, u32[]{:S(2)}) %collective-permute-start.5) | collective-permute-done | bytes 1048608 | tf_op jit(solution)/shard_map/ppermute | solution.py:429
  138.4 11.7 %shard_map.323.refs_1_ = bf16[1024,1536]{1,0:T(8,128)(2,1)} custom-call(bf16[256,2048]{1,0:T(8,128)(2,1)} %bitcast.94, bf16[256,2048]{1,0:T(8,128)(2,1)} %copy-done.57, bf16[128,2048]{1,0:T(8,128)(2,1)} %collective-permute-done.2.refs_2_.refs_4_, bf16[128,2048]{1,0:T(8,128)(2,1)} %collective-permute-done.3.refs_3_.refs_5_, ...), custom_call_target="tpu_custom_call" | custom-call | flops 12884901888 | bytes 33554432 | tf_op jit(solution)/shard_map/pallas_call | solution.py:45
  150.0 13.9 %shard_map.324 = (bf16[1024,512]{1,0:T(8,128)(2,1)}, f32[2,2,1024]{2,1,0:T(2,128)}) custom-call(f32[1024,1]{1,0:T(8,128)} %bitcast.107, bf16[1024,1536]{1,0:T(8,128)(2,1)} %shard_map.323.refs_1_), custom_call_target="tpu_custom_call" | custom-call | flops 17179869184 | bytes 9437184 | tf_op jit(solution)/shard_map/pallas_call | solution.py:45
  174.6 12.4 %shard_map.326.refs_1_ = bf16[1024,1536]{1,0:T(8,128)(2,1)} custom-call(bf16[256,2048]{1,0:T(8,128)(2,1)} %bitcast.89, bf16[256,2048]{1,0:T(8,128)(2,1)} %collective-permute-done.4.refs_7_.refs_1_.refs_8_, bf16[128,2048]{1,0:T(8,128)(2,1)} %collective-permute-done.13.refs_2_.refs_9_, bf16[128,2048]{1,0:T(8,128)(2,1)} %collective-permute-done.14.refs_3_.refs_10_, ...), custom_call_target="tpu_custom_call" | custom-call | flops 12884901888 | bytes 33554432 | tf_op jit(solution)/shard_map/pallas_call | solution.py:45
  187.0 14.3 %shard_map.327 = (bf16[1024,512]{1,0:T(8,128)(2,1)}, f32[2,2,1024]{2,1,0:T(2,128)}) custom-call(f32[1024,1]{1,0:T(8,128)} %bitcast.105, bf16[1024,1536]{1,0:T(8,128)(2,1)} %shard_map.326.refs_1_), custom_call_target="tpu_custom_call" | custom-call | flops 17179869184 | bytes 9437184 | tf_op jit(solution)/shard_map/pallas_call | solution.py:45
  220.7 15.6 %collective-permute-done.21.refs_4_ = bf16[512,1024]{1,0:T(8,128)(2,1)S(1)} collective-permute-done((bf16[512,1024]{1,0:T(8,128)(2,1)}, bf16[512,1024]{1,0:T(8,128)(2,1)S(1)}, u32[]{:S(2)}, u32[]{:S(2)}) %collective-permute-start.21) | collective-permute-done | bytes 1048608 | tf_op jit(solution)/shard_map/ppermute | solution.py:429
  239.5 19.2 %collective-permute-done.16.refs_4_.refs_9_ = bf16[256,2048]{1,0:T(8,128)(2,1)S(1)} collective-permute-done((bf16[256,2048]{1,0:T(8,128)(2,1)}, bf16[256,2048]{1,0:T(8,128)(2,1)S(1)}, u32[]{:S(2)}, u32[]{:S(2)}) %collective-permute-start.16) | collective-permute-done | bytes 1048608 | tf_op jit(solution)/shard_map/ppermute | solution.py:429
  261.9 9.5 collective-permute-done.22.refs_5_
  282.6 16.1 %shard_map.330 = (f32[1024,2048]{1,0:T(8,128)}, bf16[1024,2048]{1,0:T(8,128)(2,1)}) custom-call(bf16[256,2048]{1,0:T(8,128)(2,1)} %get-tuple-element.124.refs_0_, bf16[256,2048]{1,0:T(8,128)(2,1)} %copy-done.29, bf16[128,2048]{1,0:T(8,128)(2,1)} %collective-permute-done.17.refs_2_, bf16[128,2048]{1,0:T(8,128)(2,1)} %collective-permute-done.18.refs_3_, ...), custom_call_target="tpu_custom_call" | custom-call | flops 17179869184 | bytes 58720256 | tf_op jit(solution)/shard_map/pallas_call | solution.py:45
  306.1 22.0 %all-gather.11.cloned.1.call-done.refs_1_.refs_5_ = bf16[2048,2048]{1,0:T(8,128)(2,1)} async-done(((bf16[256,2048]{1,0:T(8,128)(2,1)}), bf16[2048,2048]{1,0:T(8,128)(2,1)}) %all-gather.11.cloned.1.call-update) | async-done | bytes 8388624 | tf_op jit(solution)/shard_map/all_gather | solution.py:485
  328.1 23.9 %shard_map.332 = (bf16[512,1024]{1,0:T(8,128)(2,1)}, bf16[256,1024]{1,0:T(8,128)(2,1)}, bf16[256,1024]{1,0:T(8,128)(2,1)}, bf16[512,1024]{1,0:T(8,128)(2,1)}, bf...) custom-call(bf16[1024,2048]{1,0:T(8,128)(2,1)} %get-tuple-element.125.refs_0_.refs_10_, ...), custom_call_target="tpu_custom_call" | custom-call | flops 17179869184 | bytes 33554432 | tf_op jit(solution)/shard_map/pallas_call | solution.py:45
  354.6 16.1 %shard_map.333 = (f32[1024,2048]{1,0:T(8,128)}, bf16[1024,2048]{1,0:T(8,128)(2,1)}) custom-call(bf16[256,2048]{1,0:T(8,128)(2,1)} %get-tuple-element.131.refs_0_.refs_5_, bf16[256,2048]{1,0:T(8,128)(2,1)} %copy-done.58, bf16[128,2048]{1,0:T(8,128)(2,1)} %collective-permute-done.29.refs_2_.refs_7_, bf16[128,2048]{1,0:T(8,128)(2,1)} %collective-permute-done.30.refs_3_.refs_8_, ...), custom_call_target="tpu_custom_call" | custom-call | flops 17179869184 | bytes 58720256 | tf_op jit(solution)/shard_map/pallas_call | solution.py:45
  381.6 14.2 %shard_map.334 = (bf16[512,1024]{1,0:T(8,128)(2,1)}, bf16[256,1024]{1,0:T(8,128)(2,1)}, bf16[256,1024]{1,0:T(8,128)(2,1)}, bf16[512,1024]{1,0:T(8,128)(2,1)}, bf...) custom-call(bf16[1024,2048]{1,0:T(8,128)(2,1)} %get-tuple-element.139.refs_0_.refs_11_, ...), custom_call_target="tpu_custom_call" | custom-call | flops 17179869184 | bytes 33554432 | tf_op jit(solution)/shard_map/pallas_call | solution.py:45
  409.6 9.4 collective-permute-done.33.refs_4_
  422.9 18.6 %collective-permute-done.36.refs_10_.refs_4_ = bf16[256,2048]{1,0:T(8,128)(2,1)S(1)} collective-permute-done((bf16[256,2048]{1,0:T(8,128)(2,1)}, bf16[256,2048]{1,0:T(8,128)(2,1)S(1)}, u32[]{:S(2)}, u32[]{:S(2)}) %collective-permute-start.36) | collective-permute-done | bytes 1048608 | tf_op jit(solution)/shard_map/ppermute | solution.py:429
  443.8 11.6 %all-to-all-start.1 = ((bf16[8,32,2048]{2,1,0:T(8,128)(2,1)}), bf16[8,32,2048]{2,1,0:T(8,128)(2,1)S(1)}, u32[]{:S(2)}, u32[]{:S(2)}) async-start(bf16[8,32,2048]{2,1,0:T(8,128)(2,1)} %bitcast.103), calls=%async_computation.1 | async-start | bytes 2097152 | tf_op jit(solution)/shard_map/all_to_all | solution.py:686
  465.5 18.5 %shard_map.337 = (bf16[1024,2048]{1,0:T(8,128)(2,1)}, f32[1,2048]{1,0:T(1,128)}) custom-call(bf16[256,2048]{1,0:T(8,128)(2,1)} %get-tuple-element.148.refs_0_, bf16[256,2048]{1,0:T(8,128)(2,1)} %copy-done.31, bf16[128,2048]{1,0:T(8,128)(2,1)} %collective-permute-done.37.refs_2_, bf16[128,2048]{1,0:T(8,128)(2,1)} %copy-done.76, bf16[256,2048]{1,0:T(8,128)(2,1)} %copy-done.30, ...), custom_call_target="tpu_custom_call" | custom-call | flops 17179869184 | bytes 41959424 | tf_op jit(solution)/shard_map/pallas_call | solution.py:45
  499.2 14.7 %shard_map.338 = (bf16[512,1024]{1,0:T(8,128)(2,1)}, bf16[256,1024]{1,0:T(8,128)(2,1)}, bf16[256,1024]{1,0:T(8,128)(2,1)}, bf16[512,1024]{1,0:T(8,128)(2,1)}, bf...) custom-call(bf16[1024,2048]{1,0:T(8,128)(2,1)} %get-tuple-element.151.refs_0_.refs_10_, ...), custom_call_target="tpu_custom_call" | custom-call | flops 17179869184 | bytes 33554432 | tf_op jit(solution)/shard_map/pallas_call | solution.py:45
  515.8 18.6 %shard_map.339 = (bf16[1024,2048]{1,0:T(8,128)(2,1)}, f32[1,2048]{1,0:T(1,128)}) custom-call(bf16[256,2048]{1,0:T(8,128)(2,1)} %get-tuple-element.152.refs_0_.refs_5_, bf16[256,2048]{1,0:T(8,128)(2,1)} %copy-done.59, bf16[128,2048]{1,0:T(8,128)(2,1)} %collective-permute-done.45.refs_2_.refs_7_, bf16[128,2048]{1,0:T(8,128)(2,1)} %collective-permute-done.46.refs_3_.refs_8_, ...), custom_call_target="tpu_custom_call" | custom-call | flops 17179869184 | bytes 41959424 | tf_op jit(solution)/shard_map/pallas_call | solution.py:45
  543.9 14.2 %shard_map.340 = (bf16[512,1024]{1,0:T(8,128)(2,1)}, bf16[256,1024]{1,0:T(8,128)(2,1)}, bf16[256,1024]{1,0:T(8,128)(2,1)}, bf16[512,1024]{1,0:T(8,128)(2,1)}, bf...) custom-call(bf16[1024,2048]{1,0:T(8,128)(2,1)} %get-tuple-element.162.refs_0_.refs_11_, ...), custom_call_target="tpu_custom_call" | custom-call | flops 17179869184 | bytes 33554432 | tf_op jit(solution)/shard_map/pallas_call | solution.py:45
  568.4 24.3 %shard_map.342.refs_12_ = bf16[2048,2048]{1,0:T(8,128)(2,1)} custom-call(bf16[256,2048]{1,0:T(8,128)(2,1)} %get-tuple-element.148.refs_0_, bf16[256,2048]{1,0:T(8,128)(2,1)} %copy-done.31, bf16[128,2048]{1,0:T(8,128)(2,1)} %collective-permute-done.37.refs_2_, bf16[128,2048]{1,0:T(8,128)(2,1)} %copy-done.76, bf16[256,2048]{1,0:T(8,128)(2,1)} %copy-done.30, ...), custom_call_target="tpu_custom_call" | custom-call | flops 34359738368 | bytes 50331648 | tf_op jit(solution)/shard_map/pallas_call | solution.py:45
  592.7 24.3 %shard_map.343.refs_6_.refs_10_ = bf16[2048,2048]{1,0:T(8,128)(2,1)} custom-call(bf16[256,2048]{1,0:T(8,128)(2,1)} %get-tuple-element.124.refs_0_, bf16[256,2048]{1,0:T(8,128)(2,1)} %copy-done.29, bf16[128,2048]{1,0:T(8,128)(2,1)} %collective-permute-done.17.refs_2_, bf16[128,2048]{1,0:T(8,128)(2,1)} %collective-permute-done.18.refs_3_, ...), custom_call_target="tpu_custom_call" | custom-call | flops 34359738368 | bytes 50331648 | tf_op jit(solution)/shard_map/pallas_call | solution.py:45
  659.2 14.5 %shard_map.345 = (bf16[1024,1536]{1,0:T(8,128)(2,1)}, f32[2,1,768]{2,1,0:T(1,128)}) custom-call(f32[1024,1]{1,0:T(8,128)} %bitcast.108, bf16[1024,1536]{1,0:T(8,128)(2,1)} %shard_map.323.refs_1_, bf16[1024,512]{1,0:T(8,128)(2,1)} %get-tuple-element.115.refs_0_.refs_2_.refs_10_, bf16[1024,512]{1,0:T(8,128)(2,1)} %shard_map.344.refs_3_, ...), custom_call_target="tpu_custom_call" | custom-call | flops 42949672960 | bytes 18874368 | tf_op jit(solution)/shard_map/pallas_call | solution.py:45
  676.9 11.6 %shard_map.347 = (bf16[512,1024]{1,0:T(8,128)(2,1)}, bf16[256,1024]{1,0:T(8,128)(2,1)}, bf16[256,1024]{1,0:T(8,128)(2,1)}, bf16[512,1024]{1,0:T(8,128)(2,1)}, bf...) custom-call(bf16[1024,1536]{1,0:T(8,128)(2,1)} %get-tuple-element.167.refs_0_.refs_12_, ...), custom_call_target="tpu_custom_call" | custom-call | flops 12884901888 | bytes 27262976 | tf_op jit(solution)/shard_map/pallas_call | solution.py:45
  698.3 10.8 %shard_map.349.refs_5_ = bf16[2048,512]{1,0:T(8,128)(2,1)} custom-call(bf16[256,2048]{1,0:T(8,128)(2,1)} %get-tuple-element.164.refs_0_, bf16[256,2048]{1,0:T(8,128)(2,1)} %collective-permute-done.47.refs_1_, bf16[128,2048]{1,0:T(8,128)(2,1)} %collective-permute-done.49.refs_2_, bf16[128,2048]{1,0:T(8,128)(2,1)} %collective-permute-done.50.refs_3_, ...), custom_call_target="tpu_custom_call" | custom-call | flops 8589934592 | bytes 25165824 | tf_op jit(solution)/shard_map/pallas_call | solution.py:45
  732.2 14.5 %shard_map.350 = (bf16[1024,1536]{1,0:T(8,128)(2,1)}, f32[2,1,768]{2,1,0:T(1,128)}) custom-call(f32[1024,1]{1,0:T(8,128)} %bitcast.106, bf16[1024,1536]{1,0:T(8,128)(2,1)} %shard_map.326.refs_1_, bf16[1024,512]{1,0:T(8,128)(2,1)} %get-tuple-element.122.refs_0_.refs_11_.refs_2_, bf16[1024,512]{1,0:T(8,128)(2,1)} %shard_map.348.refs_12_.refs_3_, ...), custom_call_target="tpu_custom_call" | custom-call | flops 42949672960 | bytes 18874368 | tf_op jit(solution)/shard_map/pallas_call | solution.py:45
  757.1 20.2 %shard_map.352 = (bf16[1088,1536]{1,0:T(8,128)(2,1)}, bf16[1088,1536]{1,0:T(8,128)(2,1)}) custom-call(s32[1]{0:T(128)} %bitcast.24.refs_0_, f32[1,1536]{1,0:T(1,128)} %bitcast.116, bf16[256,2048]{1,0:T(8,128)(2,1)} %bitcast.96, bf16[256,2048]{1,0:T(8,128)(2,1)} %copy-done.57, bf16[128,2048]{1,0:T(8,128)(2,1)} %collective-permute-done.2.refs_2_.refs_4_, ...), custom_call_target="tpu_custom_call" | custom-call | flops 25769803776 | bytes 41943040 | tf_op jit(solution)/shard_map/pallas_call | solution.py:45
  778.2 11.6 %shard_map.353 = (bf16[512,1024]{1,0:T(8,128)(2,1)}, bf16[256,1024]{1,0:T(8,128)(2,1)}, bf16[256,1024]{1,0:T(8,128)(2,1)}, bf16[512,1024]{1,0:T(8,128)(2,1)}, bf...) custom-call(bf16[1024,1536]{1,0:T(8,128)(2,1)} %get-tuple-element.189.refs_7_.refs_13_.refs_0_, ...), custom_call_target="tpu_custom_call" | custom-call | flops 12884901888 | bytes 27262976 | tf_op jit(solution)/shard_map/pallas_call | solution.py:45
  821.2 53.3 %collective-permute-done.72.refs_7_ = bf16[272,1536]{1,0:T(8,128)(2,1)} collective-permute-done((bf16[272,1536]{1,0:T(8,128)(2,1)}, bf16[272,1536]{1,0:T(8,128)(2,1)}, u32[]{:S(2)}, u32[]{:S(2)}) %collective-permute-start.72) | collective-permute-done | bytes 835616 | tf_op jit(solution)/shard_map/ppermute | solution.py:482
  904.2 36.2 %reduce-scatter.6.cloned.1.call-done = bf16[256,2048]{1,0:T(8,128)(2,1)} async-done(((bf16[2048,2048]{1,0:T(8,128)(2,1)}), bf16[256,2048]{1,0:T(8,128)(2,1)}) %reduce-scatter.6.cloned.1.call-update) | async-done | bytes 1048592 | tf_op jit(solution)/shard_map/reduce_scatter | solution.py:488
  (535 shorter events, 353.8 us)
Async XLA Ops:
  10.8 51.3 %all-to-all-start = ((bf16[8,2,32,2048]{3,2,1,0:T(8,128)(2,1)}), bf16[8,2,32,2048]{3,2,1,0:T(8,128)(2,1)S(1)}, u32[]{:S(2)}, u32[]{:S(2)}) async-start(bf16[8,2,32,2048]{3,2,1,0:T(8,128)(2,1)} %bitcast.84), calls=%async_computation | async-start | bytes 4194304 | tf_op jit(solution)/shard_map/all_to_all | solution.py:584
  16.7 116.5 %all-gather.5.cloned.1.call-start = ((), (), s32[]{:S(2)}) async-start(), calls=%async_computation.8 | async-start | bytes 7667712 | tf_op jit(solution)/shard_map/all_gather | solution.py:485
  64.3 101.2 %all-gather.7.cloned.1.call-start = ((), (), s32[]{:S(2)}) async-start(), calls=%async_computation.9 | async-start | bytes 2359296 | tf_op jit(solution)/shard_map/all_gather | solution.py:485
  66.9 212.1 %all-gather.9.cloned.1.call-start = ((), (), s32[]{:S(2)}) async-start(), calls=%async_computation.10 | async-start | bytes 9437184 | tf_op jit(solution)/shard_map/all_gather | solution.py:485
  69.7 258.4 %all-gather.11.cloned.1.call-start = ((), (), s32[]{:S(2)}) async-start(), calls=%async_computation.11 | async-start | bytes 9437184 | tf_op jit(solution)/shard_map/all_gather | solution.py:485
  126.7 45.4 %collective-permute-start.13 = (bf16[128,2048]{1,0:T(8,128)(2,1)S(1)}, bf16[128,2048]{1,0:T(8,128)(2,1)}, u32[]{:S(2)}, u32[]{:S(2)}) collective-permute-start(bf16[128,2048]{1,0:T(8,128)(2,1)S(1)} %slice.434), channel_id=1, source_target_pairs={{0,1},{1,0},{2,3},{3,2},{4,5},{5,4},{6,7},{7,6},{8,9},{9,8},{10,11... | collective-permute-start | bytes 1572872 | tf_op jit(solution)/shard_map/ppermute | solution.py:429
  128.2 45.3 %collective-permute-start.14 = (bf16[128,2048]{1,0:T(8,128)(2,1)S(1)}, bf16[128,2048]{1,0:T(8,128)(2,1)}, u32[]{:S(2)}, u32[]{:S(2)}) collective-permute-start(bf16[128,2048]{1,0:T(8,128)(2,1)S(1)} %slice.435), channel_id=1, source_target_pairs={{0,2},{1,3},{2,0},{3,1},{4,6},{5,7},{6,4},{7,5},{8,10},{9,11},{10,... | collective-permute-start | bytes 1572872 | tf_op jit(solution)/shard_map/ppermute | solution.py:429
  135.5 75.2 %collective-permute-start.10 = (bf16[6,512]{1,0:T(8,128)(2,1)S(1)}, bf16[6,512]{1,0:T(8,128)(2,1)S(1)}, u32[]{:S(2)}, u32[]{:S(2)}) collective-permute-start(bf16[6,512]{1,0:T(8,128)(2,1)S(1)} %reshape.279), channel_id=1, source_target_pairs={{0,1},{1,0},{2,3},{3,2},{4,5},{5,4},{6,7},{7,6},{8,9},{9,8},{10,11... | collective-permute-start | bytes 18440 | tf_op jit(solution)/shard_map/ppermute | solution.py:429
  136.9 75.2 %collective-permute-start.11 = (bf16[6,512]{1,0:T(8,128)(2,1)S(1)}, bf16[6,512]{1,0:T(8,128)(2,1)S(1)}, u32[]{:S(2)}, u32[]{:S(2)}) collective-permute-start(bf16[6,512]{1,0:T(8,128)(2,1)S(1)} %reshape.279), channel_id=1, source_target_pairs={{0,2},{1,3},{2,0},{3,1},{4,6},{5,7},{6,4},{7,5},{8,10},{9,11},{10,... | collective-permute-start | bytes 18440 | tf_op jit(solution)/shard_map/ppermute | solution.py:429
  138.1 75.4 %collective-permute-start.12 = (bf16[6,512]{1,0:T(8,128)(2,1)S(1)}, bf16[6,512]{1,0:T(8,128)(2,1)S(1)}, u32[]{:S(2)}, u32[]{:S(2)}) collective-permute-start(bf16[6,512]{1,0:T(8,128)(2,1)S(1)} %reshape.279), channel_id=1, source_target_pairs={{0,3},{1,2},{2,1},{3,0},{4,7},{5,6},{6,5},{7,4},{8,11},{9,10},{10,... | collective-permute-start | bytes 18440 | tf_op jit(solution)/shard_map/ppermute | solution.py:429
  220.4 38.3 %collective-permute-start.16 = (bf16[256,2048]{1,0:T(8,128)(2,1)}, bf16[256,2048]{1,0:T(8,128)(2,1)S(1)}, u32[]{:S(2)}, u32[]{:S(2)}) collective-permute-start(bf16[256,2048]{1,0:T(8,128)(2,1)} %get-tuple-element.124.refs_0_), channel_id=1, source_target_pairs={{0,2},{1,3},{2,0},{3,1},{4,6},{5,7},{6,4},{7,5},{8,10},{9,11},{10,... | collective-permute-start | bytes 3145736 | tf_op jit(solution)/shard_map/ppermute | solution.py:429
  220.7 39.3 %collective-permute-start.15 = (bf16[256,2048]{1,0:T(8,128)(2,1)}, bf16[256,2048]{1,0:T(8,128)(2,1)S(1)}, u32[]{:S(2)}, u32[]{:S(2)}) collective-permute-start(bf16[256,2048]{1,0:T(8,128)(2,1)} %get-tuple-element.124.refs_0_), channel_id=1, source_target_pairs={{0,1},{1,0},{2,3},{3,2},{4,5},{5,4},{6,7},{7,6},{8,9},{9,8},{10,11... | collective-permute-start | bytes 3145736 | tf_op jit(solution)/shard_map/ppermute | solution.py:429
  303.9 50.7 %collective-permute-start.29 = (bf16[128,2048]{1,0:T(8,128)(2,1)S(1)}, bf16[128,2048]{1,0:T(8,128)(2,1)}, u32[]{:S(2)}, u32[]{:S(2)}) collective-permute-start(bf16[128,2048]{1,0:T(8,128)(2,1)S(1)} %slice.445), channel_id=1, source_target_pairs={{0,1},{1,0},{2,3},{3,2},{4,5},{5,4},{6,7},{7,6},{8,9},{9,8},{10,11... | collective-permute-start | bytes 1572872 | tf_op jit(solution)/shard_map/ppermute | solution.py:429
  306.0 48.6 %collective-permute-start.30 = (bf16[128,2048]{1,0:T(8,128)(2,1)}, bf16[128,2048]{1,0:T(8,128)(2,1)}, u32[]{:S(2)}, u32[]{:S(2)}) collective-permute-start(bf16[128,2048]{1,0:T(8,128)(2,1)} %slice.446), channel_id=1, source_target_pairs={{0,2},{1,3},{2,0},{3,1},{4,6},{5,7},{6,4},{7,5},{8,10},{9,11},{10,... | collective-permute-start | bytes 1572872 | tf_op jit(solution)/shard_map/ppermute | solution.py:429
  443.8 46.2 %all-to-all-start.1 = ((bf16[8,32,2048]{2,1,0:T(8,128)(2,1)}), bf16[8,32,2048]{2,1,0:T(8,128)(2,1)S(1)}, u32[]{:S(2)}, u32[]{:S(2)}) async-start(bf16[8,32,2048]{2,1,0:T(8,128)(2,1)} %bitcast.103), calls=%async_computation.1 | async-start | bytes 2097152 | tf_op jit(solution)/shard_map/all_to_all | solution.py:686
  490.0 77.4 %all-to-all-start.2 = ((bf16[8,32,2048]{2,1,0:T(8,128)(2,1)}), bf16[8,32,2048]{2,1,0:T(8,128)(2,1)S(1)}, u32[]{:S(2)}, u32[]{:S(2)}) async-start(bf16[8,32,2048]{2,1,0:T(8,128)(2,1)} %bitcast.17), calls=%async_computation.2 | async-start | bytes 2097152 | tf_op jit(solution)/shard_map/all_to_all | solution.py:686
  499.2 254.2 %reduce-scatter.4.cloned.1.call-start = ((), (), s32[]{:S(2)}) async-start(), calls=%async_computation.12 | async-start | bytes 9437184 | tf_op jit(solution)/shard_map/reduce_scatter | solution.py:488
  558.1 62.0 %collective-permute-start.53 = (bf16[512,1024]{1,0:T(8,128)(2,1)}, bf16[512,1024]{1,0:T(8,128)(2,1)S(1)}, u32[]{:S(2)}, u32[]{:S(2)}) collective-permute-start(bf16[512,1024]{1,0:T(8,128)(2,1)} %get-tuple-element.172), channel_id=1, source_target_pairs={{0,2},{1,3},{2,0},{3,1},{4,6},{5,7},{6,4},{7,5},{8,10},{9,11},{10,... | collective-permute-start | bytes 3145736 | tf_op jit(solution)/shard_map/ppermute | solution.py:429
  558.9 60.0 %collective-permute-start.51 = (bf16[512,1024]{1,0:T(8,128)(2,1)}, bf16[512,1024]{1,0:T(8,128)(2,1)S(1)}, u32[]{:S(2)}, u32[]{:S(2)}) collective-permute-start(bf16[512,1024]{1,0:T(8,128)(2,1)} %get-tuple-element.163.refs_10_), channel_id=1, source_target_pairs={{0,1},{1,0},{2,3},{3,2},{4,5},{5,4},{6,7},{7,6},{8,9},{9,8},{10,11... | collective-permute-start | bytes 3145736 | tf_op jit(solution)/shard_map/ppermute | solution.py:429
  565.5 57.7 %collective-permute-start.48 = (bf16[256,2048]{1,0:T(8,128)(2,1)}, bf16[256,2048]{1,0:T(8,128)(2,1)}, u32[]{:S(2)}, u32[]{:S(2)}) collective-permute-start(bf16[256,2048]{1,0:T(8,128)(2,1)} %get-tuple-element.164.refs_0_), channel_id=1, source_target_pairs={{0,2},{1,3},{2,0},{3,1},{4,6},{5,7},{6,4},{7,5},{8,10},{9,11},{10,... | collective-permute-start | bytes 3145736 | tf_op jit(solution)/shard_map/ppermute | solution.py:429
  566.3 55.1 %collective-permute-start.47 = (bf16[256,2048]{1,0:T(8,128)(2,1)}, bf16[256,2048]{1,0:T(8,128)(2,1)}, u32[]{:S(2)}, u32[]{:S(2)}) collective-permute-start(bf16[256,2048]{1,0:T(8,128)(2,1)} %get-tuple-element.164.refs_0_), channel_id=1, source_target_pairs={{0,1},{1,0},{2,3},{3,2},{4,5},{5,4},{6,7},{7,6},{8,9},{9,8},{10,11... | collective-permute-start | bytes 3145736 | tf_op jit(solution)/shard_map/ppermute | solution.py:429
  626.4 274.6 %reduce-scatter.8.cloned.1.call-start = ((), (), s32[]{:S(2)}) async-start(), calls=%async_computation.14 | async-start | bytes 2359296 | tf_op jit(solution)/shard_map/reduce_scatter | solution.py:488
  713.7 226.7 %reduce-scatter.6.cloned.1.call-start = ((), (), s32[]{:S(2)}) async-start(), calls=%async_computation.13 | async-start | bytes 9437184 | tf_op jit(solution)/shard_map/reduce_scatter | solution.py:488
  792.1 96.9 %all-to-all-start.3 = ((bf16[8,32,2048]{2,1,0:T(8,128)(2,1)}), bf16[8,32,2048]{2,1,0:T(8,128)(2,1)S(1)}, u32[]{:S(2)}, u32[]{:S(2)}) async-start(bf16[8,32,2048]{2,1,0:T(8,128)(2,1)} %bitcast.97), calls=%async_computation.3 | async-start | bytes 2097152 | tf_op jit(solution)/shard_map/all_to_all | solution.py:686
  800.6 73.9 %collective-permute-start.72 = (bf16[272,1536]{1,0:T(8,128)(2,1)}, bf16[272,1536]{1,0:T(8,128)(2,1)}, u32[]{:S(2)}, u32[]{:S(2)}) collective-permute-start(bf16[272,1536]{1,0:T(8,128)(2,1)} %add_convert_fusion.2), channel_id=1, source_target_pairs={{0,8},{4,12},{8,16},{12,20},{1,9},{5,13},{9,17},{13,21},{2,10},{6,... | collective-permute-start | bytes 2506760 | tf_op jit(solution)/shard_map/ppermute | solution.py:482
  803.7 73.7 %collective-permute-start.73 = (bf16[272,1536]{1,0:T(8,128)(2,1)}, bf16[272,1536]{1,0:T(8,128)(2,1)}, u32[]{:S(2)}, u32[]{:S(2)}) collective-permute-start(bf16[272,1536]{1,0:T(8,128)(2,1)} %add_convert_fusion.2), channel_id=1, source_target_pairs={{24,16},{28,20},{16,8},{20,12},{25,17},{29,21},{17,9},{21,13},{26,... | collective-permute-start | bytes 2506760 | tf_op jit(solution)/shard_map/ppermute | solution.py:482
  805.7 82.7 %collective-permute-start.74 = (f32[112,128]{1,0:T(8,128)S(1)}, f32[112,128]{1,0:T(8,128)S(1)}, u32[]{:S(2)}, u32[]{:S(2)}) collective-permute-start(f32[112,128]{1,0:T(8,128)S(1)} %add.384), channel_id=1, source_target_pairs={{0,16},{4,20},{8,24},{12,28},{16,0},{20,4},{24,8},{28,12},{1,17},{... | collective-permute-start | bytes 172040 | tf_op jit(solution)/shard_map/ppermute | solution.py:531
  817.0 72.0 %collective-permute-start.70 = (bf16[256,1024]{1,0:T(8,128)(2,1)}, bf16[256,1024]{1,0:T(8,128)(2,1)}, u32[]{:S(2)}, u32[]{:S(2)}) collective-permute-start(bf16[256,1024]{1,0:T(8,128)(2,1)} %add_convert_fusion.3), channel_id=1, source_target_pairs={{0,1},{1,0},{2,3},{3,2},{4,5},{5,4},{6,7},{7,6},{8,9},{9,8},{10,11... | collective-permute-start | bytes 1572872 | tf_op jit(solution)/shard_map/ppermute | solution.py:429
  820.6 68.4 %collective-permute-start.68 = (bf16[256,1024]{1,0:T(8,128)(2,1)}, bf16[256,1024]{1,0:T(8,128)(2,1)}, u32[]{:S(2)}, u32[]{:S(2)}) collective-permute-start(bf16[256,1024]{1,0:T(8,128)(2,1)} %add_convert_fusion.4), channel_id=1, source_target_pairs={{0,2},{1,3},{2,0},{3,1},{4,6},{5,7},{6,4},{7,5},{8,10},{9,11},{10,... | collective-permute-start | bytes 1572872 | tf_op jit(solution)/shard_map/ppermute | solution.py:429
  881.6 64.7 %collective-permute-start.75 = (bf16[272,1536]{1,0:T(8,128)(2,1)}, bf16[272,1536]{1,0:T(8,128)(2,1)}, u32[]{:S(2)}, u32[]{:S(2)}) collective-permute-start(bf16[272,1536]{1,0:T(8,128)(2,1)} %get-tuple-element.256), channel_id=1, source_target_pairs={{0,8},{4,12},{8,16},{12,20},{16,24},{20,28},{24,0},{28,4},{1,9},{5... | collective-permute-start | bytes 2506760 | tf_op jit(solution)/shard_map/ppermute | solution.py:482
  881.8 64.5 %collective-permute-start.76 = (bf16[272,1536]{1,0:T(8,128)(2,1)}, bf16[272,1536]{1,0:T(8,128)(2,1)}, u32[]{:S(2)}, u32[]{:S(2)}) collective-permute-start(bf16[272,1536]{1,0:T(8,128)(2,1)} %get-tuple-element.257), channel_id=1, source_target_pairs={{0,24},{4,28},{8,0},{12,4},{16,8},{20,12},{24,16},{28,20},{1,25},{... | collective-permute-start | bytes 2506760 | tf_op jit(solution)/shard_map/ppermute | solution.py:482
  894.4 64.3 %all-to-all-start.4 = ((bf16[8,32,2048]{2,1,0:T(8,128)(2,1)}), bf16[8,32,2048]{2,1,0:T(8,128)(2,1)}, u32[]{:S(2)}, u32[]{:S(2)}) async-start(bf16[8,32,2048]{2,1,0:T(8,128)(2,1)} %bitcast.98), calls=%async_computation.5 | async-start | bytes 2097152 | tf_op jit(solution)/shard_map/all_to_all | solution.py:686
  (146 other events, 2144.9 us)
Sparse Core Ops, SparseCore 0:
  64.4 68.6 all-gather.4
  135.3 30.1 all-gather.6
  167.1 78.9 all-gather.8
  247.5 80.5 all-gather.10
  626.5 90.1 reduce-scatter.3
  719.4 33.2 reduce-scatter.7
  755.0 185.3 reduce-scatter.5

commit v6 on v5

--- a/solution.py
+++ b/solution.py
@@ -673,7 +673,9 @@
         )
         hidden.append(wide)
         active.append(narrow)
-        terms.append(terms_matmul(narrow, down_full, spans, sums[-1][1] if sums else near(first_pieces[1])))
+        before = (narrow,)
+    for s in over:
+        terms.append(terms_matmul(active[s], down_full, spans, before))
         sums.append(tensor.scatter(terms[s]))
         before = (terms[s][0][0],)
     second, down_pieces = [], []
@@ -708,10 +710,10 @@
         )
         hidden_grad.append(grad)
         up_sums.append(total)
-        held = first_sums[-1][1] if first_sums else (*near(down_pieces[1]), returned_rows[0])
-        terms.append(terms_matmul(grad, up_full, spans, held))
-        first_sums.append(tensor.scatter(terms[s]))
-        before = (terms[s][0][0],)
+        if s == 0:
+            terms.append(terms_matmul(grad, up_full, spans, (*near(down_pieces[1]), returned_rows[0])))
+            first_sums.append(tensor.scatter(terms[s]))
+            before = (terms[s][0][0],)
     first_back = []
 
     def back_to_first(s, later):
@@ -722,12 +724,15 @@
         )
         return tensor.gather(first_back[s][1])
 
-    grad_pieces = [back_to_first(0, before)]
-    flying = (*first_sums[1][1], *near(grad_pieces[0]))
-    down_terms = weight_grad(down_pieces, active, (first_back[0][0], *returned_rows))
-    up_terms = weight_grad(first_pieces, hidden_grad, (down_terms,))
-    down_sum = group.scatter(touched(down_terms, up_terms, *flying))
-    up_sum = group.scatter(touched(up_terms, *flying))
+    down_terms = weight_grad(down_pieces, active, (hidden_grad[1], *first_sums[0][1], *returned_rows))
+    down_terms = touched(down_terms, *first_sums[0][2])
+    down_sum = group.scatter(down_terms)
+    grad_pieces = [back_to_first(0, (down_terms,))]
+    terms.append(terms_matmul(hidden_grad[1], up_full, spans, (first_back[0][0],)))
+    first_sums.append(tensor.scatter(terms[1]))
+    up_terms = weight_grad(first_pieces, hidden_grad, (terms[1][0][0],))
+    up_terms = touched(up_terms, *first_sums[1][1], *near(grad_pieces[0]))
+    up_sum = group.scatter(up_terms)
     grad_pieces.append(back_to_first(1, (up_terms,)))
 
     def attention_in(s, later):
@@ -766,9 +771,9 @@
     qkv_sum, bias_sum, qkv_terms, *qkv_stage = group.weight_scatter(
         token_pieces, qkv_grad, bias_terms, (token_grad[0], down_sum, stages[1])
     )
-    terms.append(terms_matmul(qkv_grad[-1], qkv_weight, spans, (qkv_terms,)))
+    terms.append(terms_matmul(qkv_grad[-1], qkv_weight, spans, (qkv_terms, *returned_grads)))
     last_grad = input_grad(
-        tensor.scatter(terms[-1])[0], first_back[-1][0], (*qkv_stage[1], *returned_grads, stages[2])
+        tensor.scatter(terms[-1])[0], first_back[-1][0], (*qkv_stage[1], up_sum, stages[2])
     )
     returned_grads.append(give_back(last_grad))
 
@@ -777,7 +782,7 @@
         jnp.arange(places.shape[0], dtype=jnp.int32)
     )
     result = jnp.take(jnp.concatenate(returned_rows, axis=0), inverse, axis=0, mode="clip")
-    inverse = inverse + nothing(up_sum, mid_sum).astype(jnp.int32)
+    inverse = inverse + nothing(mid_sum).astype(jnp.int32)
     token_gradient = jnp.take(jnp.concatenate(returned_grads, axis=0), inverse, axis=0, mode="clip")
 
     row_shares = lax.dynamic_slice_in_dim(

time: 985 us -> 947 us (0.961)
  waiting for transfers between devices: 306 us -> 262 us
  starting transfers between devices: 110 us -> 121 us
    ppermute x5, waiting for transfers between devices: 56.1 us -> 15.7 us  [send(): return lax.ppermute(array, 'dp', pairs)]
    reduce_scatter x3, waiting for transfers between devices: 36.2 us -> 0.01 us  [scatter(): lax.psum_scatter(terms, 'dp', scatter_dimension=0, tiled=True).astype(f32)]
    ppermute x67, waiting for transfers between devices: 145 us -> 181 us  [swap(): lax.ppermute(array, 'tensor', [(i, i ^ bit) for i in range(self.size)])]
    all_gather x4, waiting for transfers between devices: 27.2 us -> 9.89 us  [gather(): return lax.all_gather(shard, 'dp', axis=0, tiled=True)]
    ppermute x67, starting transfers between devices: 50.5 us -> 60.9 us  [swap(): lax.ppermute(array, 'tensor', [(i, i ^ bit) for i in range(self.size)])]
    unnamed x202 -> x196, local copies, waits for them, and re-layouts: 34.3 us -> 33.6 us
  transfers between devices with their start and end apart: 89 -> 89, of which waited for: 28 -> 25; matrix products, arithmetic and copies ran while one was open for 11% -> 12% of each run, Pallas kernels for 40% -> 40%
where the time goes in v6:
time: 947 us; the launch traced here: 932 us
  Pallas kernels  384 us (41%)
  waiting for transfers between devices  262 us (28%)
  starting transfers between devices  121 us (13%)
  local copies, waits for them, and re-layouts  84.4 us (9%)
  other arithmetic  56 us (6%)
  between operations  25.5 us (3%)
    pallas_call x32, Pallas kernels, launch(): pl.pallas_call(run, grid=grid, in_specs=list(in_specs) + [pl.BlockSpec(me...  384 us
    ppermute x67, waiting for transfers between devices, swap(): lax.ppermute(array, 'tensor', [(i, i ^ bit) for i in range(self.size)])  181 us
    ppermute x67, starting transfers between devices, swap(): lax.ppermute(array, 'tensor', [(i, i ^ bit) for i in range(self.size)])  60.9 us
    all_to_all x1, waiting for transfers between devices, local(): came = lax.all_to_all(sent, 'dp', split_axis=0, concat_axis=0, tiled=True)  41.3 us
    all_to_all x4, starting transfers between devices, give_back(): lax.all_to_all(rows.reshape(groups, arrival_rows, model_width), 'dp', spl...  38.5 us
    unnamed x196, local copies, waits for them, and re-layouts  33.6 us
  transfers between devices with their start and end apart: 89, of which 25 were waited for; matrix products, arithmetic and copies ran while one was open for 12% of the time, Pallas kernels for 40%

profile of v6, /device:TPU:9, one launch (start us, length us, event | category | flops | bytes accessed | tf_op | source)
XLA Modules:
  0.0 931.8 jit_solution(9019017799838550947)
XLA Ops:
  20.8 41.3 %all-to-all-done = bf16[8,2,32,2048]{3,2,1,0:T(8,128)(2,1)S(1)} async-done(((bf16[8,2,32,2048]{3,2,1,0:T(8,128)(2,1)}), bf16[8,2,32,2048]{3,2,1,0:T(8,128)(2,1)S(1)}, u32[]{:S(2)}, u32[]{:S(2)}) %all-to-all-start) | async-done | bytes 2097184 | tf_op jit(solution)/shard_map/all_to_all | solution.py:584
  73.3 22.1 %collective-permute-done.refs_1_.refs_3_ = bf16[256,2048]{1,0:T(8,128)(2,1)S(1)} collective-permute-done((bf16[256,2048]{1,0:T(8,128)(2,1)}, bf16[256,2048]{1,0:T(8,128)(2,1)S(1)}, u32[]{:S(2)}, u32[]{:S(2)}) %collective-permute-start) | collective-permute-done | bytes 1048608 | tf_op jit(solution)/shard_map/ppermute | solution.py:429
  110.4 10.9 %collective-permute-done.5.refs_8_.refs_4_.refs_11_ = bf16[256,2048]{1,0:T(8,128)(2,1)} collective-permute-done((bf16[256,2048]{1,0:T(8,128)(2,1)S(1)}, bf16[256,2048]{1,0:T(8,128)(2,1)}, u32[]{:S(2)}, u32[]{:S(2)}) %collective-permute-start.5) | collective-permute-done | bytes 1048608 | tf_op jit(solution)/shard_map/ppermute | solution.py:429
  137.9 11.7 %shard_map.323.refs_1_ = bf16[1024,1536]{1,0:T(8,128)(2,1)} custom-call(bf16[256,2048]{1,0:T(8,128)(2,1)} %bitcast.2.refs_0_.refs_6_.refs_2_, bf16[256,2048]{1,0:T(8,128)(2,1)} %copy-done.53, bf16[128,2048]{1,0:T(8,128)(2,1)} %collective-permute-done.2.refs_2_.refs_4_, bf16[128,2048]{1,0:T(8,128)(2,1)} %collective-permute-done.3.refs_3_.refs_5_, ...), custom_call_target="tpu_custom_call" | custom-call | flops 12884901888 | bytes 33554432 | tf_op jit(solution)/shard_map/pallas_call | solution.py:45
  149.6 14.0 %shard_map.324 = (bf16[1024,512]{1,0:T(8,128)(2,1)}, f32[2,2,1024]{2,1,0:T(2,128)}) custom-call(f32[1024,1]{1,0:T(8,128)} %bitcast.99, bf16[1024,1536]{1,0:T(8,128)(2,1)} %shard_map.323.refs_1_), custom_call_target="tpu_custom_call" | custom-call | flops 17179869184 | bytes 9437184 | tf_op jit(solution)/shard_map/pallas_call | solution.py:45
  175.4 12.2 %shard_map.326.refs_1_ = bf16[1024,1536]{1,0:T(8,128)(2,1)} custom-call(bf16[256,2048]{1,0:T(8,128)(2,1)} %bitcast.86, bf16[256,2048]{1,0:T(8,128)(2,1)} %collective-permute-done.4.refs_7_.refs_1_.refs_8_, bf16[128,2048]{1,0:T(8,128)(2,1)} %collective-permute-done.13.refs_2_.refs_9_, bf16[128,2048]{1,0:T(8,128)(2,1)} %copy-done.73, ...), custom_call_target="tpu_custom_call" | custom-call | flops 12884901888 | bytes 33554432 | tf_op jit(solution)/shard_map/pallas_call | solution.py:45
  187.6 14.2 %shard_map.327 = (bf16[1024,512]{1,0:T(8,128)(2,1)}, f32[2,2,1024]{2,1,0:T(2,128)}) custom-call(f32[1024,1]{1,0:T(8,128)} %bitcast.97, bf16[1024,1536]{1,0:T(8,128)(2,1)} %shard_map.326.refs_1_), custom_call_target="tpu_custom_call" | custom-call | flops 17179869184 | bytes 9437184 | tf_op jit(solution)/shard_map/pallas_call | solution.py:45
  215.8 31.8 %collective-permute-done.12 = bf16[6,512]{1,0:T(8,128)(2,1)S(1)} collective-permute-done((bf16[6,512]{1,0:T(8,128)(2,1)S(1)}, bf16[6,512]{1,0:T(8,128)(2,1)S(1)}, u32[]{:S(2)}, u32[]{:S(2)}) %collective-permute-start.12) | collective-permute-done | bytes 6176 | tf_op jit(solution)/shard_map/ppermute | solution.py:429
  259.6 17.5 %collective-permute-done.16.refs_4_.refs_9_ = bf16[256,2048]{1,0:T(8,128)(2,1)S(1)} collective-permute-done((bf16[256,2048]{1,0:T(8,128)(2,1)}, bf16[256,2048]{1,0:T(8,128)(2,1)S(1)}, u32[]{:S(2)}, u32[]{:S(2)}) %collective-permute-start.16) | collective-permute-done | bytes 1048608 | tf_op jit(solution)/shard_map/ppermute | solution.py:429
  278.2 11.2 %collective-permute-done.22.refs_5_ = bf16[256,1024]{1,0:T(8,128)(2,1)S(1)} collective-permute-done((bf16[256,1024]{1,0:T(8,128)(2,1)S(1)}, bf16[256,1024]{1,0:T(8,128)(2,1)S(1)}, u32[]{:S(2)}, u32[]{:S(2)}) %collective-permute-start.22) | collective-permute-done | bytes 524320 | tf_op jit(solution)/shard_map/ppermute | solution.py:429
  301.6 15.6 %collective-permute-done.24.refs_4_.refs_9_ = bf16[256,2048]{1,0:T(8,128)(2,1)S(1)} collective-permute-done((bf16[256,2048]{1,0:T(8,128)(2,1)}, bf16[256,2048]{1,0:T(8,128)(2,1)S(1)}, u32[]{:S(2)}, u32[]{:S(2)}) %collective-permute-start.24) | collective-permute-done | bytes 1048608 | tf_op jit(solution)/shard_map/ppermute | solution.py:429
  328.5 16.1 %shard_map.330 = (f32[1024,2048]{1,0:T(8,128)}, bf16[1024,2048]{1,0:T(8,128)(2,1)}) custom-call(bf16[256,2048]{1,0:T(8,128)(2,1)} %get-tuple-element.124.refs_0_, bf16[256,2048]{1,0:T(8,128)(2,1)} %collective-permute-done.15.refs_1_.refs_8_, bf16[128,2048]{1,0:T(8,128)(2,1)} %collective-permute-done.17.refs_2_, ...), custom_call_target="tpu_custom_call" | custom-call | flops 17179869184 | bytes 58720256 | tf_op jit(solution)/shard_map/pallas_call | solution.py:45
  344.6 16.5 %shard_map.332 = (f32[1024,2048]{1,0:T(8,128)}, bf16[1024,2048]{1,0:T(8,128)(2,1)}) custom-call(bf16[256,2048]{1,0:T(8,128)(2,1)} %get-tuple-element.131.refs_0_.refs_5_, bf16[256,2048]{1,0:T(8,128)(2,1)} %copy-done.55, bf16[128,2048]{1,0:T(8,128)(2,1)} %collective-permute-done.25.refs_2_.refs_7_, bf16[128,2048]{1,0:T(8,128)(2,1)} %collective-permute-done.26.refs_3_.refs_8_, ...), custom_call_target="tpu_custom_call" | custom-call | flops 17179869184 | bytes 58720256 | tf_op jit(solution)/shard_map/pallas_call | solution.py:45
  361.1 14.2 %shard_map.333 = (bf16[512,1024]{1,0:T(8,128)(2,1)}, bf16[256,1024]{1,0:T(8,128)(2,1)}, bf16[256,1024]{1,0:T(8,128)(2,1)}, bf16[512,1024]{1,0:T(8,128)(2,1)}, bf...) custom-call(bf16[1024,2048]{1,0:T(8,128)(2,1)} %get-tuple-element.125.refs_7_.refs_0_.refs_10_, ...), custom_call_target="tpu_custom_call" | custom-call | flops 17179869184 | bytes 33554432 | tf_op jit(solution)/shard_map/pallas_call | solution.py:45
  376.5 14.3 %shard_map.334 = (bf16[512,1024]{1,0:T(8,128)(2,1)}, bf16[256,1024]{1,0:T(8,128)(2,1)}, bf16[256,1024]{1,0:T(8,128)(2,1)}, bf16[512,1024]{1,0:T(8,128)(2,1)}, bf...) custom-call(bf16[1024,2048]{1,0:T(8,128)(2,1)} %get-tuple-element.132.refs_2_.refs_0_.refs_11_, ...), custom_call_target="tpu_custom_call" | custom-call | flops 17179869184 | bytes 33554432 | tf_op jit(solution)/shard_map/pallas_call | solution.py:45
  398.3 29.6 %collective-permute-done.30.refs_5_ = bf16[256,1024]{1,0:T(8,128)(2,1)S(1)} collective-permute-done((bf16[256,1024]{1,0:T(8,128)(2,1)S(1)}, bf16[256,1024]{1,0:T(8,128)(2,1)S(1)}, u32[]{:S(2)}, u32[]{:S(2)}) %collective-permute-start.30) | collective-permute-done | bytes 524320 | tf_op jit(solution)/shard_map/ppermute | solution.py:429
  442.2 10.3 %collective-permute-done.36.refs_10_.refs_4_ = bf16[256,2048]{1,0:T(8,128)(2,1)S(1)} collective-permute-done((bf16[256,2048]{1,0:T(8,128)(2,1)}, bf16[256,2048]{1,0:T(8,128)(2,1)S(1)}, u32[]{:S(2)}, u32[]{:S(2)}) %collective-permute-start.36) | collective-permute-done | bytes 1048608 | tf_op jit(solution)/shard_map/ppermute | solution.py:429
  459.4 18.4 %all-to-all-start.1 = ((bf16[8,32,2048]{2,1,0:T(8,128)(2,1)}), bf16[8,32,2048]{2,1,0:T(8,128)(2,1)S(1)}, u32[]{:S(2)}, u32[]{:S(2)}) async-start(bf16[8,32,2048]{2,1,0:T(8,128)(2,1)} %bitcast.95), calls=%async_computation.1 | async-start | bytes 2097152 | tf_op jit(solution)/shard_map/all_to_all | solution.py:688
  488.0 18.5 %shard_map.337 = (bf16[1024,2048]{1,0:T(8,128)(2,1)}, f32[1,2048]{1,0:T(1,128)}) custom-call(bf16[256,2048]{1,0:T(8,128)(2,1)} %get-tuple-element.148.refs_0_, bf16[256,2048]{1,0:T(8,128)(2,1)} %copy-done.27, bf16[128,2048]{1,0:T(8,128)(2,1)} %collective-permute-done.37.refs_2_, bf16[128,2048]{1,0:T(8,128)(2,1)} %copy-done.74, bf16[256,2048]{1,0:T(8,128)(2,1)} %copy-done.26, ...), custom_call_target="tpu_custom_call" | custom-call | flops 17179869184 | bytes 41959424 | tf_op jit(solution)/shard_map/pallas_call | solution.py:45
  521.3 14.3 %shard_map.338 = (bf16[512,1024]{1,0:T(8,128)(2,1)}, bf16[256,1024]{1,0:T(8,128)(2,1)}, bf16[256,1024]{1,0:T(8,128)(2,1)}, bf16[512,1024]{1,0:T(8,128)(2,1)}, bf...) custom-call(bf16[1024,2048]{1,0:T(8,128)(2,1)} %get-tuple-element.151.refs_0_.refs_10_, ...), custom_call_target="tpu_custom_call" | custom-call | flops 17179869184 | bytes 33554432 | tf_op jit(solution)/shard_map/pallas_call | solution.py:45
  537.2 18.6 %shard_map.339 = (bf16[1024,2048]{1,0:T(8,128)(2,1)}, f32[1,2048]{1,0:T(1,128)}) custom-call(bf16[256,2048]{1,0:T(8,128)(2,1)} %get-tuple-element.152.refs_0_.refs_5_, bf16[256,2048]{1,0:T(8,128)(2,1)} %copy-done.57, bf16[128,2048]{1,0:T(8,128)(2,1)} %collective-permute-done.45.refs_2_.refs_7_, bf16[128,2048]{1,0:T(8,128)(2,1)} %collective-permute-done.46.refs_3_.refs_8_, ...), custom_call_target="tpu_custom_call" | custom-call | flops 17179869184 | bytes 41959424 | tf_op jit(solution)/shard_map/pallas_call | solution.py:45
  566.3 24.3 %shard_map.340 = bf16[2048,2048]{1,0:T(8,128)(2,1)} custom-call(bf16[256,2048]{1,0:T(8,128)(2,1)} %get-tuple-element.148.refs_0_, bf16[256,2048]{1,0:T(8,128)(2,1)} %copy-done.27, bf16[128,2048]{1,0:T(8,128)(2,1)} %collective-permute-done.37.refs_2_, bf16[128,2048]{1,0:T(8,128)(2,1)} %copy-done.74, bf16[256,2048]{1,0:T(8,128)(2,1)} %copy-done.26, ...), custom_call_target="tpu_custom_call" | custom-call | flops 34359738368 | bytes 50331648 | tf_op jit(solution)/shard_map/pallas_call | solution.py:45
  604.3 14.2 %shard_map.342 = (bf16[512,1024]{1,0:T(8,128)(2,1)}, bf16[256,1024]{1,0:T(8,128)(2,1)}, bf16[256,1024]{1,0:T(8,128)(2,1)}, bf16[512,1024]{1,0:T(8,128)(2,1)}, bf...) custom-call(bf16[1024,2048]{1,0:T(8,128)(2,1)} %get-tuple-element.162.refs_12_.refs_0_.refs_11_, ...), custom_call_target="tpu_custom_call" | custom-call | flops 17179869184 | bytes 33554432 | tf_op jit(solution)/shard_map/pallas_call | solution.py:45
  620.4 24.4 %shard_map.343 = bf16[2048,2048]{1,0:T(8,128)(2,1)} custom-call(bf16[256,2048]{1,0:T(8,128)(2,1)} %get-tuple-element.124.refs_0_, bf16[256,2048]{1,0:T(8,128)(2,1)} %collective-permute-done.15.refs_1_.refs_8_, bf16[128,2048]{1,0:T(8,128)(2,1)} %collective-permute-done.17.refs_2_, bf16[128,2048]{1,0:T(8,128)(2,1)} %collective-permute-done.18.refs_3_, ...), custom_call_target="tpu_custom_call" | custom-call | flops 34359738368 | bytes 50331648 | tf_op jit(solution)/shard_map/pallas_call | solution.py:45
  683.9 14.9 %shard_map.345 = (bf16[1024,1536]{1,0:T(8,128)(2,1)}, f32[2,1,768]{2,1,0:T(1,128)}) custom-call(f32[1024,1]{1,0:T(8,128)} %bitcast.100, bf16[1024,1536]{1,0:T(8,128)(2,1)} %shard_map.323.refs_1_, bf16[1024,512]{1,0:T(8,128)(2,1)} %get-tuple-element.115.refs_0_.refs_2_.refs_10_, bf16[1024,512]{1,0:T(8,128)(2,1)} %shard_map.344.refs_3_, ...), custom_call_target="tpu_custom_call" | custom-call | flops 42949672960 | bytes 18874368 | tf_op jit(solution)/shard_map/pallas_call | solution.py:45
  705.5 11.6 %shard_map.347 = (bf16[512,1024]{1,0:T(8,128)(2,1)}, bf16[256,1024]{1,0:T(8,128)(2,1)}, bf16[256,1024]{1,0:T(8,128)(2,1)}, bf16[512,1024]{1,0:T(8,128)(2,1)}, bf...) custom-call(bf16[1024,1536]{1,0:T(8,128)(2,1)} %get-tuple-element.168.refs_0_.refs_12_, ...), custom_call_target="tpu_custom_call" | custom-call | flops 12884901888 | bytes 27262976 | tf_op jit(solution)/shard_map/pallas_call | solution.py:45
  733.5 10.8 %shard_map.349.refs_5_ = bf16[2048,512]{1,0:T(8,128)(2,1)} custom-call(bf16[256,2048]{1,0:T(8,128)(2,1)} %get-tuple-element.163.refs_0_, bf16[256,2048]{1,0:T(8,128)(2,1)} %copy-done.56, bf16[128,2048]{1,0:T(8,128)(2,1)} %collective-permute-done.49.refs_2_, bf16[128,2048]{1,0:T(8,128)(2,1)} %collective-permute-done.50.refs_3_, ...), custom_call_target="tpu_custom_call" | custom-call | flops 8589934592 | bytes 25165824 | tf_op jit(solution)/shard_map/pallas_call | solution.py:45
  749.4 14.6 %shard_map.350 = (bf16[1024,1536]{1,0:T(8,128)(2,1)}, f32[2,1,768]{2,1,0:T(1,128)}) custom-call(f32[1024,1]{1,0:T(8,128)} %bitcast.98, bf16[1024,1536]{1,0:T(8,128)(2,1)} %shard_map.326.refs_1_, bf16[1024,512]{1,0:T(8,128)(2,1)} %get-tuple-element.122.refs_0_.refs_11_.refs_2_, bf16[1024,512]{1,0:T(8,128)(2,1)} %shard_map.348.refs_12_.refs_3_, ...), custom_call_target="tpu_custom_call" | custom-call | flops 42949672960 | bytes 18874368 | tf_op jit(solution)/shard_map/pallas_call | solution.py:45
  779.7 20.2 %shard_map.352 = (bf16[1088,1536]{1,0:T(8,128)(2,1)}, bf16[1088,1536]{1,0:T(8,128)(2,1)}) custom-call(s32[1]{0:T(128)} %bitcast.26.refs_0_, f32[1,1536]{1,0:T(1,128)} %bitcast.108, bf16[256,2048]{1,0:T(8,128)(2,1)} %bitcast.2.refs_0_.refs_6_.refs_2_, bf16[256,2048]{1,0:T(8,128)(2,1)} %copy-done.53, bf16[128,2048]{1,0:T(8,128)(2,1)} %collective-permute-done.2.refs_2_.refs_4_, ...), custom_call_target="tpu_custom_call" | custom-call | flops 25769803776 | bytes 41943040 | tf_op jit(solution)/shard_map/pallas_call | solution.py:45
  806.3 11.6 %shard_map.353 = (bf16[512,1024]{1,0:T(8,128)(2,1)}, bf16[256,1024]{1,0:T(8,128)(2,1)}, bf16[256,1024]{1,0:T(8,128)(2,1)}, bf16[512,1024]{1,0:T(8,128)(2,1)}, bf...) custom-call(bf16[1024,1536]{1,0:T(8,128)(2,1)} %get-tuple-element.189.refs_7_.refs_13_.refs_0_, ...), custom_call_target="tpu_custom_call" | custom-call | flops 12884901888 | bytes 27262976 | tf_op jit(solution)/shard_map/pallas_call | solution.py:45
  831.4 11.4 %collective-permute-done.69.refs_4_ = bf16[512,1024]{1,0:T(8,128)(2,1)} collective-permute-done((bf16[512,1024]{1,0:T(8,128)(2,1)}, bf16[512,1024]{1,0:T(8,128)(2,1)}, u32[]{:S(2)}, u32[]{:S(2)}) %collective-permute-start.69) | collective-permute-done | bytes 1048608 | tf_op jit(solution)/shard_map/ppermute | solution.py:429
  886.9 11.1 %collective-permute-done.76 = bf16[272,1536]{1,0:T(8,128)(2,1)} collective-permute-done((bf16[272,1536]{1,0:T(8,128)(2,1)}, bf16[272,1536]{1,0:T(8,128)(2,1)}, u32[]{:S(2)}, u32[]{:S(2)}) %collective-permute-start.76) | collective-permute-done | bytes 835616 | tf_op jit(solution)/shard_map/ppermute | solution.py:482
  (529 shorter events, 363.9 us)
Async XLA Ops:
  10.8 51.3 %all-to-all-start = ((bf16[8,2,32,2048]{3,2,1,0:T(8,128)(2,1)}), bf16[8,2,32,2048]{3,2,1,0:T(8,128)(2,1)S(1)}, u32[]{:S(2)}, u32[]{:S(2)}) async-start(bf16[8,2,32,2048]{3,2,1,0:T(8,128)(2,1)} %bitcast.81), calls=%async_computation | async-start | bytes 4194304 | tf_op jit(solution)/shard_map/all_to_all | solution.py:584
  16.7 116.4 %all-gather.5.cloned.1.call-start = ((), (), s32[]{:S(2)}) async-start(), calls=%async_computation.8 | async-start | bytes 7667712 | tf_op jit(solution)/shard_map/all_gather | solution.py:485
  64.2 101.2 %all-gather.7.cloned.1.call-start = ((), (), s32[]{:S(2)}) async-start(), calls=%async_computation.9 | async-start | bytes 2359296 | tf_op jit(solution)/shard_map/all_gather | solution.py:485
  66.9 252.5 %all-gather.9.cloned.1.call-start = ((), (), s32[]{:S(2)}) async-start(), calls=%async_computation.10 | async-start | bytes 9437184 | tf_op jit(solution)/shard_map/all_gather | solution.py:485
  69.7 291.4 %all-gather.11.cloned.1.call-start = ((), (), s32[]{:S(2)}) async-start(), calls=%async_computation.11 | async-start | bytes 9437184 | tf_op jit(solution)/shard_map/all_gather | solution.py:485
  72.0 36.3 %collective-permute-start.1 = (bf16[256,2048]{1,0:T(8,128)(2,1)}, bf16[256,2048]{1,0:T(8,128)(2,1)}, u32[]{:S(2)}, u32[]{:S(2)}) collective-permute-start(bf16[256,2048]{1,0:T(8,128)(2,1)} %bitcast.2.refs_0_.refs_6_.refs_2_), channel_id=1, source_target_pairs={{0,2},{1,3},{2,0},{3,1},{4,6},{5,7},{6,4},{7,5},{8,10},{9,11},{10,... | collective-permute-start | bytes 3145736 | tf_op jit(solution)/shard_map/ppermute | solution.py:429
  122.4 50.9 %collective-permute-start.13 = (bf16[128,2048]{1,0:T(8,128)(2,1)S(1)}, bf16[128,2048]{1,0:T(8,128)(2,1)}, u32[]{:S(2)}, u32[]{:S(2)}) collective-permute-start(bf16[128,2048]{1,0:T(8,128)(2,1)S(1)} %slice.430), channel_id=1, source_target_pairs={{0,1},{1,0},{2,3},{3,2},{4,5},{5,4},{6,7},{7,6},{8,9},{9,8},{10,11... | collective-permute-start | bytes 1572872 | tf_op jit(solution)/shard_map/ppermute | solution.py:429
  123.8 50.8 %collective-permute-start.14 = (bf16[128,2048]{1,0:T(8,128)(2,1)S(1)}, bf16[128,2048]{1,0:T(8,128)(2,1)S(1)}, u32[]{:S(2)}, u32[]{:S(2)}) collective-permute-start(bf16[128,2048]{1,0:T(8,128)(2,1)S(1)} %slice.431), channel_id=1, source_target_pairs={{0,2},{1,3},{2,0},{3,1},{4,6},{5,7},{6,4},{7,5},{8,10},{9,11},{10,... | collective-permute-start | bytes 1572872 | tf_op jit(solution)/shard_map/ppermute | solution.py:429
  135.5 79.0 %collective-permute-start.10 = (bf16[6,512]{1,0:T(8,128)(2,1)S(1)}, bf16[6,512]{1,0:T(8,128)(2,1)S(1)}, u32[]{:S(2)}, u32[]{:S(2)}) collective-permute-start(bf16[6,512]{1,0:T(8,128)(2,1)S(1)} %reshape.283), channel_id=1, source_target_pairs={{0,1},{1,0},{2,3},{3,2},{4,5},{5,4},{6,7},{7,6},{8,9},{9,8},{10,11... | collective-permute-start | bytes 18440 | tf_op jit(solution)/shard_map/ppermute | solution.py:429
  136.7 78.8 %collective-permute-start.11 = (bf16[6,512]{1,0:T(8,128)(2,1)S(1)}, bf16[6,512]{1,0:T(8,128)(2,1)S(1)}, u32[]{:S(2)}, u32[]{:S(2)}) collective-permute-start(bf16[6,512]{1,0:T(8,128)(2,1)S(1)} %reshape.283), channel_id=1, source_target_pairs={{0,2},{1,3},{2,0},{3,1},{4,6},{5,7},{6,4},{7,5},{8,10},{9,11},{10,... | collective-permute-start | bytes 18440 | tf_op jit(solution)/shard_map/ppermute | solution.py:429
  210.0 46.1 %collective-permute-start.21 = (bf16[512,1024]{1,0:T(8,128)(2,1)}, bf16[512,1024]{1,0:T(8,128)(2,1)S(1)}, u32[]{:S(2)}, u32[]{:S(2)}) collective-permute-start(bf16[512,1024]{1,0:T(8,128)(2,1)} %get-tuple-element.129), channel_id=1, source_target_pairs={{0,2},{1,3},{2,0},{3,1},{4,6},{5,7},{6,4},{7,5},{8,10},{9,11},{10,... | collective-permute-start | bytes 3145736 | tf_op jit(solution)/shard_map/ppermute | solution.py:429
  211.7 36.6 %collective-permute-start.7 = (bf16[256,1024]{1,0:T(8,128)(2,1)S(1)}, bf16[256,1024]{1,0:T(8,128)(2,1)S(1)}, u32[]{:S(2)}, u32[]{:S(2)}) collective-permute-start(bf16[256,1024]{1,0:T(8,128)(2,1)S(1)} %add_convert_fusion.18), channel_id=1, source_target_pairs={{0,2},{1,3},{2,0},{3,1},{4,6},{5,7},{6,4},{7,5},{8,10},{9,11},{10,... | collective-permute-start | bytes 1572872 | tf_op jit(solution)/shard_map/ppermute | solution.py:429
  212.8 44.9 %collective-permute-start.19 = (bf16[512,1024]{1,0:T(8,128)(2,1)}, bf16[512,1024]{1,0:T(8,128)(2,1)S(1)}, u32[]{:S(2)}, u32[]{:S(2)}) collective-permute-start(bf16[512,1024]{1,0:T(8,128)(2,1)} %get-tuple-element.123.refs_8_), channel_id=1, source_target_pairs={{0,1},{1,0},{2,3},{3,2},{4,5},{5,4},{6,7},{7,6},{8,9},{9,8},{10,11... | collective-permute-start | bytes 3145736 | tf_op jit(solution)/shard_map/ppermute | solution.py:429
  214.4 33.8 %collective-permute-start.9 = (bf16[256,1024]{1,0:T(8,128)(2,1)S(1)}, bf16[256,1024]{1,0:T(8,128)(2,1)S(1)}, u32[]{:S(2)}, u32[]{:S(2)}) collective-permute-start(bf16[256,1024]{1,0:T(8,128)(2,1)S(1)} %add_convert_fusion.17), channel_id=1, source_target_pairs={{0,1},{1,0},{2,3},{3,2},{4,5},{5,4},{6,7},{7,6},{8,9},{9,8},{10,11... | collective-permute-start | bytes 1572872 | tf_op jit(solution)/shard_map/ppermute | solution.py:429
  256.3 33.2 %collective-permute-start.22 = (bf16[256,1024]{1,0:T(8,128)(2,1)S(1)}, bf16[256,1024]{1,0:T(8,128)(2,1)S(1)}, u32[]{:S(2)}, u32[]{:S(2)}) collective-permute-start(bf16[256,1024]{1,0:T(8,128)(2,1)S(1)} %add_convert_fusion.15), channel_id=1, source_target_pairs={{0,1},{1,0},{2,3},{3,2},{4,5},{5,4},{6,7},{7,6},{8,9},{9,8},{10,11... | collective-permute-start | bytes 1572872 | tf_op jit(solution)/shard_map/ppermute | solution.py:429
  390.9 47.5 %collective-permute-start.33 = (bf16[512,1024]{1,0:T(8,128)(2,1)}, bf16[512,1024]{1,0:T(8,128)(2,1)S(1)}, u32[]{:S(2)}, u32[]{:S(2)}) collective-permute-start(bf16[512,1024]{1,0:T(8,128)(2,1)} %get-tuple-element.145), channel_id=1, source_target_pairs={{0,2},{1,3},{2,0},{3,1},{4,6},{5,7},{6,4},{7,5},{8,10},{9,11},{10,... | collective-permute-start | bytes 3145736 | tf_op jit(solution)/shard_map/ppermute | solution.py:429
  391.2 49.6 %collective-permute-start.31 = (bf16[512,1024]{1,0:T(8,128)(2,1)}, bf16[512,1024]{1,0:T(8,128)(2,1)S(1)}, u32[]{:S(2)}, u32[]{:S(2)}) collective-permute-start(bf16[512,1024]{1,0:T(8,128)(2,1)} %get-tuple-element.140.refs_9_), channel_id=1, source_target_pairs={{0,1},{1,0},{2,3},{3,2},{4,5},{5,4},{6,7},{7,6},{8,9},{9,8},{10,11... | collective-permute-start | bytes 3145736 | tf_op jit(solution)/shard_map/ppermute | solution.py:429
  394.2 33.7 %collective-permute-start.30 = (bf16[256,1024]{1,0:T(8,128)(2,1)S(1)}, bf16[256,1024]{1,0:T(8,128)(2,1)S(1)}, u32[]{:S(2)}, u32[]{:S(2)}) collective-permute-start(bf16[256,1024]{1,0:T(8,128)(2,1)S(1)} %add_convert_fusion.13), channel_id=1, source_target_pairs={{0,1},{1,0},{2,3},{3,2},{4,5},{5,4},{6,7},{7,6},{8,9},{9,8},{10,11... | collective-permute-start | bytes 1572872 | tf_op jit(solution)/shard_map/ppermute | solution.py:429
  440.7 37.1 %collective-permute-start.34 = (bf16[256,1024]{1,0:T(8,128)(2,1)}, bf16[256,1024]{1,0:T(8,128)(2,1)}, u32[]{:S(2)}, u32[]{:S(2)}) collective-permute-start(bf16[256,1024]{1,0:T(8,128)(2,1)} %add_convert_fusion.11), channel_id=1, source_target_pairs={{0,1},{1,0},{2,3},{3,2},{4,5},{5,4},{6,7},{7,6},{8,9},{9,8},{10,11... | collective-permute-start | bytes 1572872 | tf_op jit(solution)/shard_map/ppermute | solution.py:429
  442.0 35.9 %collective-permute-start.32 = (bf16[256,1024]{1,0:T(8,128)(2,1)}, bf16[256,1024]{1,0:T(8,128)(2,1)}, u32[]{:S(2)}, u32[]{:S(2)}) collective-permute-start(bf16[256,1024]{1,0:T(8,128)(2,1)} %add_convert_fusion.12), channel_id=1, source_target_pairs={{0,2},{1,3},{2,0},{3,1},{4,6},{5,7},{6,4},{7,5},{8,10},{9,11},{10,... | collective-permute-start | bytes 1572872 | tf_op jit(solution)/shard_map/ppermute | solution.py:429
  453.5 33.7 %collective-permute-start.37 = (bf16[128,2048]{1,0:T(8,128)(2,1)}, bf16[128,2048]{1,0:T(8,128)(2,1)}, u32[]{:S(2)}, u32[]{:S(2)}) collective-permute-start(bf16[128,2048]{1,0:T(8,128)(2,1)} %slice.445), channel_id=1, source_target_pairs={{0,1},{1,0},{2,3},{3,2},{4,5},{5,4},{6,7},{7,6},{8,9},{9,8},{10,11... | collective-permute-start | bytes 1572872 | tf_op jit(solution)/shard_map/ppermute | solution.py:429
  459.4 54.3 %all-to-all-start.1 = ((bf16[8,32,2048]{2,1,0:T(8,128)(2,1)}), bf16[8,32,2048]{2,1,0:T(8,128)(2,1)S(1)}, u32[]{:S(2)}, u32[]{:S(2)}) async-start(bf16[8,32,2048]{2,1,0:T(8,128)(2,1)} %bitcast.95), calls=%async_computation.1 | async-start | bytes 2097152 | tf_op jit(solution)/shard_map/all_to_all | solution.py:688
  513.7 51.7 %all-to-all-start.2 = ((bf16[8,32,2048]{2,1,0:T(8,128)(2,1)}), bf16[8,32,2048]{2,1,0:T(8,128)(2,1)S(1)}, u32[]{:S(2)}, u32[]{:S(2)}) async-start(bf16[8,32,2048]{2,1,0:T(8,128)(2,1)} %bitcast.17), calls=%async_computation.2 | async-start | bytes 2097152 | tf_op jit(solution)/shard_map/all_to_all | solution.py:688
  521.3 254.8 %reduce-scatter.4.cloned.1.call-start = ((), (), s32[]{:S(2)}) async-start(), calls=%async_computation.12 | async-start | bytes 9437184 | tf_op jit(solution)/shard_map/reduce_scatter | solution.py:488
  595.6 270.4 %reduce-scatter.6.cloned.1.call-start = ((), (), s32[]{:S(2)}) async-start(), calls=%async_computation.13 | async-start | bytes 9437184 | tf_op jit(solution)/shard_map/reduce_scatter | solution.py:488
  603.0 44.0 %collective-permute-start.47 = (bf16[256,2048]{1,0:T(8,128)(2,1)}, bf16[256,2048]{1,0:T(8,128)(2,1)S(1)}, u32[]{:S(2)}, u32[]{:S(2)}) collective-permute-start(bf16[256,2048]{1,0:T(8,128)(2,1)} %get-tuple-element.163.refs_0_), channel_id=1, source_target_pairs={{0,1},{1,0},{2,3},{3,2},{4,5},{5,4},{6,7},{7,6},{8,9},{9,8},{10,11... | collective-permute-start | bytes 3145736 | tf_op jit(solution)/shard_map/ppermute | solution.py:429
  603.3 41.5 %collective-permute-start.48 = (bf16[256,2048]{1,0:T(8,128)(2,1)}, bf16[256,2048]{1,0:T(8,128)(2,1)}, u32[]{:S(2)}, u32[]{:S(2)}) collective-permute-start(bf16[256,2048]{1,0:T(8,128)(2,1)} %get-tuple-element.163.refs_0_), channel_id=1, source_target_pairs={{0,2},{1,3},{2,0},{3,1},{4,6},{5,7},{6,4},{7,5},{8,10},{9,11},{10,... | collective-permute-start | bytes 3145736 | tf_op jit(solution)/shard_map/ppermute | solution.py:429
  770.7 34.6 %all-to-all-start.3 = ((bf16[8,32,2048]{2,1,0:T(8,128)(2,1)}), bf16[8,32,2048]{2,1,0:T(8,128)(2,1)S(1)}, u32[]{:S(2)}, u32[]{:S(2)}) async-start(bf16[8,32,2048]{2,1,0:T(8,128)(2,1)} %bitcast.90), calls=%async_computation.3 | async-start | bytes 2097152 | tf_op jit(solution)/shard_map/all_to_all | solution.py:688
  776.0 105.2 %reduce-scatter.8.cloned.1.call-start = ((), (), s32[]{:S(2)}) async-start(), calls=%async_computation.14 | async-start | bytes 2359296 | tf_op jit(solution)/shard_map/reduce_scatter | solution.py:488
  829.3 35.2 %collective-permute-start.74 = (f32[112,128]{1,0:T(8,128)}, f32[112,128]{1,0:T(8,128)S(1)}, u32[]{:S(2)}, u32[]{:S(2)}) collective-permute-start(f32[112,128]{1,0:T(8,128)} %add.379), channel_id=1, source_target_pairs={{0,16},{4,20},{8,24},{12,28},{16,0},{20,4},{24,8},{28,12},{1,17},{... | collective-permute-start | bytes 172040 | tf_op jit(solution)/shard_map/ppermute | solution.py:531
  858.7 39.2 %collective-permute-start.76 = (bf16[272,1536]{1,0:T(8,128)(2,1)}, bf16[272,1536]{1,0:T(8,128)(2,1)}, u32[]{:S(2)}, u32[]{:S(2)}) collective-permute-start(bf16[272,1536]{1,0:T(8,128)(2,1)} %get-tuple-element.257), channel_id=1, source_target_pairs={{0,24},{4,28},{8,0},{12,4},{16,8},{20,12},{24,16},{28,20},{1,25},{... | collective-permute-start | bytes 2506760 | tf_op jit(solution)/shard_map/ppermute | solution.py:482
  873.5 44.8 %all-to-all-start.4 = ((bf16[8,32,2048]{2,1,0:T(8,128)(2,1)}), bf16[8,32,2048]{2,1,0:T(8,128)(2,1)}, u32[]{:S(2)}, u32[]{:S(2)}) async-start(bf16[8,32,2048]{2,1,0:T(8,128)(2,1)} %bitcast.89), calls=%async_computation.6 | async-start | bytes 2097152 | tf_op jit(solution)/shard_map/all_to_all | solution.py:688
  (143 other events, 1924.3 us)
Sparse Core Ops, SparseCore 0:
  64.4 68.6 all-gather.4
  135.3 30.1 all-gather.6
  167.0 78.9 all-gather.8
  247.4 80.5 all-gather.10
  595.7 89.1 reduce-scatter.3
  687.0 87.0 reduce-scatter.5
  805.5 35.0 reduce-scatter.7

commit v7 on v6

--- a/solution.py
+++ b/solution.py
@@ -651,7 +651,7 @@
         mix, log = attend(qkv[s], biases[s], 2)
         mixed.append(mix)
         logs.append(log)
-        terms.append(terms_matmul(mix, mid_weight, spans, sums[-1][1] if sums else ()))
+        terms.append(terms_matmul(mix, mid_weight, spans, sums[-1][1] if sums else (row_vectors,)))
         sums.append(tensor.scatter(terms[s]))
         before = (terms[s][0][0],)
     first, first_pieces = [], []
@@ -674,13 +674,11 @@
         hidden.append(wide)
         active.append(narrow)
         before = (narrow,)
+    second, down_pieces = [], []
     for s in over:
         terms.append(terms_matmul(active[s], down_full, spans, before))
         sums.append(tensor.scatter(terms[s]))
-        before = (terms[s][0][0],)
-    second, down_pieces = [], []
-    for s in over:
-        second.append(second_norm(sums[s][0], first[s][1], cotangent[s], row_vectors, before))
+        second.append(second_norm(sums[s][0], first[s][1], cotangent[s], row_vectors, (terms[s][0][0],)))
         down_pieces.append(tensor.gather(second[s][2]))
         before = near(down_pieces[s])
 
@@ -692,29 +690,21 @@
     returned_rows = [give_back(s[0]) for s in second]
 
     hidden_grad, up_sums, terms, first_sums = [], [], [], []
-    before = ()
 
     def through_gelu(product, wide):
         grad = (product * gelu_slope(wide)).astype(bf16)
         return grad, jnp.sum(grad.astype(f32), axis=0, keepdims=True)
 
-    for s in over:
+    first_back = []
+
+    def back_to_hidden(s, later, held):
         grad, total = rows_matmul(
-            down_pieces[s],
-            down_full,
-            hidden_width,
-            through_gelu,
-            [hidden[s]],
-            [(slot_rows, bf16), (1, f32)],
-            before,
+            down_pieces[s], down_full, hidden_width, through_gelu, [hidden[s]], [(slot_rows, bf16), (1, f32)], later
         )
         hidden_grad.append(grad)
         up_sums.append(total)
-        if s == 0:
-            terms.append(terms_matmul(grad, up_full, spans, (*near(down_pieces[1]), returned_rows[0])))
-            first_sums.append(tensor.scatter(terms[s]))
-            before = (terms[s][0][0],)
-    first_back = []
+        terms.append(terms_matmul(grad, up_full, spans, held))
+        first_sums.append(tensor.scatter(terms[s]))
 
     def back_to_first(s, later):
         first_back.append(
@@ -724,16 +714,13 @@
         )
         return tensor.gather(first_back[s][1])
 
-    down_terms = weight_grad(down_pieces, active, (hidden_grad[1], *first_sums[0][1], *returned_rows))
-    down_terms = touched(down_terms, *first_sums[0][2])
+    back_to_hidden(0, (), (returned_rows[0],))
+    grad_pieces = [back_to_first(0, (terms[0][0][0],))]
+    down_terms = weight_grad(down_pieces, active, (first_back[0][0],))
+    down_terms = touched(down_terms, *near(grad_pieces[0]))
     down_sum = group.scatter(down_terms)
-    grad_pieces = [back_to_first(0, (down_terms,))]
-    terms.append(terms_matmul(hidden_grad[1], up_full, spans, (first_back[0][0],)))
-    first_sums.append(tensor.scatter(terms[1]))
-    up_terms = weight_grad(first_pieces, hidden_grad, (terms[1][0][0],))
-    up_terms = touched(up_terms, *first_sums[1][1], *near(grad_pieces[0]))
-    up_sum = group.scatter(up_terms)
-    grad_pieces.append(back_to_first(1, (up_terms,)))
+    back_to_hidden(1, (down_terms,), (returned_rows[1],))
+    last_first = (terms[1][0][0],)
 
     def attention_in(s, later):
         return rows_matmul(
@@ -749,29 +736,32 @@
     def attention_back(s, mixed_grad, later):
         return attend_back(qkv[s], biases[s], mixed[s], mixed_grad, logs[s], 2, later)
 
-    mixed_grad = [attention_in(0, (up_terms,))]
+    mixed_grad = [attention_in(0, last_first)]
+    backs = [attention_back(0, mixed_grad[0], first_sums[1][1])]
+    terms = [terms_matmul(backs[0][0], qkv_weight, spans)]
+    sums = [tensor.scatter(terms[0])]
+    grad_pieces.append(back_to_first(1, (terms[0][0][0],)))
+    up_terms = weight_grad(first_pieces, hidden_grad, (first_back[1][0],))
+    up_terms = touched(up_terms, *near(grad_pieces[1]), *sums[0][1])
+    up_sum = group.scatter(up_terms)
     row_grads = jnp.concatenate(
         [sum(f[2] for f in first_back)[:3], sum(s[3] for s in second)[:3]], axis=0
     ).reshape(-1, 128)
-    row_grads, stages = add_up(row_grads, "tensor", (mixed_grad[0],))
-    stages = [(stage,) for stage in stages] + [(), ()]
-    backs = [attention_back(0, mixed_grad[0], ())]
-    terms = [terms_matmul(backs[0][0], qkv_weight, spans, (*stages[0], *near(grad_pieces[1])))]
-    sums = [tensor.scatter(terms[0])]
-    mixed_grad.append(attention_in(1, (terms[0][0][0], *stages[1])))
+    mixed_grad.append(attention_in(1, (up_terms,)))
     mid_terms = weight_grad(grad_pieces, mixed, (mixed_grad[1],))
+    row_grads, spread = add_up(row_grads, "tensor", (mixed_grad[1],))
     small = jnp.concatenate([row_grads, sum(up_sums).reshape(-1, 128)], axis=0)
-    small, stages = add_up(small, "dp", (mixed_grad[1], mid_terms, None))
-    mid_sum = group.scatter(touched(mid_terms, *sums[0][1]))
-    backs.append(attention_back(1, mixed_grad[1], (mid_terms, *sums[0][1], stages[0])))
+    small, stages = add_up(small, "dp")
+    mid_sum = group.scatter(mid_terms)
+    backs.append(attention_back(1, mixed_grad[1], (mid_terms, spread[0])))
     token_grad = [input_grad(sums[0][0], first_back[0][0], (backs[1][0],))]
     returned_grads = [give_back(token_grad[0])]
     qkv_grad = [b[0] for b in backs]
     bias_terms = sum(b[1] for b in backs).reshape(1, -1)
     qkv_sum, bias_sum, qkv_terms, *qkv_stage = group.weight_scatter(
-        token_pieces, qkv_grad, bias_terms, (token_grad[0], down_sum, stages[1])
-    )
-    terms.append(terms_matmul(qkv_grad[-1], qkv_weight, spans, (qkv_terms, *returned_grads)))
+        token_pieces, qkv_grad, bias_terms, (token_grad[0], down_sum, spread[1])
+    )
+    terms.append(terms_matmul(qkv_grad[-1], qkv_weight, spans, (qkv_terms, stages[0], *returned_grads)))
     last_grad = input_grad(
         tensor.scatter(terms[-1])[0], first_back[-1][0], (*qkv_stage[1], up_sum, stages[2])
     )

time: 947 us -> 1060 us (1.12)
  waiting for transfers between devices: 262 us -> 364 us
  starting transfers between devices: 121 us -> 142 us
    ppermute x67, waiting for transfers between devices: 181 us -> 232 us  [swap(): lax.ppermute(array, 'tensor', [(i, i ^ bit) for i in range(self.size)])]
    all_to_all x4, starting transfers between devices: 38.5 us -> 74.7 us  [give_back(): lax.all_to_all(rows.reshape(groups, arrival_rows, model_width), 'dp', spl...]
    ppermute x5, waiting for transfers between devices: 5.71 us -> 37.8 us  [add_up(): lax.ppermute(array, axis, [(i, i ^ bit) for i in range(size)])]
    all_to_all x4, waiting for transfers between devices: 8.03 us -> 36.3 us  [give_back(): lax.all_to_all(rows.reshape(groups, arrival_rows, model_width), 'dp', spl...]
    unnamed x196 -> x220, local copies, waits for them, and re-layouts: 33.6 us -> 37.4 us
  transfers between devices with their start and end apart: 89 -> 89, of which waited for: 25 -> 32; matrix products, arithmetic and copies ran while one was open for 12% -> 9% of each run, Pallas kernels for 40% -> 35%
where the time goes in v7:
time: 1060 us; the launch traced here: 1040 us
  Pallas kernels  384 us (36%)
  waiting for transfers between devices  364 us (34%)
  starting transfers between devices  142 us (13%)
  local copies, waits for them, and re-layouts  78.9 us (7%)
  other arithmetic  48.7 us (5%)
  between operations  22.9 us (2%)
    pallas_call x32, Pallas kernels, launch(): pl.pallas_call(run, grid=grid, in_specs=list(in_specs) + [pl.BlockSpec(me...  384 us
    ppermute x67, waiting for transfers between devices, swap(): lax.ppermute(array, 'tensor', [(i, i ^ bit) for i in range(self.size)])  232 us
    all_to_all x4, starting transfers between devices, give_back(): lax.all_to_all(rows.reshape(groups, arrival_rows, model_width), 'dp', spl...  74.7 us
    ppermute x67, starting transfers between devices, swap(): lax.ppermute(array, 'tensor', [(i, i ^ bit) for i in range(self.size)])  52.1 us
    all_to_all x1, waiting for transfers between devices, local(): came = lax.all_to_all(sent, 'dp', split_axis=0, concat_axis=0, tiled=True)  41.3 us
    ppermute x5, waiting for transfers between devices, add_up(): lax.ppermute(array, axis, [(i, i ^ bit) for i in range(size)])  37.8 us
    unnamed x220, local copies, waits for them, and re-layouts  37.4 us
    all_to_all x4, waiting for transfers between devices, give_back(): lax.all_to_all(rows.reshape(groups, arrival_rows, model_width), 'dp', spl...  36.3 us
  transfers between devices with their start and end apart: 89, of which 32 were waited for; matrix products, arithmetic and copies ran while one was open for 9% of the time, Pallas kernels for 35%

profile of v7, /device:TPU:9, one launch (start us, length us, event | category | flops | bytes accessed | tf_op | source)
XLA Modules:
  0.0 1041.1 jit_solution(9919051790086547265)
XLA Ops:
  20.8 41.3 %all-to-all-done = bf16[8,2,32,2048]{3,2,1,0:T(8,128)(2,1)S(1)} async-done(((bf16[8,2,32,2048]{3,2,1,0:T(8,128)(2,1)}), bf16[8,2,32,2048]{3,2,1,0:T(8,128)(2,1)S(1)}, u32[]{:S(2)}, u32[]{:S(2)}) %all-to-all-start) | async-done | bytes 2097184 | tf_op jit(solution)/shard_map/all_to_all | solution.py:584
  73.3 22.1 %collective-permute-done.refs_1_.refs_3_ = bf16[256,2048]{1,0:T(8,128)(2,1)S(1)} collective-permute-done((bf16[256,2048]{1,0:T(8,128)(2,1)}, bf16[256,2048]{1,0:T(8,128)(2,1)S(1)}, u32[]{:S(2)}, u32[]{:S(2)}) %collective-permute-start) | collective-permute-done | bytes 1048608 | tf_op jit(solution)/shard_map/ppermute | solution.py:429
  138.1 11.6 %shard_map.323.refs_1_ = bf16[1024,1536]{1,0:T(8,128)(2,1)} custom-call(bf16[256,2048]{1,0:T(8,128)(2,1)} %bitcast.2.refs_0_.refs_6_.refs_2_, bf16[256,2048]{1,0:T(8,128)(2,1)} %copy-done.58, bf16[128,2048]{1,0:T(8,128)(2,1)} %collective-permute-done.2.refs_2_.refs_4_, bf16[128,2048]{1,0:T(8,128)(2,1)} %collective-permute-done.3.refs_3_.refs_5_, ...), custom_call_target="tpu_custom_call" | custom-call | flops 12884901888 | bytes 33554432 | tf_op jit(solution)/shard_map/pallas_call | solution.py:45
  149.7 14.0 %shard_map.324 = (bf16[1024,512]{1,0:T(8,128)(2,1)}, f32[2,2,1024]{2,1,0:T(2,128)}) custom-call(f32[1024,1]{1,0:T(8,128)} %bitcast.96, bf16[1024,1536]{1,0:T(8,128)(2,1)} %shard_map.323.refs_1_), custom_call_target="tpu_custom_call" | custom-call | flops 17179869184 | bytes 9437184 | tf_op jit(solution)/shard_map/pallas_call | solution.py:45
  175.4 12.3 %shard_map.326.refs_1_ = bf16[1024,1536]{1,0:T(8,128)(2,1)} custom-call(bf16[256,2048]{1,0:T(8,128)(2,1)} %bitcast.83, bf16[256,2048]{1,0:T(8,128)(2,1)} %collective-permute-done.4.refs_7_.refs_1_.refs_8_, bf16[128,2048]{1,0:T(8,128)(2,1)} %collective-permute-done.13.refs_2_.refs_9_, bf16[128,2048]{1,0:T(8,128)(2,1)} %copy-done.84, ...), custom_call_target="tpu_custom_call" | custom-call | flops 12884901888 | bytes 33554432 | tf_op jit(solution)/shard_map/pallas_call | solution.py:45
  187.6 14.3 %shard_map.327 = (bf16[1024,512]{1,0:T(8,128)(2,1)}, f32[2,2,1024]{2,1,0:T(2,128)}) custom-call(f32[1024,1]{1,0:T(8,128)} %bitcast.94, bf16[1024,1536]{1,0:T(8,128)(2,1)} %shard_map.326.refs_1_), custom_call_target="tpu_custom_call" | custom-call | flops 17179869184 | bytes 9437184 | tf_op jit(solution)/shard_map/pallas_call | solution.py:45
  224.4 21.3 %collective-permute-done.10.refs_2_ = bf16[256,1024]{1,0:T(8,128)(2,1)S(1)} collective-permute-done((bf16[256,1024]{1,0:T(8,128)(2,1)S(1)}, bf16[256,1024]{1,0:T(8,128)(2,1)S(1)}, u32[]{:S(2)}, u32[]{:S(2)}) %collective-permute-start.10) | collective-permute-done | bytes 524320 | tf_op jit(solution)/shard_map/ppermute | solution.py:429
  256.8 18.6 %collective-permute-done.16.refs_4_.refs_9_ = bf16[256,2048]{1,0:T(8,128)(2,1)S(1)} collective-permute-done((bf16[256,2048]{1,0:T(8,128)(2,1)}, bf16[256,2048]{1,0:T(8,128)(2,1)S(1)}, u32[]{:S(2)}, u32[]{:S(2)}) %collective-permute-start.16) | collective-permute-done | bytes 1048608 | tf_op jit(solution)/shard_map/ppermute | solution.py:429
  298.6 16.3 %collective-permute-done.24.refs_4_.refs_9_ = bf16[256,2048]{1,0:T(8,128)(2,1)S(1)} collective-permute-done((bf16[256,2048]{1,0:T(8,128)(2,1)}, bf16[256,2048]{1,0:T(8,128)(2,1)S(1)}, u32[]{:S(2)}, u32[]{:S(2)}) %collective-permute-start.24) | collective-permute-done | bytes 1048608 | tf_op jit(solution)/shard_map/ppermute | solution.py:429
  327.4 16.1 %shard_map.330 = (f32[1024,2048]{1,0:T(8,128)}, bf16[1024,2048]{1,0:T(8,128)(2,1)}) custom-call(bf16[256,2048]{1,0:T(8,128)(2,1)} %get-tuple-element.124.refs_0_, bf16[256,2048]{1,0:T(8,128)(2,1)} %collective-permute-done.15.refs_1_.refs_8_, bf16[128,2048]{1,0:T(8,128)(2,1)} %collective-permute-done.17.refs_2_, ...), custom_call_target="tpu_custom_call" | custom-call | flops 17179869184 | bytes 58720256 | tf_op jit(solution)/shard_map/pallas_call | solution.py:45
  343.6 16.6 %shard_map.332 = (f32[1024,2048]{1,0:T(8,128)}, bf16[1024,2048]{1,0:T(8,128)(2,1)}) custom-call(bf16[256,2048]{1,0:T(8,128)(2,1)} %get-tuple-element.131.refs_0_.refs_5_, bf16[256,2048]{1,0:T(8,128)(2,1)} %copy-done.60, bf16[128,2048]{1,0:T(8,128)(2,1)} %collective-permute-done.25.refs_2_.refs_7_, bf16[128,2048]{1,0:T(8,128)(2,1)} %collective-permute-done.26.refs_3_.refs_8_, ...), custom_call_target="tpu_custom_call" | custom-call | flops 17179869184 | bytes 58720256 | tf_op jit(solution)/shard_map/pallas_call | solution.py:45
  360.2 14.2 %shard_map.333 = (bf16[512,1024]{1,0:T(8,128)(2,1)}, bf16[256,1024]{1,0:T(8,128)(2,1)}, bf16[256,1024]{1,0:T(8,128)(2,1)}, bf16[512,1024]{1,0:T(8,128)(2,1)}, bf...) custom-call(bf16[1024,2048]{1,0:T(8,128)(2,1)} %get-tuple-element.125.refs_7_.refs_0_.refs_10_, ...), custom_call_target="tpu_custom_call" | custom-call | flops 17179869184 | bytes 33554432 | tf_op jit(solution)/shard_map/pallas_call | solution.py:45
  374.7 17.4 %collective-permute-done.29.refs_4_ = bf16[512,1024]{1,0:T(8,128)(2,1)S(1)} collective-permute-done((bf16[512,1024]{1,0:T(8,128)(2,1)}, bf16[512,1024]{1,0:T(8,128)(2,1)S(1)}, u32[]{:S(2)}, u32[]{:S(2)}) %collective-permute-start.29) | collective-permute-done | bytes 1048608 | tf_op jit(solution)/shard_map/ppermute | solution.py:429
  415.0 13.9 %all-to-all-start.1 = ((bf16[8,32,2048]{2,1,0:T(8,128)(2,1)}), bf16[8,32,2048]{2,1,0:T(8,128)(2,1)S(1)}, u32[]{:S(2)}, u32[]{:S(2)}) async-start(bf16[8,32,2048]{2,1,0:T(8,128)(2,1)} %bitcast.92), calls=%async_computation.1 | async-start | bytes 2097152 | tf_op jit(solution)/shard_map/all_to_all | solution.py:686
  431.8 14.4 %shard_map.335 = (bf16[512,1024]{1,0:T(8,128)(2,1)}, bf16[256,1024]{1,0:T(8,128)(2,1)}, bf16[256,1024]{1,0:T(8,128)(2,1)}, bf16[512,1024]{1,0:T(8,128)(2,1)}, bf...) custom-call(bf16[1024,2048]{1,0:T(8,128)(2,1)} %get-tuple-element.132.refs_2_.refs_0_.refs_11_, ...), custom_call_target="tpu_custom_call" | custom-call | flops 17179869184 | bytes 33554432 | tf_op jit(solution)/shard_map/pallas_call | solution.py:45
  447.8 18.5 %shard_map.337 = (bf16[1024,2048]{1,0:T(8,128)(2,1)}, f32[1,2048]{1,0:T(1,128)}) custom-call(bf16[256,2048]{1,0:T(8,128)(2,1)} %get-tuple-element.141.refs_0_, bf16[256,2048]{1,0:T(8,128)(2,1)} %copy-done.64, bf16[128,2048]{1,0:T(8,128)(2,1)} %collective-permute-done.37.refs_2_, bf16[128,2048]{1,0:T(8,128)(2,1)} %collective-permute-done.38.refs_3_, ...), custom_call_target="tpu_custom_call" | custom-call | flops 17179869184 | bytes 41959424 | tf_op jit(solution)/shard_map/pallas_call | solution.py:45
  467.4 14.3 %shard_map.338 = (bf16[512,1024]{1,0:T(8,128)(2,1)}, bf16[256,1024]{1,0:T(8,128)(2,1)}, bf16[256,1024]{1,0:T(8,128)(2,1)}, bf16[512,1024]{1,0:T(8,128)(2,1)}, bf...) custom-call(bf16[1024,2048]{1,0:T(8,128)(2,1)} %get-tuple-element.151.refs_0_.refs_10_, ...), custom_call_target="tpu_custom_call" | custom-call | flops 17179869184 | bytes 33554432 | tf_op jit(solution)/shard_map/pallas_call | solution.py:45
  514.1 15.5 %collective-permute-done.48.refs_9_.refs_4_ = bf16[256,2048]{1,0:T(8,128)(2,1)S(1)} collective-permute-done((bf16[256,2048]{1,0:T(8,128)(2,1)}, bf16[256,2048]{1,0:T(8,128)(2,1)S(1)}, u32[]{:S(2)}, u32[]{:S(2)}) %collective-permute-start.48) | collective-permute-done | bytes 1048608 | tf_op jit(solution)/shard_map/ppermute | solution.py:429
  550.5 24.5 %shard_map.340 = bf16[2048,2048]{1,0:T(8,128)(2,1)} custom-call(bf16[256,2048]{1,0:T(8,128)(2,1)} %get-tuple-element.141.refs_0_, bf16[256,2048]{1,0:T(8,128)(2,1)} %copy-done.64, bf16[128,2048]{1,0:T(8,128)(2,1)} %collective-permute-done.37.refs_2_, bf16[128,2048]{1,0:T(8,128)(2,1)} %collective-permute-done.38.refs_3_, bf16[256,2048]{1,0:T(8,128)(2,1)} %copy-done.63, ...), custom_call_target="tpu_custom_call" | custom-call | flops 34359738368 | bytes 50331648 | tf_op jit(solution)/shard_map/pallas_call | solution.py:45
  579.7 34.7 %all-to-all-start.2 = ((bf16[8,32,2048]{2,1,0:T(8,128)(2,1)}), bf16[8,32,2048]{2,1,0:T(8,128)(2,1)S(1)}, u32[]{:S(2)}, u32[]{:S(2)}) async-start(bf16[8,32,2048]{2,1,0:T(8,128)(2,1)} %bitcast.17), calls=%async_computation.2 | async-start | bytes 2097152 | tf_op jit(solution)/shard_map/all_to_all | solution.py:686
  614.4 19.3 %shard_map.341 = (bf16[1024,2048]{1,0:T(8,128)(2,1)}, f32[1,2048]{1,0:T(1,128)}) custom-call(bf16[256,2048]{1,0:T(8,128)(2,1)} %get-tuple-element.161.refs_5_.refs_0_, bf16[256,2048]{1,0:T(8,128)(2,1)} %copy-done.67, bf16[128,2048]{1,0:T(8,128)(2,1)} %collective-permute-done.49.refs_7_.refs_2_, bf16[128,2048]{1,0:T(8,128)(2,1)} %copy-done.86, ...), custom_call_target="tpu_custom_call" | custom-call | flops 17179869184 | bytes 41959424 | tf_op jit(solution)/shard_map/pallas_call | solution.py:45
  633.7 19.7 %all-to-all-done.2.refs_2_ = bf16[8,32,2048]{2,1,0:T(8,128)(2,1)S(1)} async-done(((bf16[8,32,2048]{2,1,0:T(8,128)(2,1)}), bf16[8,32,2048]{2,1,0:T(8,128)(2,1)S(1)}, u32[]{:S(2)}, u32[]{:S(2)}) %all-to-all-start.2) | async-done | bytes 1048608 | tf_op jit(solution)/shard_map/all_to_all | solution.py:686
  654.4 14.2 %shard_map.342 = (bf16[512,1024]{1,0:T(8,128)(2,1)}, bf16[256,1024]{1,0:T(8,128)(2,1)}, bf16[256,1024]{1,0:T(8,128)(2,1)}, bf16[512,1024]{1,0:T(8,128)(2,1)}, bf...) custom-call(bf16[1024,2048]{1,0:T(8,128)(2,1)} %get-tuple-element.164.refs_0_.refs_11_, ...), custom_call_target="tpu_custom_call" | custom-call | flops 17179869184 | bytes 33554432 | tf_op jit(solution)/shard_map/pallas_call | solution.py:45
  682.1 21.5 %collective-permute-done.46.refs_3_ = bf16[128,2048]{1,0:T(8,128)(2,1)} collective-permute-done((bf16[128,2048]{1,0:T(8,128)(2,1)S(1)}, bf16[128,2048]{1,0:T(8,128)(2,1)}, u32[]{:S(2)}, u32[]{:S(2)}) %collective-permute-start.46) | collective-permute-done | bytes 524320 | tf_op jit(solution)/shard_map/ppermute | solution.py:429
  713.4 14.9 %shard_map.344 = (bf16[1024,1536]{1,0:T(8,128)(2,1)}, f32[2,1,768]{2,1,0:T(1,128)}) custom-call(f32[1024,1]{1,0:T(8,128)} %bitcast.97, bf16[1024,1536]{1,0:T(8,128)(2,1)} %shard_map.323.refs_1_, bf16[1024,512]{1,0:T(8,128)(2,1)} %get-tuple-element.115.refs_0_.refs_2_.refs_10_, bf16[1024,512]{1,0:T(8,128)(2,1)} %shard_map.343.refs_3_, ...), custom_call_target="tpu_custom_call" | custom-call | flops 42949672960 | bytes 18874368 | tf_op jit(solution)/shard_map/pallas_call | solution.py:45
  728.2 11.6 %shard_map.345 = (bf16[512,1024]{1,0:T(8,128)(2,1)}, bf16[256,1024]{1,0:T(8,128)(2,1)}, bf16[256,1024]{1,0:T(8,128)(2,1)}, bf16[512,1024]{1,0:T(8,128)(2,1)}, bf...) custom-call(bf16[1024,1536]{1,0:T(8,128)(2,1)} %get-tuple-element.168.refs_0_.refs_12_, ...), custom_call_target="tpu_custom_call" | custom-call | flops 12884901888 | bytes 27262976 | tf_op jit(solution)/shard_map/pallas_call | solution.py:45
  749.9 24.4 %shard_map.347 = bf16[2048,2048]{1,0:T(8,128)(2,1)} custom-call(bf16[256,2048]{1,0:T(8,128)(2,1)} %get-tuple-element.124.refs_0_, bf16[256,2048]{1,0:T(8,128)(2,1)} %collective-permute-done.15.refs_1_.refs_8_, bf16[128,2048]{1,0:T(8,128)(2,1)} %collective-permute-done.17.refs_2_, bf16[128,2048]{1,0:T(8,128)(2,1)} %collective-permute-done.18.refs_3_, ...), custom_call_target="tpu_custom_call" | custom-call | flops 34359738368 | bytes 50331648 | tf_op jit(solution)/shard_map/pallas_call | solution.py:45
  825.7 14.6 %shard_map.350 = (bf16[1024,1536]{1,0:T(8,128)(2,1)}, f32[2,1,768]{2,1,0:T(1,128)}) custom-call(f32[1024,1]{1,0:T(8,128)} %bitcast.95, bf16[1024,1536]{1,0:T(8,128)(2,1)} %shard_map.326.refs_1_, bf16[1024,512]{1,0:T(8,128)(2,1)} %get-tuple-element.122.refs_0_.refs_11_.refs_2_, bf16[1024,512]{1,0:T(8,128)(2,1)} %shard_map.348.refs_12_.refs_3_, ...), custom_call_target="tpu_custom_call" | custom-call | flops 42949672960 | bytes 18874368 | tf_op jit(solution)/shard_map/pallas_call | solution.py:45
  845.7 16.2 %all-to-all-start.3 = ((bf16[8,32,2048]{2,1,0:T(8,128)(2,1)}), bf16[8,32,2048]{2,1,0:T(8,128)(2,1)S(1)}, u32[]{:S(2)}, u32[]{:S(2)}) async-start(bf16[8,32,2048]{2,1,0:T(8,128)(2,1)} %bitcast.87), calls=%async_computation.3 | async-start | bytes 2097152 | tf_op jit(solution)/shard_map/all_to_all | solution.py:686
  866.3 20.2 %shard_map.352 = (bf16[1088,1536]{1,0:T(8,128)(2,1)}, bf16[1088,1536]{1,0:T(8,128)(2,1)}) custom-call(s32[1]{0:T(128)} %bitcast.24.refs_0_, f32[1,1536]{1,0:T(1,128)} %bitcast.106, bf16[256,2048]{1,0:T(8,128)(2,1)} %bitcast.2.refs_0_.refs_6_.refs_2_, bf16[256,2048]{1,0:T(8,128)(2,1)} %copy-done.58, bf16[128,2048]{1,0:T(8,128)(2,1)} %collective-permute-done.2.refs_2_.refs_4_, ...), custom_call_target="tpu_custom_call" | custom-call | flops 25769803776 | bytes 41943040 | tf_op jit(solution)/shard_map/pallas_call | solution.py:45
  901.4 11.7 %shard_map.353 = (bf16[512,1024]{1,0:T(8,128)(2,1)}, bf16[256,1024]{1,0:T(8,128)(2,1)}, bf16[256,1024]{1,0:T(8,128)(2,1)}, bf16[512,1024]{1,0:T(8,128)(2,1)}, bf...) custom-call(bf16[1024,1536]{1,0:T(8,128)(2,1)} %get-tuple-element.188.refs_7_.refs_13_.refs_0_, ...), custom_call_target="tpu_custom_call" | custom-call | flops 12884901888 | bytes 27262976 | tf_op jit(solution)/shard_map/pallas_call | solution.py:45
  923.4 32.9 %collective-permute-done.73 = f32[112,128]{1,0:T(8,128)S(1)} collective-permute-done((f32[112,128]{1,0:T(8,128)S(1)}, f32[112,128]{1,0:T(8,128)S(1)}, u32[]{:S(2)}, u32[]{:S(2)}) %collective-permute-start.73) | collective-permute-done | bytes 57376 | tf_op jit(solution)/shard_map/ppermute | solution.py:531
  (548 shorter events, 425.0 us)
Async XLA Ops:
  10.8 51.3 %all-to-all-start = ((bf16[8,2,32,2048]{3,2,1,0:T(8,128)(2,1)}), bf16[8,2,32,2048]{3,2,1,0:T(8,128)(2,1)S(1)}, u32[]{:S(2)}, u32[]{:S(2)}) async-start(bf16[8,2,32,2048]{3,2,1,0:T(8,128)(2,1)} %bitcast.78), calls=%async_computation | async-start | bytes 4194304 | tf_op jit(solution)/shard_map/all_to_all | solution.py:584
  16.7 116.4 %all-gather.5.cloned.1.call-start = ((), (), s32[]{:S(2)}) async-start(), calls=%async_computation.8 | async-start | bytes 7667712 | tf_op jit(solution)/shard_map/all_gather | solution.py:485
  64.2 101.2 %all-gather.7.cloned.1.call-start = ((), (), s32[]{:S(2)}) async-start(), calls=%async_computation.9 | async-start | bytes 2359296 | tf_op jit(solution)/shard_map/all_gather | solution.py:485
  66.9 251.0 %all-gather.9.cloned.1.call-start = ((), (), s32[]{:S(2)}) async-start(), calls=%async_computation.10 | async-start | bytes 9437184 | tf_op jit(solution)/shard_map/all_gather | solution.py:485
  69.8 290.4 %all-gather.11.cloned.1.call-start = ((), (), s32[]{:S(2)}) async-start(), calls=%async_computation.11 | async-start | bytes 9437184 | tf_op jit(solution)/shard_map/all_gather | solution.py:485
  72.1 36.3 %collective-permute-start.1 = (bf16[256,2048]{1,0:T(8,128)(2,1)}, bf16[256,2048]{1,0:T(8,128)(2,1)}, u32[]{:S(2)}, u32[]{:S(2)}) collective-permute-start(bf16[256,2048]{1,0:T(8,128)(2,1)} %bitcast.2.refs_0_.refs_6_.refs_2_), channel_id=1, source_target_pairs={{0,2},{1,3},{2,0},{3,1},{4,6},{5,7},{6,4},{7,5},{8,10},{9,11},{10,... | collective-permute-start | bytes 3145736 | tf_op jit(solution)/shard_map/ppermute | solution.py:429
  122.5 52.1 %collective-permute-start.13 = (bf16[128,2048]{1,0:T(8,128)(2,1)S(1)}, bf16[128,2048]{1,0:T(8,128)(2,1)}, u32[]{:S(2)}, u32[]{:S(2)}) collective-permute-start(bf16[128,2048]{1,0:T(8,128)(2,1)S(1)} %slice.410), channel_id=1, source_target_pairs={{0,1},{1,0},{2,3},{3,2},{4,5},{5,4},{6,7},{7,6},{8,9},{9,8},{10,11... | collective-permute-start | bytes 1572872 | tf_op jit(solution)/shard_map/ppermute | solution.py:429
  123.9 50.7 %collective-permute-start.14 = (bf16[128,2048]{1,0:T(8,128)(2,1)S(1)}, bf16[128,2048]{1,0:T(8,128)(2,1)S(1)}, u32[]{:S(2)}, u32[]{:S(2)}) collective-permute-start(bf16[128,2048]{1,0:T(8,128)(2,1)S(1)} %slice.411), channel_id=1, source_target_pairs={{0,2},{1,3},{2,0},{3,1},{4,6},{5,7},{6,4},{7,5},{8,10},{9,11},{10,... | collective-permute-start | bytes 1572872 | tf_op jit(solution)/shard_map/ppermute | solution.py:429
  210.1 42.2 %collective-permute-start.21 = (bf16[512,1024]{1,0:T(8,128)(2,1)}, bf16[512,1024]{1,0:T(8,128)(2,1)S(1)}, u32[]{:S(2)}, u32[]{:S(2)}) collective-permute-start(bf16[512,1024]{1,0:T(8,128)(2,1)} %get-tuple-element.129), channel_id=1, source_target_pairs={{0,2},{1,3},{2,0},{3,1},{4,6},{5,7},{6,4},{7,5},{8,10},{9,11},{10,... | collective-permute-start | bytes 3145736 | tf_op jit(solution)/shard_map/ppermute | solution.py:429
  211.9 42.0 %collective-permute-start.19 = (bf16[512,1024]{1,0:T(8,128)(2,1)}, bf16[512,1024]{1,0:T(8,128)(2,1)S(1)}, u32[]{:S(2)}, u32[]{:S(2)}) collective-permute-start(bf16[512,1024]{1,0:T(8,128)(2,1)} %get-tuple-element.123.refs_8_), channel_id=1, source_target_pairs={{0,1},{1,0},{2,3},{3,2},{4,5},{5,4},{6,7},{7,6},{8,9},{9,8},{10,11... | collective-permute-start | bytes 3145736 | tf_op jit(solution)/shard_map/ppermute | solution.py:429
  415.0 51.3 %all-to-all-start.1 = ((bf16[8,32,2048]{2,1,0:T(8,128)(2,1)}), bf16[8,32,2048]{2,1,0:T(8,128)(2,1)S(1)}, u32[]{:S(2)}, u32[]{:S(2)}) async-start(bf16[8,32,2048]{2,1,0:T(8,128)(2,1)} %bitcast.92), calls=%async_computation.1 | async-start | bytes 2097152 | tf_op jit(solution)/shard_map/all_to_all | solution.py:686
  428.9 433.6 %reduce-scatter.4.cloned.1.call-start = ((), (), s32[]{:S(2)}) async-start(), calls=%async_computation.12 | async-start | bytes 9437184 | tf_op jit(solution)/shard_map/reduce_scatter | solution.py:488
  446.2 36.7 %collective-permute-start.35 = (bf16[512,1024]{1,0:T(8,128)(2,1)}, bf16[512,1024]{1,0:T(8,128)(2,1)S(1)}, u32[]{:S(2)}, u32[]{:S(2)}) collective-permute-start(bf16[512,1024]{1,0:T(8,128)(2,1)} %get-tuple-element.146), channel_id=1, source_target_pairs={{0,2},{1,3},{2,0},{3,1},{4,6},{5,7},{6,4},{7,5},{8,10},{9,11},{10,... | collective-permute-start | bytes 3145736 | tf_op jit(solution)/shard_map/ppermute | solution.py:429
  446.9 37.8 %collective-permute-start.33 = (bf16[512,1024]{1,0:T(8,128)(2,1)}, bf16[512,1024]{1,0:T(8,128)(2,1)S(1)}, u32[]{:S(2)}, u32[]{:S(2)}) collective-permute-start(bf16[512,1024]{1,0:T(8,128)(2,1)} %get-tuple-element.143.refs_9_), channel_id=1, source_target_pairs={{0,1},{1,0},{2,3},{3,2},{4,5},{5,4},{6,7},{7,6},{8,9},{9,8},{10,11... | collective-permute-start | bytes 3145736 | tf_op jit(solution)/shard_map/ppermute | solution.py:429
  579.7 73.8 %all-to-all-start.2 = ((bf16[8,32,2048]{2,1,0:T(8,128)(2,1)}), bf16[8,32,2048]{2,1,0:T(8,128)(2,1)S(1)}, u32[]{:S(2)}, u32[]{:S(2)}) async-start(bf16[8,32,2048]{2,1,0:T(8,128)(2,1)} %bitcast.17), calls=%async_computation.2 | async-start | bytes 2097152 | tf_op jit(solution)/shard_map/all_to_all | solution.py:686
  614.4 361.2 %reduce-scatter.6.cloned.1.call-start = ((), (), s32[]{:S(2)}) async-start(), calls=%async_computation.13 | async-start | bytes 9437184 | tf_op jit(solution)/shard_map/reduce_scatter | solution.py:488
  668.6 41.2 %collective-permute-start.52 = (bf16[512,1024]{1,0:T(8,128)(2,1)}, bf16[512,1024]{1,0:T(8,128)(2,1)S(1)}, u32[]{:S(2)}, u32[]{:S(2)}) collective-permute-start(bf16[512,1024]{1,0:T(8,128)(2,1)} %get-tuple-element.167), channel_id=1, source_target_pairs={{0,2},{1,3},{2,0},{3,1},{4,6},{5,7},{6,4},{7,5},{8,10},{9,11},{10,... | collective-permute-start | bytes 3145736 | tf_op jit(solution)/shard_map/ppermute | solution.py:429
  671.4 39.6 %collective-permute-start.51 = (bf16[512,1024]{1,0:T(8,128)(2,1)}, bf16[512,1024]{1,0:T(8,128)(2,1)S(1)}, u32[]{:S(2)}, u32[]{:S(2)}) collective-permute-start(bf16[512,1024]{1,0:T(8,128)(2,1)} %get-tuple-element.165.refs_6_), channel_id=1, source_target_pairs={{0,1},{1,0},{2,3},{3,2},{4,5},{5,4},{6,7},{7,6},{8,9},{9,8},{10,11... | collective-permute-start | bytes 3145736 | tf_op jit(solution)/shard_map/ppermute | solution.py:429
  740.4 34.4 %collective-permute-start.55 = (bf16[512,1024]{1,0:T(8,128)(2,1)}, bf16[512,1024]{1,0:T(8,128)(2,1)S(1)}, u32[]{:S(2)}, u32[]{:S(2)}) collective-permute-start(bf16[512,1024]{1,0:T(8,128)(2,1)} %get-tuple-element.173), channel_id=1, source_target_pairs={{0,2},{1,3},{2,0},{3,1},{4,6},{5,7},{6,4},{7,5},{8,10},{9,11},{10,... | collective-permute-start | bytes 3145736 | tf_op jit(solution)/shard_map/ppermute | solution.py:429
  748.6 36.2 %collective-permute-start.59 = (bf16[256,2048]{1,0:T(8,128)(2,1)}, bf16[256,2048]{1,0:T(8,128)(2,1)S(1)}, u32[]{:S(2)}, u32[]{:S(2)}) collective-permute-start(bf16[256,2048]{1,0:T(8,128)(2,1)} %get-tuple-element.181.refs_0_.refs_5_), channel_id=1, source_target_pairs={{0,1},{1,0},{2,3},{3,2},{4,5},{5,4},{6,7},{7,6},{8,9},{9,8},{10,11... | collective-permute-start | bytes 3145736 | tf_op jit(solution)/shard_map/ppermute | solution.py:429
  748.7 37.6 %collective-permute-start.60 = (bf16[256,2048]{1,0:T(8,128)(2,1)}, bf16[256,2048]{1,0:T(8,128)(2,1)}, u32[]{:S(2)}, u32[]{:S(2)}) collective-permute-start(bf16[256,2048]{1,0:T(8,128)(2,1)} %get-tuple-element.181.refs_0_.refs_5_), channel_id=1, source_target_pairs={{0,2},{1,3},{2,0},{3,1},{4,6},{5,7},{6,4},{7,5},{8,10},{9,11},{10,... | collective-permute-start | bytes 3145736 | tf_op jit(solution)/shard_map/ppermute | solution.py:429
  797.2 43.1 %collective-permute-start.56 = (bf16[256,1024]{1,0:T(8,128)(2,1)}, bf16[256,1024]{1,0:T(8,128)(2,1)S(1)}, u32[]{:S(2)}, u32[]{:S(2)}) collective-permute-start(bf16[256,1024]{1,0:T(8,128)(2,1)} %add_convert_fusion.7), channel_id=1, source_target_pairs={{0,1},{1,0},{2,3},{3,2},{4,5},{5,4},{6,7},{7,6},{8,9},{9,8},{10,11... | collective-permute-start | bytes 1572872 | tf_op jit(solution)/shard_map/ppermute | solution.py:429
  797.7 42.6 %collective-permute-start.54 = (bf16[256,1024]{1,0:T(8,128)(2,1)S(1)}, bf16[256,1024]{1,0:T(8,128)(2,1)S(1)}, u32[]{:S(2)}, u32[]{:S(2)}) collective-permute-start(bf16[256,1024]{1,0:T(8,128)(2,1)S(1)} %add_convert_fusion.8), channel_id=1, source_target_pairs={{0,2},{1,3},{2,0},{3,1},{4,6},{5,7},{6,4},{7,5},{8,10},{9,11},{10,... | collective-permute-start | bytes 1572872 | tf_op jit(solution)/shard_map/ppermute | solution.py:429
  825.1 40.6 %collective-permute-start.64 = (f32[96,128]{1,0:T(8,128)S(1)}, f32[96,128]{1,0:T(8,128)S(1)}, u32[]{:S(2)}, u32[]{:S(2)}) collective-permute-start(f32[96,128]{1,0:T(8,128)S(1)} %add.343), channel_id=1, source_target_pairs={{0,2},{1,3},{2,0},{3,1},{4,6},{5,7},{6,4},{7,5},{8,10},{9,11},{10,... | collective-permute-start | bytes 147464 | tf_op jit(solution)/shard_map/ppermute | solution.py:531
  845.7 54.7 %all-to-all-start.3 = ((bf16[8,32,2048]{2,1,0:T(8,128)(2,1)}), bf16[8,32,2048]{2,1,0:T(8,128)(2,1)S(1)}, u32[]{:S(2)}, u32[]{:S(2)}) async-start(bf16[8,32,2048]{2,1,0:T(8,128)(2,1)} %bitcast.87), calls=%async_computation.3 | async-start | bytes 2097152 | tf_op jit(solution)/shard_map/all_to_all | solution.py:686
  861.9 131.4 %reduce-scatter.8.cloned.1.call-start = ((), (), s32[]{:S(2)}) async-start(), calls=%async_computation.14 | async-start | bytes 2359296 | tf_op jit(solution)/shard_map/reduce_scatter | solution.py:488
  913.0 43.9 %collective-permute-start.68 = (bf16[512,1024]{1,0:T(8,128)(2,1)}, bf16[512,1024]{1,0:T(8,128)(2,1)}, u32[]{:S(2)}, u32[]{:S(2)}) collective-permute-start(bf16[512,1024]{1,0:T(8,128)(2,1)} %get-tuple-element.198), channel_id=1, source_target_pairs={{0,2},{1,3},{2,0},{3,1},{4,6},{5,7},{6,4},{7,5},{8,10},{9,11},{10,... | collective-permute-start | bytes 3145736 | tf_op jit(solution)/shard_map/ppermute | solution.py:429
  914.6 45.6 %collective-permute-start.66 = (bf16[512,1024]{1,0:T(8,128)(2,1)}, bf16[512,1024]{1,0:T(8,128)(2,1)}, u32[]{:S(2)}, u32[]{:S(2)}) collective-permute-start(bf16[512,1024]{1,0:T(8,128)(2,1)} %get-tuple-element.195), channel_id=1, source_target_pairs={{0,1},{1,0},{2,3},{3,2},{4,5},{5,4},{6,7},{7,6},{8,9},{9,8},{10,11... | collective-permute-start | bytes 3145736 | tf_op jit(solution)/shard_map/ppermute | solution.py:429
  917.8 45.3 %collective-permute-start.71 = (bf16[272,1536]{1,0:T(8,128)(2,1)S(1)}, bf16[272,1536]{1,0:T(8,128)(2,1)S(1)}, u32[]{:S(2)}, u32[]{:S(2)}) collective-permute-start(bf16[272,1536]{1,0:T(8,128)(2,1)S(1)} %add_convert_fusion.2), channel_id=1, source_target_pairs={{0,8},{4,12},{8,16},{12,20},{1,9},{5,13},{9,17},{13,21},{2,10},{6,... | collective-permute-start | bytes 2506760 | tf_op jit(solution)/shard_map/ppermute | solution.py:482
  921.1 42.0 %collective-permute-start.72 = (bf16[272,1536]{1,0:T(8,128)(2,1)S(1)}, bf16[272,1536]{1,0:T(8,128)(2,1)S(1)}, u32[]{:S(2)}, u32[]{:S(2)}) collective-permute-start(bf16[272,1536]{1,0:T(8,128)(2,1)S(1)} %add_convert_fusion.2), channel_id=1, source_target_pairs={{24,16},{28,20},{16,8},{20,12},{25,17},{29,21},{17,9},{21,13},{26,... | collective-permute-start | bytes 2506760 | tf_op jit(solution)/shard_map/ppermute | solution.py:482
  967.6 38.8 %collective-permute-start.76 = (bf16[272,1536]{1,0:T(8,128)(2,1)}, bf16[272,1536]{1,0:T(8,128)(2,1)}, u32[]{:S(2)}, u32[]{:S(2)}) collective-permute-start(bf16[272,1536]{1,0:T(8,128)(2,1)} %get-tuple-element.257), channel_id=1, source_target_pairs={{0,24},{4,28},{8,0},{12,4},{16,8},{20,12},{24,16},{28,20},{1,25},{... | collective-permute-start | bytes 2506760 | tf_op jit(solution)/shard_map/ppermute | solution.py:482
  982.9 44.7 %all-to-all-start.4 = ((bf16[8,32,2048]{2,1,0:T(8,128)(2,1)}), bf16[8,32,2048]{2,1,0:T(8,128)(2,1)}, u32[]{:S(2)}, u32[]{:S(2)}) async-start(bf16[8,32,2048]{2,1,0:T(8,128)(2,1)} %bitcast.86), calls=%async_computation.6 | async-start | bytes 2097152 | tf_op jit(solution)/shard_map/all_to_all | solution.py:686
  (155 other events, 2192.1 us)
Sparse Core Ops, SparseCore 0:
  64.4 68.6 all-gather.4
  135.3 30.1 all-gather.6
  167.0 78.8 all-gather.8
  247.4 80.6 all-gather.10
  579.8 139.6 reduce-scatter.3
  791.5 116.0 reduce-scatter.5
  910.5 40.2 reduce-scatter.7

commit v8 on v6

--- a/solution.py
+++ b/solution.py
@@ -651,14 +651,14 @@
         mix, log = attend(qkv[s], biases[s], 2)
         mixed.append(mix)
         logs.append(log)
-        terms.append(terms_matmul(mix, mid_weight, spans, sums[-1][1] if sums else ()))
+        terms.append(terms_matmul(mix, mid_weight, spans, sums[-1][2] if sums else (row_vectors,)))
         sums.append(tensor.scatter(terms[s]))
         before = (terms[s][0][0],)
     first, first_pieces = [], []
     for s in over:
         first.append(first_norm(sums[s][0], arrived[s], row_vectors, before))
         first_pieces.append(tensor.gather(first[s][0]))
-        before = near(first_pieces[s])
+        before = tuple(first_pieces[s][1:])
     hidden, active, terms, sums = [], [], [], []
     before = ()
     for s in over:

time: 947 us -> 943 us (level)
  waiting for transfers between devices: 262 us -> 272 us
    ppermute x67, waiting for transfers between devices: 181 us -> 192 us  [swap(): lax.ppermute(array, 'tensor', [(i, i ^ bit) for i in range(self.size)])]
    unnamed x196 -> x204, local copies, waits for them, and re-layouts: 33.6 us -> 29.5 us
  transfers between devices with their start and end apart: 89 -> 89, of which waited for: 25 -> 27; matrix products, arithmetic and copies ran while one was open for 12% -> 11% of each run, Pallas kernels for 40% -> 40%
where the time goes in v8:
time: 943 us; the launch traced here: 928 us
  Pallas kernels  383 us (41%)
  waiting for transfers between devices  272 us (29%)
  starting transfers between devices  115 us (12%)
  local copies, waits for them, and re-layouts  78.7 us (8%)
  other arithmetic  53.4 us (6%)
  between operations  25.5 us (3%)
    pallas_call x32, Pallas kernels, launch(): pl.pallas_call(run, grid=grid, in_specs=list(in_specs) + [pl.BlockSpec(me...  383 us
    ppermute x67, waiting for transfers between devices, swap(): lax.ppermute(array, 'tensor', [(i, i ^ bit) for i in range(self.size)])  192 us
    ppermute x67, starting transfers between devices, swap(): lax.ppermute(array, 'tensor', [(i, i ^ bit) for i in range(self.size)])  54 us
    all_to_all x1, waiting for transfers between devices, local(): came = lax.all_to_all(sent, 'dp', split_axis=0, concat_axis=0, tiled=True)  41.3 us
    all_to_all x4, starting transfers between devices, give_back(): lax.all_to_all(rows.reshape(groups, arrival_rows, model_width), 'dp', spl...  38.5 us
    unnamed x204, local copies, waits for them, and re-layouts  29.5 us
  transfers between devices with their start and end apart: 89, of which 27 were waited for; matrix products, arithmetic and copies ran while one was open for 11% of the time, Pallas kernels for 40%

profile of v8, /device:TPU:9, one launch (start us, length us, event | category | flops | bytes accessed | tf_op | source)
XLA Modules:
  0.0 927.7 jit_solution(1163354367180982767)
XLA Ops:
  20.8 41.3 %all-to-all-done = bf16[8,2,32,2048]{3,2,1,0:T(8,128)(2,1)S(1)} async-done(((bf16[8,2,32,2048]{3,2,1,0:T(8,128)(2,1)}), bf16[8,2,32,2048]{3,2,1,0:T(8,128)(2,1)S(1)}, u32[]{:S(2)}, u32[]{:S(2)}) %all-to-all-start) | async-done | bytes 2097184 | tf_op jit(solution)/shard_map/all_to_all | solution.py:584
  73.9 21.9 %collective-permute-done.refs_1_.refs_3_ = bf16[256,2048]{1,0:T(8,128)(2,1)S(1)} collective-permute-done((bf16[256,2048]{1,0:T(8,128)(2,1)S(1)}, bf16[256,2048]{1,0:T(8,128)(2,1)S(1)}, u32[]{:S(2)}, u32[]{:S(2)}) %collective-permute-start) | collective-permute-done | bytes 1048608 | tf_op jit(solution)/shard_map/ppermute | solution.py:429
  110.0 11.7 %collective-permute-done.5.refs_8_.refs_4_.refs_11_ = bf16[256,2048]{1,0:T(8,128)(2,1)} collective-permute-done((bf16[256,2048]{1,0:T(8,128)(2,1)S(1)}, bf16[256,2048]{1,0:T(8,128)(2,1)}, u32[]{:S(2)}, u32[]{:S(2)}) %collective-permute-start.5) | collective-permute-done | bytes 1048608 | tf_op jit(solution)/shard_map/ppermute | solution.py:429
  138.2 11.6 %shard_map.323.refs_1_ = bf16[1024,1536]{1,0:T(8,128)(2,1)} custom-call(bf16[256,2048]{1,0:T(8,128)(2,1)} %bitcast.86, bf16[256,2048]{1,0:T(8,128)(2,1)} %copy-done.58, bf16[128,2048]{1,0:T(8,128)(2,1)} %collective-permute-done.2.refs_2_.refs_4_, bf16[128,2048]{1,0:T(8,128)(2,1)} %collective-permute-done.3.refs_3_.refs_5_, ...), custom_call_target="tpu_custom_call" | custom-call | flops 12884901888 | bytes 33554432 | tf_op jit(solution)/shard_map/pallas_call | solution.py:45
  149.8 13.9 %shard_map.324 = (bf16[1024,512]{1,0:T(8,128)(2,1)}, f32[2,2,1024]{2,1,0:T(2,128)}) custom-call(f32[1024,1]{1,0:T(8,128)} %bitcast.104, bf16[1024,1536]{1,0:T(8,128)(2,1)} %shard_map.323.refs_1_), custom_call_target="tpu_custom_call" | custom-call | flops 17179869184 | bytes 9437184 | tf_op jit(solution)/shard_map/pallas_call | solution.py:45
  174.6 12.4 %shard_map.326.refs_1_ = bf16[1024,1536]{1,0:T(8,128)(2,1)} custom-call(bf16[256,2048]{1,0:T(8,128)(2,1)} %bitcast.93, bf16[256,2048]{1,0:T(8,128)(2,1)} %collective-permute-done.4.refs_7_.refs_1_.refs_8_, bf16[128,2048]{1,0:T(8,128)(2,1)} %collective-permute-done.13.refs_2_.refs_9_, bf16[128,2048]{1,0:T(8,128)(2,1)} %collective-permute-done.14.refs_3_.refs_10_, ...), custom_call_target="tpu_custom_call" | custom-call | flops 12884901888 | bytes 33554432 | tf_op jit(solution)/shard_map/pallas_call | solution.py:45
  200.8 14.1 %shard_map.327 = (bf16[1024,512]{1,0:T(8,128)(2,1)}, f32[2,2,1024]{2,1,0:T(2,128)}) custom-call(f32[1024,1]{1,0:T(8,128)} %bitcast.102, bf16[1024,1536]{1,0:T(8,128)(2,1)} %shard_map.326.refs_1_), custom_call_target="tpu_custom_call" | custom-call | flops 17179869184 | bytes 9437184 | tf_op jit(solution)/shard_map/pallas_call | solution.py:45
  231.1 20.5 %collective-permute-done.16.refs_4_.refs_11_ = bf16[256,2048]{1,0:T(8,128)(2,1)S(1)} collective-permute-done((bf16[256,2048]{1,0:T(8,128)(2,1)}, bf16[256,2048]{1,0:T(8,128)(2,1)S(1)}, u32[]{:S(2)}, u32[]{:S(2)}) %collective-permute-start.16) | collective-permute-done | bytes 1048608 | tf_op jit(solution)/shard_map/ppermute | solution.py:429
  252.9 21.3 %collective-permute-done.21.refs_4_ = bf16[512,1024]{1,0:T(8,128)(2,1)S(1)} collective-permute-done((bf16[512,1024]{1,0:T(8,128)(2,1)}, bf16[512,1024]{1,0:T(8,128)(2,1)S(1)}, u32[]{:S(2)}, u32[]{:S(2)}) %collective-permute-start.21) | collective-permute-done | bytes 1048608 | tf_op jit(solution)/shard_map/ppermute | solution.py:429
  285.5 11.2 %collective-permute-done.22.refs_5_ = bf16[256,1024]{1,0:T(8,128)(2,1)} collective-permute-done((bf16[256,1024]{1,0:T(8,128)(2,1)S(1)}, bf16[256,1024]{1,0:T(8,128)(2,1)}, u32[]{:S(2)}, u32[]{:S(2)}) %collective-permute-start.22) | collective-permute-done | bytes 524320 | tf_op jit(solution)/shard_map/ppermute | solution.py:429
  304.3 20.2 %collective-permute-done.24.refs_4_.refs_9_ = bf16[256,2048]{1,0:T(8,128)(2,1)S(1)} collective-permute-done((bf16[256,2048]{1,0:T(8,128)(2,1)}, bf16[256,2048]{1,0:T(8,128)(2,1)S(1)}, u32[]{:S(2)}, u32[]{:S(2)}) %collective-permute-start.24) | collective-permute-done | bytes 1048608 | tf_op jit(solution)/shard_map/ppermute | solution.py:429
  326.3 16.2 %shard_map.330 = (f32[1024,2048]{1,0:T(8,128)}, bf16[1024,2048]{1,0:T(8,128)(2,1)}) custom-call(bf16[256,2048]{1,0:T(8,128)(2,1)} %get-tuple-element.124.refs_0_, bf16[256,2048]{1,0:T(8,128)(2,1)} %copy-done.32, bf16[128,2048]{1,0:T(8,128)(2,1)} %copy-done.36, bf16[128,2048]{1,0:T(8,128)(2,1)} %collective-permute-done.18.refs_3_.refs_10_, ...), custom_call_target="tpu_custom_call" | custom-call | flops 17179869184 | bytes 58720256 | tf_op jit(solution)/shard_map/pallas_call | solution.py:45
  342.5 16.5 %shard_map.332 = (f32[1024,2048]{1,0:T(8,128)}, bf16[1024,2048]{1,0:T(8,128)(2,1)}) custom-call(bf16[256,2048]{1,0:T(8,128)(2,1)} %get-tuple-element.131.refs_0_.refs_5_, bf16[256,2048]{1,0:T(8,128)(2,1)} %copy-done.60, bf16[128,2048]{1,0:T(8,128)(2,1)} %collective-permute-done.25.refs_2_.refs_7_, bf16[128,2048]{1,0:T(8,128)(2,1)} %collective-permute-done.26.refs_3_.refs_8_, ...), custom_call_target="tpu_custom_call" | custom-call | flops 17179869184 | bytes 58720256 | tf_op jit(solution)/shard_map/pallas_call | solution.py:45
  359.0 14.2 %shard_map.333 = (bf16[512,1024]{1,0:T(8,128)(2,1)}, bf16[256,1024]{1,0:T(8,128)(2,1)}, bf16[256,1024]{1,0:T(8,128)(2,1)}, bf16[512,1024]{1,0:T(8,128)(2,1)}, bf...) custom-call(bf16[1024,2048]{1,0:T(8,128)(2,1)} %get-tuple-element.125.refs_7_.refs_0_.refs_10_, ...), custom_call_target="tpu_custom_call" | custom-call | flops 17179869184 | bytes 33554432 | tf_op jit(solution)/shard_map/pallas_call | solution.py:45
  374.6 14.2 %shard_map.334 = (bf16[512,1024]{1,0:T(8,128)(2,1)}, bf16[256,1024]{1,0:T(8,128)(2,1)}, bf16[256,1024]{1,0:T(8,128)(2,1)}, bf16[512,1024]{1,0:T(8,128)(2,1)}, bf...) custom-call(bf16[1024,2048]{1,0:T(8,128)(2,1)} %get-tuple-element.132.refs_2_.refs_0_.refs_11_, ...), custom_call_target="tpu_custom_call" | custom-call | flops 17179869184 | bytes 33554432 | tf_op jit(solution)/shard_map/pallas_call | solution.py:45
  399.5 27.3 %collective-permute-done.30.refs_5_ = bf16[256,1024]{1,0:T(8,128)(2,1)S(1)} collective-permute-done((bf16[256,1024]{1,0:T(8,128)(2,1)S(1)}, bf16[256,1024]{1,0:T(8,128)(2,1)S(1)}, u32[]{:S(2)}, u32[]{:S(2)}) %collective-permute-start.30) | collective-permute-done | bytes 524320 | tf_op jit(solution)/shard_map/ppermute | solution.py:429
  441.5 12.3 %collective-permute-done.36.refs_10_.refs_4_ = bf16[256,2048]{1,0:T(8,128)(2,1)S(1)} collective-permute-done((bf16[256,2048]{1,0:T(8,128)(2,1)}, bf16[256,2048]{1,0:T(8,128)(2,1)S(1)}, u32[]{:S(2)}, u32[]{:S(2)}) %collective-permute-start.36) | collective-permute-done | bytes 1048608 | tf_op jit(solution)/shard_map/ppermute | solution.py:429
  459.4 15.7 %all-to-all-start.1 = ((bf16[8,32,2048]{2,1,0:T(8,128)(2,1)}), bf16[8,32,2048]{2,1,0:T(8,128)(2,1)S(1)}, u32[]{:S(2)}, u32[]{:S(2)}) async-start(bf16[8,32,2048]{2,1,0:T(8,128)(2,1)} %bitcast.100), calls=%async_computation.1 | async-start | bytes 2097152 | tf_op jit(solution)/shard_map/all_to_all | solution.py:688
  483.9 18.5 %shard_map.337 = (bf16[1024,2048]{1,0:T(8,128)(2,1)}, f32[1,2048]{1,0:T(1,128)}) custom-call(bf16[256,2048]{1,0:T(8,128)(2,1)} %get-tuple-element.148.refs_0_, bf16[256,2048]{1,0:T(8,128)(2,1)} %copy-done.27, bf16[128,2048]{1,0:T(8,128)(2,1)} %collective-permute-done.37.refs_2_, bf16[128,2048]{1,0:T(8,128)(2,1)} %copy-done.78, bf16[256,2048]{1,0:T(8,128)(2,1)} %copy-done.26, ...), custom_call_target="tpu_custom_call" | custom-call | flops 17179869184 | bytes 41959424 | tf_op jit(solution)/shard_map/pallas_call | solution.py:45
  517.9 14.3 %shard_map.338 = (bf16[512,1024]{1,0:T(8,128)(2,1)}, bf16[256,1024]{1,0:T(8,128)(2,1)}, bf16[256,1024]{1,0:T(8,128)(2,1)}, bf16[512,1024]{1,0:T(8,128)(2,1)}, bf...) custom-call(bf16[1024,2048]{1,0:T(8,128)(2,1)} %get-tuple-element.151.refs_0_.refs_10_, ...), custom_call_target="tpu_custom_call" | custom-call | flops 17179869184 | bytes 33554432 | tf_op jit(solution)/shard_map/pallas_call | solution.py:45
  533.7 18.6 %shard_map.339 = (bf16[1024,2048]{1,0:T(8,128)(2,1)}, f32[1,2048]{1,0:T(1,128)}) custom-call(bf16[256,2048]{1,0:T(8,128)(2,1)} %get-tuple-element.152.refs_0_.refs_5_, bf16[256,2048]{1,0:T(8,128)(2,1)} %copy-done.62, bf16[128,2048]{1,0:T(8,128)(2,1)} %collective-permute-done.45.refs_2_.refs_7_, bf16[128,2048]{1,0:T(8,128)(2,1)} %collective-permute-done.46.refs_3_.refs_8_, ...), custom_call_target="tpu_custom_call" | custom-call | flops 17179869184 | bytes 41959424 | tf_op jit(solution)/shard_map/pallas_call | solution.py:45
  562.8 24.3 %shard_map.340 = bf16[2048,2048]{1,0:T(8,128)(2,1)} custom-call(bf16[256,2048]{1,0:T(8,128)(2,1)} %get-tuple-element.148.refs_0_, bf16[256,2048]{1,0:T(8,128)(2,1)} %copy-done.27, bf16[128,2048]{1,0:T(8,128)(2,1)} %collective-permute-done.37.refs_2_, bf16[128,2048]{1,0:T(8,128)(2,1)} %copy-done.78, bf16[256,2048]{1,0:T(8,128)(2,1)} %copy-done.26, ...), custom_call_target="tpu_custom_call" | custom-call | flops 34359738368 | bytes 50331648 | tf_op jit(solution)/shard_map/pallas_call | solution.py:45
  600.9 14.2 %shard_map.342 = (bf16[512,1024]{1,0:T(8,128)(2,1)}, bf16[256,1024]{1,0:T(8,128)(2,1)}, bf16[256,1024]{1,0:T(8,128)(2,1)}, bf16[512,1024]{1,0:T(8,128)(2,1)}, bf...) custom-call(bf16[1024,2048]{1,0:T(8,128)(2,1)} %get-tuple-element.162.refs_12_.refs_0_.refs_11_, ...), custom_call_target="tpu_custom_call" | custom-call | flops 17179869184 | bytes 33554432 | tf_op jit(solution)/shard_map/pallas_call | solution.py:45
  616.8 24.4 %shard_map.343 = bf16[2048,2048]{1,0:T(8,128)(2,1)} custom-call(bf16[256,2048]{1,0:T(8,128)(2,1)} %get-tuple-element.124.refs_0_, bf16[256,2048]{1,0:T(8,128)(2,1)} %copy-done.32, bf16[128,2048]{1,0:T(8,128)(2,1)} %copy-done.36, bf16[128,2048]{1,0:T(8,128)(2,1)} %collective-permute-done.18.refs_3_.refs_10_, bf16[256,2048]{1,0:T(8,128)(2,1)} %copy-done.31, ...), custom_call_target="tpu_custom_call" | custom-call | flops 34359738368 | bytes 50331648 | tf_op jit(solution)/shard_map/pallas_call | solution.py:45
  679.9 14.9 %shard_map.345 = (bf16[1024,1536]{1,0:T(8,128)(2,1)}, f32[2,1,768]{2,1,0:T(1,128)}) custom-call(f32[1024,1]{1,0:T(8,128)} %bitcast.105, bf16[1024,1536]{1,0:T(8,128)(2,1)} %shard_map.323.refs_1_, bf16[1024,512]{1,0:T(8,128)(2,1)} %get-tuple-element.115.refs_0_.refs_2_.refs_10_, bf16[1024,512]{1,0:T(8,128)(2,1)} %shard_map.344.refs_3_, ...), custom_call_target="tpu_custom_call" | custom-call | flops 42949672960 | bytes 18874368 | tf_op jit(solution)/shard_map/pallas_call | solution.py:45
  702.5 11.6 %shard_map.347 = (bf16[512,1024]{1,0:T(8,128)(2,1)}, bf16[256,1024]{1,0:T(8,128)(2,1)}, bf16[256,1024]{1,0:T(8,128)(2,1)}, bf16[512,1024]{1,0:T(8,128)(2,1)}, bf...) custom-call(bf16[1024,1536]{1,0:T(8,128)(2,1)} %get-tuple-element.168.refs_0_.refs_12_, ...), custom_call_target="tpu_custom_call" | custom-call | flops 12884901888 | bytes 27262976 | tf_op jit(solution)/shard_map/pallas_call | solution.py:45
  729.4 10.9 %shard_map.349.refs_5_ = bf16[2048,512]{1,0:T(8,128)(2,1)} custom-call(bf16[256,2048]{1,0:T(8,128)(2,1)} %get-tuple-element.163.refs_0_, bf16[256,2048]{1,0:T(8,128)(2,1)} %copy-done.61, bf16[128,2048]{1,0:T(8,128)(2,1)} %collective-permute-done.49.refs_2_, bf16[128,2048]{1,0:T(8,128)(2,1)} %collective-permute-done.50.refs_3_, ...), custom_call_target="tpu_custom_call" | custom-call | flops 8589934592 | bytes 25165824 | tf_op jit(solution)/shard_map/pallas_call | solution.py:45
  746.0 14.6 %shard_map.350 = (bf16[1024,1536]{1,0:T(8,128)(2,1)}, f32[2,1,768]{2,1,0:T(1,128)}) custom-call(f32[1024,1]{1,0:T(8,128)} %bitcast.103, bf16[1024,1536]{1,0:T(8,128)(2,1)} %shard_map.326.refs_1_, bf16[1024,512]{1,0:T(8,128)(2,1)} %get-tuple-element.122.refs_0_.refs_11_.refs_2_, bf16[1024,512]{1,0:T(8,128)(2,1)} %shard_map.348.refs_12_.refs_3_, ...), custom_call_target="tpu_custom_call" | custom-call | flops 42949672960 | bytes 18874368 | tf_op jit(solution)/shard_map/pallas_call | solution.py:45
  776.5 20.2 %shard_map.352 = (bf16[1088,1536]{1,0:T(8,128)(2,1)}, bf16[1088,1536]{1,0:T(8,128)(2,1)}) custom-call(s32[1]{0:T(128)} %bitcast.26.refs_0_, f32[1,1536]{1,0:T(1,128)} %bitcast.113, bf16[256,2048]{1,0:T(8,128)(2,1)} %bitcast.88, bf16[256,2048]{1,0:T(8,128)(2,1)} %copy-done.58, bf16[128,2048]{1,0:T(8,128)(2,1)} %collective-permute-done.2.refs_2_.refs_4_, ...), custom_call_target="tpu_custom_call" | custom-call | flops 25769803776 | bytes 41943040 | tf_op jit(solution)/shard_map/pallas_call | solution.py:45
  803.1 11.6 %shard_map.353 = (bf16[512,1024]{1,0:T(8,128)(2,1)}, bf16[256,1024]{1,0:T(8,128)(2,1)}, bf16[256,1024]{1,0:T(8,128)(2,1)}, bf16[512,1024]{1,0:T(8,128)(2,1)}, bf...) custom-call(bf16[1024,1536]{1,0:T(8,128)(2,1)} %get-tuple-element.189.refs_7_.refs_13_.refs_0_, ...), custom_call_target="tpu_custom_call" | custom-call | flops 12884901888 | bytes 27262976 | tf_op jit(solution)/shard_map/pallas_call | solution.py:45
  827.2 12.4 %collective-permute-done.69.refs_4_ = bf16[512,1024]{1,0:T(8,128)(2,1)} collective-permute-done((bf16[512,1024]{1,0:T(8,128)(2,1)}, bf16[512,1024]{1,0:T(8,128)(2,1)}, u32[]{:S(2)}, u32[]{:S(2)}) %collective-permute-start.69) | collective-permute-done | bytes 1048608 | tf_op jit(solution)/shard_map/ppermute | solution.py:429
  882.7 11.2 %collective-permute-done.76 = bf16[272,1536]{1,0:T(8,128)(2,1)} collective-permute-done((bf16[272,1536]{1,0:T(8,128)(2,1)}, bf16[272,1536]{1,0:T(8,128)(2,1)}, u32[]{:S(2)}, u32[]{:S(2)}) %collective-permute-start.76) | collective-permute-done | bytes 835616 | tf_op jit(solution)/shard_map/ppermute | solution.py:482
  (537 shorter events, 364.0 us)
Async XLA Ops:
  10.8 51.3 %all-to-all-start = ((bf16[8,2,32,2048]{3,2,1,0:T(8,128)(2,1)}), bf16[8,2,32,2048]{3,2,1,0:T(8,128)(2,1)S(1)}, u32[]{:S(2)}, u32[]{:S(2)}) async-start(bf16[8,2,32,2048]{3,2,1,0:T(8,128)(2,1)} %bitcast.81), calls=%async_computation | async-start | bytes 4194304 | tf_op jit(solution)/shard_map/all_to_all | solution.py:584
  16.7 116.5 %all-gather.5.cloned.1.call-start = ((), (), s32[]{:S(2)}) async-start(), calls=%async_computation.8 | async-start | bytes 7667712 | tf_op jit(solution)/shard_map/all_gather | solution.py:485
  64.3 101.2 %all-gather.7.cloned.1.call-start = ((), (), s32[]{:S(2)}) async-start(), calls=%async_computation.9 | async-start | bytes 2359296 | tf_op jit(solution)/shard_map/all_gather | solution.py:485
  66.9 259.3 %all-gather.9.cloned.1.call-start = ((), (), s32[]{:S(2)}) async-start(), calls=%async_computation.10 | async-start | bytes 9437184 | tf_op jit(solution)/shard_map/all_gather | solution.py:485
  69.8 289.2 %all-gather.11.cloned.1.call-start = ((), (), s32[]{:S(2)}) async-start(), calls=%async_computation.11 | async-start | bytes 9437184 | tf_op jit(solution)/shard_map/all_gather | solution.py:485
  72.6 36.1 %collective-permute-start.1 = (bf16[256,2048]{1,0:T(8,128)(2,1)S(1)}, bf16[256,2048]{1,0:T(8,128)(2,1)}, u32[]{:S(2)}, u32[]{:S(2)}) collective-permute-start(bf16[256,2048]{1,0:T(8,128)(2,1)S(1)} %bitcast.85), channel_id=1, source_target_pairs={{0,2},{1,3},{2,0},{3,1},{4,6},{5,7},{6,4},{7,5},{8,10},{9,11},{10,... | collective-permute-start | bytes 3145736 | tf_op jit(solution)/shard_map/ppermute | solution.py:429
  123.6 51.0 %collective-permute-start.13 = (bf16[128,2048]{1,0:T(8,128)(2,1)}, bf16[128,2048]{1,0:T(8,128)(2,1)}, u32[]{:S(2)}, u32[]{:S(2)}) collective-permute-start(bf16[128,2048]{1,0:T(8,128)(2,1)} %slice.430), channel_id=1, source_target_pairs={{0,1},{1,0},{2,3},{3,2},{4,5},{5,4},{6,7},{7,6},{8,9},{9,8},{10,11... | collective-permute-start | bytes 1572872 | tf_op jit(solution)/shard_map/ppermute | solution.py:429
  124.9 49.7 %collective-permute-start.14 = (bf16[128,2048]{1,0:T(8,128)(2,1)S(1)}, bf16[128,2048]{1,0:T(8,128)(2,1)}, u32[]{:S(2)}, u32[]{:S(2)}) collective-permute-start(bf16[128,2048]{1,0:T(8,128)(2,1)S(1)} %slice.431), channel_id=1, source_target_pairs={{0,2},{1,3},{2,0},{3,1},{4,6},{5,7},{6,4},{7,5},{8,10},{9,11},{10,... | collective-permute-start | bytes 1572872 | tf_op jit(solution)/shard_map/ppermute | solution.py:429
  229.0 45.1 %collective-permute-start.21 = (bf16[512,1024]{1,0:T(8,128)(2,1)}, bf16[512,1024]{1,0:T(8,128)(2,1)S(1)}, u32[]{:S(2)}, u32[]{:S(2)}) collective-permute-start(bf16[512,1024]{1,0:T(8,128)(2,1)} %get-tuple-element.129), channel_id=1, source_target_pairs={{0,2},{1,3},{2,0},{3,1},{4,6},{5,7},{6,4},{7,5},{8,10},{9,11},{10,... | collective-permute-start | bytes 3145736 | tf_op jit(solution)/shard_map/ppermute | solution.py:429
  230.0 44.8 %collective-permute-start.19 = (bf16[512,1024]{1,0:T(8,128)(2,1)}, bf16[512,1024]{1,0:T(8,128)(2,1)S(1)}, u32[]{:S(2)}, u32[]{:S(2)}) collective-permute-start(bf16[512,1024]{1,0:T(8,128)(2,1)} %get-tuple-element.123.refs_8_), channel_id=1, source_target_pairs={{0,1},{1,0},{2,3},{3,2},{4,5},{5,4},{6,7},{7,6},{8,9},{9,8},{10,11... | collective-permute-start | bytes 3145736 | tf_op jit(solution)/shard_map/ppermute | solution.py:429
  251.6 33.9 %collective-permute-start.17 = (bf16[128,2048]{1,0:T(8,128)(2,1)S(1)}, bf16[128,2048]{1,0:T(8,128)(2,1)S(1)}, u32[]{:S(2)}, u32[]{:S(2)}) collective-permute-start(bf16[128,2048]{1,0:T(8,128)(2,1)S(1)} %slice.432), channel_id=1, source_target_pairs={{0,1},{1,0},{2,3},{3,2},{4,5},{5,4},{6,7},{7,6},{8,9},{9,8},{10,11... | collective-permute-start | bytes 1572872 | tf_op jit(solution)/shard_map/ppermute | solution.py:429
  252.1 33.4 %collective-permute-start.18 = (bf16[128,2048]{1,0:T(8,128)(2,1)S(1)}, bf16[128,2048]{1,0:T(8,128)(2,1)}, u32[]{:S(2)}, u32[]{:S(2)}) collective-permute-start(bf16[128,2048]{1,0:T(8,128)(2,1)S(1)} %slice.433), channel_id=1, source_target_pairs={{0,2},{1,3},{2,0},{3,1},{4,6},{5,7},{6,4},{7,5},{8,10},{9,11},{10,... | collective-permute-start | bytes 1572872 | tf_op jit(solution)/shard_map/ppermute | solution.py:429
  388.9 48.8 %collective-permute-start.33 = (bf16[512,1024]{1,0:T(8,128)(2,1)}, bf16[512,1024]{1,0:T(8,128)(2,1)S(1)}, u32[]{:S(2)}, u32[]{:S(2)}) collective-permute-start(bf16[512,1024]{1,0:T(8,128)(2,1)} %get-tuple-element.145), channel_id=1, source_target_pairs={{0,2},{1,3},{2,0},{3,1},{4,6},{5,7},{6,4},{7,5},{8,10},{9,11},{10,... | collective-permute-start | bytes 3145736 | tf_op jit(solution)/shard_map/ppermute | solution.py:429
  389.9 50.4 %collective-permute-start.31 = (bf16[512,1024]{1,0:T(8,128)(2,1)}, bf16[512,1024]{1,0:T(8,128)(2,1)S(1)}, u32[]{:S(2)}, u32[]{:S(2)}) collective-permute-start(bf16[512,1024]{1,0:T(8,128)(2,1)} %get-tuple-element.140.refs_9_), channel_id=1, source_target_pairs={{0,1},{1,0},{2,3},{3,2},{4,5},{5,4},{6,7},{7,6},{8,9},{9,8},{10,11... | collective-permute-start | bytes 3145736 | tf_op jit(solution)/shard_map/ppermute | solution.py:429
  395.4 31.5 %collective-permute-start.30 = (bf16[256,1024]{1,0:T(8,128)(2,1)S(1)}, bf16[256,1024]{1,0:T(8,128)(2,1)S(1)}, u32[]{:S(2)}, u32[]{:S(2)}) collective-permute-start(bf16[256,1024]{1,0:T(8,128)(2,1)S(1)} %add_convert_fusion.13), channel_id=1, source_target_pairs={{0,1},{1,0},{2,3},{3,2},{4,5},{5,4},{6,7},{7,6},{8,9},{9,8},{10,11... | collective-permute-start | bytes 1572872 | tf_op jit(solution)/shard_map/ppermute | solution.py:429
  440.1 35.0 %collective-permute-start.34 = (bf16[256,1024]{1,0:T(8,128)(2,1)}, bf16[256,1024]{1,0:T(8,128)(2,1)}, u32[]{:S(2)}, u32[]{:S(2)}) collective-permute-start(bf16[256,1024]{1,0:T(8,128)(2,1)} %add_convert_fusion.11), channel_id=1, source_target_pairs={{0,1},{1,0},{2,3},{3,2},{4,5},{5,4},{6,7},{7,6},{8,9},{9,8},{10,11... | collective-permute-start | bytes 1572872 | tf_op jit(solution)/shard_map/ppermute | solution.py:429
  441.4 33.7 %collective-permute-start.32 = (bf16[256,1024]{1,0:T(8,128)(2,1)}, bf16[256,1024]{1,0:T(8,128)(2,1)}, u32[]{:S(2)}, u32[]{:S(2)}) collective-permute-start(bf16[256,1024]{1,0:T(8,128)(2,1)} %add_convert_fusion.12), channel_id=1, source_target_pairs={{0,2},{1,3},{2,0},{3,1},{4,6},{5,7},{6,4},{7,5},{8,10},{9,11},{10,... | collective-permute-start | bytes 1572872 | tf_op jit(solution)/shard_map/ppermute | solution.py:429
  459.4 48.4 %all-to-all-start.1 = ((bf16[8,32,2048]{2,1,0:T(8,128)(2,1)}), bf16[8,32,2048]{2,1,0:T(8,128)(2,1)S(1)}, u32[]{:S(2)}, u32[]{:S(2)}) async-start(bf16[8,32,2048]{2,1,0:T(8,128)(2,1)} %bitcast.100), calls=%async_computation.1 | async-start | bytes 2097152 | tf_op jit(solution)/shard_map/all_to_all | solution.py:688
  507.7 54.1 %all-to-all-start.2 = ((bf16[8,32,2048]{2,1,0:T(8,128)(2,1)}), bf16[8,32,2048]{2,1,0:T(8,128)(2,1)S(1)}, u32[]{:S(2)}, u32[]{:S(2)}) async-start(bf16[8,32,2048]{2,1,0:T(8,128)(2,1)} %bitcast.17), calls=%async_computation.2 | async-start | bytes 2097152 | tf_op jit(solution)/shard_map/all_to_all | solution.py:688
  517.9 254.9 %reduce-scatter.4.cloned.1.call-start = ((), (), s32[]{:S(2)}) async-start(), calls=%async_computation.12 | async-start | bytes 9437184 | tf_op jit(solution)/shard_map/reduce_scatter | solution.py:488
  592.1 269.9 %reduce-scatter.6.cloned.1.call-start = ((), (), s32[]{:S(2)}) async-start(), calls=%async_computation.13 | async-start | bytes 9437184 | tf_op jit(solution)/shard_map/reduce_scatter | solution.py:488
  599.4 44.6 %collective-permute-start.47 = (bf16[256,2048]{1,0:T(8,128)(2,1)}, bf16[256,2048]{1,0:T(8,128)(2,1)S(1)}, u32[]{:S(2)}, u32[]{:S(2)}) collective-permute-start(bf16[256,2048]{1,0:T(8,128)(2,1)} %get-tuple-element.163.refs_0_), channel_id=1, source_target_pairs={{0,1},{1,0},{2,3},{3,2},{4,5},{5,4},{6,7},{7,6},{8,9},{9,8},{10,11... | collective-permute-start | bytes 3145736 | tf_op jit(solution)/shard_map/ppermute | solution.py:429
  600.4 40.8 %collective-permute-start.48 = (bf16[256,2048]{1,0:T(8,128)(2,1)}, bf16[256,2048]{1,0:T(8,128)(2,1)}, u32[]{:S(2)}, u32[]{:S(2)}) collective-permute-start(bf16[256,2048]{1,0:T(8,128)(2,1)} %get-tuple-element.163.refs_0_), channel_id=1, source_target_pairs={{0,2},{1,3},{2,0},{3,1},{4,6},{5,7},{6,4},{7,5},{8,10},{9,11},{10,... | collective-permute-start | bytes 3145736 | tf_op jit(solution)/shard_map/ppermute | solution.py:429
  615.2 31.6 %collective-permute-start.51 = (bf16[512,1024]{1,0:T(8,128)(2,1)}, bf16[512,1024]{1,0:T(8,128)(2,1)S(1)}, u32[]{:S(2)}, u32[]{:S(2)}) collective-permute-start(bf16[512,1024]{1,0:T(8,128)(2,1)} %get-tuple-element.165.refs_12_), channel_id=1, source_target_pairs={{0,1},{1,0},{2,3},{3,2},{4,5},{5,4},{6,7},{7,6},{8,9},{9,8},{10,11... | collective-permute-start | bytes 3145736 | tf_op jit(solution)/shard_map/ppermute | solution.py:429
  615.8 30.0 %collective-permute-start.52 = (bf16[512,1024]{1,0:T(8,128)(2,1)}, bf16[512,1024]{1,0:T(8,128)(2,1)S(1)}, u32[]{:S(2)}, u32[]{:S(2)}) collective-permute-start(bf16[512,1024]{1,0:T(8,128)(2,1)} %get-tuple-element.166), channel_id=1, source_target_pairs={{0,2},{1,3},{2,0},{3,1},{4,6},{5,7},{6,4},{7,5},{8,10},{9,11},{10,... | collective-permute-start | bytes 3145736 | tf_op jit(solution)/shard_map/ppermute | solution.py:429
  742.3 33.6 %collective-permute-start.66 = (f32[112,128]{1,0:T(8,128)S(1)}, f32[112,128]{1,0:T(8,128)S(1)}, u32[]{:S(2)}, u32[]{:S(2)}) collective-permute-start(f32[112,128]{1,0:T(8,128)S(1)} %add_add_fusion), channel_id=1, source_target_pairs={{0,8},{4,12},{8,0},{12,4},{16,24},{20,28},{24,16},{28,20},{1,9},{5... | collective-permute-start | bytes 172040 | tf_op jit(solution)/shard_map/ppermute | solution.py:531
  767.3 34.9 %all-to-all-start.3 = ((bf16[8,32,2048]{2,1,0:T(8,128)(2,1)}), bf16[8,32,2048]{2,1,0:T(8,128)(2,1)S(1)}, u32[]{:S(2)}, u32[]{:S(2)}) async-start(bf16[8,32,2048]{2,1,0:T(8,128)(2,1)} %bitcast.90), calls=%async_computation.3 | async-start | bytes 2097152 | tf_op jit(solution)/shard_map/all_to_all | solution.py:688
  772.8 104.3 %reduce-scatter.8.cloned.1.call-start = ((), (), s32[]{:S(2)}) async-start(), calls=%async_computation.14 | async-start | bytes 2359296 | tf_op jit(solution)/shard_map/reduce_scatter | solution.py:488
  818.7 30.9 %collective-permute-start.72 = (bf16[272,1536]{1,0:T(8,128)(2,1)}, bf16[272,1536]{1,0:T(8,128)(2,1)S(1)}, u32[]{:S(2)}, u32[]{:S(2)}) collective-permute-start(bf16[272,1536]{1,0:T(8,128)(2,1)} %add_convert_fusion.2), channel_id=1, source_target_pairs={{0,8},{4,12},{8,16},{12,20},{1,9},{5,13},{9,17},{13,21},{2,10},{6,... | collective-permute-start | bytes 2506760 | tf_op jit(solution)/shard_map/ppermute | solution.py:482
  825.2 35.3 %collective-permute-start.74 = (f32[112,128]{1,0:T(8,128)}, f32[112,128]{1,0:T(8,128)S(1)}, u32[]{:S(2)}, u32[]{:S(2)}) collective-permute-start(f32[112,128]{1,0:T(8,128)} %add.379), channel_id=1, source_target_pairs={{0,16},{4,20},{8,24},{12,28},{16,0},{20,4},{24,8},{28,12},{1,17},{... | collective-permute-start | bytes 172040 | tf_op jit(solution)/shard_map/ppermute | solution.py:531
  854.8 39.0 %collective-permute-start.76 = (bf16[272,1536]{1,0:T(8,128)(2,1)}, bf16[272,1536]{1,0:T(8,128)(2,1)}, u32[]{:S(2)}, u32[]{:S(2)}) collective-permute-start(bf16[272,1536]{1,0:T(8,128)(2,1)} %get-tuple-element.257), channel_id=1, source_target_pairs={{0,24},{4,28},{8,0},{12,4},{16,8},{20,12},{24,16},{28,20},{1,25},{... | collective-permute-start | bytes 2506760 | tf_op jit(solution)/shard_map/ppermute | solution.py:482
  869.4 44.8 %all-to-all-start.4 = ((bf16[8,32,2048]{2,1,0:T(8,128)(2,1)}), bf16[8,32,2048]{2,1,0:T(8,128)(2,1)}, u32[]{:S(2)}, u32[]{:S(2)}) async-start(bf16[8,32,2048]{2,1,0:T(8,128)(2,1)} %bitcast.89), calls=%async_computation.6 | async-start | bytes 2097152 | tf_op jit(solution)/shard_map/all_to_all | solution.py:688
  (147 other events, 2156.8 us)
Sparse Core Ops, SparseCore 0:
  64.4 68.6 all-gather.4
  135.3 30.1 all-gather.6
  167.1 78.9 all-gather.8
  247.5 80.5 all-gather.10
  592.2 89.1 reduce-scatter.3
  683.5 86.9 reduce-scatter.5
  802.3 34.6 reduce-scatter.7

commit v9 on v8

--- a/solution.py
+++ b/solution.py
@@ -428,12 +428,16 @@
     def swap(self, array, bit):
         return lax.ppermute(array, "tensor", [(i, i ^ bit) for i in range(self.size)])
 
-    def gather(self, block):
+    def gather(self, block, earlier=()):
         if not self.square:
             return [lax.all_gather(block, "tensor", axis=0, tiled=True)]
         half = block.shape[0] // 2
         along_x, along_y = self.swap(block, 1), self.swap(block, 2)
-        far_top, far_bottom = self.swap(along_y[:half], 1), self.swap(along_x[half:], 2)
+        onward_x, onward_y = along_y[:half], along_x[half:]
+        if earlier:
+            zero = nothing(*earlier).astype(block.dtype)
+            onward_x, onward_y = onward_x + zero, onward_y + zero
+        far_top, far_bottom = self.swap(onward_x, 1), self.swap(onward_y, 2)
         return [block, along_x, far_top, far_bottom, along_y]
 
     def spans(self, rows):
@@ -654,14 +658,12 @@
         terms.append(terms_matmul(mix, mid_weight, spans, sums[-1][2] if sums else (row_vectors,)))
         sums.append(tensor.scatter(terms[s]))
         before = (terms[s][0][0],)
-    first, first_pieces = [], []
-    for s in over:
-        first.append(first_norm(sums[s][0], arrived[s], row_vectors, before))
-        first_pieces.append(tensor.gather(first[s][0]))
-        before = tuple(first_pieces[s][1:])
+    first = [first_norm(sums[0][0], arrived[0], row_vectors, before)]
+    first_pieces = [tensor.gather(first[0][0])]
+    first.append(first_norm(sums[1][0], arrived[1], row_vectors, tuple(first_pieces[0][1:])))
     hidden, active, terms, sums = [], [], [], []
-    before = ()
-    for s in over:
+
+    def to_hidden(s, later):
         wide, narrow = rows_matmul(
             first_pieces[s],
             up_full,
@@ -669,20 +671,28 @@
             lambda product, bias: (product + bias, gelu(product + bias).astype(bf16)),
             [hidden_bias],
             [(slot_rows, f32), (slot_rows, bf16)],
-            before,
+            later,
         )
         hidden.append(wide)
         active.append(narrow)
-        before = (narrow,)
-    for s in over:
-        terms.append(terms_matmul(active[s], down_full, spans, before))
+
+    def from_hidden(s, later):
+        terms.append(terms_matmul(active[s], down_full, spans, later))
         sums.append(tensor.scatter(terms[s]))
-        before = (terms[s][0][0],)
+
+    to_hidden(0, (first[1][0],))
+    first_pieces.append(tensor.gather(first[1][0], (active[0],)))
+    from_hidden(0, tuple(first_pieces[1][1:]))
+    to_hidden(1, (terms[0][0][0],))
     second, down_pieces = [], []
-    for s in over:
-        second.append(second_norm(sums[s][0], first[s][1], cotangent[s], row_vectors, before))
+
+    def to_second(s, later):
+        second.append(second_norm(sums[s][0], first[s][1], cotangent[s], row_vectors, later))
         down_pieces.append(tensor.gather(second[s][2]))
-        before = near(down_pieces[s])
+
+    from_hidden(1, sums[0][1])
+    to_second(0, (terms[1][0][0],))
+    to_second(1, near(down_pieces[0]))
 
     def give_back(rows):
         return lax.all_to_all(

time: 943 us -> 920 us (0.976)
  waiting for transfers between devices: 272 us -> 244 us
    ppermute x67, waiting for transfers between devices: 192 us -> 162 us  [swap(): lax.ppermute(array, 'tensor', [(i, i ^ bit) for i in range(self.size)])]
    unnamed x204 -> x198, local copies, waits for them, and re-layouts: 29.5 us -> 30 us
  transfers between devices with their start and end apart: 89 -> 89, of which waited for: 27 -> 28; matrix products, arithmetic and copies ran while one was open for 11% -> 12% of each run, Pallas kernels for 40% -> 41%
where the time goes in v9:
time: 920 us; the launch traced here: 904 us
  Pallas kernels  383 us (42%)
  waiting for transfers between devices  244 us (27%)
  starting transfers between devices  117 us (13%)
  local copies, waits for them, and re-layouts  80.4 us (9%)
  other arithmetic  53.8 us (6%)
  between operations  26.1 us (3%)
    pallas_call x32, Pallas kernels, launch(): pl.pallas_call(run, grid=grid, in_specs=list(in_specs) + [pl.BlockSpec(me...  383 us
    ppermute x67, waiting for transfers between devices, swap(): lax.ppermute(array, 'tensor', [(i, i ^ bit) for i in range(self.size)])  162 us
    ppermute x67, starting transfers between devices, swap(): lax.ppermute(array, 'tensor', [(i, i ^ bit) for i in range(self.size)])  56.5 us
    all_to_all x1, waiting for transfers between devices, local(): came = lax.all_to_all(sent, 'dp', split_axis=0, concat_axis=0, tiled=True)  41.3 us
    all_to_all x4, starting transfers between devices, give_back(): lax.all_to_all(rows.reshape(groups, arrival_rows, model_width), 'dp', spl...  38.2 us
    unnamed x198, local copies, waits for them, and re-layouts  30 us
  transfers between devices with their start and end apart: 89, of which 28 were waited for; matrix products, arithmetic and copies ran while one was open for 12% of the time, Pallas kernels for 41%

profile of v9, /device:TPU:9, one launch (start us, length us, event | category | flops | bytes accessed | tf_op | source)
XLA Modules:
  0.0 904.1 jit_solution(7187480368872365612)
XLA Ops:
  20.8 41.3 %all-to-all-done = bf16[8,2,32,2048]{3,2,1,0:T(8,128)(2,1)S(1)} async-done(((bf16[8,2,32,2048]{3,2,1,0:T(8,128)(2,1)}), bf16[8,2,32,2048]{3,2,1,0:T(8,128)(2,1)S(1)}, u32[]{:S(2)}, u32[]{:S(2)}) %all-to-all-start) | async-done | bytes 2097184 | tf_op jit(solution)/shard_map/all_to_all | solution.py:588
  72.3 21.9 %collective-permute-done.refs_1_.refs_3_ = bf16[256,2048]{1,0:T(8,128)(2,1)S(1)} collective-permute-done((bf16[256,2048]{1,0:T(8,128)(2,1)S(1)}, bf16[256,2048]{1,0:T(8,128)(2,1)S(1)}, u32[]{:S(2)}, u32[]{:S(2)}) %collective-permute-start) | collective-permute-done | bytes 1048608 | tf_op jit(solution)/shard_map/ppermute | solution.py:429
  110.4 11.8 %collective-permute-done.5.refs_8_.refs_4_.refs_11_ = bf16[256,2048]{1,0:T(8,128)(2,1)} collective-permute-done((bf16[256,2048]{1,0:T(8,128)(2,1)}, bf16[256,2048]{1,0:T(8,128)(2,1)}, u32[]{:S(2)}, u32[]{:S(2)}) %collective-permute-start.5) | collective-permute-done | bytes 1048608 | tf_op jit(solution)/shard_map/ppermute | solution.py:429
  138.1 11.6 %shard_map.323.refs_1_ = bf16[1024,1536]{1,0:T(8,128)(2,1)} custom-call(bf16[256,2048]{1,0:T(8,128)(2,1)} %bitcast.87, bf16[256,2048]{1,0:T(8,128)(2,1)} %copy-done.55, bf16[128,2048]{1,0:T(8,128)(2,1)} %collective-permute-done.2.refs_2_.refs_4_, bf16[128,2048]{1,0:T(8,128)(2,1)} %collective-permute-done.3.refs_3_.refs_5_, ...), custom_call_target="tpu_custom_call" | custom-call | flops 12884901888 | bytes 33554432 | tf_op jit(solution)/shard_map/pallas_call | solution.py:45
  149.7 13.9 %shard_map.324 = (bf16[1024,512]{1,0:T(8,128)(2,1)}, f32[2,2,1024]{2,1,0:T(2,128)}) custom-call(f32[1024,1]{1,0:T(8,128)} %bitcast.100, bf16[1024,1536]{1,0:T(8,128)(2,1)} %shard_map.323.refs_1_), custom_call_target="tpu_custom_call" | custom-call | flops 17179869184 | bytes 9437184 | tf_op jit(solution)/shard_map/pallas_call | solution.py:45
  174.5 12.4 %shard_map.326.refs_1_ = bf16[1024,1536]{1,0:T(8,128)(2,1)} custom-call(bf16[256,2048]{1,0:T(8,128)(2,1)} %bitcast.8.refs_0_.refs_6_.refs_7_, bf16[256,2048]{1,0:T(8,128)(2,1)} %collective-permute-done.4.refs_7_.refs_1_.refs_8_, bf16[128,2048]{1,0:T(8,128)(2,1)} %collective-permute-done.13.refs_2_.refs_9_, ...), custom_call_target="tpu_custom_call" | custom-call | flops 12884901888 | bytes 33554432 | tf_op jit(solution)/shard_map/pallas_call | solution.py:45
  187.0 9.5 %collective-permute-done.11.refs_4_ = bf16[512,1024]{1,0:T(8,128)(2,1)S(1)} collective-permute-done((bf16[512,1024]{1,0:T(8,128)(2,1)}, bf16[512,1024]{1,0:T(8,128)(2,1)S(1)}, u32[]{:S(2)}, u32[]{:S(2)}) %collective-permute-start.11) | collective-permute-done | bytes 1048608 | tf_op jit(solution)/shard_map/ppermute | solution.py:429
  200.2 14.1 %shard_map.327 = (bf16[1024,512]{1,0:T(8,128)(2,1)}, f32[2,2,1024]{2,1,0:T(2,128)}) custom-call(f32[1024,1]{1,0:T(8,128)} %bitcast.98, bf16[1024,1536]{1,0:T(8,128)(2,1)} %shard_map.326.refs_1_), custom_call_target="tpu_custom_call" | custom-call | flops 17179869184 | bytes 9437184 | tf_op jit(solution)/shard_map/pallas_call | solution.py:45
  230.5 19.9 %collective-permute-done.16.refs_11_.refs_4_ = bf16[256,2048]{1,0:T(8,128)(2,1)S(1)} collective-permute-done((bf16[256,2048]{1,0:T(8,128)(2,1)}, bf16[256,2048]{1,0:T(8,128)(2,1)S(1)}, u32[]{:S(2)}, u32[]{:S(2)}) %collective-permute-start.16) | collective-permute-done | bytes 1048608 | tf_op jit(solution)/shard_map/ppermute | solution.py:429
  251.6 21.3 %collective-permute-done.21.refs_4_ = bf16[512,1024]{1,0:T(8,128)(2,1)S(1)} collective-permute-done((bf16[512,1024]{1,0:T(8,128)(2,1)}, bf16[512,1024]{1,0:T(8,128)(2,1)S(1)}, u32[]{:S(2)}, u32[]{:S(2)}) %collective-permute-start.21) | collective-permute-done | bytes 1048608 | tf_op jit(solution)/shard_map/ppermute | solution.py:429
  284.2 11.2 %collective-permute-done.22.refs_5_ = bf16[256,1024]{1,0:T(8,128)(2,1)} collective-permute-done((bf16[256,1024]{1,0:T(8,128)(2,1)S(1)}, bf16[256,1024]{1,0:T(8,128)(2,1)}, u32[]{:S(2)}, u32[]{:S(2)}) %collective-permute-start.22) | collective-permute-done | bytes 524320 | tf_op jit(solution)/shard_map/ppermute | solution.py:429
  302.3 16.2 %shard_map.331 = (f32[1024,2048]{1,0:T(8,128)}, bf16[1024,2048]{1,0:T(8,128)(2,1)}) custom-call(bf16[256,2048]{1,0:T(8,128)(2,1)} %get-tuple-element.124.refs_0_, bf16[256,2048]{1,0:T(8,128)(2,1)} %copy-done.30, bf16[128,2048]{1,0:T(8,128)(2,1)} %copy-done.33, bf16[128,2048]{1,0:T(8,128)(2,1)} %collective-permute-done.18.refs_10_.refs_3_, ...), custom_call_target="tpu_custom_call" | custom-call | flops 17179869184 | bytes 58720256 | tf_op jit(solution)/shard_map/pallas_call | solution.py:45
  334.9 14.6 %shard_map.332 = (bf16[512,1024]{1,0:T(8,128)(2,1)}, bf16[256,1024]{1,0:T(8,128)(2,1)}, bf16[256,1024]{1,0:T(8,128)(2,1)}, bf16[512,1024]{1,0:T(8,128)(2,1)}, bf...) custom-call(bf16[1024,2048]{1,0:T(8,128)(2,1)} %get-tuple-element.131.refs_0_.refs_10_, ...), custom_call_target="tpu_custom_call" | custom-call | flops 17179869184 | bytes 33554432 | tf_op jit(solution)/shard_map/pallas_call | solution.py:45
  352.4 16.0 %shard_map.333 = (f32[1024,2048]{1,0:T(8,128)}, bf16[1024,2048]{1,0:T(8,128)(2,1)}) custom-call(bf16[256,2048]{1,0:T(8,128)(2,1)} %get-tuple-element.130.refs_7_.refs_0_.refs_5_, bf16[256,2048]{1,0:T(8,128)(2,1)} %copy-done.60, bf16[128,2048]{1,0:T(8,128)(2,1)} %collective-permute-done.25.refs_3_.refs_2_.refs_7_, ...), custom_call_target="tpu_custom_call" | custom-call | flops 17179869184 | bytes 58720256 | tf_op jit(solution)/shard_map/pallas_call | solution.py:45
  376.5 14.2 %shard_map.334 = (bf16[512,1024]{1,0:T(8,128)(2,1)}, bf16[256,1024]{1,0:T(8,128)(2,1)}, bf16[256,1024]{1,0:T(8,128)(2,1)}, bf16[512,1024]{1,0:T(8,128)(2,1)}, bf...) custom-call(bf16[1024,2048]{1,0:T(8,128)(2,1)} %get-tuple-element.139.refs_0_.refs_11_, ...), custom_call_target="tpu_custom_call" | custom-call | flops 17179869184 | bytes 33554432 | tf_op jit(solution)/shard_map/pallas_call | solution.py:45
  414.8 18.7 %collective-permute-done.36.refs_10_.refs_4_ = bf16[256,2048]{1,0:T(8,128)(2,1)S(1)} collective-permute-done((bf16[256,2048]{1,0:T(8,128)(2,1)}, bf16[256,2048]{1,0:T(8,128)(2,1)S(1)}, u32[]{:S(2)}, u32[]{:S(2)}) %collective-permute-start.36) | collective-permute-done | bytes 1048608 | tf_op jit(solution)/shard_map/ppermute | solution.py:429
  435.8 14.9 %all-to-all-start.1 = ((bf16[8,32,2048]{2,1,0:T(8,128)(2,1)}), bf16[8,32,2048]{2,1,0:T(8,128)(2,1)S(1)}, u32[]{:S(2)}, u32[]{:S(2)}) async-start(bf16[8,32,2048]{2,1,0:T(8,128)(2,1)} %bitcast.96), calls=%async_computation.1 | async-start | bytes 2097152 | tf_op jit(solution)/shard_map/all_to_all | solution.py:698
  460.4 18.5 %shard_map.337 = (bf16[1024,2048]{1,0:T(8,128)(2,1)}, f32[1,2048]{1,0:T(1,128)}) custom-call(bf16[256,2048]{1,0:T(8,128)(2,1)} %get-tuple-element.148.refs_0_, bf16[256,2048]{1,0:T(8,128)(2,1)} %copy-done.24, bf16[128,2048]{1,0:T(8,128)(2,1)} %collective-permute-done.37.refs_2_, bf16[128,2048]{1,0:T(8,128)(2,1)} %copy-done.75, bf16[256,2048]{1,0:T(8,128)(2,1)} %copy-done.23, ...), custom_call_target="tpu_custom_call" | custom-call | flops 17179869184 | bytes 41959424 | tf_op jit(solution)/shard_map/pallas_call | solution.py:45
  482.9 10.7 %all-to-all-start.2 = ((bf16[8,32,2048]{2,1,0:T(8,128)(2,1)}), bf16[8,32,2048]{2,1,0:T(8,128)(2,1)S(1)}, u32[]{:S(2)}, u32[]{:S(2)}) async-start(bf16[8,32,2048]{2,1,0:T(8,128)(2,1)} %bitcast.18), calls=%async_computation.2 | async-start | bytes 2097152 | tf_op jit(solution)/shard_map/all_to_all | solution.py:698
  493.7 14.3 %shard_map.338 = (bf16[512,1024]{1,0:T(8,128)(2,1)}, bf16[256,1024]{1,0:T(8,128)(2,1)}, bf16[256,1024]{1,0:T(8,128)(2,1)}, bf16[512,1024]{1,0:T(8,128)(2,1)}, bf...) custom-call(bf16[1024,2048]{1,0:T(8,128)(2,1)} %get-tuple-element.151.refs_0_.refs_10_, ...), custom_call_target="tpu_custom_call" | custom-call | flops 17179869184 | bytes 33554432 | tf_op jit(solution)/shard_map/pallas_call | solution.py:45
  509.5 18.6 %shard_map.339 = (bf16[1024,2048]{1,0:T(8,128)(2,1)}, f32[1,2048]{1,0:T(1,128)}) custom-call(bf16[256,2048]{1,0:T(8,128)(2,1)} %get-tuple-element.152.refs_0_.refs_5_, bf16[256,2048]{1,0:T(8,128)(2,1)} %copy-done.57, bf16[128,2048]{1,0:T(8,128)(2,1)} %collective-permute-done.45.refs_2_.refs_7_, bf16[128,2048]{1,0:T(8,128)(2,1)} %collective-permute-done.46.refs_3_.refs_8_, ...), custom_call_target="tpu_custom_call" | custom-call | flops 17179869184 | bytes 41959424 | tf_op jit(solution)/shard_map/pallas_call | solution.py:45
  538.6 24.3 %shard_map.340 = bf16[2048,2048]{1,0:T(8,128)(2,1)} custom-call(bf16[256,2048]{1,0:T(8,128)(2,1)} %get-tuple-element.148.refs_0_, bf16[256,2048]{1,0:T(8,128)(2,1)} %copy-done.24, bf16[128,2048]{1,0:T(8,128)(2,1)} %collective-permute-done.37.refs_2_, bf16[128,2048]{1,0:T(8,128)(2,1)} %copy-done.75, bf16[256,2048]{1,0:T(8,128)(2,1)} %copy-done.23, ...), custom_call_target="tpu_custom_call" | custom-call | flops 34359738368 | bytes 50331648 | tf_op jit(solution)/shard_map/pallas_call | solution.py:45
  576.6 14.2 %shard_map.342 = (bf16[512,1024]{1,0:T(8,128)(2,1)}, bf16[256,1024]{1,0:T(8,128)(2,1)}, bf16[256,1024]{1,0:T(8,128)(2,1)}, bf16[512,1024]{1,0:T(8,128)(2,1)}, bf...) custom-call(bf16[1024,2048]{1,0:T(8,128)(2,1)} %get-tuple-element.162.refs_12_.refs_0_.refs_11_, ...), custom_call_target="tpu_custom_call" | custom-call | flops 17179869184 | bytes 33554432 | tf_op jit(solution)/shard_map/pallas_call | solution.py:45
  592.6 24.4 %shard_map.343 = bf16[2048,2048]{1,0:T(8,128)(2,1)} custom-call(bf16[256,2048]{1,0:T(8,128)(2,1)} %get-tuple-element.124.refs_0_, bf16[256,2048]{1,0:T(8,128)(2,1)} %copy-done.30, bf16[128,2048]{1,0:T(8,128)(2,1)} %copy-done.33, bf16[128,2048]{1,0:T(8,128)(2,1)} %collective-permute-done.18.refs_10_.refs_3_, bf16[256,2048]{1,0:T(8,128)(2,1)} %copy-done.29, ...), custom_call_target="tpu_custom_call" | custom-call | flops 34359738368 | bytes 50331648 | tf_op jit(solution)/shard_map/pallas_call | solution.py:45
  656.2 14.8 %shard_map.345 = (bf16[1024,1536]{1,0:T(8,128)(2,1)}, f32[2,1,768]{2,1,0:T(1,128)}) custom-call(f32[1024,1]{1,0:T(8,128)} %bitcast.101, bf16[1024,1536]{1,0:T(8,128)(2,1)} %shard_map.323.refs_1_, bf16[1024,512]{1,0:T(8,128)(2,1)} %get-tuple-element.115.refs_0_.refs_2_.refs_10_, bf16[1024,512]{1,0:T(8,128)(2,1)} %shard_map.344.refs_3_, ...), custom_call_target="tpu_custom_call" | custom-call | flops 42949672960 | bytes 18874368 | tf_op jit(solution)/shard_map/pallas_call | solution.py:45
  677.7 11.6 %shard_map.347 = (bf16[512,1024]{1,0:T(8,128)(2,1)}, bf16[256,1024]{1,0:T(8,128)(2,1)}, bf16[256,1024]{1,0:T(8,128)(2,1)}, bf16[512,1024]{1,0:T(8,128)(2,1)}, bf...) custom-call(bf16[1024,1536]{1,0:T(8,128)(2,1)} %get-tuple-element.168.refs_0_.refs_12_, ...), custom_call_target="tpu_custom_call" | custom-call | flops 12884901888 | bytes 27262976 | tf_op jit(solution)/shard_map/pallas_call | solution.py:45
  705.9 10.8 %shard_map.349.refs_5_ = bf16[2048,512]{1,0:T(8,128)(2,1)} custom-call(bf16[256,2048]{1,0:T(8,128)(2,1)} %get-tuple-element.163.refs_0_, bf16[256,2048]{1,0:T(8,128)(2,1)} %copy-done.56, bf16[128,2048]{1,0:T(8,128)(2,1)} %collective-permute-done.49.refs_2_, bf16[128,2048]{1,0:T(8,128)(2,1)} %collective-permute-done.50.refs_3_, ...), custom_call_target="tpu_custom_call" | custom-call | flops 8589934592 | bytes 25165824 | tf_op jit(solution)/shard_map/pallas_call | solution.py:45
  721.7 14.6 %shard_map.350 = (bf16[1024,1536]{1,0:T(8,128)(2,1)}, f32[2,1,768]{2,1,0:T(1,128)}) custom-call(f32[1024,1]{1,0:T(8,128)} %bitcast.99, bf16[1024,1536]{1,0:T(8,128)(2,1)} %shard_map.326.refs_1_, bf16[1024,512]{1,0:T(8,128)(2,1)} %get-tuple-element.122.refs_0_.refs_11_.refs_2_, bf16[1024,512]{1,0:T(8,128)(2,1)} %shard_map.348.refs_12_.refs_3_, ...), custom_call_target="tpu_custom_call" | custom-call | flops 42949672960 | bytes 18874368 | tf_op jit(solution)/shard_map/pallas_call | solution.py:45
  752.0 20.2 %shard_map.352 = (bf16[1088,1536]{1,0:T(8,128)(2,1)}, bf16[1088,1536]{1,0:T(8,128)(2,1)}) custom-call(s32[1]{0:T(128)} %bitcast.27.refs_0_, f32[1,1536]{1,0:T(1,128)} %bitcast.109, bf16[256,2048]{1,0:T(8,128)(2,1)} %bitcast.89, bf16[256,2048]{1,0:T(8,128)(2,1)} %copy-done.55, bf16[128,2048]{1,0:T(8,128)(2,1)} %collective-permute-done.2.refs_2_.refs_4_, ...), custom_call_target="tpu_custom_call" | custom-call | flops 25769803776 | bytes 41943040 | tf_op jit(solution)/shard_map/pallas_call | solution.py:45
  778.6 11.6 %shard_map.353 = (bf16[512,1024]{1,0:T(8,128)(2,1)}, bf16[256,1024]{1,0:T(8,128)(2,1)}, bf16[256,1024]{1,0:T(8,128)(2,1)}, bf16[512,1024]{1,0:T(8,128)(2,1)}, bf...) custom-call(bf16[1024,1536]{1,0:T(8,128)(2,1)} %get-tuple-element.189.refs_7_.refs_13_.refs_0_, ...), custom_call_target="tpu_custom_call" | custom-call | flops 12884901888 | bytes 27262976 | tf_op jit(solution)/shard_map/pallas_call | solution.py:45
  803.7 11.4 %collective-permute-done.69.refs_4_ = bf16[512,1024]{1,0:T(8,128)(2,1)} collective-permute-done((bf16[512,1024]{1,0:T(8,128)(2,1)}, bf16[512,1024]{1,0:T(8,128)(2,1)}, u32[]{:S(2)}, u32[]{:S(2)}) %collective-permute-start.69) | collective-permute-done | bytes 1048608 | tf_op jit(solution)/shard_map/ppermute | solution.py:429
  859.2 11.1 %collective-permute-done.76 = bf16[272,1536]{1,0:T(8,128)(2,1)} collective-permute-done((bf16[272,1536]{1,0:T(8,128)(2,1)}, bf16[272,1536]{1,0:T(8,128)(2,1)}, u32[]{:S(2)}, u32[]{:S(2)}) %collective-permute-start.76) | collective-permute-done | bytes 835616 | tf_op jit(solution)/shard_map/ppermute | solution.py:486
  (532 shorter events, 363.1 us)
Async XLA Ops:
  10.8 51.3 %all-to-all-start = ((bf16[8,2,32,2048]{3,2,1,0:T(8,128)(2,1)}), bf16[8,2,32,2048]{3,2,1,0:T(8,128)(2,1)S(1)}, u32[]{:S(2)}, u32[]{:S(2)}) async-start(bf16[8,2,32,2048]{3,2,1,0:T(8,128)(2,1)} %bitcast.82), calls=%async_computation | async-start | bytes 4194304 | tf_op jit(solution)/shard_map/all_to_all | solution.py:588
  16.7 116.4 %all-gather.5.cloned.1.call-start = ((), (), s32[]{:S(2)}) async-start(), calls=%async_computation.8 | async-start | bytes 7667712 | tf_op jit(solution)/shard_map/all_gather | solution.py:489
  64.2 101.2 %all-gather.7.cloned.1.call-start = ((), (), s32[]{:S(2)}) async-start(), calls=%async_computation.9 | async-start | bytes 2359296 | tf_op jit(solution)/shard_map/all_gather | solution.py:489
  66.9 235.5 %all-gather.9.cloned.1.call-start = ((), (), s32[]{:S(2)}) async-start(), calls=%async_computation.10 | async-start | bytes 9437184 | tf_op jit(solution)/shard_map/all_gather | solution.py:489
  69.7 258.4 %all-gather.11.cloned.1.call-start = ((), (), s32[]{:S(2)}) async-start(), calls=%async_computation.11 | async-start | bytes 9437184 | tf_op jit(solution)/shard_map/all_gather | solution.py:489
  71.1 38.0 %collective-permute-start.1 = (bf16[256,2048]{1,0:T(8,128)(2,1)S(1)}, bf16[256,2048]{1,0:T(8,128)(2,1)}, u32[]{:S(2)}, u32[]{:S(2)}) collective-permute-start(bf16[256,2048]{1,0:T(8,128)(2,1)S(1)} %bitcast.86), channel_id=1, source_target_pairs={{0,2},{1,3},{2,0},{3,1},{4,6},{5,7},{6,4},{7,5},{8,10},{9,11},{10,... | collective-permute-start | bytes 3145736 | tf_op jit(solution)/shard_map/ppermute | solution.py:429
  123.3 51.2 %collective-permute-start.13 = (bf16[128,2048]{1,0:T(8,128)(2,1)S(1)}, bf16[128,2048]{1,0:T(8,128)(2,1)}, u32[]{:S(2)}, u32[]{:S(2)}) collective-permute-start(bf16[128,2048]{1,0:T(8,128)(2,1)S(1)} %slice.434), channel_id=1, source_target_pairs={{0,1},{1,0},{2,3},{3,2},{4,5},{5,4},{6,7},{7,6},{8,9},{9,8},{10,11... | collective-permute-start | bytes 1572872 | tf_op jit(solution)/shard_map/ppermute | solution.py:429
  125.5 49.0 %collective-permute-start.14 = (bf16[128,2048]{1,0:T(8,128)(2,1)}, bf16[128,2048]{1,0:T(8,128)(2,1)}, u32[]{:S(2)}, u32[]{:S(2)}) collective-permute-start(bf16[128,2048]{1,0:T(8,128)(2,1)} %slice.435), channel_id=1, source_target_pairs={{0,2},{1,3},{2,0},{3,1},{4,6},{5,7},{6,4},{7,5},{8,10},{9,11},{10,... | collective-permute-start | bytes 1572872 | tf_op jit(solution)/shard_map/ppermute | solution.py:429
  228.5 44.4 %collective-permute-start.21 = (bf16[512,1024]{1,0:T(8,128)(2,1)}, bf16[512,1024]{1,0:T(8,128)(2,1)S(1)}, u32[]{:S(2)}, u32[]{:S(2)}) collective-permute-start(bf16[512,1024]{1,0:T(8,128)(2,1)} %get-tuple-element.128), channel_id=1, source_target_pairs={{0,2},{1,3},{2,0},{3,1},{4,6},{5,7},{6,4},{7,5},{8,10},{9,11},{10,... | collective-permute-start | bytes 3145736 | tf_op jit(solution)/shard_map/ppermute | solution.py:429
  229.3 44.1 %collective-permute-start.19 = (bf16[512,1024]{1,0:T(8,128)(2,1)}, bf16[512,1024]{1,0:T(8,128)(2,1)S(1)}, u32[]{:S(2)}, u32[]{:S(2)}) collective-permute-start(bf16[512,1024]{1,0:T(8,128)(2,1)} %get-tuple-element.123.refs_8_), channel_id=1, source_target_pairs={{0,1},{1,0},{2,3},{3,2},{4,5},{5,4},{6,7},{7,6},{8,9},{9,8},{10,11... | collective-permute-start | bytes 3145736 | tf_op jit(solution)/shard_map/ppermute | solution.py:429
  250.4 33.8 %collective-permute-start.17 = (bf16[128,2048]{1,0:T(8,128)(2,1)S(1)}, bf16[128,2048]{1,0:T(8,128)(2,1)S(1)}, u32[]{:S(2)}, u32[]{:S(2)}) collective-permute-start(bf16[128,2048]{1,0:T(8,128)(2,1)S(1)} %slice.436), channel_id=1, source_target_pairs={{0,1},{1,0},{2,3},{3,2},{4,5},{5,4},{6,7},{7,6},{8,9},{9,8},{10,11... | collective-permute-start | bytes 1572872 | tf_op jit(solution)/shard_map/ppermute | solution.py:429
  250.8 33.5 %collective-permute-start.18 = (bf16[128,2048]{1,0:T(8,128)(2,1)S(1)}, bf16[128,2048]{1,0:T(8,128)(2,1)}, u32[]{:S(2)}, u32[]{:S(2)}) collective-permute-start(bf16[128,2048]{1,0:T(8,128)(2,1)S(1)} %slice.437), channel_id=1, source_target_pairs={{0,2},{1,3},{2,0},{3,1},{4,6},{5,7},{6,4},{7,5},{8,10},{9,11},{10,... | collective-permute-start | bytes 1572872 | tf_op jit(solution)/shard_map/ppermute | solution.py:429
  401.5 31.9 %collective-permute-start.36 = (bf16[256,2048]{1,0:T(8,128)(2,1)}, bf16[256,2048]{1,0:T(8,128)(2,1)S(1)}, u32[]{:S(2)}, u32[]{:S(2)}) collective-permute-start(bf16[256,2048]{1,0:T(8,128)(2,1)} %get-tuple-element.148.refs_0_), channel_id=1, source_target_pairs={{0,2},{1,3},{2,0},{3,1},{4,6},{5,7},{6,4},{7,5},{8,10},{9,11},{10,... | collective-permute-start | bytes 3145736 | tf_op jit(solution)/shard_map/ppermute | solution.py:429
  403.0 31.7 %collective-permute-start.35 = (bf16[256,2048]{1,0:T(8,128)(2,1)}, bf16[256,2048]{1,0:T(8,128)(2,1)S(1)}, u32[]{:S(2)}, u32[]{:S(2)}) collective-permute-start(bf16[256,2048]{1,0:T(8,128)(2,1)} %get-tuple-element.148.refs_0_), channel_id=1, source_target_pairs={{0,1},{1,0},{2,3},{3,2},{4,5},{5,4},{6,7},{7,6},{8,9},{9,8},{10,11... | collective-permute-start | bytes 3145736 | tf_op jit(solution)/shard_map/ppermute | solution.py:429
  413.3 37.3 %collective-permute-start.34 = (bf16[256,1024]{1,0:T(8,128)(2,1)}, bf16[256,1024]{1,0:T(8,128)(2,1)}, u32[]{:S(2)}, u32[]{:S(2)}) collective-permute-start(bf16[256,1024]{1,0:T(8,128)(2,1)} %add_convert_fusion.11), channel_id=1, source_target_pairs={{0,1},{1,0},{2,3},{3,2},{4,5},{5,4},{6,7},{7,6},{8,9},{9,8},{10,11... | collective-permute-start | bytes 1572872 | tf_op jit(solution)/shard_map/ppermute | solution.py:429
  414.8 35.9 %collective-permute-start.32 = (bf16[256,1024]{1,0:T(8,128)(2,1)}, bf16[256,1024]{1,0:T(8,128)(2,1)}, u32[]{:S(2)}, u32[]{:S(2)}) collective-permute-start(bf16[256,1024]{1,0:T(8,128)(2,1)} %add_convert_fusion.12), channel_id=1, source_target_pairs={{0,2},{1,3},{2,0},{3,1},{4,6},{5,7},{6,4},{7,5},{8,10},{9,11},{10,... | collective-permute-start | bytes 1572872 | tf_op jit(solution)/shard_map/ppermute | solution.py:429
  435.8 47.1 %all-to-all-start.1 = ((bf16[8,32,2048]{2,1,0:T(8,128)(2,1)}), bf16[8,32,2048]{2,1,0:T(8,128)(2,1)S(1)}, u32[]{:S(2)}, u32[]{:S(2)}) async-start(bf16[8,32,2048]{2,1,0:T(8,128)(2,1)} %bitcast.96), calls=%async_computation.1 | async-start | bytes 2097152 | tf_op jit(solution)/shard_map/all_to_all | solution.py:698
  482.9 54.7 %all-to-all-start.2 = ((bf16[8,32,2048]{2,1,0:T(8,128)(2,1)}), bf16[8,32,2048]{2,1,0:T(8,128)(2,1)S(1)}, u32[]{:S(2)}, u32[]{:S(2)}) async-start(bf16[8,32,2048]{2,1,0:T(8,128)(2,1)} %bitcast.18), calls=%async_computation.2 | async-start | bytes 2097152 | tf_op jit(solution)/shard_map/all_to_all | solution.py:698
  493.7 254.6 %reduce-scatter.4.cloned.1.call-start = ((), (), s32[]{:S(2)}) async-start(), calls=%async_computation.12 | async-start | bytes 9437184 | tf_op jit(solution)/shard_map/reduce_scatter | solution.py:492
  567.8 270.5 %reduce-scatter.6.cloned.1.call-start = ((), (), s32[]{:S(2)}) async-start(), calls=%async_computation.13 | async-start | bytes 9437184 | tf_op jit(solution)/shard_map/reduce_scatter | solution.py:492
  575.1 44.4 %collective-permute-start.47 = (bf16[256,2048]{1,0:T(8,128)(2,1)}, bf16[256,2048]{1,0:T(8,128)(2,1)S(1)}, u32[]{:S(2)}, u32[]{:S(2)}) collective-permute-start(bf16[256,2048]{1,0:T(8,128)(2,1)} %get-tuple-element.163.refs_0_), channel_id=1, source_target_pairs={{0,1},{1,0},{2,3},{3,2},{4,5},{5,4},{6,7},{7,6},{8,9},{9,8},{10,11... | collective-permute-start | bytes 3145736 | tf_op jit(solution)/shard_map/ppermute | solution.py:429
  575.9 41.1 %collective-permute-start.48 = (bf16[256,2048]{1,0:T(8,128)(2,1)}, bf16[256,2048]{1,0:T(8,128)(2,1)}, u32[]{:S(2)}, u32[]{:S(2)}) collective-permute-start(bf16[256,2048]{1,0:T(8,128)(2,1)} %get-tuple-element.163.refs_0_), channel_id=1, source_target_pairs={{0,2},{1,3},{2,0},{3,1},{4,6},{5,7},{6,4},{7,5},{8,10},{9,11},{10,... | collective-permute-start | bytes 3145736 | tf_op jit(solution)/shard_map/ppermute | solution.py:429
  590.8 31.3 %collective-permute-start.51 = (bf16[512,1024]{1,0:T(8,128)(2,1)}, bf16[512,1024]{1,0:T(8,128)(2,1)S(1)}, u32[]{:S(2)}, u32[]{:S(2)}) collective-permute-start(bf16[512,1024]{1,0:T(8,128)(2,1)} %get-tuple-element.165.refs_12_), channel_id=1, source_target_pairs={{0,1},{1,0},{2,3},{3,2},{4,5},{5,4},{6,7},{7,6},{8,9},{9,8},{10,11... | collective-permute-start | bytes 3145736 | tf_op jit(solution)/shard_map/ppermute | solution.py:429
  689.3 29.7 %collective-permute-start.60 = (bf16[512,1024]{1,0:T(8,128)(2,1)}, bf16[512,1024]{1,0:T(8,128)(2,1)S(1)}, u32[]{:S(2)}, u32[]{:S(2)}) collective-permute-start(bf16[512,1024]{1,0:T(8,128)(2,1)} %get-tuple-element.184), channel_id=1, source_target_pairs={{0,2},{1,3},{2,0},{3,1},{4,6},{5,7},{6,4},{7,5},{8,10},{9,11},{10,... | collective-permute-start | bytes 3145736 | tf_op jit(solution)/shard_map/ppermute | solution.py:429
  690.4 29.4 %collective-permute-start.58 = (bf16[512,1024]{1,0:T(8,128)(2,1)}, bf16[512,1024]{1,0:T(8,128)(2,1)S(1)}, u32[]{:S(2)}, u32[]{:S(2)}) collective-permute-start(bf16[512,1024]{1,0:T(8,128)(2,1)} %get-tuple-element.181.refs_6_), channel_id=1, source_target_pairs={{0,1},{1,0},{2,3},{3,2},{4,5},{5,4},{6,7},{7,6},{8,9},{9,8},{10,11... | collective-permute-start | bytes 3145736 | tf_op jit(solution)/shard_map/ppermute | solution.py:429
  718.7 32.7 %collective-permute-start.66 = (f32[112,128]{1,0:T(8,128)S(1)}, f32[112,128]{1,0:T(8,128)S(1)}, u32[]{:S(2)}, u32[]{:S(2)}) collective-permute-start(f32[112,128]{1,0:T(8,128)S(1)} %add_add_fusion), channel_id=1, source_target_pairs={{0,8},{4,12},{8,0},{12,4},{16,24},{20,28},{24,16},{28,20},{1,9},{5... | collective-permute-start | bytes 172040 | tf_op jit(solution)/shard_map/ppermute | solution.py:535
  742.9 34.7 %all-to-all-start.3 = ((bf16[8,32,2048]{2,1,0:T(8,128)(2,1)}), bf16[8,32,2048]{2,1,0:T(8,128)(2,1)S(1)}, u32[]{:S(2)}, u32[]{:S(2)}) async-start(bf16[8,32,2048]{2,1,0:T(8,128)(2,1)} %bitcast.91), calls=%async_computation.3 | async-start | bytes 2097152 | tf_op jit(solution)/shard_map/all_to_all | solution.py:698
  748.3 105.2 %reduce-scatter.8.cloned.1.call-start = ((), (), s32[]{:S(2)}) async-start(), calls=%async_computation.14 | async-start | bytes 2359296 | tf_op jit(solution)/shard_map/reduce_scatter | solution.py:492
  795.1 30.7 %collective-permute-start.72 = (bf16[272,1536]{1,0:T(8,128)(2,1)}, bf16[272,1536]{1,0:T(8,128)(2,1)S(1)}, u32[]{:S(2)}, u32[]{:S(2)}) collective-permute-start(bf16[272,1536]{1,0:T(8,128)(2,1)} %add_convert_fusion.2), channel_id=1, source_target_pairs={{0,8},{4,12},{8,16},{12,20},{1,9},{5,13},{9,17},{13,21},{2,10},{6,... | collective-permute-start | bytes 2506760 | tf_op jit(solution)/shard_map/ppermute | solution.py:486
  801.6 35.2 %collective-permute-start.74 = (f32[112,128]{1,0:T(8,128)}, f32[112,128]{1,0:T(8,128)S(1)}, u32[]{:S(2)}, u32[]{:S(2)}) collective-permute-start(f32[112,128]{1,0:T(8,128)} %add.392), channel_id=1, source_target_pairs={{0,16},{4,20},{8,24},{12,28},{16,0},{20,4},{24,8},{28,12},{1,17},{... | collective-permute-start | bytes 172040 | tf_op jit(solution)/shard_map/ppermute | solution.py:535
  831.0 39.3 %collective-permute-start.76 = (bf16[272,1536]{1,0:T(8,128)(2,1)}, bf16[272,1536]{1,0:T(8,128)(2,1)}, u32[]{:S(2)}, u32[]{:S(2)}) collective-permute-start(bf16[272,1536]{1,0:T(8,128)(2,1)} %get-tuple-element.257), channel_id=1, source_target_pairs={{0,24},{4,28},{8,0},{12,4},{16,8},{20,12},{24,16},{28,20},{1,25},{... | collective-permute-start | bytes 2506760 | tf_op jit(solution)/shard_map/ppermute | solution.py:486
  845.7 44.8 %all-to-all-start.4 = ((bf16[8,32,2048]{2,1,0:T(8,128)(2,1)}), bf16[8,32,2048]{2,1,0:T(8,128)(2,1)}, u32[]{:S(2)}, u32[]{:S(2)}) async-start(bf16[8,32,2048]{2,1,0:T(8,128)(2,1)} %bitcast.90), calls=%async_computation.6 | async-start | bytes 2097152 | tf_op jit(solution)/shard_map/all_to_all | solution.py:698
  (144 other events, 2043.3 us)
Sparse Core Ops, SparseCore 0:
  64.4 68.6 all-gather.4
  135.3 30.1 all-gather.6
  167.0 78.9 all-gather.8
  247.4 80.5 all-gather.10
  567.9 89.2 reduce-scatter.3
  659.4 87.0 reduce-scatter.5
  777.7 34.9 reduce-scatter.7

commit v10 on v9

--- a/solution.py
+++ b/solution.py
@@ -721,7 +721,7 @@
         hidden_grad.append(grad)
         up_sums.append(total)
         if s == 0:
-            terms.append(terms_matmul(grad, up_full, spans, (*near(down_pieces[1]), returned_rows[0])))
+            terms.append(terms_matmul(grad, up_full, spans, near(down_pieces[1])))
             first_sums.append(tensor.scatter(terms[s]))
             before = (terms[s][0][0],)
     first_back = []

time: 920 us -> 916 us (level)
    unnamed x198 -> x200, local copies, waits for them, and re-layouts: 30 us -> 30.9 us
  transfers between devices with their start and end apart: 89 -> 89, of which waited for: 28 -> 26; matrix products, arithmetic and copies ran while one was open for 12% -> 12% of each run, Pallas kernels for 41% -> 41%
where the time goes in v10:
time: 916 us; the launch traced here: 900 us
  Pallas kernels  383 us (42%)
  waiting for transfers between devices  240 us (26%)
  starting transfers between devices  116 us (13%)
  local copies, waits for them, and re-layouts  80.2 us (9%)
  other arithmetic  54.7 us (6%)
  between operations  26.1 us (3%)
    pallas_call x32, Pallas kernels, launch(): pl.pallas_call(run, grid=grid, in_specs=list(in_specs) + [pl.BlockSpec(me...  383 us
    ppermute x67, waiting for transfers between devices, swap(): lax.ppermute(array, 'tensor', [(i, i ^ bit) for i in range(self.size)])  158 us
    ppermute x67, starting transfers between devices, swap(): lax.ppermute(array, 'tensor', [(i, i ^ bit) for i in range(self.size)])  54.5 us
    all_to_all x1, waiting for transfers between devices, local(): came = lax.all_to_all(sent, 'dp', split_axis=0, concat_axis=0, tiled=True)  41.3 us
    all_to_all x4, starting transfers between devices, give_back(): lax.all_to_all(rows.reshape(groups, arrival_rows, model_width), 'dp', spl...  38.7 us
    unnamed x200, local copies, waits for them, and re-layouts  30.9 us
  transfers between devices with their start and end apart: 89, of which 26 were waited for; matrix products, arithmetic and copies ran while one was open for 12% of the time, Pallas kernels for 41%

profile of v10, /device:TPU:9, one launch (start us, length us, event | category | flops | bytes accessed | tf_op | source)
XLA Modules:
  0.0 900.0 jit_solution(16356236077615742060)
XLA Ops:
  20.8 41.3 %all-to-all-done = bf16[8,2,32,2048]{3,2,1,0:T(8,128)(2,1)S(1)} async-done(((bf16[8,2,32,2048]{3,2,1,0:T(8,128)(2,1)}), bf16[8,2,32,2048]{3,2,1,0:T(8,128)(2,1)S(1)}, u32[]{:S(2)}, u32[]{:S(2)}) %all-to-all-start) | async-done | bytes 2097184 | tf_op jit(solution)/shard_map/all_to_all | solution.py:588
  72.3 21.9 %collective-permute-done.refs_1_.refs_3_ = bf16[256,2048]{1,0:T(8,128)(2,1)S(1)} collective-permute-done((bf16[256,2048]{1,0:T(8,128)(2,1)S(1)}, bf16[256,2048]{1,0:T(8,128)(2,1)S(1)}, u32[]{:S(2)}, u32[]{:S(2)}) %collective-permute-start) | collective-permute-done | bytes 1048608 | tf_op jit(solution)/shard_map/ppermute | solution.py:429
  110.3 11.9 %collective-permute-done.5.refs_8_.refs_4_.refs_11_ = bf16[256,2048]{1,0:T(8,128)(2,1)} collective-permute-done((bf16[256,2048]{1,0:T(8,128)(2,1)}, bf16[256,2048]{1,0:T(8,128)(2,1)}, u32[]{:S(2)}, u32[]{:S(2)}) %collective-permute-start.5) | collective-permute-done | bytes 1048608 | tf_op jit(solution)/shard_map/ppermute | solution.py:429
  138.1 11.7 %shard_map.323.refs_1_ = bf16[1024,1536]{1,0:T(8,128)(2,1)} custom-call(bf16[256,2048]{1,0:T(8,128)(2,1)} %bitcast.87, bf16[256,2048]{1,0:T(8,128)(2,1)} %copy-done.56, bf16[128,2048]{1,0:T(8,128)(2,1)} %collective-permute-done.2.refs_2_.refs_4_, bf16[128,2048]{1,0:T(8,128)(2,1)} %collective-permute-done.3.refs_3_.refs_5_, ...), custom_call_target="tpu_custom_call" | custom-call | flops 12884901888 | bytes 33554432 | tf_op jit(solution)/shard_map/pallas_call | solution.py:45
  149.8 14.0 %shard_map.324 = (bf16[1024,512]{1,0:T(8,128)(2,1)}, f32[2,2,1024]{2,1,0:T(2,128)}) custom-call(f32[1024,1]{1,0:T(8,128)} %bitcast.101, bf16[1024,1536]{1,0:T(8,128)(2,1)} %shard_map.323.refs_1_), custom_call_target="tpu_custom_call" | custom-call | flops 17179869184 | bytes 9437184 | tf_op jit(solution)/shard_map/pallas_call | solution.py:45
  174.5 12.5 %shard_map.326.refs_1_ = bf16[1024,1536]{1,0:T(8,128)(2,1)} custom-call(bf16[256,2048]{1,0:T(8,128)(2,1)} %bitcast.8.refs_0_.refs_6_.refs_7_, bf16[256,2048]{1,0:T(8,128)(2,1)} %collective-permute-done.4.refs_7_.refs_1_.refs_8_, bf16[128,2048]{1,0:T(8,128)(2,1)} %collective-permute-done.13.refs_2_.refs_9_, ...), custom_call_target="tpu_custom_call" | custom-call | flops 12884901888 | bytes 33554432 | tf_op jit(solution)/shard_map/pallas_call | solution.py:45
  187.0 9.3 %collective-permute-done.11.refs_4_ = bf16[512,1024]{1,0:T(8,128)(2,1)S(1)} collective-permute-done((bf16[512,1024]{1,0:T(8,128)(2,1)}, bf16[512,1024]{1,0:T(8,128)(2,1)S(1)}, u32[]{:S(2)}, u32[]{:S(2)}) %collective-permute-start.11) | collective-permute-done | bytes 1048608 | tf_op jit(solution)/shard_map/ppermute | solution.py:429
  200.1 14.1 %shard_map.327 = (bf16[1024,512]{1,0:T(8,128)(2,1)}, f32[2,2,1024]{2,1,0:T(2,128)}) custom-call(f32[1024,1]{1,0:T(8,128)} %bitcast.99, bf16[1024,1536]{1,0:T(8,128)(2,1)} %shard_map.326.refs_1_), custom_call_target="tpu_custom_call" | custom-call | flops 17179869184 | bytes 9437184 | tf_op jit(solution)/shard_map/pallas_call | solution.py:45
  230.3 19.8 %collective-permute-done.16.refs_11_.refs_4_ = bf16[256,2048]{1,0:T(8,128)(2,1)S(1)} collective-permute-done((bf16[256,2048]{1,0:T(8,128)(2,1)}, bf16[256,2048]{1,0:T(8,128)(2,1)S(1)}, u32[]{:S(2)}, u32[]{:S(2)}) %collective-permute-start.16) | collective-permute-done | bytes 1048608 | tf_op jit(solution)/shard_map/ppermute | solution.py:429
  251.4 21.3 %collective-permute-done.21.refs_4_ = bf16[512,1024]{1,0:T(8,128)(2,1)S(1)} collective-permute-done((bf16[512,1024]{1,0:T(8,128)(2,1)}, bf16[512,1024]{1,0:T(8,128)(2,1)S(1)}, u32[]{:S(2)}, u32[]{:S(2)}) %collective-permute-start.21) | collective-permute-done | bytes 1048608 | tf_op jit(solution)/shard_map/ppermute | solution.py:429
  284.0 11.2 %collective-permute-done.22.refs_5_ = bf16[256,1024]{1,0:T(8,128)(2,1)} collective-permute-done((bf16[256,1024]{1,0:T(8,128)(2,1)S(1)}, bf16[256,1024]{1,0:T(8,128)(2,1)}, u32[]{:S(2)}, u32[]{:S(2)}) %collective-permute-start.22) | collective-permute-done | bytes 524320 | tf_op jit(solution)/shard_map/ppermute | solution.py:429
  302.1 16.2 %shard_map.331 = (f32[1024,2048]{1,0:T(8,128)}, bf16[1024,2048]{1,0:T(8,128)(2,1)}) custom-call(bf16[256,2048]{1,0:T(8,128)(2,1)} %get-tuple-element.124.refs_0_, bf16[256,2048]{1,0:T(8,128)(2,1)} %copy-done.29, bf16[128,2048]{1,0:T(8,128)(2,1)} %copy-done.32, bf16[128,2048]{1,0:T(8,128)(2,1)} %collective-permute-done.18.refs_10_.refs_3_, ...), custom_call_target="tpu_custom_call" | custom-call | flops 17179869184 | bytes 58720256 | tf_op jit(solution)/shard_map/pallas_call | solution.py:45
  334.7 14.6 %shard_map.332 = (bf16[512,1024]{1,0:T(8,128)(2,1)}, bf16[256,1024]{1,0:T(8,128)(2,1)}, bf16[256,1024]{1,0:T(8,128)(2,1)}, bf16[512,1024]{1,0:T(8,128)(2,1)}, bf...) custom-call(bf16[1024,2048]{1,0:T(8,128)(2,1)} %get-tuple-element.131.refs_0_.refs_10_, ...), custom_call_target="tpu_custom_call" | custom-call | flops 17179869184 | bytes 33554432 | tf_op jit(solution)/shard_map/pallas_call | solution.py:45
  352.1 16.0 %shard_map.333 = (f32[1024,2048]{1,0:T(8,128)}, bf16[1024,2048]{1,0:T(8,128)(2,1)}) custom-call(bf16[256,2048]{1,0:T(8,128)(2,1)} %get-tuple-element.130.refs_7_.refs_0_.refs_5_, bf16[256,2048]{1,0:T(8,128)(2,1)} %copy-done.61, bf16[128,2048]{1,0:T(8,128)(2,1)} %collective-permute-done.25.refs_3_.refs_2_.refs_7_, ...), custom_call_target="tpu_custom_call" | custom-call | flops 17179869184 | bytes 58720256 | tf_op jit(solution)/shard_map/pallas_call | solution.py:45
  376.1 14.2 %shard_map.334 = (bf16[512,1024]{1,0:T(8,128)(2,1)}, bf16[256,1024]{1,0:T(8,128)(2,1)}, bf16[256,1024]{1,0:T(8,128)(2,1)}, bf16[512,1024]{1,0:T(8,128)(2,1)}, bf...) custom-call(bf16[1024,2048]{1,0:T(8,128)(2,1)} %get-tuple-element.139.refs_0_.refs_11_, ...), custom_call_target="tpu_custom_call" | custom-call | flops 17179869184 | bytes 33554432 | tf_op jit(solution)/shard_map/pallas_call | solution.py:45
  414.3 18.7 %collective-permute-done.36.refs_10_.refs_4_ = bf16[256,2048]{1,0:T(8,128)(2,1)S(1)} collective-permute-done((bf16[256,2048]{1,0:T(8,128)(2,1)}, bf16[256,2048]{1,0:T(8,128)(2,1)S(1)}, u32[]{:S(2)}, u32[]{:S(2)}) %collective-permute-start.36) | collective-permute-done | bytes 1048608 | tf_op jit(solution)/shard_map/ppermute | solution.py:429
  435.3 15.8 %all-to-all-start.1 = ((bf16[8,32,2048]{2,1,0:T(8,128)(2,1)}), bf16[8,32,2048]{2,1,0:T(8,128)(2,1)S(1)}, u32[]{:S(2)}, u32[]{:S(2)}) async-start(bf16[8,32,2048]{2,1,0:T(8,128)(2,1)} %bitcast.96), calls=%async_computation.1 | async-start | bytes 2097152 | tf_op jit(solution)/shard_map/all_to_all | solution.py:698
  460.2 18.6 %shard_map.337 = (bf16[1024,2048]{1,0:T(8,128)(2,1)}, f32[1,2048]{1,0:T(1,128)}) custom-call(bf16[256,2048]{1,0:T(8,128)(2,1)} %get-tuple-element.148.refs_0_, bf16[256,2048]{1,0:T(8,128)(2,1)} %copy-done.23, bf16[128,2048]{1,0:T(8,128)(2,1)} %collective-permute-done.37.refs_2_, bf16[128,2048]{1,0:T(8,128)(2,1)} %copy-done.76, bf16[256,2048]{1,0:T(8,128)(2,1)} %copy-done.22, ...), custom_call_target="tpu_custom_call" | custom-call | flops 17179869184 | bytes 41959424 | tf_op jit(solution)/shard_map/pallas_call | solution.py:45
  483.2 14.3 %shard_map.338 = (bf16[512,1024]{1,0:T(8,128)(2,1)}, bf16[256,1024]{1,0:T(8,128)(2,1)}, bf16[256,1024]{1,0:T(8,128)(2,1)}, bf16[512,1024]{1,0:T(8,128)(2,1)}, bf...) custom-call(bf16[1024,2048]{1,0:T(8,128)(2,1)} %get-tuple-element.151.refs_0_.refs_10_, ...), custom_call_target="tpu_custom_call" | custom-call | flops 17179869184 | bytes 33554432 | tf_op jit(solution)/shard_map/pallas_call | solution.py:45
  498.8 11.1 %all-to-all-start.2 = ((bf16[8,32,2048]{2,1,0:T(8,128)(2,1)}), bf16[8,32,2048]{2,1,0:T(8,128)(2,1)S(1)}, u32[]{:S(2)}, u32[]{:S(2)}) async-start(bf16[8,32,2048]{2,1,0:T(8,128)(2,1)} %bitcast.97), calls=%async_computation.2 | async-start | bytes 2097152 | tf_op jit(solution)/shard_map/all_to_all | solution.py:698
  509.9 18.6 %shard_map.339 = (bf16[1024,2048]{1,0:T(8,128)(2,1)}, f32[1,2048]{1,0:T(1,128)}) custom-call(bf16[256,2048]{1,0:T(8,128)(2,1)} %get-tuple-element.152.refs_0_.refs_5_, bf16[256,2048]{1,0:T(8,128)(2,1)} %copy-done.58, bf16[128,2048]{1,0:T(8,128)(2,1)} %collective-permute-done.45.refs_2_.refs_7_, bf16[128,2048]{1,0:T(8,128)(2,1)} %collective-permute-done.46.refs_3_.refs_8_, ...), custom_call_target="tpu_custom_call" | custom-call | flops 17179869184 | bytes 41959424 | tf_op jit(solution)/shard_map/pallas_call | solution.py:45
  535.4 24.3 %shard_map.340 = bf16[2048,2048]{1,0:T(8,128)(2,1)} custom-call(bf16[256,2048]{1,0:T(8,128)(2,1)} %get-tuple-element.148.refs_0_, bf16[256,2048]{1,0:T(8,128)(2,1)} %copy-done.23, bf16[128,2048]{1,0:T(8,128)(2,1)} %collective-permute-done.37.refs_2_, bf16[128,2048]{1,0:T(8,128)(2,1)} %copy-done.76, bf16[256,2048]{1,0:T(8,128)(2,1)} %copy-done.22, ...), custom_call_target="tpu_custom_call" | custom-call | flops 34359738368 | bytes 50331648 | tf_op jit(solution)/shard_map/pallas_call | solution.py:45
  572.4 14.2 %shard_map.342 = (bf16[512,1024]{1,0:T(8,128)(2,1)}, bf16[256,1024]{1,0:T(8,128)(2,1)}, bf16[256,1024]{1,0:T(8,128)(2,1)}, bf16[512,1024]{1,0:T(8,128)(2,1)}, bf...) custom-call(bf16[1024,2048]{1,0:T(8,128)(2,1)} %get-tuple-element.162.refs_12_.refs_0_.refs_11_, ...), custom_call_target="tpu_custom_call" | custom-call | flops 17179869184 | bytes 33554432 | tf_op jit(solution)/shard_map/pallas_call | solution.py:45
  588.0 24.4 %shard_map.343 = bf16[2048,2048]{1,0:T(8,128)(2,1)} custom-call(bf16[256,2048]{1,0:T(8,128)(2,1)} %get-tuple-element.124.refs_0_, bf16[256,2048]{1,0:T(8,128)(2,1)} %copy-done.29, bf16[128,2048]{1,0:T(8,128)(2,1)} %copy-done.32, bf16[128,2048]{1,0:T(8,128)(2,1)} %collective-permute-done.18.refs_10_.refs_3_, bf16[256,2048]{1,0:T(8,128)(2,1)} %copy-done.28, ...), custom_call_target="tpu_custom_call" | custom-call | flops 34359738368 | bytes 50331648 | tf_op jit(solution)/shard_map/pallas_call | solution.py:45
  652.5 14.8 %shard_map.345 = (bf16[1024,1536]{1,0:T(8,128)(2,1)}, f32[2,1,768]{2,1,0:T(1,128)}) custom-call(f32[1024,1]{1,0:T(8,128)} %bitcast.102, bf16[1024,1536]{1,0:T(8,128)(2,1)} %shard_map.323.refs_1_, bf16[1024,512]{1,0:T(8,128)(2,1)} %get-tuple-element.115.refs_0_.refs_2_.refs_10_, bf16[1024,512]{1,0:T(8,128)(2,1)} %shard_map.344.refs_3_, ...), custom_call_target="tpu_custom_call" | custom-call | flops 42949672960 | bytes 18874368 | tf_op jit(solution)/shard_map/pallas_call | solution.py:45
  675.8 11.5 %shard_map.347 = (bf16[512,1024]{1,0:T(8,128)(2,1)}, bf16[256,1024]{1,0:T(8,128)(2,1)}, bf16[256,1024]{1,0:T(8,128)(2,1)}, bf16[512,1024]{1,0:T(8,128)(2,1)}, bf...) custom-call(bf16[1024,1536]{1,0:T(8,128)(2,1)} %get-tuple-element.168.refs_0_.refs_12_, ...), custom_call_target="tpu_custom_call" | custom-call | flops 12884901888 | bytes 27262976 | tf_op jit(solution)/shard_map/pallas_call | solution.py:45
  701.9 10.8 %shard_map.349.refs_5_ = bf16[2048,512]{1,0:T(8,128)(2,1)} custom-call(bf16[256,2048]{1,0:T(8,128)(2,1)} %get-tuple-element.163.refs_0_, bf16[256,2048]{1,0:T(8,128)(2,1)} %copy-done.57, bf16[128,2048]{1,0:T(8,128)(2,1)} %collective-permute-done.49.refs_2_, bf16[128,2048]{1,0:T(8,128)(2,1)} %collective-permute-done.50.refs_3_, ...), custom_call_target="tpu_custom_call" | custom-call | flops 8589934592 | bytes 25165824 | tf_op jit(solution)/shard_map/pallas_call | solution.py:45
  718.6 14.7 %shard_map.350 = (bf16[1024,1536]{1,0:T(8,128)(2,1)}, f32[2,1,768]{2,1,0:T(1,128)}) custom-call(f32[1024,1]{1,0:T(8,128)} %bitcast.100, bf16[1024,1536]{1,0:T(8,128)(2,1)} %shard_map.326.refs_1_, bf16[1024,512]{1,0:T(8,128)(2,1)} %get-tuple-element.122.refs_0_.refs_11_.refs_2_, bf16[1024,512]{1,0:T(8,128)(2,1)} %shard_map.348.refs_12_.refs_3_, ...), custom_call_target="tpu_custom_call" | custom-call | flops 42949672960 | bytes 18874368 | tf_op jit(solution)/shard_map/pallas_call | solution.py:45
  748.4 20.2 %shard_map.352 = (bf16[1088,1536]{1,0:T(8,128)(2,1)}, bf16[1088,1536]{1,0:T(8,128)(2,1)}) custom-call(s32[1]{0:T(128)} %bitcast.27.refs_0_, f32[1,1536]{1,0:T(1,128)} %bitcast.110, bf16[256,2048]{1,0:T(8,128)(2,1)} %bitcast.89, bf16[256,2048]{1,0:T(8,128)(2,1)} %copy-done.56, bf16[128,2048]{1,0:T(8,128)(2,1)} %collective-permute-done.2.refs_2_.refs_4_, ...), custom_call_target="tpu_custom_call" | custom-call | flops 25769803776 | bytes 41943040 | tf_op jit(solution)/shard_map/pallas_call | solution.py:45
  775.2 11.6 %shard_map.353 = (bf16[512,1024]{1,0:T(8,128)(2,1)}, bf16[256,1024]{1,0:T(8,128)(2,1)}, bf16[256,1024]{1,0:T(8,128)(2,1)}, bf16[512,1024]{1,0:T(8,128)(2,1)}, bf...) custom-call(bf16[1024,1536]{1,0:T(8,128)(2,1)} %get-tuple-element.189.refs_7_.refs_13_.refs_0_, ...), custom_call_target="tpu_custom_call" | custom-call | flops 12884901888 | bytes 27262976 | tf_op jit(solution)/shard_map/pallas_call | solution.py:45
  799.7 11.9 %collective-permute-done.69.refs_4_ = bf16[512,1024]{1,0:T(8,128)(2,1)} collective-permute-done((bf16[512,1024]{1,0:T(8,128)(2,1)}, bf16[512,1024]{1,0:T(8,128)(2,1)}, u32[]{:S(2)}, u32[]{:S(2)}) %collective-permute-start.69) | collective-permute-done | bytes 1048608 | tf_op jit(solution)/shard_map/ppermute | solution.py:429
  855.1 11.1 %collective-permute-done.76 = bf16[272,1536]{1,0:T(8,128)(2,1)} collective-permute-done((bf16[272,1536]{1,0:T(8,128)(2,1)}, bf16[272,1536]{1,0:T(8,128)(2,1)}, u32[]{:S(2)}, u32[]{:S(2)}) %collective-permute-start.76) | collective-permute-done | bytes 835616 | tf_op jit(solution)/shard_map/ppermute | solution.py:486
  (534 shorter events, 357.4 us)
Async XLA Ops:
  10.8 51.3 %all-to-all-start = ((bf16[8,2,32,2048]{3,2,1,0:T(8,128)(2,1)}), bf16[8,2,32,2048]{3,2,1,0:T(8,128)(2,1)S(1)}, u32[]{:S(2)}, u32[]{:S(2)}) async-start(bf16[8,2,32,2048]{3,2,1,0:T(8,128)(2,1)} %bitcast.82), calls=%async_computation | async-start | bytes 4194304 | tf_op jit(solution)/shard_map/all_to_all | solution.py:588
  16.7 116.4 %all-gather.5.cloned.1.call-start = ((), (), s32[]{:S(2)}) async-start(), calls=%async_computation.8 | async-start | bytes 7667712 | tf_op jit(solution)/shard_map/all_gather | solution.py:489
  64.2 101.2 %all-gather.7.cloned.1.call-start = ((), (), s32[]{:S(2)}) async-start(), calls=%async_computation.9 | async-start | bytes 2359296 | tf_op jit(solution)/shard_map/all_gather | solution.py:489
  66.9 235.2 %all-gather.9.cloned.1.call-start = ((), (), s32[]{:S(2)}) async-start(), calls=%async_computation.10 | async-start | bytes 9437184 | tf_op jit(solution)/shard_map/all_gather | solution.py:489
  69.7 258.4 %all-gather.11.cloned.1.call-start = ((), (), s32[]{:S(2)}) async-start(), calls=%async_computation.11 | async-start | bytes 9437184 | tf_op jit(solution)/shard_map/all_gather | solution.py:489
  71.1 37.9 %collective-permute-start.1 = (bf16[256,2048]{1,0:T(8,128)(2,1)S(1)}, bf16[256,2048]{1,0:T(8,128)(2,1)}, u32[]{:S(2)}, u32[]{:S(2)}) collective-permute-start(bf16[256,2048]{1,0:T(8,128)(2,1)S(1)} %bitcast.86), channel_id=1, source_target_pairs={{0,2},{1,3},{2,0},{3,1},{4,6},{5,7},{6,4},{7,5},{8,10},{9,11},{10,... | collective-permute-start | bytes 3145736 | tf_op jit(solution)/shard_map/ppermute | solution.py:429
  123.3 51.2 %collective-permute-start.13 = (bf16[128,2048]{1,0:T(8,128)(2,1)S(1)}, bf16[128,2048]{1,0:T(8,128)(2,1)}, u32[]{:S(2)}, u32[]{:S(2)}) collective-permute-start(bf16[128,2048]{1,0:T(8,128)(2,1)S(1)} %slice.434), channel_id=1, source_target_pairs={{0,1},{1,0},{2,3},{3,2},{4,5},{5,4},{6,7},{7,6},{8,9},{9,8},{10,11... | collective-permute-start | bytes 1572872 | tf_op jit(solution)/shard_map/ppermute | solution.py:429
  125.5 49.1 %collective-permute-start.14 = (bf16[128,2048]{1,0:T(8,128)(2,1)}, bf16[128,2048]{1,0:T(8,128)(2,1)}, u32[]{:S(2)}, u32[]{:S(2)}) collective-permute-start(bf16[128,2048]{1,0:T(8,128)(2,1)} %slice.435), channel_id=1, source_target_pairs={{0,2},{1,3},{2,0},{3,1},{4,6},{5,7},{6,4},{7,5},{8,10},{9,11},{10,... | collective-permute-start | bytes 1572872 | tf_op jit(solution)/shard_map/ppermute | solution.py:429
  228.3 44.4 %collective-permute-start.21 = (bf16[512,1024]{1,0:T(8,128)(2,1)}, bf16[512,1024]{1,0:T(8,128)(2,1)S(1)}, u32[]{:S(2)}, u32[]{:S(2)}) collective-permute-start(bf16[512,1024]{1,0:T(8,128)(2,1)} %get-tuple-element.128), channel_id=1, source_target_pairs={{0,2},{1,3},{2,0},{3,1},{4,6},{5,7},{6,4},{7,5},{8,10},{9,11},{10,... | collective-permute-start | bytes 3145736 | tf_op jit(solution)/shard_map/ppermute | solution.py:429
  229.1 44.0 %collective-permute-start.19 = (bf16[512,1024]{1,0:T(8,128)(2,1)}, bf16[512,1024]{1,0:T(8,128)(2,1)S(1)}, u32[]{:S(2)}, u32[]{:S(2)}) collective-permute-start(bf16[512,1024]{1,0:T(8,128)(2,1)} %get-tuple-element.123.refs_8_), channel_id=1, source_target_pairs={{0,1},{1,0},{2,3},{3,2},{4,5},{5,4},{6,7},{7,6},{8,9},{9,8},{10,11... | collective-permute-start | bytes 3145736 | tf_op jit(solution)/shard_map/ppermute | solution.py:429
  250.2 33.8 %collective-permute-start.17 = (bf16[128,2048]{1,0:T(8,128)(2,1)S(1)}, bf16[128,2048]{1,0:T(8,128)(2,1)S(1)}, u32[]{:S(2)}, u32[]{:S(2)}) collective-permute-start(bf16[128,2048]{1,0:T(8,128)(2,1)S(1)} %slice.436), channel_id=1, source_target_pairs={{0,1},{1,0},{2,3},{3,2},{4,5},{5,4},{6,7},{7,6},{8,9},{9,8},{10,11... | collective-permute-start | bytes 1572872 | tf_op jit(solution)/shard_map/ppermute | solution.py:429
  250.6 33.4 %collective-permute-start.18 = (bf16[128,2048]{1,0:T(8,128)(2,1)S(1)}, bf16[128,2048]{1,0:T(8,128)(2,1)}, u32[]{:S(2)}, u32[]{:S(2)}) collective-permute-start(bf16[128,2048]{1,0:T(8,128)(2,1)S(1)} %slice.437), channel_id=1, source_target_pairs={{0,2},{1,3},{2,0},{3,1},{4,6},{5,7},{6,4},{7,5},{8,10},{9,11},{10,... | collective-permute-start | bytes 1572872 | tf_op jit(solution)/shard_map/ppermute | solution.py:429
  401.2 31.8 %collective-permute-start.36 = (bf16[256,2048]{1,0:T(8,128)(2,1)}, bf16[256,2048]{1,0:T(8,128)(2,1)S(1)}, u32[]{:S(2)}, u32[]{:S(2)}) collective-permute-start(bf16[256,2048]{1,0:T(8,128)(2,1)} %get-tuple-element.148.refs_0_), channel_id=1, source_target_pairs={{0,2},{1,3},{2,0},{3,1},{4,6},{5,7},{6,4},{7,5},{8,10},{9,11},{10,... | collective-permute-start | bytes 3145736 | tf_op jit(solution)/shard_map/ppermute | solution.py:429
  402.7 31.5 %collective-permute-start.35 = (bf16[256,2048]{1,0:T(8,128)(2,1)}, bf16[256,2048]{1,0:T(8,128)(2,1)S(1)}, u32[]{:S(2)}, u32[]{:S(2)}) collective-permute-start(bf16[256,2048]{1,0:T(8,128)(2,1)} %get-tuple-element.148.refs_0_), channel_id=1, source_target_pairs={{0,1},{1,0},{2,3},{3,2},{4,5},{5,4},{6,7},{7,6},{8,9},{9,8},{10,11... | collective-permute-start | bytes 3145736 | tf_op jit(solution)/shard_map/ppermute | solution.py:429
  412.9 38.2 %collective-permute-start.34 = (bf16[256,1024]{1,0:T(8,128)(2,1)}, bf16[256,1024]{1,0:T(8,128)(2,1)}, u32[]{:S(2)}, u32[]{:S(2)}) collective-permute-start(bf16[256,1024]{1,0:T(8,128)(2,1)} %add_convert_fusion.11), channel_id=1, source_target_pairs={{0,1},{1,0},{2,3},{3,2},{4,5},{5,4},{6,7},{7,6},{8,9},{9,8},{10,11... | collective-permute-start | bytes 1572872 | tf_op jit(solution)/shard_map/ppermute | solution.py:429
  414.3 36.8 %collective-permute-start.32 = (bf16[256,1024]{1,0:T(8,128)(2,1)}, bf16[256,1024]{1,0:T(8,128)(2,1)}, u32[]{:S(2)}, u32[]{:S(2)}) collective-permute-start(bf16[256,1024]{1,0:T(8,128)(2,1)} %add_convert_fusion.12), channel_id=1, source_target_pairs={{0,2},{1,3},{2,0},{3,1},{4,6},{5,7},{6,4},{7,5},{8,10},{9,11},{10,... | collective-permute-start | bytes 1572872 | tf_op jit(solution)/shard_map/ppermute | solution.py:429
  435.3 63.5 %all-to-all-start.1 = ((bf16[8,32,2048]{2,1,0:T(8,128)(2,1)}), bf16[8,32,2048]{2,1,0:T(8,128)(2,1)S(1)}, u32[]{:S(2)}, u32[]{:S(2)}) async-start(bf16[8,32,2048]{2,1,0:T(8,128)(2,1)} %bitcast.96), calls=%async_computation.1 | async-start | bytes 2097152 | tf_op jit(solution)/shard_map/all_to_all | solution.py:698
  497.4 31.1 %collective-permute-start.43 = (bf16[512,1024]{1,0:T(8,128)(2,1)}, bf16[512,1024]{1,0:T(8,128)(2,1)S(1)}, u32[]{:S(2)}, u32[]{:S(2)}) collective-permute-start(bf16[512,1024]{1,0:T(8,128)(2,1)} %get-tuple-element.157), channel_id=1, source_target_pairs={{0,2},{1,3},{2,0},{3,1},{4,6},{5,7},{6,4},{7,5},{8,10},{9,11},{10,... | collective-permute-start | bytes 3145736 | tf_op jit(solution)/shard_map/ppermute | solution.py:429
  498.4 34.0 %collective-permute-start.41 = (bf16[512,1024]{1,0:T(8,128)(2,1)}, bf16[512,1024]{1,0:T(8,128)(2,1)}, u32[]{:S(2)}, u32[]{:S(2)}) collective-permute-start(bf16[512,1024]{1,0:T(8,128)(2,1)} %get-tuple-element.154.refs_7_), channel_id=1, source_target_pairs={{0,1},{1,0},{2,3},{3,2},{4,5},{5,4},{6,7},{7,6},{8,9},{9,8},{10,11... | collective-permute-start | bytes 3145736 | tf_op jit(solution)/shard_map/ppermute | solution.py:429
  498.8 35.6 %all-to-all-start.2 = ((bf16[8,32,2048]{2,1,0:T(8,128)(2,1)}), bf16[8,32,2048]{2,1,0:T(8,128)(2,1)S(1)}, u32[]{:S(2)}, u32[]{:S(2)}) async-start(bf16[8,32,2048]{2,1,0:T(8,128)(2,1)} %bitcast.97), calls=%async_computation.2 | async-start | bytes 2097152 | tf_op jit(solution)/shard_map/all_to_all | solution.py:698
  509.9 234.8 %reduce-scatter.4.cloned.1.call-start = ((), (), s32[]{:S(2)}) async-start(), calls=%async_computation.12 | async-start | bytes 9437184 | tf_op jit(solution)/shard_map/reduce_scatter | solution.py:492
  563.4 270.8 %reduce-scatter.6.cloned.1.call-start = ((), (), s32[]{:S(2)}) async-start(), calls=%async_computation.13 | async-start | bytes 9437184 | tf_op jit(solution)/shard_map/reduce_scatter | solution.py:492
  570.8 44.9 %collective-permute-start.47 = (bf16[256,2048]{1,0:T(8,128)(2,1)}, bf16[256,2048]{1,0:T(8,128)(2,1)S(1)}, u32[]{:S(2)}, u32[]{:S(2)}) collective-permute-start(bf16[256,2048]{1,0:T(8,128)(2,1)} %get-tuple-element.163.refs_0_), channel_id=1, source_target_pairs={{0,1},{1,0},{2,3},{3,2},{4,5},{5,4},{6,7},{7,6},{8,9},{9,8},{10,11... | collective-permute-start | bytes 3145736 | tf_op jit(solution)/shard_map/ppermute | solution.py:429
  572.2 40.3 %collective-permute-start.48 = (bf16[256,2048]{1,0:T(8,128)(2,1)}, bf16[256,2048]{1,0:T(8,128)(2,1)}, u32[]{:S(2)}, u32[]{:S(2)}) collective-permute-start(bf16[256,2048]{1,0:T(8,128)(2,1)} %get-tuple-element.163.refs_0_), channel_id=1, source_target_pairs={{0,2},{1,3},{2,0},{3,1},{4,6},{5,7},{6,4},{7,5},{8,10},{9,11},{10,... | collective-permute-start | bytes 3145736 | tf_op jit(solution)/shard_map/ppermute | solution.py:429
  586.5 32.7 %collective-permute-start.51 = (bf16[512,1024]{1,0:T(8,128)(2,1)}, bf16[512,1024]{1,0:T(8,128)(2,1)S(1)}, u32[]{:S(2)}, u32[]{:S(2)}) collective-permute-start(bf16[512,1024]{1,0:T(8,128)(2,1)} %get-tuple-element.165.refs_12_), channel_id=1, source_target_pairs={{0,1},{1,0},{2,3},{3,2},{4,5},{5,4},{6,7},{7,6},{8,9},{9,8},{10,11... | collective-permute-start | bytes 3145736 | tf_op jit(solution)/shard_map/ppermute | solution.py:429
  714.6 33.2 %collective-permute-start.66 = (f32[112,128]{1,0:T(8,128)S(1)}, f32[112,128]{1,0:T(8,128)S(1)}, u32[]{:S(2)}, u32[]{:S(2)}) collective-permute-start(f32[112,128]{1,0:T(8,128)S(1)} %add_add_fusion), channel_id=1, source_target_pairs={{0,8},{4,12},{8,0},{12,4},{16,24},{20,28},{24,16},{28,20},{1,9},{5... | collective-permute-start | bytes 172040 | tf_op jit(solution)/shard_map/ppermute | solution.py:535
  740.0 34.0 %all-to-all-start.3 = ((bf16[8,32,2048]{2,1,0:T(8,128)(2,1)}), bf16[8,32,2048]{2,1,0:T(8,128)(2,1)S(1)}, u32[]{:S(2)}, u32[]{:S(2)}) async-start(bf16[8,32,2048]{2,1,0:T(8,128)(2,1)} %bitcast.91), calls=%async_computation.3 | async-start | bytes 2097152 | tf_op jit(solution)/shard_map/all_to_all | solution.py:698
  744.7 104.7 %reduce-scatter.8.cloned.1.call-start = ((), (), s32[]{:S(2)}) async-start(), calls=%async_computation.14 | async-start | bytes 2359296 | tf_op jit(solution)/shard_map/reduce_scatter | solution.py:492
  791.2 30.7 %collective-permute-start.72 = (bf16[272,1536]{1,0:T(8,128)(2,1)}, bf16[272,1536]{1,0:T(8,128)(2,1)S(1)}, u32[]{:S(2)}, u32[]{:S(2)}) collective-permute-start(bf16[272,1536]{1,0:T(8,128)(2,1)} %add_convert_fusion.2), channel_id=1, source_target_pairs={{0,8},{4,12},{8,16},{12,20},{1,9},{5,13},{9,17},{13,21},{2,10},{6,... | collective-permute-start | bytes 2506760 | tf_op jit(solution)/shard_map/ppermute | solution.py:486
  797.7 35.1 %collective-permute-start.74 = (f32[112,128]{1,0:T(8,128)}, f32[112,128]{1,0:T(8,128)S(1)}, u32[]{:S(2)}, u32[]{:S(2)}) collective-permute-start(f32[112,128]{1,0:T(8,128)} %add.392), channel_id=1, source_target_pairs={{0,16},{4,20},{8,24},{12,28},{16,0},{20,4},{24,8},{28,12},{1,17},{... | collective-permute-start | bytes 172040 | tf_op jit(solution)/shard_map/ppermute | solution.py:535
  826.8 39.3 %collective-permute-start.76 = (bf16[272,1536]{1,0:T(8,128)(2,1)}, bf16[272,1536]{1,0:T(8,128)(2,1)}, u32[]{:S(2)}, u32[]{:S(2)}) collective-permute-start(bf16[272,1536]{1,0:T(8,128)(2,1)} %get-tuple-element.257), channel_id=1, source_target_pairs={{0,24},{4,28},{8,0},{12,4},{16,8},{20,12},{24,16},{28,20},{1,25},{... | collective-permute-start | bytes 2506760 | tf_op jit(solution)/shard_map/ppermute | solution.py:486
  841.7 44.8 %all-to-all-start.4 = ((bf16[8,32,2048]{2,1,0:T(8,128)(2,1)}), bf16[8,32,2048]{2,1,0:T(8,128)(2,1)}, u32[]{:S(2)}, u32[]{:S(2)}) async-start(bf16[8,32,2048]{2,1,0:T(8,128)(2,1)} %bitcast.90), calls=%async_computation.6 | async-start | bytes 2097152 | tf_op jit(solution)/shard_map/all_to_all | solution.py:698
  (145 other events, 2066.1 us)
Sparse Core Ops, SparseCore 0:
  64.4 68.6 all-gather.4
  135.3 30.1 all-gather.6
  167.0 78.9 all-gather.8
  247.4 80.5 all-gather.10
  563.5 88.5 reduce-scatter.3
  654.3 87.0 reduce-scatter.5
  774.2 34.2 reduce-scatter.7
